TPU v7x, 32 devices: a whole 2x2x4 slice. The times are simulated.
32 devices in a mesh: expert: 4 (over x, core), shard: 8 (over z, y).
Axes of the slice: x: 2, y: 2, z: 4, core: 2. Of those that a mesh axis runs over, the one named last changes fastest.
Arguments:
- tokens: bfloat16 [32768, 768], P(('expert', 'shard')), may hold values from -6 to 6
- segments: int32 [32, 1024], P(('expert', 'shard')), may hold values from 0 to 12, never falling along the last dimension, each value on 1 to 256 neighbouring positions
- parents: int32 [32, 13], P(('expert', 'shard')), may hold values from 0 to 11, as said below
- adapter_of: int32 [32], P(('expert', 'shard')), may hold values from 0 to 7
- routes: int32 [32768, 2], P(('expert', 'shard')), may hold values from 0 to 11, all different within a row; in each aligned block of 1024 rows (0 to 1023, 1024 to 2047, ...) at most 192 rows name the same one
- norm_gain: float32 [2, 2, 768], replicated, may hold values from 0.5 to 1.5
- query_key_value_weight: bfloat16 [2, 768, 2304], P(None, 'shard'), may hold values from -0.21875 to 0.21875
- output_weight: bfloat16 [2, 768, 768], P(None, 'shard'), may hold values from -1.75 to 1.75
- adapter_down: bfloat16 [2, 4, 8, 768, 16], replicated, may hold values from -0.21875 to 0.21875
- adapter_up: bfloat16 [2, 4, 8, 768, 16], replicated, may hold values from -0.29882812 to 0.29882812
- router: float32 [2, 768, 12], replicated, may hold values from -0.15625 to 0.15625
- router_residual: float32 [12, 12], replicated, may hold values from -1.5 to 1.5
- const_proj: float32 [2, 2, 768, 2], replicated, may hold values from -0.21875 to 0.21875
- const_vec: float32 [2, 2, 768], replicated, may hold values from -6 to 6
- w_gate_up: bfloat16 [2, 8, 768, 4096], P(None, 'expert', 'shard'), may hold values from -0.21875 to 0.21875
- w_down: bfloat16 [2, 8, 2048, 768], P(None, 'expert', 'shard'), may hold values from -0.125 to 0.125
- out_grad: bfloat16 [32768, 768], P(('expert', 'shard')), may hold values from -6 to 6
Outputs:
- block_out: float32 [32768, 768], P(('expert', 'shard'))
- grad_tokens: float32 [32768, 768], P(('expert', 'shard'))
- grad_adapter_down: float32 [2, 4, 8, 768, 16], P(None, None, 'expert', 'shard')
- grad_adapter_up: float32 [2, 4, 8, 768, 16], P(None, None, 'expert', 'shard')
Inputs may be any that keep to these rules, and one draw needn't show every extreme that they name: Within a tree segment numbers never fall, and each of the 13 segments holds 1 to 256 tokens. parents[t, s] < s for s >= 1 and parents[t, 0] = 0. `routes`: each row names two different experts: 0 to 7 feed-forward, 8 zero, 9 copy, the last two constant. In the rows of one device no expert is named by more than 192 rows, a bound that some block reaches.
All inputs are finite; a program needn't handle non-finite values.
Results may differ from a plain program's by a relative error of at most 0.024.
Values may be sent and summed in bfloat16 or wider, within the bound.
A program may use at most 320 MiB of HBM per device.

v0:
```python
import math

import jax
import jax.numpy as jnp
from jax import lax
from jax.sharding import PartitionSpec as P

D = 768
HEADS = 12
HD = 64
FF = 2048
NFFN = 8
NEXP = 12
NA = 8
NSEG = 13
LAYERS = 2
CAP = 192


HIGH_ACCURACY = lax.Precision.HIGHEST
ADAPTER_SCALE = 2.0
EPSILON = 1e-06


def rounded(value):
    return value.astype(jnp.bfloat16)


def rms_norm(value, gain):
    return value * lax.rsqrt(jnp.mean(value * value, axis=-1, keepdims=True) + EPSILON) * gain


def ancestry(parents):
    indices = jnp.arange(NSEG, dtype=jnp.int32)
    table_rows = [(indices == 0).astype(jnp.float32)]
    for segment in range(1, NSEG):
        inherit = jnp.zeros((NSEG,), jnp.float32)
        for earlier in range(segment):
            inherit = inherit + jnp.where(parents[segment] == earlier, table_rows[earlier], 0.0)
        table_rows.append(jnp.maximum(inherit, (indices == segment).astype(jnp.float32)))
    return jnp.stack(table_rows)


def tree_mask(segments, parents):
    length = segments.shape[0]
    ancestors = ancestry(parents)
    member = (segments[:, None] == jnp.arange(NSEG, dtype=jnp.int32)[None, :]).astype(jnp.float32)
    reach = jnp.dot(
        jnp.dot(member, ancestors, precision=HIGH_ACCURACY), member.T, precision=HIGH_ACCURACY
    )
    places = jnp.arange(length, dtype=jnp.int32)
    allowed = (reach > 0.5) & (places[:, None] >= places[None, :])
    depth = jnp.sum(allowed.astype(jnp.int32), axis=1) - 1
    return (allowed, depth)


def rotate(values, depth):
    half = values.shape[-1] // 2
    inverse = jnp.exp(-math.log(10000.0) * jnp.arange(half, dtype=jnp.float32) / half)
    angles = depth.astype(jnp.float32)[:, None] * inverse[None, :]
    cosine = jnp.cos(angles)[:, None, :]
    sine = jnp.sin(angles)[:, None, :]
    first = values[..., :half]
    second = values[..., half:]
    return jnp.concatenate(
        [first * cosine - second * sine, first * sine + second * cosine], axis=-1
    )


def dispatch_index(routes):
    flat = routes.reshape(-1)
    pairs = flat.shape[0]
    hits = (flat[:, None] == jnp.arange(NEXP, dtype=jnp.int32)[None, :]).astype(jnp.int32)
    slots = jnp.sum((jnp.cumsum(hits, axis=0) - hits) * hits, axis=1)
    target = jnp.where(flat < NFFN, flat * CAP + slots, NFFN * CAP)
    holder = (
        jnp.full((NFFN * CAP + 1,), pairs, jnp.int32)
        .at[target]
        .set(jnp.arange(pairs, dtype=jnp.int32))
    )
    return (holder[: NFFN * CAP], target)


def mixture(normalized_rows, earlier, chosen, routes, router, residual_map, const_proj, const_vec):
    logits = jnp.dot(normalized_rows, router, precision=HIGH_ACCURACY) + jnp.dot(
        earlier, residual_map, precision=HIGH_ACCURACY
    )
    member = (routes[:, :, None] == jnp.arange(NEXP, dtype=jnp.int32)[None, None, :]).astype(
        jnp.float32
    )
    picked = jnp.einsum("tke,te->tk", member, logits, precision=HIGH_ACCURACY)
    gates = jax.nn.softmax(picked, axis=1)
    value = chosen + jnp.where((routes == NFFN + 1)[:, :, None], normalized_rows[:, None, :], 0.0)
    for which in range(2):
        share = jax.nn.softmax(
            jnp.dot(normalized_rows, const_proj[which], precision=HIGH_ACCURACY), axis=-1
        )
        constant = share[:, :1] * normalized_rows + share[:, 1:] * const_vec[which][None, :]
        value = value + jnp.where(
            (routes == NFFN + 2 + which)[:, :, None], constant[:, None, :], 0.0
        )
    return (jnp.sum(gates[:, :, None] * value, axis=1), logits)


def gather_mixer(layer_qkv, layer_out):
    return (
        lax.all_gather(layer_qkv, "shard", axis=0, tiled=True),
        lax.all_gather(layer_out, "shard", axis=0, tiled=True),
    )


def gather_experts(layer_gate_up, layer_down):
    return (
        lax.all_gather(layer_gate_up, "shard", axis=1, tiled=True),
        lax.all_gather(layer_down, "shard", axis=1, tiled=True),
    )


def attend_forward(
    normalized_second,
    tree_segments,
    tree_parents,
    down_sel,
    lift_selected,
    query_key_value_full,
    out_full,
):
    length = normalized_second.shape[0]
    scale = 1.0 / math.sqrt(HD)
    allowed, depth = tree_mask(tree_segments, tree_parents)
    narrow = rounded(
        jnp.einsum(
            "ld,pdr->lpr", normalized_second, down_sel[:3], preferred_element_type=jnp.float32
        )
    )
    additional_term = jnp.einsum(
        "lpr,pdr->lpd", narrow, lift_selected[:3], preferred_element_type=jnp.float32
    ).reshape(length, 3 * D)
    projected_output = (
        jnp.dot(normalized_second, query_key_value_full, preferred_element_type=jnp.float32)
        + ADAPTER_SCALE * additional_term
    )
    query = rounded(rotate(projected_output[:, :D].reshape(length, HEADS, HD), depth)).transpose(
        1, 0, 2
    )
    keys = rounded(
        rotate(projected_output[:, D : 2 * D].reshape(length, HEADS, HD), depth)
    ).transpose(1, 0, 2)
    values = rounded(projected_output[:, 2 * D :].reshape(length, HEADS, HD)).transpose(1, 0, 2)

    def one_head(items):
        head_query, head_keys, head_values = items
        scores = (
            jnp.einsum("qd,kd->qk", head_query, head_keys, preferred_element_type=jnp.float32)
            * scale
        )
        masked = jnp.where(allowed, scores, -1e30)
        top = jnp.max(masked, axis=-1, keepdims=True)
        weights = jnp.exp(masked - top)
        total = jnp.sum(weights, axis=-1, keepdims=True)
        head_out = jnp.dot(
            rounded(weights / total), head_values, preferred_element_type=jnp.float32
        )
        return (head_out, (top + jnp.log(total))[:, 0])

    head_outs, log_total = lax.map(one_head, (query, keys, values))
    mixed_b = rounded(head_outs.transpose(1, 0, 2).reshape(length, D))
    reduced_output = rounded(jnp.dot(mixed_b, down_sel[3], preferred_element_type=jnp.float32))
    attended = jnp.dot(
        mixed_b, out_full, preferred_element_type=jnp.float32
    ) + ADAPTER_SCALE * jnp.einsum(
        "lr,dr->ld", reduced_output, lift_selected[3], preferred_element_type=jnp.float32
    )
    return (attended, (narrow, query, keys, values, log_total, mixed_b, reduced_output))


def attend_backward(
    grad_attended,
    normalized_second,
    kept,
    tree_segments,
    tree_parents,
    down_sel,
    lift_selected,
    query_key_value_full,
    out_full,
):
    narrow, query, keys, values, log_total, mixed_b, reduced_output = kept
    length = normalized_second.shape[0]
    scale = 1.0 / math.sqrt(HD)
    allowed, depth = tree_mask(tree_segments, tree_parents)
    grad_second_stream = rounded(grad_attended)
    grad_lift_output = ADAPTER_SCALE * jnp.einsum(
        "ld,lr->dr", grad_second_stream, reduced_output, preferred_element_type=jnp.float32
    )
    grad_narrow_out = rounded(
        ADAPTER_SCALE
        * jnp.dot(grad_second_stream, lift_selected[3], preferred_element_type=jnp.float32)
    )
    grad_down_out = jnp.einsum(
        "ld,lr->dr", mixed_b, grad_narrow_out, preferred_element_type=jnp.float32
    )
    grad_mixed = jnp.einsum(
        "le,de->ld", grad_second_stream, out_full, preferred_element_type=jnp.float32
    )
    grad_mixed = grad_mixed + jnp.einsum(
        "lr,dr->ld", grad_narrow_out, down_sel[3], preferred_element_type=jnp.float32
    )
    grad_heads = rounded(grad_mixed).reshape(length, HEADS, HD).transpose(1, 0, 2)

    def head_back(items):
        head_query, head_keys, head_values, head_grad, head_total = items
        scores = (
            jnp.einsum("qd,kd->qk", head_query, head_keys, preferred_element_type=jnp.float32)
            * scale
        )
        probs = jnp.exp(jnp.where(allowed, scores, -1e30) - head_total[:, None])
        grad_values = jnp.einsum(
            "qk,qd->kd", rounded(probs), head_grad, preferred_element_type=jnp.float32
        )
        grad_probs = jnp.einsum(
            "qd,kd->qk", head_grad, head_values, preferred_element_type=jnp.float32
        )
        grad_scores = rounded(
            probs * (grad_probs - jnp.sum(probs * grad_probs, axis=-1, keepdims=True))
        )
        grad_query = (
            jnp.einsum("qk,kd->qd", grad_scores, head_keys, preferred_element_type=jnp.float32)
            * scale
        )
        grad_keys = (
            jnp.einsum("qk,qd->kd", grad_scores, head_query, preferred_element_type=jnp.float32)
            * scale
        )
        return (grad_query, grad_keys, grad_values)

    grad_query, grad_keys, grad_values = lax.map(
        head_back, (query, keys, values, grad_heads, log_total)
    )
    back_query = rotate(rounded(grad_query).astype(jnp.float32).transpose(1, 0, 2), -depth).reshape(
        length, D
    )
    back_keys = rotate(rounded(grad_keys).astype(jnp.float32).transpose(1, 0, 2), -depth).reshape(
        length, D
    )
    back_values = grad_values.transpose(1, 0, 2).reshape(length, D)
    grad_projected = rounded(jnp.concatenate([back_query, back_keys, back_values], axis=1))
    grad_parts = grad_projected.reshape(length, 3, D)
    grad_lift_input = ADAPTER_SCALE * jnp.einsum(
        "lpd,lpr->pdr", grad_parts, narrow, preferred_element_type=jnp.float32
    )
    grad_narrow = rounded(
        ADAPTER_SCALE
        * jnp.einsum(
            "lpd,pdr->lpr", grad_parts, lift_selected[:3], preferred_element_type=jnp.float32
        )
    )
    grad_down_in = jnp.einsum(
        "ld,lpr->pdr", normalized_second, grad_narrow, preferred_element_type=jnp.float32
    )
    grad_normed = jnp.einsum(
        "le,de->ld", grad_projected, query_key_value_full, preferred_element_type=jnp.float32
    )
    grad_normed = grad_normed + jnp.einsum(
        "lpr,pdr->ld", grad_narrow, down_sel[:3], preferred_element_type=jnp.float32
    )
    grad_down = jnp.concatenate([grad_down_in, grad_down_out[None]], axis=0)
    grad_up = jnp.concatenate([grad_lift_input, grad_lift_output[None]], axis=0)
    return (grad_normed, grad_down, grad_up)


def per_device(
    tokens,
    segments,
    parents,
    adapter_of,
    routes,
    norm_gain,
    query_key_value_weight,
    output_weight,
    adapter_down,
    adapter_up,
    router,
    router_residual,
    const_proj,
    const_vec,
    w_gate_up,
    w_down,
    out_grad,
):
    token_count = tokens.shape[0]
    trees_here = segments.shape[0]
    length = segments.shape[1]
    owners = lax.axis_size("expert")
    local_experts = NFFN // owners
    pair_table, target = dispatch_index(routes)
    token_table = pair_table // 2
    pick_adapter = (adapter_of[:, None] == jnp.arange(NA, dtype=jnp.int32)[None, :]).astype(
        jnp.float32
    )
    zero_row = jnp.zeros((1, D), jnp.bfloat16)
    stream = tokens.astype(jnp.float32)
    earlier = jnp.zeros((token_count, NEXP), jnp.float32)
    saved = []
    for layer in range(LAYERS):
        query_key_value_full, out_full = gather_mixer(
            query_key_value_weight[layer], output_weight[layer]
        )
        down_sel = jnp.take(adapter_down[layer], adapter_of, axis=1).transpose(1, 0, 2, 3)
        lift_selected = jnp.take(adapter_up[layer], adapter_of, axis=1).transpose(1, 0, 2, 3)
        normalized_second = rounded(rms_norm(stream, norm_gain[layer, 0])).reshape(
            trees_here, length, D
        )

        def tree_forward(items):
            return attend_forward(
                items[0], items[1], items[2], items[3], items[4], query_key_value_full, out_full
            )

        attended, kept = lax.map(
            tree_forward, (normalized_second, segments, parents, down_sel, lift_selected)
        )
        middle = stream + attended.reshape(token_count, D)
        normed_two = rms_norm(middle, norm_gain[layer, 1])
        sent = rounded(normed_two)
        gate_up_full, down_full = gather_experts(w_gate_up[layer], w_down[layer])
        buffer = jnp.concatenate([sent, zero_row])[token_table].reshape(
            owners, local_experts, CAP, D
        )
        received = lax.all_to_all(buffer, "expert", split_axis=0, concat_axis=2, tiled=True)[0]
        parts = jnp.einsum(
            "end,edf->enf", received, gate_up_full, preferred_element_type=jnp.float32
        )
        active = rounded(jax.nn.silu(parts[..., :FF]) * parts[..., FF:])
        produced = rounded(
            jnp.einsum("enf,efd->end", active, down_full, preferred_element_type=jnp.float32)
        )
        returned = lax.all_to_all(
            produced[None], "expert", split_axis=2, concat_axis=0, tiled=True
        ).reshape(NFFN * CAP, D)
        chosen = (
            jnp.concatenate([returned, zero_row])
            .astype(jnp.float32)[target]
            .reshape(token_count, 2, D)
        )
        mixed_out, logits = mixture(
            normed_two,
            earlier,
            chosen,
            routes,
            router[layer],
            router_residual,
            const_proj[layer],
            const_vec[layer],
        )
        held = ()
        saved.append(
            (
                stream,
                normalized_second,
                kept,
                middle,
                parts,
                chosen,
                earlier,
                down_sel,
                lift_selected,
                held,
            )
        )
        earlier = logits
        stream = middle + mixed_out
    grad_stream = out_grad.astype(jnp.float32)
    grad_logits = jnp.zeros((token_count, NEXP), jnp.float32)
    tree_down = [None] * LAYERS
    tree_up = [None] * LAYERS
    for layer in reversed(range(LAYERS)):
        (
            stream_in,
            normalized_second,
            kept,
            middle,
            parts,
            chosen,
            earlier_in,
            down_sel,
            lift_selected,
            held,
        ) = saved[layer]
        query_key_value_full, out_full = (
            lax.all_gather(query_key_value_weight[layer], "shard", axis=0, tiled=True),
            lax.all_gather(output_weight[layer], "shard", axis=0, tiled=True),
        )
        gate_up_full, down_full = (
            lax.all_gather(w_gate_up[layer], "shard", axis=1, tiled=True),
            lax.all_gather(w_down[layer], "shard", axis=1, tiled=True),
        )
        normed_two, norm_back = jax.vjp(lambda value: rms_norm(value, norm_gain[layer, 1]), middle)
        _, mix_back = jax.vjp(
            lambda normed_in, earlier_arg, chosen_in: mixture(
                normed_in,
                earlier_arg,
                chosen_in,
                routes,
                router[layer],
                router_residual,
                const_proj[layer],
                const_vec[layer],
            ),
            normed_two,
            earlier_in,
            chosen,
        )
        grad_normed, grad_earlier, grad_chosen = mix_back((grad_stream, grad_logits))
        slot_grads = jnp.concatenate([rounded(grad_chosen.reshape(2 * token_count, D)), zero_row])[
            pair_table
        ]
        grad_received = lax.all_to_all(
            slot_grads.reshape(owners, local_experts, CAP, D),
            "expert",
            split_axis=0,
            concat_axis=2,
            tiled=True,
        )[0]
        gate_part = parts[..., :FF]
        upper_part = parts[..., FF:]
        grad_active = jnp.einsum(
            "end,efd->enf", grad_received, down_full, preferred_element_type=jnp.float32
        )
        sigma = jax.nn.sigmoid(gate_part)
        grad_gate = grad_active * upper_part * sigma * (1.0 + gate_part * (1.0 - sigma))
        grad_upper = grad_active * gate_part * sigma
        grad_parts = rounded(jnp.concatenate([grad_gate, grad_upper], axis=-1))
        grad_rows = rounded(
            jnp.einsum("enf,edf->end", grad_parts, gate_up_full, preferred_element_type=jnp.float32)
        )
        grad_back = lax.all_to_all(
            grad_rows[None], "expert", split_axis=2, concat_axis=0, tiled=True
        ).reshape(NFFN * CAP, D)
        grad_sent = (
            jnp.zeros((token_count + 1, D), jnp.float32)
            .at[token_table]
            .add(grad_back.astype(jnp.float32))[:token_count]
        )
        grad_middle = grad_stream + norm_back(grad_normed + grad_sent)[0]

        def tree_backward(items):
            return attend_backward(
                items[0],
                items[1],
                items[2],
                items[3],
                items[4],
                items[5],
                items[6],
                query_key_value_full,
                out_full,
            )

        grad_tree_normed, grad_down_trees, grad_up_trees = lax.map(
            tree_backward,
            (
                grad_middle.reshape(trees_here, length, D),
                normalized_second,
                kept,
                segments,
                parents,
                down_sel,
                lift_selected,
            ),
        )
        _, first_back = jax.vjp(lambda value: rms_norm(value, norm_gain[layer, 0]), stream_in)
        grad_stream = grad_middle + first_back(grad_tree_normed.reshape(token_count, D))[0]
        grad_logits = grad_earlier
        tree_down[layer] = grad_down_trees
        tree_up[layer] = grad_up_trees
    grad_down_all = jnp.stack(
        [
            jnp.einsum("tn,tpdr->pndr", pick_adapter, tree_down[layer], precision=HIGH_ACCURACY)
            for layer in range(LAYERS)
        ]
    )
    grad_up_all = jnp.stack(
        [
            jnp.einsum("tn,tpdr->pndr", pick_adapter, tree_up[layer], precision=HIGH_ACCURACY)
            for layer in range(LAYERS)
        ]
    )
    reduced = (
        lax.psum_scatter(
            grad_down_all.astype(jnp.bfloat16), "expert", scatter_dimension=2, tiled=True
        ).astype(jnp.float32),
        lax.psum_scatter(
            grad_up_all.astype(jnp.bfloat16), "expert", scatter_dimension=2, tiled=True
        ).astype(jnp.float32),
    )
    final_down, final_up = (
        lax.psum_scatter(
            reduced[0].astype(jnp.bfloat16), "shard", scatter_dimension=3, tiled=True
        ).astype(jnp.float32),
        lax.psum_scatter(
            reduced[1].astype(jnp.bfloat16), "shard", scatter_dimension=3, tiled=True
        ).astype(jnp.float32),
    )
    return (stream, grad_stream, final_down, final_up)


def solution(mesh):
    in_specs = (
        P(("expert", "shard"), None),
        P(("expert", "shard"), None),
        P(("expert", "shard"), None),
        P(("expert", "shard")),
        P(("expert", "shard"), None),
        P(),
        P(None, "shard", None),
        P(None, "shard", None),
        P(),
        P(),
        P(),
        P(),
        P(),
        P(),
        P(None, "expert", "shard", None),
        P(None, "expert", "shard", None),
        P(("expert", "shard"), None),
    )
    out_specs = (
        P(("expert", "shard"), None),
        P(("expert", "shard"), None),
        P(None, None, "expert", "shard", None),
        P(None, None, "expert", "shard", None),
    )
    return jax.shard_map(
        per_device, mesh=mesh, in_specs=in_specs, out_specs=out_specs, check_vma=False
    )
```

profile of v0, /device:TPU:9, one launch (start us, length us, event | category | flops | bytes accessed | tf_op | source)
XLA Modules:
  0.0 1782.1 jit_solution(6934357293459673752)
XLA Ops:
  180.5 61.3 %while.65 = (s32[]{:T(128)}, bf16[12,1024,64]{1,2,0:T(8,128)(2,1)}, f32[12,1024]{1,0:T(8,128)S(1)}, bf16[12,1024,64]{2,1,0:T(8,128)(2,1)}, bf16[12,1024,64]{2,1,...) while((s32[]{:T(128)}, bf16[12,1024,64]{1,2,0:T(8,128)(2,1)}, ...), condition=%wide.region_5.7_spmd, body=%wide.region_2.0_spmd.sunk | while | flops 276823040 | bytes 14723177 | solution.py:166
  257.5 13.8 all-to-all-start
  302.2 20.4 %fusion.100 = f32[2,768,4096]{2,1,0:T(8,128)} fusion(bf16[2,768,768]{2,1,0:T(8,128)(2,1)} %bitcast.743, bf16[1,2,768,4096]{3,2,1,0:T(8,128)(2,1)} %all-gather.21.cloned.1.call-done), kind=kOutput, calls=%fused_computation.121 | convolution fusion | flops 9663676416 | bytes 40108032 | tf_op jit(solution)/shard_map/end,edf->enf/dot_general | solution.py:331
  322.6 70.2 %all-gather.23.cloned.1.call-done = bf16[1,2,2048,768]{3,2,1,0:T(8,128)(2,1)} async-done(((bf16[1,2,256,768]{3,2,1,0:T(8,128)(2,1)}), bf16[1,2,2048,768]{3,2,1,0:T(8,128)(2,1)}) %all-gather.23.cloned.1.call-update) | async-done | bytes 6291472 | tf_op jit(solution)/shard_map/all_gather | solution.py:115
  421.7 21.8 %all-to-all-done.1 = bf16[1,2,768,768]{3,1,0,2:T(2,128)(2,1)} async-done(((bf16[1,2,768,768]{3,1,0,2:T(2,128)(2,1)}), bf16[1,2,768,768]{3,1,0,2:T(2,128)(2,1)}, u32[]{:S(2)}, u32[]{:S(2)}) %all-to-all-start.1) | async-done | bytes 2359328 | tf_op jit(solution)/shard_map/all_to_all | solution.py:338
  448.0 13.1 gather_fusion.1
  469.4 19.6 %multiply_reduce_fusion.5 = (f32[1024,768]{1,0:T(8,128)S(1)}, f32[1024,2,768]{2,1,0:T(2,128)}) fusion(f32[1024,2]{1,0:T(8,128)S(1)} %fusion.209, f32[1024,768]{1,0:T(8,128)} %get-tuple-element.641, pred[1024,2]{1,0:T(8,128)(4,1)S(1)} %copy-done.43, f32[1024,768]{1,0:T(8,128)} %get-tuple-element.640, pred[1024,2]{1,0:T(8,128)(4,1)S(1)} %copy-done.45, ...), kind=kLoop, calls=%fused_computation.159 | loop fusion | flops 11796480 | bytes 25180160 | tf_op jit(solution)/shard_map/reduce_sum | solution.py:102
  547.5 53.8 %while.72 = (s32[]{:T(128)}, bf16[12,1024,64]{1,2,0:T(8,128)(2,1)S(1)}, f32[12,1024]{1,0:T(8,128)S(1)}, bf16[12,1024,64]{2,1,0:T(8,128)(2,1)}, bf16[12,1024,64]{...) while((s32[]{:T(128)}, ...), condition=%wide.region_23.25_spmd, body=%wide.region_20.24_spmd.sunk | while | flops 276823040 | bytes 14723177 | solution.py:166
  689.0 19.9 %fusion.97 = f32[2,768,4096]{2,1,0:T(8,128)} fusion(bf16[2,768,768]{2,1,0:T(8,128)(2,1)} %bitcast.742, bf16[1,2,768,4096]{3,2,1,0:T(8,128)(2,1)} %all-gather.29.cloned.1.call-done), kind=kOutput, calls=%fused_computation.118 | convolution fusion | flops 9663676416 | bytes 40108032 | tf_op jit(solution)/shard_map/end,edf->enf/dot_general | solution.py:331
  708.8 67.9 %all-gather.31.cloned.1.call-done = bf16[1,2,2048,768]{3,2,1,0:T(8,128)(2,1)} async-done(((bf16[1,2,256,768]{3,2,1,0:T(8,128)(2,1)}), bf16[1,2,2048,768]{3,2,1,0:T(8,128)(2,1)}) %all-gather.31.cloned.1.call-update) | async-done | bytes 6291472 | tf_op jit(solution)/shard_map/all_gather | solution.py:115
  776.7 17.8 %multiply_convert_fusion.5 = (bf16[2,768,2048]{2,1,0:T(8,128)(2,1)}, bf16[2,768,2048]{2,1,0:T(8,128)(2,1)}) fusion(f32[2,768,4096]{2,1,0:T(8,128)} %fusion.97, bf16[2,768,768]{2,1,0:T(8,128)(2,1)} %bitcast.741, bf16[1,2,2048,768]{3,2,1,0:T(8,128)(2,1)} %all-gather.31.cloned.1.call-done), kind=kOutput, calls=%fused_computation.126 | convolution fusion | flops 4872732672 | bytes 46399488 | tf_op jit(solution)/shard_map/end,efd->enf/dot_general | solution.py:427
  794.6 17.1 convert_bitcast_fusion.5
  865.6 19.0 %all-to-all-done.3 = bf16[1,2,768,768]{3,1,0,2:T(2,128)(2,1)} async-done(((bf16[1,2,768,768]{3,1,0,2:T(2,128)(2,1)}), bf16[1,2,768,768]{3,1,0,2:T(2,128)(2,1)}, u32[]{:S(2)}, u32[]{:S(2)}) %all-to-all-start.3) | async-done | bytes 2359328 | tf_op jit(solution)/shard_map/all_to_all | solution.py:338
  910.3 47.4 %multiply_reduce_fusion.3 = (f32[1024,2]{1,0:T(8,128)}, f32[1024,768]{1,0:T(8,128)}, f32[1024,768]{1,0:T(8,128)S(1)}, f32[1024,768]{1,0:T(8,128)S(1)}, f32[1024,768]{1,0:T(8,128)}) fusion(f32[1024,768]{1,0:T(8,128)} %convert_element_type.885, f32[1024,2]{1,0:T(8,128)} %fusion.211, pred[1024,2]{1,0:T(8,128)(4,1)S(1)} %copy-done.44, ...), kind=kLoop, calls=%fused_computation.156 | loop fusion | flops 23590912 | bytes 31479808 | tf_op jit(solution)/shard_map/transpose(jvp())/reduce_sum | solution.py:102
  979.6 13.1 scatter_custom_fusion.1
  1015.5 148.7 %while.73 = (s32[]{:T(128)}, bf16[12,1024,64]{1,2,0:T(8,128)(2,1)}, bf16[12,1024,64]{1,2,0:T(8,128)(2,1)}, bf16[12,1024,64]{1,2,0:T(8,128)(2,1)S(1)}, bf16[12,10...) while((s32[]{:T(128)}, bf16[12,1024,64]{1,2,0:T(8,128)(2,1)}, ...), condition=%wide.region_47.49_spmd, body=%wide.region_45.48_spmd.sunk | while | flops 680655872 | bytes 35153016 | solution.py:237
  1229.3 35.5 %fusion.105 = (f32[1024,768]{1,0:T(8,128)}, f32[1024,768]{1,0:T(8,128)}, f32[1024,768]{1,0:T(8,128)}, f32[1024,2]{1,0:T(8,128)S(1)}) fusion(pred[1024,2]{1,0:T(8,128)(4,1)S(1)} %copy-done.44, f32[1024,768]{1,0:T(8,128)} %copy-done.12, f32[1024,2]{1,0:T(8,128)S(1)} %copy-done.33, pred[1024,2]{1,0:T(8,128)(4,1)S(1)} %copy-done.50, ...), kind=kLoop, calls=%fused_computation.142 | loop fusion | flops 11794432 | bytes 18896896 | tf_op jit(solution)/shard_map/transpose(jvp(jit(_where)))/reduce_sum | solution.py:99
  1281.8 18.8 %multiply_convert_fusion.3 = (bf16[2,768,2048]{2,1,0:T(8,128)(2,1)}, bf16[2,768,2048]{2,1,0:T(8,128)(2,1)}) fusion(f32[2,768,4096]{2,1,0:T(8,128)} %fusion.100, bf16[2,768,768]{2,1,0:T(8,128)(2,1)S(1)} %bitcast.744, bf16[1,2,2048,768]{3,2,1,0:T(8,128)(2,1)} %all-gather.23.cloned.1.call-done), kind=kOutput, calls=%fused_computation.124 | convolution fusion | flops 4872732672 | bytes 46399488 | tf_op jit(solution)/shard_map/end,efd->enf/dot_general | solution.py:427
  1300.7 16.7 convert_bitcast_fusion.4
  1355.1 13.2 scatter_custom_fusion.2
  1389.7 148.8 %while.74 = (s32[]{:T(128)}, bf16[12,1024,64]{1,2,0:T(8,128)(2,1)}, bf16[12,1024,64]{1,2,0:T(8,128)(2,1)}, bf16[12,1024,64]{1,2,0:T(8,128)(2,1)S(1)}, bf16[12,10...) while((s32[]{:T(128)}, bf16[12,1024,64]{1,2,0:T(8,128)(2,1)}, ...), condition=%wide.region_64.66_spmd, body=%wide.region_62.65_spmd.sunk | while | flops 680655872 | bytes 35153016 | solution.py:237
  1566.8 66.3 %all-reduce.19.cloned.1.call-done = (bf16[2,4,8,768,16]{3,4,2,1,0:T(8,128)(2,1)}, bf16[2,4,8,768,16]{3,4,2,1,0:T(8,128)(2,1)}) async-done(((bf16[2,4,8,768,16]{3,4,2,1,0:T(8,128)(2,1)}, bf16[2,4,8,768,16]{3,4,2,1,0:T(8,128)(2,1)}), (bf16[2,4,8,768,16]{3,4,2,1,0:T(8,128)(2,1)}, bf16[2,4,8,768,16]{3,4,2,1,0:T(8,128)(2,1)})) %all-reduce.19.cloned.1.call-update) | async-done | bytes 3145744
  1680.7 28.5 %reduce-scatter.13.cloned.1.call-done = bf16[96,256]{1,0:T(8,128)(2,1)} async-done(((bf16[768,256]{1,0:T(8,128)(2,1)}), bf16[96,256]{1,0:T(8,128)(2,1)}) %reduce-scatter.13.cloned.1.call-update) | async-done | bytes 49168
  1711.4 61.6 %reduce-scatter.15.cloned.1.call-done = bf16[96,256]{1,0:T(8,128)(2,1)} async-done(((bf16[768,256]{1,0:T(8,128)(2,1)}), bf16[96,256]{1,0:T(8,128)(2,1)}) %reduce-scatter.15.cloned.1.call-update) | async-done | bytes 49168
  (1018 shorter events, 1110.3 us)
Async XLA Ops:
  7.2 128.6 %all-gather.17.cloned.1.call-start = ((), (), s32[]{:S(2)}) async-start(), calls=%async_computation.10 | async-start | bytes 3981312 | tf_op jit(solution)/shard_map/all_gather | solution.py:107
  9.4 234.8 %all-gather.19.cloned.1.call-start = ((), (), s32[]{:S(2)}) async-start(), calls=%async_computation.11 | async-start | bytes 1327104 | tf_op jit(solution)/shard_map/all_gather | solution.py:108
  11.2 291.0 %all-gather.21.cloned.1.call-start = ((), (), s32[]{:S(2)}) async-start(), calls=%async_computation.12 | async-start | bytes 14155776 | tf_op jit(solution)/shard_map/all_gather | solution.py:114
  15.3 377.5 %all-gather.23.cloned.1.call-start = ((), (), s32[]{:S(2)}) async-start(), calls=%async_computation.13 | async-start | bytes 7077888 | tf_op jit(solution)/shard_map/all_gather | solution.py:115
  16.6 489.8 %all-gather.25.cloned.1.call-start = ((), (), s32[]{:S(2)}) async-start(), calls=%async_computation.14 | async-start | bytes 3981312 | tf_op jit(solution)/shard_map/all_gather | solution.py:107
  17.2 585.8 %all-gather.27.cloned.1.call-start = ((), (), s32[]{:S(2)}) async-start(), calls=%async_computation.15 | async-start | bytes 1327104 | tf_op jit(solution)/shard_map/all_gather | solution.py:108
  17.8 671.2 %all-gather.29.cloned.1.call-start = ((), (), s32[]{:S(2)}) async-start(), calls=%async_computation.16 | async-start | bytes 14155776 | tf_op jit(solution)/shard_map/all_gather | solution.py:114
  18.5 758.2 %all-gather.31.cloned.1.call-start = ((), (), s32[]{:S(2)}) async-start(), calls=%async_computation.17 | async-start | bytes 7077888 | tf_op jit(solution)/shard_map/all_gather | solution.py:115
  96.2 320.7 %copy-start.150 = (f32[768]{0:T(1024)}, f32[768]{0:T(1024)S(1)}, u32[]{:S(2)}) copy-start(f32[768]{0:T(1024)S(1)} %get-tuple-element.506) | copy-start | bytes 9220
  96.2 320.8 %copy-start.152 = (f32[768]{0:T(1024)}, f32[768]{0:T(1024)S(1)}, u32[]{:S(2)}) copy-start(f32[768]{0:T(1024)S(1)} %get-tuple-element.507) | copy-start | bytes 9220
  257.5 41.5 %all-to-all-start = ((bf16[4,2,192,768]{3,2,1,0:T(8,128)(2,1)}), bf16[4,2,192,768]{3,2,1,0:T(8,128)(2,1)}, u32[]{:S(2)}, u32[]{:S(2)}) async-start(bf16[4,2,192,768]{3,2,1,0:T(8,128)(2,1)} %bitcast.719), calls=%async_computation | async-start | bytes 4718592 | tf_op jit(solution)/shard_map/all_to_all | solution.py:330
  409.6 33.8 %all-to-all-start.1 = ((bf16[1,2,768,768]{3,1,0,2:T(2,128)(2,1)}), bf16[1,2,768,768]{3,1,0,2:T(2,128)(2,1)}, u32[]{:S(2)}, u32[]{:S(2)}) async-start(bf16[1,2,768,768]{3,1,0,2:T(2,128)(2,1)} %copy.145), calls=%async_computation.1 | async-start | bytes 4718592 | tf_op jit(solution)/shard_map/all_to_all | solution.py:338
  415.8 248.7 %copy-start.140 = (f32[1024]{0:T(1024)}, f32[1024]{0:T(1024)S(1)}, u32[]{:S(2)}) copy-start(f32[1024]{0:T(1024)S(1)} %get-tuple-element.722) | copy-start | bytes 12292
  415.8 249.3 %copy-start.138 = (f32[1024]{0:T(1024)}, f32[1024]{0:T(1024)S(1)}, u32[]{:S(2)}) copy-start(f32[1024]{0:T(1024)S(1)} %get-tuple-element.723) | copy-start | bytes 12292
  416.4 247.5 %copy-start.132 = (f32[1024]{0:T(1024)}, f32[1024]{0:T(1024)S(1)}, u32[]{:S(2)}) copy-start(f32[1024]{0:T(1024)S(1)} %fusion.210) | copy-start | bytes 12292
  616.7 36.5 %all-to-all-start.2 = ((bf16[4,2,192,768]{3,2,1,0:T(8,128)(2,1)}), bf16[4,2,192,768]{3,2,1,0:T(8,128)(2,1)}, u32[]{:S(2)}, u32[]{:S(2)}) async-start(bf16[4,2,192,768]{3,2,1,0:T(8,128)(2,1)} %bitcast.718), calls=%async_computation.2 | async-start | bytes 4718592 | tf_op jit(solution)/shard_map/all_to_all | solution.py:330
  653.2 32.6 %all-to-all-start.4 = ((bf16[4,2,192,768]{3,2,1,0:T(8,128)(2,1)}), bf16[4,2,192,768]{3,2,1,0:T(8,128)(2,1)}, u32[]{:S(2)}, u32[]{:S(2)}) async-start(bf16[4,2,192,768]{3,2,1,0:T(8,128)(2,1)} %bitcast.717), calls=%async_computation.4 | async-start | bytes 4718592 | tf_op jit(solution)/shard_map/all_to_all | solution.py:418
  817.2 34.2 %all-to-all-start.5 = ((bf16[1,2,768,768]{3,1,0,2:T(2,128)(2,1)}), bf16[1,2,768,768]{3,1,0,2:T(2,128)(2,1)}, u32[]{:S(2)}, u32[]{:S(2)}) async-start(bf16[1,2,768,768]{3,1,0,2:T(2,128)(2,1)} %copy.167), calls=%async_computation.5 | async-start | bytes 4718592 | tf_op jit(solution)/shard_map/all_to_all | solution.py:437
  851.3 33.2 %all-to-all-start.3 = ((bf16[1,2,768,768]{3,1,0,2:T(2,128)(2,1)}), bf16[1,2,768,768]{3,1,0,2:T(2,128)(2,1)}, u32[]{:S(2)}, u32[]{:S(2)}) async-start(bf16[1,2,768,768]{3,1,0,2:T(2,128)(2,1)} %copy.161), calls=%async_computation.3 | async-start | bytes 4718592 | tf_op jit(solution)/shard_map/all_to_all | solution.py:338
  1223.5 56.5 %all-to-all-start.6 = ((bf16[4,2,192,768]{3,2,1,0:T(8,128)(2,1)}), bf16[4,2,192,768]{3,2,1,0:T(8,128)(2,1)}, u32[]{:S(2)}, u32[]{:S(2)}) async-start(bf16[4,2,192,768]{3,2,1,0:T(8,128)(2,1)} %bitcast.237), calls=%async_computation.6 | async-start | bytes 4718592 | tf_op jit(solution)/shard_map/all_to_all | solution.py:418
  1321.2 31.3 %all-to-all-start.7 = ((bf16[1,2,768,768]{3,1,0,2:T(2,128)(2,1)}), bf16[1,2,768,768]{3,1,0,2:T(2,128)(2,1)S(1)}, u32[]{:S(2)}, u32[]{:S(2)}) async-start(bf16[1,2,768,768]{3,1,0,2:T(2,128)(2,1)} %copy.182), calls=%async_computation.7 | async-start | bytes 4718592 | tf_op jit(solution)/shard_map/all_to_all | solution.py:437
  1324.8 308.2 %all-reduce.19.cloned.1.call-start = ((), (), s32[]{:S(2)}) async-start(), calls=%async_computation.20 | async-start | bytes 6291456
  1565.5 143.8 %reduce-scatter.13.cloned.1.call-start = ((), (), s32[]{:S(2)}) async-start(), calls=%async_computation.18 | async-start | bytes 442368
  1649.7 123.3 %reduce-scatter.15.cloned.1.call-start = ((), (), s32[]{:S(2)}) async-start(), calls=%async_computation.19 | async-start | bytes 442368
  (202 other events, 3842.2 us)
Sparse Core Ops, SparseCore 0:
  10.2 64.7 all-gather.16
  77.2 39.6 all-gather.18
  119.1 174.4 all-gather.20
  295.6 97.1 all-gather.22
  394.8 64.1 all-gather.24
  461.0 39.6 all-gather.26
  502.9 174.3 all-gather.28
  679.5 97.1 all-gather.30
  1565.6 67.4 all-reduce.18
  1649.8 59.3 reduce-scatter.12
  1712.5 60.3 reduce-scatter.14
where the time goes:
time: 1800 us; the launch traced here: 1780 us
  matrix products  648 us (36%)
  waiting for transfers between devices  375 us (21%)
  local copies, waits for them, and re-layouts  348 us (19%)
  other arithmetic  289 us (16%)
  between operations  68.3 us (4%)
  starting transfers between devices  52.2 us (3%)
    unnamed x14, waiting for transfers between devices  159 us
    all_gather x2, waiting for transfers between devices, gather_experts(): lax.all_gather(layer_down, 'shard', axis=1, tiled=True)  138 us
    reduce_sum x2, other arithmetic, mixture(): return (jnp.sum(gates[:, :, None] * value, axis=1), logits)  67.1 us
    dot_general x24, matrix products, head_back(): jnp.einsum('qd,kd->qk', head_query, head_keys, preferred_element_type=jnp...  59.4 us
    dot_general x24, matrix products, head_back(): jnp.einsum('qk,qd->kd', grad_scores, head_query, preferred_element_type=j...  56.9 us
    unnamed x432, local copies, waits for them, and re-layouts  54.1 us
    dot_general x24, matrix products, head_back(): jnp.einsum('qk,kd->qd', grad_scores, head_keys, preferred_element_type=jn...  51.8 us
    dot_general x24, matrix products, one_head(): jnp.dot(rounded(weights / total), head_values, preferred_element_type=jnp...  51.6 us
  transfers between devices with their start and end apart: 19, of which 11 were waited for; matrix products, arithmetic and copies ran while one was open for 35% of the time, Pallas kernels for 0%

commit v1 on v0

v1 whole, which is shorter than its diff:
```python
import math

import jax
import jax.numpy as jnp
from jax import lax
from jax.experimental import pallas as pl
from jax.experimental.pallas import tpu as pltpu
from jax.sharding import PartitionSpec as P

D = 768
HEADS = 12
HD = 64
FF = 2048
NFFN = 8
NEXP = 12
R = 16
NA = 8
NSEG = 13
LAYERS = 2
CAP = 192
T = 1024
SLOTS = NFFN * CAP
RB = 256
NB = T // RB
PAIRS = HEADS // 2
FC = 512
EPSILON = 1e-06
BIG = 2.0**100
LOG_SCALE = math.log2(math.e) / math.sqrt(HD)
F32 = jnp.float32
BF = jnp.bfloat16
HIGHEST = lax.Precision.HIGHEST
VMEM_BYTES = 56 * 1024 * 1024


def mm(a, b):
    return lax.dot_general(a, b, (((1,), (0,)), ((), ())), preferred_element_type=F32)


def mm_nt(a, b):
    return lax.dot_general(a, b, (((1,), (1,)), ((), ())), preferred_element_type=F32)


def mm_tn(a, b):
    return lax.dot_general(a, b, (((0,), (0,)), ((), ())), preferred_element_type=F32)


def mm_exact(a, b):
    return lax.dot_general(
        a, b, (((1,), (0,)), ((), ())), preferred_element_type=F32, precision=HIGHEST
    )


def iota(shape, axis):
    return lax.broadcasted_iota(jnp.int32, shape, axis)


def sigmoid(v):
    return 1.0 / (1.0 + jnp.exp(-v))


def call(body, grid, ins, outs, scratch=(), name=None, flops=0, nbytes=0):
    def spec(entry):
        if entry[1] == "smem":
            return pl.BlockSpec(memory_space=pltpu.SMEM)
        if entry[1] is None:
            shape = entry[0].shape
            return pl.BlockSpec(shape, lambda *_: (0,) * len(shape))
        return pl.BlockSpec(entry[1], entry[2])

    return pl.pallas_call(
        body,
        grid=grid,
        in_specs=[spec(e) for e in ins],
        out_specs=[spec(e) for e in outs],
        out_shape=[jax.ShapeDtypeStruct(e[0].shape, e[0].dtype) for e in outs],
        scratch_shapes=list(scratch),
        compiler_params=pltpu.CompilerParams(
            dimension_semantics=("arbitrary",) * len(grid), vmem_limit_bytes=VMEM_BYTES
        ),
        cost_estimate=pl.CostEstimate(
            flops=int(flops), bytes_accessed=int(nbytes), transcendentals=0
        ),
        name=name,
    )(*[e[0] for e in ins])


def out(shape, dtype):
    return jax.ShapeDtypeStruct(shape, dtype)


def rows(i):
    return (i, 0)


def prep_body(par_ref, seg_ref, rt_ref, qf_ref, kf_ref, cos_ref, sin_ref, tcol_ref, trow_ref, anc):
    first = iota((1, 128), 1) & 63
    anc[...] = jnp.zeros_like(anc)
    anc[0:1, :] = (first == 0).astype(F32)
    for s in range(1, NSEG):
        above = anc[pl.ds(par_ref[0, s], 1), :]
        anc[s : s + 1, :] = jnp.maximum(above, (first == s).astype(F32))
    lane = iota((T, 128), 1)
    lane6 = lane & 63
    low = lane < 64
    member = (seg_ref[...] == lane6).astype(F32)
    ways = mm(jnp.where(low, member, 0.0).astype(BF), anc[...].astype(BF))
    qf_ref[...] = jnp.where(lane6 < NSEG, (ways - 1.0) * BIG, 0.0).astype(BF)
    ones = ((lane6 >= 16) & (lane6 < 19)).astype(F32)
    kf_ref[...] = (member + ones).astype(BF)
    hit0 = (rt_ref[:, 0:1] == lane).astype(F32)
    hit1 = (rt_ref[:, 1:2] == lane).astype(F32)
    hits = hit0 + hit1
    upto = (iota((T, T), 0) >= iota((T, T), 1)).astype(F32).astype(BF)
    seen = mm(upto, jnp.concatenate([member.astype(BF), hits.astype(BF)], axis=1))
    depth = jnp.sum(jnp.where(low, ways * seen[:, :128], 0.0), axis=1, keepdims=True) - 1.0
    before = seen[:, 128:] - hits

    def target(hit, route):
        slot = jnp.sum(hit * before, axis=1, keepdims=True)
        place = route.astype(F32) * CAP + slot
        return jnp.where(route < NFFN, place, 4.0 * SLOTS)

    t0 = target(hit0, rt_ref[:, 0:1])
    t1 = target(hit1, rt_ref[:, 1:2])
    both = jnp.where(lane == 0, t0, jnp.where(lane == 1, t1, 0.0))
    tcol_ref[...] = both.astype(jnp.int32)
    trow_ref[...] = both.T[0:8, :].astype(jnp.int32)
    inverse = jnp.exp((lane & 31).astype(F32) * (-math.log(10000.0) / 32.0))
    angle = depth * inverse
    cos_ref[...] = jnp.cos(angle)
    sine = jnp.sin(angle)
    sin_ref[...] = jnp.where((lane & 32) == 0, -sine, sine)


def prep(parents, seg_col, routes):
    return call(
        prep_body,
        (1,),
        [(parents, "smem"), (seg_col, None), (routes, None)],
        [
            (out((T, 128), BF), None),
            (out((T, 128), BF), None),
            (out((T, 128), F32), None),
            (out((T, 128), F32), None),
            (out((T, 128), jnp.int32), None),
            (out((8, T), jnp.int32), None),
        ],
        [pltpu.VMEM((128, 128), F32)],
        name="prep",
        flops=2 * T * T * 256,
        nbytes=3e6,
    )


def turn(v, cos, sin):
    first = (iota(v.shape, 1) & 32) == 0
    other = jnp.where(first, pltpu.roll(v, 96, 1), pltpu.roll(v, 32, 1))
    return v * cos + other * sin


def project_rows(x, gain, w_ref, d_ref, u_ref, cos, sin, n_ref, nar_ref, qkv_ref):
    scale = lax.rsqrt(jnp.mean(x * x, axis=1, keepdims=True) + EPSILON)
    normed = (x * scale * gain).astype(BF)
    n_ref[...] = normed
    narrow = mm(normed, d_ref[...]).astype(BF)
    nar_ref[...] = narrow
    for block in range(3):
        cols = slice(block * D, (block + 1) * D)
        part = mm(normed, w_ref[:, cols]) + mm(narrow, u_ref[:, cols])
        for j in range(PAIRS):
            piece = part[:, j * 128 : (j + 1) * 128]
            if block < 2:
                piece = turn(piece, cos, sin)
            at = block * D + j * 128
            qkv_ref[:, at : at + 128] = piece.astype(BF)


def project_body(x_ref, g_ref, w_ref, d_ref, u_ref, cos_ref, sin_ref, n_ref, nar_ref, qkv_ref):
    project_rows(
        x_ref[...].astype(F32),
        g_ref[...],
        w_ref,
        d_ref,
        u_ref,
        cos_ref[...],
        sin_ref[...],
        n_ref,
        nar_ref,
        qkv_ref,
    )


def project(x, gain, w, down, up, cos, sin):
    return call(
        project_body,
        (NB,),
        [
            (x, (RB, D), rows),
            (gain, None),
            (w, None),
            (down, None),
            (up, None),
            (cos, (RB, 128), rows),
            (sin, (RB, 128), rows),
        ],
        [
            (out((T, D), BF), (RB, D), rows),
            (out((T, 128), BF), (RB, 128), rows),
            (out((T, 3 * D), BF), (RB, 3 * D), rows),
        ],
        name="project",
        flops=2 * T * D * 3 * D,
        nbytes=12e6,
    )


def three(v):
    high = v.astype(BF)
    rest = v - high.astype(F32)
    middle = rest.astype(BF)
    return high, middle, (rest - middle.astype(F32)).astype(BF)


def attend_body(q_ref, k_ref, v_ref, qf_ref, kf_ref, mixed_ref, aug_ref):
    low = iota((T, 128), 1) < 64
    k = k_ref[...]
    kf = kf_ref[...]
    v = v_ref[...]
    one = jnp.ones((T, 128), BF)
    keys = (jnp.where(low, k, kf), jnp.where(low, kf, k))
    values = (jnp.where(low, v, one), jnp.where(low, one, v))
    low = low[:RB]
    tri = iota((RB, RB), 0) >= iota((RB, RB), 1)
    lane6 = iota((RB, 128), 1) & 63
    for i in range(NB):
        here = slice(i * RB, (i + 1) * RB)
        q = q_ref[here, :]
        qf = qf_ref[here, :]
        tops = []
        outs = []
        for h in range(2):
            qa = jnp.where(low, q, qf) if h == 0 else jnp.where(low, qf, q)
            diag = jnp.where(tri, mm_nt(qa, keys[h][here]), -BIG)
            top = jnp.max(diag, axis=1, keepdims=True)
            if i:
                off = mm_nt(qa, keys[h][: i * RB])
                top = jnp.maximum(top, jnp.max(off, axis=1, keepdims=True))
            result = mm(jnp.exp2((diag - top) * LOG_SCALE).astype(BF), values[h][here])
            if i:
                weights = jnp.exp2((off - top) * LOG_SCALE).astype(BF)
                result = result + mm(weights, values[h][: i * RB])
            tops.append(top)
            outs.append(result)
        total = jnp.where(low, outs[1], outs[0])
        mixed = jnp.where(low, outs[0], outs[1]) / pltpu.roll(total, 64, 1)
        mixed_ref[here, :] = mixed.astype(BF)
        level = -(jnp.where(low, tops[1], tops[0]) + math.sqrt(HD) * jnp.log(total))
        a, b, c = three(level)
        aug_ref[0, here, :] = jnp.where(
            lane6 == 16, a, jnp.where(lane6 == 17, b, jnp.where(lane6 == 18, c, qf))
        )


def attend(qkv, qf, kf):
    return call(
        attend_body,
        (PAIRS,),
        [
            (qkv, (T, 128), lambda j: (0, j)),
            (qkv, (T, 128), lambda j: (0, PAIRS + j)),
            (qkv, (T, 128), lambda j: (0, 2 * PAIRS + j)),
            (qf, None),
            (kf, None),
        ],
        [
            (out((T, D), BF), (T, 128), lambda j: (0, j)),
            (out((PAIRS, T, 128), BF), (1, T, 128), lambda j: (j, 0, 0)),
        ],
        name="attend",
        flops=12 * 4 * T * T * 128,
        nbytes=8e6,
    )


def settle_body(
    x_ref, mixed_ref, w_ref, d_ref, u_ref, g_ref, rt_ref, earlier_ref, res_ref,
    mid_ref, sent_ref, lg_ref, nar_ref,
):
    mixed = mixed_ref[...]
    narrow = mm(mixed, d_ref[...]).astype(BF)
    nar_ref[...] = narrow
    mid = x_ref[...].astype(F32) + mm(mixed, w_ref[...]) + mm(narrow, u_ref[...])
    mid_ref[...] = mid
    scale = lax.rsqrt(jnp.mean(mid * mid, axis=1, keepdims=True) + EPSILON)
    normed = mid * scale * g_ref[...]
    sent_ref[...] = normed.astype(BF)
    lg_ref[...] = mm_exact(normed, rt_ref[...]) + mm_exact(earlier_ref[...], res_ref[...])


def settle(x, mixed, w, down, up, gain, router, earlier, residual):
    return call(
        settle_body,
        (NB,),
        [
            (x, (RB, D), rows),
            (mixed, (RB, D), rows),
            (w, None),
            (down, None),
            (up, None),
            (gain, None),
            (router, None),
            (earlier, (RB, 128), rows),
            (residual, None),
        ],
        [
            (out((T, D), F32), (RB, D), rows),
            (out((T, D), BF), (RB, D), rows),
            (out((T, 128), F32), (RB, 128), rows),
            (out((T, 128), BF), (RB, 128), rows),
        ],
        name="settle",
        flops=2 * T * D * D * 2,
        nbytes=10e6,
    )


def dispatch_body(trow_ref, s_ref, o_ref):
    place = pl.program_id(0) * CAP + iota((CAP, T), 0)
    hit = (trow_ref[0:1, :] == place) | (trow_ref[1:2, :] == place)
    o_ref[0] = mm(hit.astype(F32).astype(BF), s_ref[...]).astype(BF)


def dispatch(trow, sent):
    return call(
        dispatch_body,
        (NFFN,),
        [(trow, None), (sent, None)],
        [(out((NFFN, CAP, D), BF), (1, CAP, D), lambda j: (j, 0, 0))],
        name="dispatch",
        flops=2 * T * SLOTS * D,
        nbytes=4e6,
    )[0]


def dispatch_grad_body(trow_ref, a_ref, b_ref, o_ref):
    place = pl.program_id(0) * CAP + iota((CAP, T), 0)
    hit0 = (trow_ref[0:1, :] == place).astype(F32).astype(BF)
    hit1 = (trow_ref[1:2, :] == place).astype(F32).astype(BF)
    o_ref[0] = (mm(hit0, a_ref[...]) + mm(hit1, b_ref[...])).astype(BF)


def dispatch_grad(trow, a, b):
    return call(
        dispatch_grad_body,
        (NFFN,),
        [(trow, None), (a, None), (b, None)],
        [(out((NFFN, CAP, D), BF), (1, CAP, D), lambda j: (j, 0, 0))],
        name="dispatch_grad",
        flops=4 * T * SLOTS * D,
        nbytes=6e6,
    )[0]


MB = 512


def expert_body(r_ref, wg_ref, wu_ref, wd_ref, p_ref, gate_ref, up_ref, acc):
    step = pl.program_id(0)

    @pl.when(step == 0)
    def _():
        acc[...] = jnp.zeros_like(acc)

    for m in range(SLOTS // MB):
        at = slice(m * MB, (m + 1) * MB)
        r = r_ref[at, :]
        gate = mm(r, wg_ref[...])
        up = mm(r, wu_ref[...])
        gate_ref[at, :] = gate.astype(BF)
        up_ref[at, :] = up.astype(BF)
        active = (gate * sigmoid(gate) * up).astype(BF)
        acc[at, :] += mm(active, wd_ref[...])

    @pl.when(step == pl.num_programs(0) - 1)
    def _():
        p_ref[...] = acc[...].astype(BF)


def expert_forward(received, gate_up, down):
    steps = FF // FC
    return call(
        expert_body,
        (steps,),
        [
            (received, None),
            (gate_up, (D, FC), lambda j: (0, j)),
            (gate_up, (D, FC), lambda j: (0, steps + j)),
            (down, (FC, D), lambda j: (j, 0)),
        ],
        [
            (out((SLOTS, D), BF), None),
            (out((SLOTS, FF), BF), (SLOTS, FC), lambda j: (0, j)),
            (out((SLOTS, FF), BF), (SLOTS, FC), lambda j: (0, j)),
        ],
        [pltpu.VMEM((SLOTS, D), F32)],
        name="expert_forward",
        flops=2 * SLOTS * D * FF * 3,
        nbytes=26e6,
    )


def expert_grad_body(g_ref, gate_ref, up_ref, wg_ref, wu_ref, wd_ref, o_ref, acc):
    step = pl.program_id(0)

    @pl.when(step == 0)
    def _():
        acc[...] = jnp.zeros_like(acc)

    for m in range(SLOTS // MB):
        at = slice(m * MB, (m + 1) * MB)
        grad = mm_nt(g_ref[at, :], wd_ref[...])
        gate = gate_ref[at, :].astype(F32)
        up = up_ref[at, :].astype(F32)
        s = sigmoid(gate)
        grad_s = grad * s
        grad_gate = (grad_s * up * (1.0 + gate * (1.0 - s))).astype(BF)
        grad_up = (grad_s * gate).astype(BF)
        acc[at, :] += mm_nt(grad_gate, wg_ref[...]) + mm_nt(grad_up, wu_ref[...])

    @pl.when(step == pl.num_programs(0) - 1)
    def _():
        o_ref[...] = acc[...].astype(BF)


def expert_backward(grads, gate, up, gate_up, down):
    steps = FF // FC
    return call(
        expert_grad_body,
        (steps,),
        [
            (grads, None),
            (gate, (SLOTS, FC), lambda j: (0, j)),
            (up, (SLOTS, FC), lambda j: (0, j)),
            (gate_up, (D, FC), lambda j: (0, j)),
            (gate_up, (D, FC), lambda j: (0, steps + j)),
            (down, (FC, D), lambda j: (j, 0)),
        ],
        [(out((SLOTS, D), BF), None)],
        [pltpu.VMEM((SLOTS, D), F32)],
        name="expert_backward",
        flops=2 * SLOTS * D * FF * 3,
        nbytes=26e6,
    )[0]


def mix_terms(logits, routes):
    lane = iota(logits.shape, 1)

    def at(place):
        return jnp.sum(jnp.where(lane == place, logits, 0.0), axis=1, keepdims=True)

    r0, r1 = routes[:, 0:1], routes[:, 1:2]
    gap = at(r0) - at(r1)
    gates = (sigmoid(gap), sigmoid(-gap))

    def weight(e):
        return jnp.where(r0 == e, gates[0], 0.0) + jnp.where(r1 == e, gates[1], 0.0)

    shares = []
    for c in range(2):
        apart = logits[:, 12 + 2 * c : 13 + 2 * c] - logits[:, 13 + 2 * c : 14 + 2 * c]
        shares.append((sigmoid(apart), sigmoid(-apart)))
    weights = [weight(NFFN + 1), weight(NFFN + 2), weight(NFFN + 3)]
    return gates, weights, shares


def rms_scale(v):
    return lax.rsqrt(jnp.mean(v * v, axis=1, keepdims=True) + EPSILON)


def combine_body(tcol_ref, ret_ref, mid_ref, lg_ref, rt_ref, g_ref, cv_ref, x_ref, c0_ref, c1_ref):
    place = iota((RB, SLOTS), 1)
    back = ret_ref[...]
    chosen = []
    for k, c_ref in enumerate((c0_ref, c1_ref)):
        hit = (tcol_ref[:, k : k + 1] == place).astype(F32).astype(BF)
        value = mm(hit, back)
        c_ref[...] = value.astype(BF)
        chosen.append(value)
    mid = mid_ref[...]
    normed = mid * rms_scale(mid) * g_ref[...]
    gates, weights, shares = mix_terms(lg_ref[...], rt_ref[...])
    same = weights[0] + weights[1] * shares[0][0] + weights[2] * shares[1][0]
    moe = gates[0] * chosen[0] + gates[1] * chosen[1] + same * normed
    moe = moe + (weights[1] * shares[0][1]) * cv_ref[0:1, :]
    moe = moe + (weights[2] * shares[1][1]) * cv_ref[1:2, :]
    x_ref[...] = mid + moe


def combine(tcol, returned, mid, logits, routes, gain, const_vec):
    return call(
        combine_body,
        (NB,),
        [
            (tcol, (RB, 128), rows),
            (returned, None),
            (mid, (RB, D), rows),
            (logits, (RB, 128), rows),
            (routes, (RB, 2), rows),
            (gain, None),
            (const_vec, None),
        ],
        [
            (out((T, D), F32), (RB, D), rows),
            (out((T, D), BF), (RB, D), rows),
            (out((T, D), BF), (RB, D), rows),
        ],
        name="combine",
        flops=4 * T * SLOTS * D,
        nbytes=12e6,
    )


def mix_grad_body(
    g_ref, mid_ref, c0_ref, c1_ref, lg_ref, rt_ref, gl_ref, gain_ref, cv_ref, wt_ref, res_ref,
    a_ref, b_ref, gn_ref, gle_ref,
):
    g = g_ref[...].astype(F32)
    mid = mid_ref[...]
    normed = mid * rms_scale(mid) * gain_ref[...]
    routes = rt_ref[...]
    gates, weights, shares = mix_terms(lg_ref[...], routes)
    a_ref[...] = (gates[0] * g).astype(BF)
    b_ref[...] = (gates[1] * g).astype(BF)

    def along(v):
        return jnp.sum(g * v, axis=1, keepdims=True)

    same = along(normed)
    const = [along(cv_ref[c : c + 1, :]) for c in range(2)]
    gate_grads = []
    for k, c_ref in enumerate((c0_ref, c1_ref)):
        r = routes[:, k : k + 1]
        value = along(c_ref[...].astype(F32)) + jnp.where(r == NFFN + 1, same, 0.0)
        for c in range(2):
            mixed = shares[c][0] * same + shares[c][1] * const[c]
            value = value + jnp.where(r == NFFN + 2 + c, mixed, 0.0)
        gate_grads.append(value)
    slope = gates[0] * gates[1] * (gate_grads[0] - gate_grads[1])
    lane = iota((RB, 128), 1)
    grad = gl_ref[...]
    grad = grad + jnp.where(lane == routes[:, 0:1], slope, 0.0)
    grad = grad - jnp.where(lane == routes[:, 1:2], slope, 0.0)
    for c in range(2):
        tilt = weights[1 + c] * shares[c][0] * shares[c][1] * (same - const[c])
        grad = grad + jnp.where(lane == 12 + 2 * c, tilt, 0.0)
        grad = grad - jnp.where(lane == 13 + 2 * c, tilt, 0.0)
    keep = weights[0] + weights[1] * shares[0][0] + weights[2] * shares[1][0]
    gn_ref[...] = mm_exact(grad, wt_ref[...]) + keep * g
    gle_ref[...] = mm_exact(grad, res_ref[...])


def mix_grad(g, mid, c0, c1, logits, routes, gl, gain, const_vec, router_t, residual_t):
    return call(
        mix_grad_body,
        (NB,),
        [
            (g, (RB, D), rows),
            (mid, (RB, D), rows),
            (c0, (RB, D), rows),
            (c1, (RB, D), rows),
            (logits, (RB, 128), rows),
            (routes, (RB, 2), rows),
            (gl, (RB, 128), rows),
            (gain, None),
            (const_vec, None),
            (router_t, None),
            (residual_t, None),
        ],
        [
            (out((T, D), BF), (RB, D), rows),
            (out((T, D), BF), (RB, D), rows),
            (out((T, D), F32), (RB, D), rows),
            (out((T, 128), F32), (RB, 128), rows),
        ],
        name="mix_grad",
        flops=2 * T * 128 * D * 6,
        nbytes=16e6,
    )


def rms_back(grad, v, gain):
    scale = rms_scale(v)
    inner = grad * gain
    return scale * inner - v * (scale**3 * jnp.mean(v * inner, axis=1, keepdims=True))


def settle_grad_body(
    tcol_ref, back_ref, gn_ref, mid_ref, g_ref, gain_ref, mixed_ref, nar_ref, w_ref, d_ref, u_ref,
    gm_ref, gx_ref, gu_ref, gd_ref,
):
    @pl.when(pl.program_id(0) == 0)
    def _():
        gu_ref[...] = jnp.zeros_like(gu_ref)
        gd_ref[...] = jnp.zeros_like(gd_ref)

    place = iota((RB, SLOTS), 1)
    hit = (tcol_ref[:, 0:1] == place) | (tcol_ref[:, 1:2] == place)
    grad = gn_ref[...] + mm(hit.astype(F32).astype(BF), back_ref[...])
    grad_mid = g_ref[...].astype(F32) + rms_back(grad, mid_ref[...], gain_ref[...])
    gm_ref[...] = grad_mid
    out_grad = grad_mid.astype(BF)
    grad_narrow = mm_nt(out_grad, u_ref[...]).astype(BF)
    mixed = mixed_ref[...]
    gu_ref[...] += 2.0 * mm_tn(nar_ref[...], out_grad)
    gd_ref[...] += mm_tn(grad_narrow, mixed)
    gx_ref[...] = (mm_nt(out_grad, w_ref[...]) + mm_nt(grad_narrow, d_ref[...])).astype(BF)


def settle_grad(tcol, back, gn, mid, g, gain, mixed, narrow, w, down, up):
    return call(
        settle_grad_body,
        (NB,),
        [
            (tcol, (RB, 128), rows),
            (back, None),
            (gn, (RB, D), rows),
            (mid, (RB, D), rows),
            (g, (RB, D), rows),
            (gain, None),
            (mixed, (RB, D), rows),
            (narrow, (RB, 128), rows),
            (w, None),
            (down, None),
            (up, None),
        ],
        [
            (out((T, D), F32), (RB, D), rows),
            (out((T, D), BF), (RB, D), rows),
            (out((128, D), F32), None),
            (out((128, D), F32), None),
        ],
        name="settle_grad",
        flops=2 * T * SLOTS * D + 2 * T * D * D * 2,
        nbytes=16e6,
    )


def attend_grad_body(
    q_ref, k_ref, v_ref, aug_ref, kf_ref, g_ref, mixed_ref, cos_ref, sin_ref,
    gq_ref, gk_ref, gv_ref, dqt,
):
    lane = iota((T, 128), 1)
    low = lane < 64
    lane6 = lane & 63
    q, k, v, kf, g = q_ref[...], k_ref[...], v_ref[...], kf_ref[...], g_ref[...]
    aug = aug_ref[0]
    product = g.astype(F32) * mixed_ref[...].astype(F32)
    d0 = jnp.sum(jnp.where(low, product, 0.0), axis=1, keepdims=True)
    d1 = jnp.sum(jnp.where(low, 0.0, product), axis=1, keepdims=True)
    a, b, c = three(-jnp.where(low, d1, d0))
    zero = jnp.zeros((T, 128), BF)
    ga = jnp.where(lane6 == 0, a, jnp.where(lane6 == 1, b, jnp.where(lane6 == 2, c, zero)))
    va = (lane6 < 3).astype(F32).astype(BF)
    qs = (jnp.where(low, q, aug), jnp.where(low, aug, q))
    ks = (jnp.where(low, k, kf), jnp.where(low, kf, k))
    vs = (jnp.where(low, v, va), jnp.where(low, va, v))
    gs = (jnp.where(low, g, ga), jnp.where(low, ga, g))
    kt = k.T
    tri = iota((RB, RB), 0) <= iota((RB, RB), 1)
    dqt[...] = jnp.zeros_like(dqt)
    low = low[:RB]
    for i in range(NB):
        here = slice(i * RB, (i + 1) * RB)
        dks = []
        dvs = []
        for h in range(2):
            dk = None
            for j in range(i, NB):
                there = slice(j * RB, (j + 1) * RB)
                p = jnp.exp2(mm_nt(ks[h][here], qs[h][there]) * LOG_SCALE)
                if i == j:
                    p = jnp.where(tri, p, 0.0)
                ds = (p * mm_nt(vs[h][here], gs[h][there])).astype(BF)
                p = p.astype(BF)
                dv_part = mm(p, g[there])
                dk_part = mm(ds, q[there])
                dk = dk_part if dk is None else dk + dk_part
                dv = dv_part if j == i else dv + dv_part
                half = slice(h * 64, (h + 1) * 64)
                dqt[half, there] += mm(kt[half, here], ds)
            dks.append(dk)
            dvs.append(dv)
        gv_ref[here, :] = jnp.where(low, dvs[0], dvs[1]).astype(BF)
        dk = (jnp.where(low, dks[0], dks[1]) * (1.0 / math.sqrt(HD))).astype(BF).astype(F32)
        gk_ref[here, :] = turn(dk, cos_ref[here, :], -sin_ref[here, :]).astype(BF)
    dq = (dqt[...].T * (1.0 / math.sqrt(HD))).astype(BF).astype(F32)
    gq_ref[...] = turn(dq, cos_ref[...], -sin_ref[...]).astype(BF)


def attend_grad(qkv, aug, kf, g, mixed, cos, sin):
    def col(j):
        return (0, j)

    return call(
        attend_grad_body,
        (PAIRS,),
        [
            (qkv, (T, 128), col),
            (qkv, (T, 128), lambda j: (0, PAIRS + j)),
            (qkv, (T, 128), lambda j: (0, 2 * PAIRS + j)),
            (aug, (1, T, 128), lambda j: (j, 0, 0)),
            (kf, None),
            (g, (T, 128), col),
            (mixed, (T, 128), col),
            (cos, None),
            (sin, None),
        ],
        [(out((T, D), BF), (T, 128), col)] * 3,
        [pltpu.VMEM((128, T), F32)],
        name="attend_grad",
        flops=12 * 10 * T * T * 128,
        nbytes=14e6,
    )


def project_grad_body(
    gq_ref, gk_ref, gv_ref, w_ref, d_ref, u_ref, n_ref, nar_ref, x_ref, gain_ref, gm_ref,
    gx_ref, gu_ref, gd_ref,
):
    @pl.when(pl.program_id(0) == 0)
    def _():
        gu_ref[...] = jnp.zeros_like(gu_ref)
        gd_ref[...] = jnp.zeros_like(gd_ref)

    grad = jnp.zeros((RB, D), F32)
    slim = jnp.zeros((RB, 128), F32)
    narrow = nar_ref[...]
    for block, ref in enumerate((gq_ref, gk_ref, gv_ref)):
        cols = slice(block * D, (block + 1) * D)
        g = ref[...]
        grad = grad + mm_nt(g, w_ref[:, cols])
        slim = slim + mm_nt(g, u_ref[:, cols])
        gu_ref[:, cols] += 2.0 * mm_tn(narrow, g)
    slim = slim.astype(BF)
    gd_ref[...] += mm_tn(slim, n_ref[...])
    grad = grad + mm_nt(slim, d_ref[...])
    gx_ref[...] = gm_ref[...] + rms_back(grad, x_ref[...].astype(F32), gain_ref[...])


def project_grad(gq, gk, gv, w, down, up, normed, narrow, x, gain, gm):
    return call(
        project_grad_body,
        (NB,),
        [
            (gq, (RB, D), rows),
            (gk, (RB, D), rows),
            (gv, (RB, D), rows),
            (w, None),
            (down, None),
            (up, None),
            (normed, (RB, D), rows),
            (narrow, (RB, 128), rows),
            (x, (RB, D), rows),
            (gain, None),
            (gm, (RB, D), rows),
        ],
        [
            (out((T, D), F32), (RB, D), rows),
            (out((128, 3 * D), F32), None),
            (out((128, D), F32), None),
        ],
        name="project_grad",
        flops=2 * T * D * 3 * D * 1.3,
        nbytes=22e6,
    )


def swap_pairs(axis):
    return [(0, 1), (1, 0)]


def gather_shared(w):
    half = w.shape[1] // 2
    core = lax.axis_index("c")
    mine = lax.dynamic_slice_in_dim(w, core * half, half, axis=1)
    mine = lax.all_gather(mine, ("z", "y"), axis=0, tiled=True)
    other = lax.ppermute(mine, "c", swap_pairs("c"))
    first = jnp.where(core == 0, mine, other)
    second = jnp.where(core == 0, other, mine)
    return jnp.concatenate([first, second], axis=1)


def gather_expert(w):
    count = w.shape[0]
    if count == 2:
        y = lax.axis_index("y")
        mine = lax.dynamic_index_in_dim(w, y, axis=0, keepdims=False)
        other = lax.ppermute(
            lax.dynamic_index_in_dim(w, 1 - y, axis=0, keepdims=False), "y", swap_pairs("y")
        )
        w = jnp.where(y == 0, jnp.stack([mine, other]), jnp.stack([other, mine]))
    elif count > 2:
        w = lax.all_to_all(w, "y", 0, 0, tiled=True)
    w = lax.all_gather(w, "z", axis=0, tiled=True)
    return w.reshape(-1, w.shape[-1])


def exchange(v):
    return lax.all_to_all(v, ("x", "c", "y"), split_axis=0, concat_axis=0, tiled=True)


def pad_to(v, shape):
    return jnp.pad(v, [(0, n - m) for m, n in zip(v.shape, shape)])


def per_device(
    tokens,
    segments,
    parents,
    adapter_of,
    routes,
    norm_gain,
    query_key_value_weight,
    output_weight,
    adapter_down,
    adapter_up,
    router,
    router_residual,
    const_proj,
    const_vec,
    w_gate_up,
    w_down,
    out_grad,
):
    qkv_full = []
    out_full = []
    gate_up_full = []
    down_full = []
    for layer in range(LAYERS):
        qkv_full.append(gather_shared(query_key_value_weight[layer]))
        out_full.append(gather_shared(output_weight[layer]))
        gate_up_full.append(gather_expert(w_gate_up[layer]))
        down_full.append(gather_expert(w_down[layer]))

    which = adapter_of[0]
    down_sel = lax.dynamic_index_in_dim(adapter_down, which, axis=2, keepdims=False)
    up_sel = lax.dynamic_index_in_dim(adapter_up, which, axis=2, keepdims=False)
    down_in = jnp.pad(
        down_sel[:, :3].transpose(0, 2, 1, 3).reshape(LAYERS, D, 3 * R), ((0, 0), (0, 0), (0, 80))
    )
    down_out = jnp.pad(down_sel[:, 3], ((0, 0), (0, 0), (0, 112)))
    up_t = 2.0 * up_sel.transpose(0, 1, 3, 2)
    up_in = jnp.zeros((LAYERS, 128, 3 * D), BF)
    for p in range(3):
        up_in = up_in.at[:, p * R : (p + 1) * R, p * D : (p + 1) * D].set(up_t[:, p])
    up_out = jnp.pad(up_t[:, 3], ((0, 0), (0, 112), (0, 0)))
    rcat = jnp.concatenate([router, const_proj[:, 0], const_proj[:, 1]], axis=2)
    rcat = jnp.pad(rcat, ((0, 0), (0, 0), (0, 112)))
    rcat_t = rcat.transpose(0, 2, 1)
    residual = pad_to(router_residual, (128, 128))
    residual_t = residual.T

    qf, kf, cos, sin, tcol, trow = prep(parents, segments.reshape(T, 1), routes)

    stream = tokens
    earlier = jnp.zeros((T, 128), F32)
    saved = []
    for layer in range(LAYERS):
        gain0 = norm_gain[layer, 0:1]
        gain1 = norm_gain[layer, 1:2]
        normed, narrow, qkv = project(
            stream, gain0, qkv_full[layer], down_in[layer], up_in[layer], cos, sin
        )
        mixed, aug = attend(qkv, qf, kf)
        mid, sent, logits, narrow_out = settle(
            stream, mixed, out_full[layer], down_out[layer], up_out[layer], gain1, rcat[layer],
            earlier, residual,
        )
        received = exchange(dispatch(trow, sent)).reshape(SLOTS, D)
        produced, gate, up = expert_forward(received, gate_up_full[layer], down_full[layer])
        returned = exchange(produced.reshape(NFFN, CAP, D)).reshape(SLOTS, D)
        following, c0, c1 = combine(tcol, returned, mid, logits, routes, gain1, const_vec[layer])
        saved.append((stream, normed, narrow, qkv, mixed, aug, mid, logits, narrow_out, gate, up, c0, c1))
        stream = following
        earlier = logits

    grad = out_grad
    grad_logits = jnp.zeros((T, 128), F32)
    tree_grads = [None] * LAYERS
    for layer in reversed(range(LAYERS)):
        x_in, normed, narrow, qkv, mixed, aug, mid, logits, narrow_out, gate, up, c0, c1 = saved[layer]
        gain0 = norm_gain[layer, 0:1]
        gain1 = norm_gain[layer, 1:2]
        a, b, grad_normed, grad_earlier = mix_grad(
            grad, mid, c0, c1, logits, routes, grad_logits, gain1, const_vec[layer], rcat_t[layer],
            residual_t,
        )
        slot_grads = exchange(dispatch_grad(trow, a, b)).reshape(SLOTS, D)
        grad_rows = expert_backward(slot_grads, gate, up, gate_up_full[layer], down_full[layer])
        back = exchange(grad_rows.reshape(NFFN, CAP, D)).reshape(SLOTS, D)
        grad_mid, grad_mixed, gu_out, gd_out = settle_grad(
            tcol, back, grad_normed, mid, grad, gain1, mixed, narrow_out, out_full[layer],
            down_out[layer], up_out[layer],
        )
        gq, gk, gv = attend_grad(qkv, aug, kf, grad_mixed, mixed, cos, sin)
        grad, gu_in, gd_in = project_grad(
            gq, gk, gv, qkv_full[layer], down_in[layer], up_in[layer], normed, narrow, x_in, gain0,
            grad_mid,
        )
        grad_logits = grad_earlier
        downs = [gd_in[p * R : (p + 1) * R] for p in range(3)] + [gd_out[:R]]
        ups = [gu_in[p * R : (p + 1) * R, p * D : (p + 1) * D] for p in range(3)] + [gu_out[:R]]
        tree_grads[layer] = jnp.stack([jnp.stack(downs), jnp.stack(ups)])

    compact = jnp.stack(tree_grads).astype(BF)
    ranks = lax.axis_size("z") * lax.axis_size("y")
    span = D // ranks
    pieces = compact.reshape(LAYERS, 2, 4, R, ranks, span).transpose(4, 0, 1, 2, 3, 5)
    pieces = lax.all_to_all(pieces, ("z", "y"), split_axis=0, concat_axis=0, tiled=True)
    owners = lax.all_gather(adapter_of, ("z", "y"), axis=0, tiled=True)
    pick = (owners[None, :] == jnp.arange(NA, dtype=jnp.int32)[:, None]).astype(F32)
    summed = jnp.dot(
        pick, pieces.reshape(ranks, -1).astype(F32), precision=HIGHEST
    ).astype(BF)
    groups = lax.axis_size("x") * lax.axis_size("c")
    each = NA // groups
    summed = lax.all_to_all(
        summed.reshape(groups, each, -1), ("x", "c"), split_axis=0, concat_axis=0, tiled=True
    )
    final = jnp.sum(summed.astype(F32), axis=0).reshape(each, LAYERS, 2, 4, R, span)
    final = final.transpose(2, 1, 3, 0, 5, 4)
    return (stream, grad, final[0], final[1])


def solution(mesh):
    owners, shards = mesh.shape["expert"], mesh.shape["shard"]
    each = NFFN // owners
    fine = jax.sharding.Mesh(
        mesh.devices.reshape(owners // 2, 2, shards // each, each), ("x", "c", "z", "y")
    )
    expert, shard = ("x", "c"), ("z", "y")
    both = expert + shard
    in_specs = (
        P(both, None),
        P(both, None),
        P(both, None),
        P(both),
        P(both, None),
        P(),
        P(None, shard, None),
        P(None, shard, None),
        P(),
        P(),
        P(),
        P(),
        P(),
        P(),
        P(None, expert, shard, None),
        P(None, expert, shard, None),
        P(both, None),
    )
    out_specs = (
        P(both, None),
        P(both, None),
        P(None, None, expert, shard, None),
        P(None, None, expert, shard, None),
    )
    return jax.shard_map(
        per_device, mesh=fine, in_specs=in_specs, out_specs=out_specs, check_vma=False
    )
```

time: 1800 us -> 961 us (0.53)
  matrix products: 648 us -> 0.25 us
  Pallas kernels: 0 us -> 392 us
  local copies, waits for them, and re-layouts: 348 us -> 50.4 us
  other arithmetic: 289 us -> 23.1 us
  blocking collectives: 0 us -> 205 us
  waiting for transfers between devices: 375 us -> 207 us
  between operations: 68.3 us -> 15.6 us
    dot_general x226 -> x1, matrix products: 647 us -> 0.25 us  [per_device(): jnp.dot(pick, pieces.reshape(ranks, -1).astype(F32), precision=HIGHEST)]
    pallas_call x0 -> x25, Pallas kernels: none -> 392 us  [call(): pl.pallas_call(body, grid=grid, in_specs=[spec(e) for e in ins], out_spec...]
    unnamed x14 -> x6, waiting for transfers between devices: 159 us -> 0.1 us
    reduce_sum x43 -> x1, other arithmetic: 132 us -> 0.36 us  [per_device(): jnp.sum(summed.astype(F32), axis=0).reshape(each, LAYERS, 2, 4, R, span)]
    all_to_all x0 -> x4, blocking collectives: none -> 111 us  [the longest x3 99.6 us: exchange(): lax.all_to_all(v, ('x', 'c', 'y'), split_axis=0, concat_axis=0, tiled=True)]
    all_gather x0 -> x2, blocking collectives: none -> 83.1 us  [gather_shared(): mine = lax.all_gather(mine, ('z', 'y'), axis=0, tiled=True)]
    gather x6 -> x0, local copies, waits for them, and re-layouts: 55.5 us -> none  [the longest x2 26.2 us: per_device(): jnp.concatenate([returned, zero_row]).astype(jnp.float32)[target]]
    convert_element_type x37 -> x0, other arithmetic: 48.8 us -> none  [the longest x29 38.4 us: rounded(): return value.astype(jnp.bfloat16)]
  transfers between devices with their start and end apart: 19 -> 20, of which waited for: 11 -> 8; matrix products, arithmetic and copies ran while one was open for 35% -> 6% of each run, Pallas kernels for 0% -> 15%
where the time goes in v1:
time: 961 us; the launch traced here: 947 us
  Pallas kernels  392 us (41%)
  waiting for transfers between devices  207 us (22%)
  blocking collectives  205 us (21%)
  starting transfers between devices  53.2 us (6%)
  local copies, waits for them, and re-layouts  50.4 us (5%)
  other arithmetic  23.1 us (2%)
  between operations  15.6 us (2%)
    pallas_call x25, Pallas kernels, call(): pl.pallas_call(body, grid=grid, in_specs=[spec(e) for e in ins], out_spec...  392 us
    all_gather x4, waiting for transfers between devices, gather_expert(): w = lax.all_gather(w, 'z', axis=0, tiled=True)  118 us
    all_to_all x3, blocking collectives, exchange(): lax.all_to_all(v, ('x', 'c', 'y'), split_axis=0, concat_axis=0, tiled=True)  99.6 us
    all_gather x2, blocking collectives, gather_shared(): mine = lax.all_gather(mine, ('z', 'y'), axis=0, tiled=True)  83.1 us
    all_to_all x5, waiting for transfers between devices, exchange(): lax.all_to_all(v, ('x', 'c', 'y'), split_axis=0, concat_axis=0, tiled=True)  56.3 us
    ppermute x4, waiting for transfers between devices, gather_expert(): lax.ppermute(lax.dynamic_index_in_dim(w, 1 - y, axis=0, keepdims=False),...  32.5 us
    all_to_all x5, starting transfers between devices, exchange(): lax.all_to_all(v, ('x', 'c', 'y'), split_axis=0, concat_axis=0, tiled=True)  24.1 us
  transfers between devices with their start and end apart: 20, of which 8 were waited for; matrix products, arithmetic and copies ran while one was open for 6% of the time, Pallas kernels for 15%

profile of v1, /device:TPU:9, one launch (start us, length us, event | category | flops | bytes accessed | tf_op | source)
XLA Modules:
  0.0 946.8 jit_solution(11112996127196290688)
XLA Ops:
  25.1 17.7 %collective-permute-done.2 = bf16[96,4096]{1,0:T(8,128)(2,1)S(1)} collective-permute-done((bf16[96,4096]{1,0:T(8,128)(2,1)S(1)}, bf16[96,4096]{1,0:T(8,128)(2,1)S(1)}, u32[]{:S(2)}, u32[]{:S(2)}) %collective-permute-start.2) | collective-permute-done | bytes 786464 | tf_op jit(solution)/shard_map/ppermute | solution.py:800
  47.0 32.0 %all-gather.1 = bf16[1,768,384]{2,1,0:T(8,128)(2,1)} all-gather(bf16[1,96,384]{2,1,0:T(8,128)(2,1)S(1)} %constant_dynamic-slice_fusion.2), channel_id=3, replica_groups=mesh['x'=2,'c'=2,'z'=4,'y'=2] {'z','y'}, dimensions={1}, use_global_device_ids=true | all-gather | bytes 663552 | tf_op jit(solution)/shard_map/all_gather | solution.py:788
  138.2 21.4 %attend.2 = (bf16[1024,768]{1,0:T(8,128)(2,1)}, bf16[6,1024,128]{2,1,0:T(8,128)(2,1)}) custom-call(bf16[1024,2304]{1,0:T(8,128)(2,1)} %get-tuple-element.107.q_ref.k_ref.v_ref, bf16[1024,2304]{1,0:T(8,128)(2,1)} %get-tuple-element.107.q_ref.k_ref.v_ref, bf16[1024,2304]{1,0:T(8,128)(2,1)} %get-tuple-element.107.q_ref.k_ref.v_ref, ...), custom_call_target="tpu_custom_call" | custom-call | flops 6442450944 | bytes 8000000 | tf_op jit(solution)/shard_map/attend/pallas_call | solution.py:71
  160.4 12.4 %settle.2 = (f32[1024,768]{1,0:T(8,128)}, bf16[1024,768]{1,0:T(8,128)(2,1)}, f32[1024,128]{1,0:T(8,128)}, bf16[1024,128]{1,0:T(8,128)(2,1)}) custom-call(bf16[1024,768]{1,0:T(8,128)(2,1)} %x_ref.5, bf16[1024,768]{1,0:T(8,128)(2,1)} %get-tuple-element.110.mixed_ref, bf16[768,768]{1,0:T(8,128)(2,1)} %pad_maximum_fusion.2.w_ref, ...), custom_call_target="tpu_custom_call" | custom-call | flops 2415919104 | bytes 10000000 | tf_op jit(solution)/shard_map/settle/pallas_call | solution.py:71
  184.9 51.1 %all-gather.3 = bf16[1,768,384]{2,1,0:T(8,128)(2,1)S(1)} all-gather(bf16[1,96,384]{2,1,0:T(8,128)(2,1)S(1)} %constant_dynamic-slice_fusion), channel_id=5, replica_groups=mesh['x'=2,'c'=2,'z'=4,'y'=2] {'z','y'}, dimensions={1}, use_global_device_ids=true | all-gather | bytes 663552 | tf_op jit(solution)/shard_map/all_gather | solution.py:788
  242.7 61.9 %all-gather.11.cloned.1.call-done = bf16[8,96,4096]{2,1,0:T(8,128)(2,1)} async-done(((bf16[2,96,4096]{2,1,0:T(8,128)(2,1)}), bf16[8,96,4096]{2,1,0:T(8,128)(2,1)}) %all-gather.11.cloned.1.call-update) | async-done | bytes 6291472 | tf_op jit(solution)/shard_map/all_gather | solution.py:806
  304.6 21.8 %expert_forward.2 = (bf16[1536,768]{1,0:T(8,128)(2,1)}, bf16[1536,2048]{1,0:T(8,128)(2,1)}, bf16[1536,2048]{1,0:T(8,128)(2,1)}) custom-call(bf16[1536,768]{1,0:T(8,128)(2,1)} %bitcast.24.r_ref, bf16[768,4096]{1,0:T(8,128)(2,1)} %bitcast.153, bf16[768,4096]{1,0:T(8,128)(2,1)} %bitcast.154, bf16[2048,768]{1,0:T(8,128)(2,1)} %bitcast.161), custom_call_target="tpu_custom_call" | custom-call | flops 14495514624 | bytes 26000000 | tf_op jit(solution)/shard_map/expert_forward/pallas_call | solution.py:71
  339.2 20.7 %all-to-all-done.1 = bf16[8,192,768]{2,1,0:T(8,128)(2,1)} async-done(((bf16[8,192,768]{2,1,0:T(8,128)(2,1)}), bf16[8,192,768]{2,1,0:T(8,128)(2,1)}, u32[]{:S(2)}, u32[]{:S(2)}) %all-to-all-start.1) | async-done | bytes 2359328 | tf_op jit(solution)/shard_map/all_to_all | solution.py:811
  381.1 21.5 %attend.3 = (bf16[1024,768]{1,0:T(8,128)(2,1)}, bf16[6,1024,128]{2,1,0:T(8,128)(2,1)}) custom-call(bf16[1024,2304]{1,0:T(8,128)(2,1)} %get-tuple-element.116.q_ref.k_ref.v_ref, bf16[1024,2304]{1,0:T(8,128)(2,1)} %get-tuple-element.116.q_ref.k_ref.v_ref, bf16[1024,2304]{1,0:T(8,128)(2,1)} %get-tuple-element.116.q_ref.k_ref.v_ref, ...), custom_call_target="tpu_custom_call" | custom-call | flops 6442450944 | bytes 8000000 | tf_op jit(solution)/shard_map/attend/pallas_call | solution.py:71
  402.6 12.5 %settle.3 = (f32[1024,768]{1,0:T(8,128)}, bf16[1024,768]{1,0:T(8,128)(2,1)}, f32[1024,128]{1,0:T(8,128)}, bf16[1024,128]{1,0:T(8,128)(2,1)}) custom-call(f32[1024,768]{1,0:T(8,128)} %get-tuple-element.115.x_ref, bf16[1024,768]{1,0:T(8,128)(2,1)} %get-tuple-element.117.mixed_ref, bf16[768,768]{1,0:T(8,128)(2,1)} %pad_maximum_fusion.3.w_ref, ...), custom_call_target="tpu_custom_call" | custom-call | flops 2415919104 | bytes 10000000 | tf_op jit(solution)/shard_map/settle/pallas_call | solution.py:71
  427.2 56.1 %all-gather.15.cloned.1.call-done = bf16[8,96,4096]{2,1,0:T(8,128)(2,1)} async-done(((bf16[2,96,4096]{2,1,0:T(8,128)(2,1)}), bf16[8,96,4096]{2,1,0:T(8,128)(2,1)}) %all-gather.15.cloned.1.call-update) | async-done | bytes 6291472 | tf_op jit(solution)/shard_map/all_gather | solution.py:806
  483.3 21.8 %expert_forward.3 = (bf16[1536,768]{1,0:T(8,128)(2,1)}, bf16[1536,2048]{1,0:T(8,128)(2,1)}, bf16[1536,2048]{1,0:T(8,128)(2,1)}) custom-call(bf16[1536,768]{1,0:T(8,128)(2,1)} %bitcast.45.r_ref, bf16[768,4096]{1,0:T(8,128)(2,1)} %bitcast.157, bf16[768,4096]{1,0:T(8,128)(2,1)} %bitcast.158, bf16[2048,768]{1,0:T(8,128)(2,1)} %bitcast.163), custom_call_target="tpu_custom_call" | custom-call | flops 14495514624 | bytes 26000000 | tf_op jit(solution)/shard_map/expert_forward/pallas_call | solution.py:71
  511.4 26.6 %all-to-all-done.3 = bf16[8,192,768]{2,1,0:T(8,128)(2,1)} async-done(((bf16[8,192,768]{2,1,0:T(8,128)(2,1)}), bf16[8,192,768]{2,1,0:T(8,128)(2,1)}, u32[]{:S(2)}, u32[]{:S(2)}) %all-to-all-start.3) | async-done | bytes 2359328 | tf_op jit(solution)/shard_map/all_to_all | solution.py:811
  548.1 15.8 %mix_grad.2 = (bf16[1024,768]{1,0:T(8,128)(2,1)}, bf16[1024,768]{1,0:T(8,128)(2,1)}, f32[1024,768]{1,0:T(8,128)}, f32[1024,128]{1,0:T(8,128)}) custom-call(bf16[1024,768]{1,0:T(8,128)(2,1)} %g_ref.3, f32[1024,768]{1,0:T(8,128)} %get-tuple-element.120.mid_ref, bf16[1024,768]{1,0:T(8,128)(2,1)} %get-tuple-element.125.c0_ref, ...), custom_call_target="tpu_custom_call" | custom-call | flops 1207959552 | bytes 16000000 | tf_op jit(solution)/shard_map/mix_grad/pallas_call | solution.py:71
  573.0 33.3 %all_to_all.50 = bf16[8,192,768]{2,1,0:T(8,128)(2,1)} all-to-all(bf16[8,192,768]{2,1,0:T(8,128)(2,1)} %dispatch_grad.2), channel_id=1, replica_groups=mesh['x'=2,'c'=2,'z'=4,'y'=2] {'x','c','y'}, dimensions={0} | all-to-all | bytes 4718592 | tf_op jit(solution)/shard_map/all_to_all | solution.py:811
  606.3 23.7 %expert_backward.2 = bf16[1536,768]{1,0:T(8,128)(2,1)} custom-call(bf16[1536,768]{1,0:T(8,128)(2,1)} %bitcast.142, bf16[1536,2048]{1,0:T(8,128)(2,1)} %get-tuple-element.129.gate_ref, bf16[1536,2048]{1,0:T(8,128)(2,1)} %get-tuple-element.130.up_ref, bf16[768,4096]{1,0:T(8,128)(2,1)} %bitcast.159, bf16[768,4096]{1,0:T(8,128)(2,1)} %bitcast.160, ...), custom_call_target="tpu_custom_call" | custom-call | flops 14495514624 | bytes 26000000 | tf_op jit(solution)/shard_map/expert_backward/pallas_call | solution.py:71
  630.0 33.3 %all_to_all.51 = bf16[8,192,768]{2,1,0:T(8,128)(2,1)} all-to-all(bf16[8,192,768]{2,1,0:T(8,128)(2,1)} %bitcast.144), channel_id=1, replica_groups=mesh['x'=2,'c'=2,'z'=4,'y'=2] {'x','c','y'}, dimensions={0} | all-to-all | bytes 4718592 | tf_op jit(solution)/shard_map/all_to_all | solution.py:811
  675.2 35.8 %attend_grad.2 = (bf16[1024,768]{1,0:T(8,128)(2,1)}, bf16[1024,768]{1,0:T(8,128)(2,1)}, bf16[1024,768]{1,0:T(8,128)(2,1)}) custom-call(bf16[1024,2304]{1,0:T(8,128)(2,1)} %get-tuple-element.116.q_ref.k_ref.v_ref, bf16[1024,2304]{1,0:T(8,128)(2,1)} %get-tuple-element.116.q_ref.k_ref.v_ref, bf16[1024,2304]{1,0:T(8,128)(2,1)} %get-tuple-element.116.q_ref.k_ref.v_ref, ...), custom_call_target="tpu_custom_call" | custom-call | flops 16106127360 | bytes 14000000 | tf_op jit(solution)/shard_map/attend_grad/pallas_call | solution.py:71
  711.0 13.4 %project_grad.2 = (f32[1024,768]{1,0:T(8,128)}, f32[128,2304]{1,0:T(8,128)}, f32[128,768]{1,0:T(8,128)}) custom-call(bf16[1024,768]{1,0:T(8,128)(2,1)} %get-tuple-element.134.gq_ref, bf16[1024,768]{1,0:T(8,128)(2,1)} %get-tuple-element.135.gk_ref, bf16[1024,768]{1,0:T(8,128)(2,1)} %get-tuple-element.136.gv_ref, bf16[768,2304]{1,0:T(8,128)(2,1)} %pad_maximum_fusion.1.w_ref, ...), custom_call_target="tpu_custom_call" | custom-call | flops 4711042048 | bytes 22000000 | tf_op jit(solution)/shard_map/project_grad/pallas_call | solution.py:71
  724.4 15.9 %mix_grad.3 = (bf16[1024,768]{1,0:T(8,128)(2,1)}, bf16[1024,768]{1,0:T(8,128)(2,1)}, f32[1024,768]{1,0:T(8,128)}, f32[1024,128]{1,0:T(8,128)}) custom-call(f32[1024,768]{1,0:T(8,128)} %get-tuple-element.140.g_ref, f32[1024,768]{1,0:T(8,128)} %get-tuple-element.113.mid_ref, bf16[1024,768]{1,0:T(8,128)(2,1)} %get-tuple-element.141.c0_ref, ...), custom_call_target="tpu_custom_call" | custom-call | flops 1207959552 | bytes 16000000 | tf_op jit(solution)/shard_map/mix_grad/pallas_call | solution.py:71
  749.3 33.0 %all_to_all.52 = bf16[8,192,768]{2,1,0:T(8,128)(2,1)} all-to-all(bf16[8,192,768]{2,1,0:T(8,128)(2,1)} %dispatch_grad.3), channel_id=1, replica_groups=mesh['x'=2,'c'=2,'z'=4,'y'=2] {'x','c','y'}, dimensions={0} | all-to-all | bytes 4718592 | tf_op jit(solution)/shard_map/all_to_all | solution.py:811
  782.4 23.7 %expert_backward.3 = bf16[1536,768]{1,0:T(8,128)(2,1)} custom-call(bf16[1536,768]{1,0:T(8,128)(2,1)} %bitcast.143, bf16[1536,2048]{1,0:T(8,128)(2,1)} %get-tuple-element.146.gate_ref, bf16[1536,2048]{1,0:T(8,128)(2,1)} %get-tuple-element.147.up_ref, bf16[768,4096]{1,0:T(8,128)(2,1)} %bitcast.155, bf16[768,4096]{1,0:T(8,128)(2,1)} %bitcast.156, ...), custom_call_target="tpu_custom_call" | custom-call | flops 14495514624 | bytes 26000000 | tf_op jit(solution)/shard_map/expert_backward/pallas_call | solution.py:71
  853.3 35.7 %attend_grad.3 = (bf16[1024,768]{1,0:T(8,128)(2,1)}, bf16[1024,768]{1,0:T(8,128)(2,1)}, bf16[1024,768]{1,0:T(8,128)(2,1)}) custom-call(bf16[1024,2304]{1,0:T(8,128)(2,1)} %get-tuple-element.107.q_ref.k_ref.v_ref, bf16[1024,2304]{1,0:T(8,128)(2,1)} %get-tuple-element.107.q_ref.k_ref.v_ref, bf16[1024,2304]{1,0:T(8,128)(2,1)} %get-tuple-element.107.q_ref.k_ref.v_ref, ...), custom_call_target="tpu_custom_call" | custom-call | flops 16106127360 | bytes 14000000 | tf_op jit(solution)/shard_map/attend_grad/pallas_call | solution.py:71
  889.0 13.2 %project_grad.3 = (f32[1024,768]{1,0:T(8,128)}, f32[128,2304]{1,0:T(8,128)}, f32[128,768]{1,0:T(8,128)}) custom-call(bf16[1024,768]{1,0:T(8,128)(2,1)} %get-tuple-element.151.gq_ref, bf16[1024,768]{1,0:T(8,128)(2,1)} %get-tuple-element.152.gk_ref, bf16[1024,768]{1,0:T(8,128)(2,1)} %get-tuple-element.153.gv_ref, bf16[768,2304]{1,0:T(8,128)(2,1)} %pad_maximum_fusion.w_ref, ...), custom_call_target="tpu_custom_call" | custom-call | flops 4711042048 | bytes 22000000 | tf_op jit(solution)/shard_map/project_grad/pallas_call | solution.py:71
  (209 shorter events, 276.9 us)
Async XLA Ops:
  7.2 90.8 %all-gather.19.cloned.1.call-start = ((), (), s32[]{:S(2)}) async-start(), calls=%async_computation.14 | async-start | bytes 1990656 | tf_op jit(solution)/shard_map/all_gather | solution.py:788
  9.3 233.4 %all-gather.21.cloned.1.call-start = ((), (), s32[]{:S(2)}) async-start(), calls=%async_computation.15 | async-start | bytes 1990656 | tf_op jit(solution)/shard_map/all_gather | solution.py:788
  10.1 232.6 %all-gather.13.cloned.1.call-start = ((), (), s32[]{:S(2)}) async-start(), calls=%async_computation.11 | async-start | bytes 3932160 | tf_op jit(solution)/shard_map/all_gather | solution.py:806
  10.3 10.0 %collective-permute-start.3 = (bf16[256,768]{1,0:T(8,128)(2,1)S(1)}, bf16[256,768]{1,0:T(8,128)(2,1)S(1)}, u32[]{:S(2)}, u32[]{:S(2)}) collective-permute-start(bf16[256,768]{1,0:T(8,128)(2,1)S(1)} %get-tuple-element.201), channel_id=1, source_target_pairs={{0,1},{1,0},{2,3},{3,2},{4,5},{5,4},{6,7},{7,6},{8,9},{9,8},{10,11... | collective-permute-start | bytes 1179656 | tf_op jit(solution)/shard_map/ppermute | solution.py:800
  21.5 283.1 %all-gather.11.cloned.1.call-start = ((), (), s32[]{:S(2)}) async-start(), calls=%async_computation.10 | async-start | bytes 7864320 | tf_op jit(solution)/shard_map/all_gather | solution.py:806
  23.8 19.0 %collective-permute-start.2 = (bf16[96,4096]{1,0:T(8,128)(2,1)S(1)}, bf16[96,4096]{1,0:T(8,128)(2,1)S(1)}, u32[]{:S(2)}, u32[]{:S(2)}) collective-permute-start(bf16[96,4096]{1,0:T(8,128)(2,1)S(1)} %get-tuple-element.185), channel_id=1, source_target_pairs={{0,1},{1,0},{2,3},{3,2},{4,5},{5,4},{6,7},{7,6},{8,9},{9,8},{10,11... | collective-permute-start | bytes 2359304 | tf_op jit(solution)/shard_map/ppermute | solution.py:800
  44.2 382.9 %all-gather.17.cloned.1.call-start = ((), (), s32[]{:S(2)}) async-start(), calls=%async_computation.13 | async-start | bytes 3932160 | tf_op jit(solution)/shard_map/all_gather | solution.py:806
  44.4 44.6 %collective-permute-start.7 = (bf16[256,768]{1,0:T(8,128)(2,1)S(1)}, bf16[256,768]{1,0:T(8,128)(2,1)S(1)}, u32[]{:S(2)}, u32[]{:S(2)}) collective-permute-start(bf16[256,768]{1,0:T(8,128)(2,1)S(1)} %get-tuple-element.197), channel_id=1, source_target_pairs={{0,1},{1,0},{2,3},{3,2},{4,5},{5,4},{6,7},{7,6},{8,9},{9,8},{10,11... | collective-permute-start | bytes 1179656 | tf_op jit(solution)/shard_map/ppermute | solution.py:800
  79.0 32.4 %collective-permute-start.1 = (bf16[768,384]{1,0:T(8,128)(2,1)}, bf16[768,384]{1,0:T(8,128)(2,1)}, u32[]{:S(2)}, u32[]{:S(2)}) collective-permute-start(bf16[768,384]{1,0:T(8,128)(2,1)} %bitcast.15), channel_id=1, source_target_pairs={{0,8},{8,0},{1,9},{9,1},{2,10},{10,2},{3,11},{11,3},{4,12},{12,4},... | collective-permute-start | bytes 1769480 | tf_op jit(solution)/shard_map/ppermute | solution.py:789
  90.0 393.3 %all-gather.15.cloned.1.call-start = ((), (), s32[]{:S(2)}) async-start(), calls=%async_computation.12 | async-start | bytes 7864320 | tf_op jit(solution)/shard_map/all_gather | solution.py:806
  91.0 29.0 %collective-permute-start.6 = (bf16[96,4096]{1,0:T(8,128)(2,1)}, bf16[96,4096]{1,0:T(8,128)(2,1)}, u32[]{:S(2)}, u32[]{:S(2)}) collective-permute-start(bf16[96,4096]{1,0:T(8,128)(2,1)} %get-tuple-element.183), channel_id=1, source_target_pairs={{0,1},{1,0},{2,3},{3,2},{4,5},{5,4},{6,7},{7,6},{8,9},{9,8},{10,11... | collective-permute-start | bytes 2359304 | tf_op jit(solution)/shard_map/ppermute | solution.py:800
  98.0 24.8 %collective-permute-start = (bf16[768,1152]{1,0:T(8,128)(2,1)}, bf16[768,1152]{1,0:T(8,128)(2,1)}, u32[]{:S(2)}, u32[]{:S(2)}) collective-permute-start(bf16[768,1152]{1,0:T(8,128)(2,1)} %bitcast.146), channel_id=1, source_target_pairs={{0,8},{8,0},{1,9},{9,1},{2,10},{10,2},{3,11},{11,3},{4,12},{12,4},... | collective-permute-start | bytes 5308424 | tf_op jit(solution)/shard_map/ppermute | solution.py:789
  101.3 6.3 copy-start.19
  179.7 63.0 %all-to-all-start = ((bf16[8,192,768]{2,1,0:T(8,128)(2,1)}), bf16[8,192,768]{2,1,0:T(8,128)(2,1)}, u32[]{:S(2)}, u32[]{:S(2)}) async-start(bf16[8,192,768]{2,1,0:T(8,128)(2,1)} %dispatch.2), calls=%async_computation | async-start | bytes 4718592 | tf_op jit(solution)/shard_map/all_to_all | solution.py:811
  236.0 97.3 %collective-permute-start.5 = (bf16[768,384]{1,0:T(8,128)(2,1)S(1)}, bf16[768,384]{1,0:T(8,128)(2,1)S(1)}, u32[]{:S(2)}, u32[]{:S(2)}) collective-permute-start(bf16[768,384]{1,0:T(8,128)(2,1)S(1)} %bitcast.136), channel_id=1, source_target_pairs={{0,8},{8,0},{1,9},{9,1},{2,10},{10,2},{3,11},{11,3},{4,12},{12,4},... | collective-permute-start | bytes 1769480 | tf_op jit(solution)/shard_map/ppermute | solution.py:789
  242.7 91.9 %collective-permute-start.4 = (bf16[768,1152]{1,0:T(8,128)(2,1)}, bf16[768,1152]{1,0:T(8,128)(2,1)}, u32[]{:S(2)}, u32[]{:S(2)}) collective-permute-start(bf16[768,1152]{1,0:T(8,128)(2,1)} %bitcast.145), channel_id=1, source_target_pairs={{0,8},{8,0},{1,9},{9,1},{2,10},{10,2},{3,11},{11,3},{4,12},{12,4},... | collective-permute-start | bytes 5308424 | tf_op jit(solution)/shard_map/ppermute | solution.py:789
  326.4 6.4 copy-start.17
  326.4 33.5 %all-to-all-start.1 = ((bf16[8,192,768]{2,1,0:T(8,128)(2,1)}), bf16[8,192,768]{2,1,0:T(8,128)(2,1)}, u32[]{:S(2)}, u32[]{:S(2)}) async-start(bf16[8,192,768]{2,1,0:T(8,128)(2,1)} %bitcast.139), calls=%async_computation.1 | async-start | bytes 4718592 | tf_op jit(solution)/shard_map/all_to_all | solution.py:811
  422.1 61.2 %all-to-all-start.2 = ((bf16[8,192,768]{2,1,0:T(8,128)(2,1)}), bf16[8,192,768]{2,1,0:T(8,128)(2,1)}, u32[]{:S(2)}, u32[]{:S(2)}) async-start(bf16[8,192,768]{2,1,0:T(8,128)(2,1)} %dispatch.3), calls=%async_computation.2 | async-start | bytes 4718592 | tf_op jit(solution)/shard_map/all_to_all | solution.py:811
  505.0 33.0 %all-to-all-start.3 = ((bf16[8,192,768]{2,1,0:T(8,128)(2,1)}), bf16[8,192,768]{2,1,0:T(8,128)(2,1)}, u32[]{:S(2)}, u32[]{:S(2)}) async-start(bf16[8,192,768]{2,1,0:T(8,128)(2,1)} %bitcast.140), calls=%async_computation.3 | async-start | bytes 4718592 | tf_op jit(solution)/shard_map/all_to_all | solution.py:811
  806.1 31.8 %all-to-all-start.7 = ((bf16[8,192,768]{2,1,0:T(8,128)(2,1)}), bf16[8,192,768]{2,1,0:T(8,128)(2,1)S(1)}, u32[]{:S(2)}, u32[]{:S(2)}) async-start(bf16[8,192,768]{2,1,0:T(8,128)(2,1)} %bitcast.138), calls=%async_computation.7 | async-start | bytes 4718592 | tf_op jit(solution)/shard_map/all_to_all | solution.py:811
  809.7 18.7 %copy-start.5 = (f32[128,2304]{1,0:T(8,128)S(1)}, f32[128,2304]{1,0:T(8,128)}, u32[]{:S(2)}) copy-start(f32[128,2304]{1,0:T(8,128)} %get-tuple-element.164) | copy-start | bytes 3538948
  903.7 9.4 copy-start.21
  906.4 18.3 %all-to-all-start.8 = ((bf16[8,2,2,4,16,96]{5,4,3,2,1,0:T(8,128)(2,1)}), bf16[8,2,2,4,16,96]{5,4,3,2,1,0:T(8,128)(2,1)S(1)}, u32[]{:S(2)}, u32[]{:S(2)}) async-start(bf16[8,2,2,4,16,96]{5,4,3,2,1,0:T(8,128)(2,1)} %maximum_bitcast_fusion), calls=%async_computation.8 | async-start | bytes 1048576 | tf_op jit(solution)/shard_map/all_to_all | solution.py:921
  (18 other events, 53.7 us)
Sparse Core Ops, SparseCore 0:
  10.2 54.3 all-gather.18
  66.8 55.9 all-gather.20
  124.4 60.4 all-gather.12
  186.3 118.2 all-gather.10
  306.0 62.1 all-gather.16
  369.6 113.6 all-gather.14

commit v2 on v1

--- a/solution.py
+++ b/solution.py
@@ -93,7 +93,35 @@
     return (i, 0)
 
 
-def prep_body(par_ref, seg_ref, rt_ref, qf_ref, kf_ref, cos_ref, sin_ref, tcol_ref, trow_ref, anc):
+def three(v):
+    high = v.astype(BF)
+    rest = v - high.astype(F32)
+    middle = rest.astype(BF)
+    return high, middle, (rest - middle.astype(F32)).astype(BF)
+
+
+def spread_lanes(v):
+    a, b, c = (part.astype(F32) for part in three(v))
+    total = a + pltpu.roll(b, 16, 1) + pltpu.roll(c, 32, 1)
+    total = total + pltpu.roll(a, 48, 1) + pltpu.roll(b, 64, 1) + pltpu.roll(a, 80, 1)
+    return total.astype(BF)
+
+
+def stack_rows(w):
+    a, b, c = three(w)
+    return jnp.concatenate([a, a, a, b, b, c, jnp.zeros((32, w.shape[1]), BF)], axis=0)
+
+
+def prep_body(
+    par_ref, seg_ref, rt_ref, rc_ref, rct_ref, res_ref, rest_ref,
+    qf_ref, kf_ref, cos_ref, sin_ref, tcol_ref, trow_ref, rs_ref, rts_ref, ress_ref, rests_ref, anc,
+):
+    for layer in range(LAYERS):
+        a, b, c = (part.astype(F32) for part in three(rc_ref[layer]))
+        rs_ref[layer] = (a + pltpu.roll(b, 16, 1) + pltpu.roll(c, 32, 1)).astype(BF)
+        rts_ref[layer] = stack_rows(rct_ref[layer])
+    ress_ref[...] = stack_rows(res_ref[...])
+    rests_ref[...] = stack_rows(rest_ref[...])
     first = iota((1, 128), 1) & 63
     anc[...] = jnp.zeros_like(anc)
     anc[0:1, :] = (first == 0).astype(F32)
@@ -133,11 +161,19 @@
     sin_ref[...] = jnp.where((lane & 32) == 0, -sine, sine)
 
 
-def prep(parents, seg_col, routes):
+def prep(parents, seg_col, routes, rcat, rcat_t, residual, residual_t):
     return call(
         prep_body,
         (1,),
-        [(parents, "smem"), (seg_col, None), (routes, None)],
+        [
+            (parents, "smem"),
+            (seg_col, None),
+            (routes, None),
+            (rcat, None),
+            (rcat_t, None),
+            (residual, None),
+            (residual_t, None),
+        ],
         [
             (out((T, 128), BF), None),
             (out((T, 128), BF), None),
@@ -145,6 +181,10 @@
             (out((T, 128), F32), None),
             (out((T, 128), jnp.int32), None),
             (out((8, T), jnp.int32), None),
+            (out((LAYERS, D, 128), BF), None),
+            (out((LAYERS, 128, D), BF), None),
+            (out((128, 128), BF), None),
+            (out((128, 128), BF), None),
         ],
         [pltpu.VMEM((128, 128), F32)],
         name="prep",
@@ -167,7 +207,7 @@
     nar_ref[...] = narrow
     for block in range(3):
         cols = slice(block * D, (block + 1) * D)
-        part = mm(normed, w_ref[:, cols]) + mm(narrow, u_ref[:, cols])
+        part = mm(normed, w_ref[block]) + mm(narrow, u_ref[:, cols])
         for j in range(PAIRS):
             piece = part[:, j * 128 : (j + 1) * 128]
             if block < 2:
@@ -198,7 +238,7 @@
         [
             (x, (RB, D), rows),
             (gain, None),
-            (w, None),
+            (w, (3, D, D), lambda i: (0, 0, 0)),
             (down, None),
             (up, None),
             (cos, (RB, 128), rows),
@@ -213,13 +253,6 @@
         flops=2 * T * D * 3 * D,
         nbytes=12e6,
     )
-
-
-def three(v):
-    high = v.astype(BF)
-    rest = v - high.astype(F32)
-    middle = rest.astype(BF)
-    return high, middle, (rest - middle.astype(F32)).astype(BF)
 
 
 def attend_body(q_ref, k_ref, v_ref, qf_ref, kf_ref, mixed_ref, aug_ref):
@@ -290,12 +323,18 @@
     mixed = mixed_ref[...]
     narrow = mm(mixed, d_ref[...]).astype(BF)
     nar_ref[...] = narrow
-    mid = x_ref[...].astype(F32) + mm(mixed, w_ref[...]) + mm(narrow, u_ref[...])
+    mid = x_ref[...].astype(F32) + mm(mixed, w_ref[0]) + mm(narrow, u_ref[...])
     mid_ref[...] = mid
     scale = lax.rsqrt(jnp.mean(mid * mid, axis=1, keepdims=True) + EPSILON)
     normed = mid * scale * g_ref[...]
     sent_ref[...] = normed.astype(BF)
-    lg_ref[...] = mm_exact(normed, rt_ref[...]) + mm_exact(earlier_ref[...], res_ref[...])
+    a, b, c = three(normed)
+    one, two, last = mm(a, rt_ref[...]), mm(b, rt_ref[...]), mm(c, rt_ref[...])
+    total = one + two + last + pltpu.roll(one + two, 112, 1) + pltpu.roll(one, 96, 1)
+    lane = iota((RB, 128), 1)
+    earlier = jnp.where(lane < NEXP, earlier_ref[...], 0.0)
+    extra = mm(spread_lanes(earlier), res_ref[...])
+    lg_ref[...] = jnp.where(lane < 16, total + extra, 0.0)
 
 
 def settle(x, mixed, w, down, up, gain, router, earlier, residual):
@@ -305,7 +344,7 @@
         [
             (x, (RB, D), rows),
             (mixed, (RB, D), rows),
-            (w, None),
+            (w, (1, D, D), lambda i: (3, 0, 0)),
             (down, None),
             (up, None),
             (gain, None),
@@ -343,114 +382,341 @@
     )[0]
 
 
-def dispatch_grad_body(trow_ref, a_ref, b_ref, o_ref):
+def dispatch_grad_body(trow_ref, g_ref, lg_ref, rt_ref, o_ref, first, second):
+    @pl.when(pl.program_id(0) == 0)
+    def _():
+        for i in range(NB):
+            at = slice(i * RB, (i + 1) * RB)
+            gates = mix_terms(lg_ref[at, :], rt_ref[at, :])[0]
+            g = g_ref[at, :].astype(F32)
+            first[at, :] = (gates[0] * g).astype(BF)
+            second[at, :] = (gates[1] * g).astype(BF)
+
     place = pl.program_id(0) * CAP + iota((CAP, T), 0)
     hit0 = (trow_ref[0:1, :] == place).astype(F32).astype(BF)
     hit1 = (trow_ref[1:2, :] == place).astype(F32).astype(BF)
-    o_ref[0] = (mm(hit0, a_ref[...]) + mm(hit1, b_ref[...])).astype(BF)
-
-
-def dispatch_grad(trow, a, b):
+    o_ref[0] = (mm(hit0, first[...]) + mm(hit1, second[...])).astype(BF)
+
+
+def dispatch_grad(trow, g, logits, routes):
     return call(
         dispatch_grad_body,
         (NFFN,),
-        [(trow, None), (a, None), (b, None)],
+        [(trow, None), (g, None), (logits, None), (routes, None)],
         [(out((NFFN, CAP, D), BF), (1, CAP, D), lambda j: (j, 0, 0))],
+        [pltpu.VMEM((T, D), BF), pltpu.VMEM((T, D), BF)],
         name="dispatch_grad",
         flops=4 * T * SLOTS * D,
         nbytes=6e6,
     )[0]
 
 
-MB = 512
-
-
-def expert_body(r_ref, wg_ref, wu_ref, wd_ref, p_ref, gate_ref, up_ref, acc):
-    step = pl.program_id(0)
-
-    @pl.when(step == 0)
-    def _():
+PR = 2 * CAP
+NP = NFFN // 2
+
+
+def flip(bit, change):
+    return bit + change - 2 * bit * change
+
+
+def owner_at(p, h, each):
+    x, c, y = (lax.axis_index(name) for name in ("x", "c", "y"))
+    far, near = 1 - p // 2, 1 - p % 2
+    c = flip(c, h)
+    if each == 2:
+        x, y = flip(x, far), flip(y, near)
+    else:
+        x = 2 * flip(x // 2, far) + flip(x % 2, near)
+    return {"x": x, "c": c, "y": y}, (x * 2 + c) * each + y
+
+
+PLACES = [(p, h) for p in range(NP) for h in range(2)]
+
+
+def greet(each):
+    barrier = pltpu.get_barrier_semaphore()
+    for p, h in PLACES[:-2] + PLACES[-1:]:
+        pl.semaphore_signal(
+            barrier, inc=1, device_id=owner_at(p, h, each)[0], device_id_type=pl.DeviceIdType.MESH
+        )
+    pl.semaphore_wait(barrier, NFFN - 1)
+
+
+def block_of(ref, p, h):
+    return ref.at[p, h * CAP : (h + 1) * CAP, :]
+
+
+def fetch_weights(split, gate_ups, down_ref, w1, w2, sems):
+    copies = []
+    if split:
+        y = lax.axis_index("y")
+        for side, ref in enumerate(gate_ups):
+            mine = flip(y, side)
+            count, size = ref.shape[0], ref.shape[1]
+            for k in range(count):
+                at = pl.multiple_of((2 * k + mine) * size, size)
+                copies.append(
+                    pltpu.make_async_copy(
+                        ref.at[k], w1.at[pl.ds(at, size), :], sems.at[side * count + k]
+                    )
+                )
+    else:
+        copies.append(pltpu.make_async_copy(gate_ups[0], w1, sems.at[0]))
+    copies.append(pltpu.make_async_copy(down_ref, w2, sems.at[8]))
+    for copy in copies:
+        copy.start()
+    return copies
+
+
+def fetch_blocks(source, rv, sems, each):
+    copies = []
+    for n, (p, h) in enumerate(PLACES):
+        number = owner_at(p, h, each)[1]
+        copies.append(pltpu.make_async_copy(source.at[number], block_of(rv, p, h), sems.at[n]))
+    for copy in copies:
+        copy.start()
+    return copies
+
+
+def give_back(pv, p, target, send, recv, each):
+    me = owner_at(NP - 1, 0, each)[1]
+    copies = []
+    for h in range(2):
+        n = 2 * p + h
+        if (p, h) == (NP - 1, 0):
+            copy = pltpu.make_async_copy(block_of(pv, p, h), target.at[me], send.at[n])
+        else:
+            copy = pltpu.make_async_remote_copy(
+                src_ref=block_of(pv, p, h),
+                dst_ref=target.at[me],
+                send_sem=send.at[n],
+                recv_sem=recv.at[n],
+                device_id=owner_at(p, h, each)[0],
+                device_id_type=pl.DeviceIdType.MESH,
+            )
+        copy.start()
+        copies.append(copy)
+    return copies
+
+
+def chunk_at(f):
+    return pl.multiple_of(f * FC, FC)
+
+
+def forward_chunk(r, w1, w2, f):
+    at = chunk_at(f)
+    gate = mm(r, w1[:, pl.ds(at, FC)])
+    up = mm(r, w1[:, pl.ds(pl.multiple_of(FF + f * FC, FC), FC)])
+    active = (gate * sigmoid(gate) * up).astype(BF)
+    return gate, up, mm(active, w2[pl.ds(at, FC), :])
+
+
+def backward_chunk(g, gate, up, w1, w2, f):
+    at = chunk_at(f)
+    grad = mm_nt(g, w2[pl.ds(at, FC), :])
+    s = sigmoid(gate)
+    grad_s = grad * s
+    grad_gate = (grad_s * up * (1.0 + gate * (1.0 - s))).astype(BF)
+    grad_up = (grad_s * gate).astype(BF)
+    return mm_nt(grad_gate, w1[:, pl.ds(at, FC)]) + mm_nt(
+        grad_up, w1[:, pl.ds(pl.multiple_of(FF + f * FC, FC), FC)]
+    )
+
+
+def expert_body(split, each, *refs):
+    count = 2 if split else 1
+    gate_ups = refs[:count]
+    down_ref, rec_ref, ret_ref, gate_ref, up_ref = refs[count : count + 5]
+    w1, w2, rv, pv, gv, uv, acc, wsem, rsem, gsem, usem, send, recv = refs[count + 5 :]
+    weights = fetch_weights(split, gate_ups, down_ref, w1, w2, wsem)
+    blocks = fetch_blocks(rec_ref, rv, rsem, each)
+    greet(each)
+    for copy in weights + blocks:
+        copy.wait()
+    stores = []
+    moves = []
+    for p in range(NP):
+        r = rv[p]
         acc[...] = jnp.zeros_like(acc)
 
-    for m in range(SLOTS // MB):
-        at = slice(m * MB, (m + 1) * MB)
-        r = r_ref[at, :]
-        gate = mm(r, wg_ref[...])
-        up = mm(r, wu_ref[...])
-        gate_ref[at, :] = gate.astype(BF)
-        up_ref[at, :] = up.astype(BF)
-        active = (gate * sigmoid(gate) * up).astype(BF)
-        acc[at, :] += mm(active, wd_ref[...])
-
-    @pl.when(step == pl.num_programs(0) - 1)
-    def _():
-        p_ref[...] = acc[...].astype(BF)
-
-
-def expert_forward(received, gate_up, down):
-    steps = FF // FC
-    return call(
-        expert_body,
-        (steps,),
-        [
-            (received, None),
-            (gate_up, (D, FC), lambda j: (0, j)),
-            (gate_up, (D, FC), lambda j: (0, steps + j)),
-            (down, (FC, D), lambda j: (j, 0)),
-        ],
-        [
-            (out((SLOTS, D), BF), None),
-            (out((SLOTS, FF), BF), (SLOTS, FC), lambda j: (0, j)),
-            (out((SLOTS, FF), BF), (SLOTS, FC), lambda j: (0, j)),
-        ],
-        [pltpu.VMEM((SLOTS, D), F32)],
-        name="expert_forward",
-        flops=2 * SLOTS * D * FF * 3,
-        nbytes=26e6,
-    )
-
-
-def expert_grad_body(g_ref, gate_ref, up_ref, wg_ref, wu_ref, wd_ref, o_ref, acc):
-    step = pl.program_id(0)
-
-    @pl.when(step == 0)
-    def _():
+        def step(f, carry):
+            gate, up, part = forward_chunk(r, w1, w2, f)
+            gv[p, :, pl.ds(chunk_at(f), FC)] = gate.astype(BF)
+            uv[p, :, pl.ds(chunk_at(f), FC)] = up.astype(BF)
+            acc[...] += part
+            return carry
+
+        lax.fori_loop(0, FF // FC, step, 0)
+        pv[p] = acc[...].astype(BF)
+        moves += give_back(pv, p, ret_ref, send, recv, each)
+        for values, ref, sems in ((gv, gate_ref, gsem), (uv, up_ref, usem)):
+            copy = pltpu.make_async_copy(values.at[p], ref.at[p], sems.at[p])
+            copy.start()
+            stores.append(copy)
+    for copy in moves + stores:
+        copy.wait()
+
+
+def comm_call(body, ins, outs, scratch, name, number, flops, nbytes):
+    return pl.pallas_call(
+        body,
+        in_specs=[pl.BlockSpec(memory_space=pl.ANY)] * len(ins),
+        out_specs=[pl.BlockSpec(memory_space=pl.ANY)] * len(outs),
+        out_shape=outs,
+        scratch_shapes=scratch,
+        compiler_params=pltpu.CompilerParams(
+            vmem_limit_bytes=VMEM_BYTES, collective_id=number, has_side_effects=True
+        ),
+        cost_estimate=pl.CostEstimate(
+            flops=int(flops), bytes_accessed=int(nbytes), transcendentals=0
+        ),
+        name=name,
+    )(*ins)
+
+
+DMA = pltpu.SemaphoreType.DMA
+WEIGHTS = [pltpu.VMEM((D, 2 * FF), BF), pltpu.VMEM((FF, D), BF)]
+ROWS = pltpu.VMEM((NP, PR, D), BF)
+WIDE = pltpu.VMEM((NP, PR, FF), BF)
+SUM = pltpu.VMEM((PR, D), F32)
+BLOCKS = jax.ShapeDtypeStruct((NFFN, CAP, D), BF)
+KEPT = jax.ShapeDtypeStruct((NP, PR, FF), BF)
+
+
+def expert_forward(received, gate_ups, down, each):
+    split = len(gate_ups) == 2
+
+    def body(*refs):
+        expert_body(split, each, *refs)
+
+    return comm_call(
+        body,
+        [*gate_ups, down, received],
+        [BLOCKS, KEPT, KEPT],
+        WEIGHTS + [ROWS, ROWS, WIDE, WIDE, SUM]
+        + [DMA((9,)), DMA((8,)), DMA((NP,)), DMA((NP,)), DMA((8,)), DMA((8,))],
+        "expert_forward",
+        1,
+        2 * SLOTS * D * FF * 3,
+        26e6,
+    )
+
+
+def expert_both_body(each, gate_up_ref, down_ref, rec_ref, sg_ref, ret_ref, gret_ref, *scratch):
+    w1, w2, rv, sv, pv, qv, acc, gacc, wsem, rsem, ssem, send, recv, gsend, grecv = scratch
+    weights = fetch_weights(False, [gate_up_ref], down_ref, w1, w2, wsem)
+    blocks = fetch_blocks(rec_ref, rv, rsem, each) + fetch_blocks(sg_ref, sv, ssem, each)
+    greet(each)
+    for copy in weights + blocks:
+        copy.wait()
+    moves = []
+    for p in range(NP):
+        r = rv[p]
+        g = sv[p]
         acc[...] = jnp.zeros_like(acc)
-
-    for m in range(SLOTS // MB):
-        at = slice(m * MB, (m + 1) * MB)
-        grad = mm_nt(g_ref[at, :], wd_ref[...])
-        gate = gate_ref[at, :].astype(F32)
-        up = up_ref[at, :].astype(F32)
-        s = sigmoid(gate)
-        grad_s = grad * s
-        grad_gate = (grad_s * up * (1.0 + gate * (1.0 - s))).astype(BF)
-        grad_up = (grad_s * gate).astype(BF)
-        acc[at, :] += mm_nt(grad_gate, wg_ref[...]) + mm_nt(grad_up, wu_ref[...])
-
-    @pl.when(step == pl.num_programs(0) - 1)
-    def _():
-        o_ref[...] = acc[...].astype(BF)
-
-
-def expert_backward(grads, gate, up, gate_up, down):
-    steps = FF // FC
-    return call(
-        expert_grad_body,
-        (steps,),
-        [
-            (grads, None),
-            (gate, (SLOTS, FC), lambda j: (0, j)),
-            (up, (SLOTS, FC), lambda j: (0, j)),
-            (gate_up, (D, FC), lambda j: (0, j)),
-            (gate_up, (D, FC), lambda j: (0, steps + j)),
-            (down, (FC, D), lambda j: (j, 0)),
-        ],
-        [(out((SLOTS, D), BF), None)],
-        [pltpu.VMEM((SLOTS, D), F32)],
-        name="expert_backward",
-        flops=2 * SLOTS * D * FF * 3,
-        nbytes=26e6,
+        gacc[...] = jnp.zeros_like(gacc)
+
+        def step(f, carry):
+            gate, up, part = forward_chunk(r, w1, w2, f)
+            acc[...] += part
+            gacc[...] += backward_chunk(g, gate, up, w1, w2, f)
+            return carry
+
+        lax.fori_loop(0, FF // FC, step, 0)
+        pv[p] = acc[...].astype(BF)
+        qv[p] = gacc[...].astype(BF)
+        moves += give_back(pv, p, ret_ref, send, recv, each)
+        moves += give_back(qv, p, gret_ref, gsend, grecv, each)
+    for copy in moves:
+        copy.wait()
+
+
+def expert_both(received, slot_grads, gate_up, down, each):
+    def body(*refs):
+        expert_both_body(each, *refs)
+
+    return comm_call(
+        body,
+        [gate_up, down, received, slot_grads],
+        [BLOCKS, BLOCKS],
+        WEIGHTS + [ROWS, ROWS, ROWS, ROWS, SUM, SUM]
+        + [DMA((9,)), DMA((8,)), DMA((8,)), DMA((8,)), DMA((8,)), DMA((8,)), DMA((8,))],
+        "expert_both",
+        2,
+        2 * SLOTS * D * FF * 6,
+        26e6,
+    )
+
+
+def expert_back_body(split, each, *refs):
+    count = 2 if split else 1
+    gate_ups = refs[:count]
+    down_ref, sg_ref, gate_ref, up_ref, ret_ref = refs[count : count + 5]
+    w1, w2, rv, pv, gv, uv, acc, wsem, gsem, usem, dsend, drecv, send, recv = refs[count + 5 :]
+    weights = fetch_weights(split, gate_ups, down_ref, w1, w2, wsem)
+    for values, ref, sems in ((gv, gate_ref, gsem), (uv, up_ref, usem)):
+        for p in range(NP):
+            copy = pltpu.make_async_copy(ref.at[p], values.at[p], sems.at[p])
+            copy.start()
+            weights.append(copy)
+    greet(each)
+    arrivals = {}
+    for p in (3, 1, 2, 0):
+        for h in range(2):
+            where, number = owner_at(p, h, each)
+            n = 2 * p + h
+            if (p, h) == (NP - 1, 0):
+                copy = pltpu.make_async_copy(sg_ref.at[number], block_of(rv, p, h), dsend.at[n])
+            else:
+                copy = pltpu.make_async_remote_copy(
+                    src_ref=sg_ref.at[number],
+                    dst_ref=block_of(rv, p, h),
+                    send_sem=dsend.at[n],
+                    recv_sem=drecv.at[n],
+                    device_id=where,
+                    device_id_type=pl.DeviceIdType.MESH,
+                )
+            copy.start()
+            arrivals[p, h] = copy
+    for copy in weights:
+        copy.wait()
+    moves = []
+    for p in (3, 1, 2, 0):
+        for h in range(2):
+            arrivals[p, h].wait()
+        g = rv[p]
+        acc[...] = jnp.zeros_like(acc)
+
+        def step(f, carry):
+            at = pl.ds(chunk_at(f), FC)
+            gate = gv[p, :, at].astype(F32)
+            up = uv[p, :, at].astype(F32)
+            acc[...] += backward_chunk(g, gate, up, w1, w2, f)
+            return carry
+
+        lax.fori_loop(0, FF // FC, step, 0)
+        pv[p] = acc[...].astype(BF)
+        moves += give_back(pv, p, ret_ref, send, recv, each)
+    for copy in moves:
+        copy.wait()
+
+
+def expert_backward(slot_grads, gate, up, gate_ups, down, each):
+    split = len(gate_ups) == 2
+
+    def body(*refs):
+        expert_back_body(split, each, *refs)
+
+    return comm_call(
+        body,
+        [*gate_ups, down, slot_grads, gate, up],
+        [BLOCKS],
+        WEIGHTS + [ROWS, ROWS, WIDE, WIDE, SUM]
+        + [DMA((9,)), DMA((NP,)), DMA((NP,)), DMA((8,)), DMA((8,)), DMA((8,)), DMA((8,))],
+        "expert_backward",
+        3,
+        2 * SLOTS * D * FF * 3,
+        26e6,
     )[0]
 
 
@@ -522,17 +788,9 @@
     )
 
 
-def mix_grad_body(
-    g_ref, mid_ref, c0_ref, c1_ref, lg_ref, rt_ref, gl_ref, gain_ref, cv_ref, wt_ref, res_ref,
-    a_ref, b_ref, gn_ref, gle_ref,
-):
-    g = g_ref[...].astype(F32)
-    mid = mid_ref[...]
-    normed = mid * rms_scale(mid) * gain_ref[...]
-    routes = rt_ref[...]
-    gates, weights, shares = mix_terms(lg_ref[...], routes)
-    a_ref[...] = (gates[0] * g).astype(BF)
-    b_ref[...] = (gates[1] * g).astype(BF)
+def mix_grad(g, mid, chosen, logits, routes, grad, gain, cv_ref, wt, res):
+    normed = mid * rms_scale(mid) * gain
+    gates, weights, shares = mix_terms(logits, routes)
 
     def along(v):
         return jnp.sum(g * v, axis=1, keepdims=True)
@@ -540,34 +798,74 @@
     same = along(normed)
     const = [along(cv_ref[c : c + 1, :]) for c in range(2)]
     gate_grads = []
-    for k, c_ref in enumerate((c0_ref, c1_ref)):
+    for k in range(2):
         r = routes[:, k : k + 1]
-        value = along(c_ref[...].astype(F32)) + jnp.where(r == NFFN + 1, same, 0.0)
+        value = along(chosen[k].astype(F32)) + jnp.where(r == NFFN + 1, same, 0.0)
         for c in range(2):
             mixed = shares[c][0] * same + shares[c][1] * const[c]
             value = value + jnp.where(r == NFFN + 2 + c, mixed, 0.0)
         gate_grads.append(value)
     slope = gates[0] * gates[1] * (gate_grads[0] - gate_grads[1])
     lane = iota((RB, 128), 1)
-    grad = gl_ref[...]
     grad = grad + jnp.where(lane == routes[:, 0:1], slope, 0.0)
     grad = grad - jnp.where(lane == routes[:, 1:2], slope, 0.0)
+    only = grad
     for c in range(2):
         tilt = weights[1 + c] * shares[c][0] * shares[c][1] * (same - const[c])
         grad = grad + jnp.where(lane == 12 + 2 * c, tilt, 0.0)
         grad = grad - jnp.where(lane == 13 + 2 * c, tilt, 0.0)
     keep = weights[0] + weights[1] * shares[0][0] + weights[2] * shares[1][0]
-    gn_ref[...] = mm_exact(grad, wt_ref[...]) + keep * g
-    gle_ref[...] = mm_exact(grad, res_ref[...])
-
-
-def mix_grad(g, mid, c0, c1, logits, routes, gl, gain, const_vec, router_t, residual_t):
+    return mm(spread_lanes(grad), wt) + keep * g, mm(spread_lanes(only), res)
+
+
+def rms_back(grad, v, gain):
+    scale = rms_scale(v)
+    inner = grad * gain
+    return scale * inner - v * (scale**3 * jnp.mean(v * inner, axis=1, keepdims=True))
+
+
+def settle_grad_body(
+    tcol_ref, back_ref, mid_ref, g_ref, c0_ref, c1_ref, lg_ref, rt_ref, gl_ref, gain_ref, cv_ref,
+    wt_ref, res_ref, mixed_ref, nar_ref, w_ref, d_ref, u_ref,
+    gm_ref, gx_ref, gle_ref, gu_ref, gd_ref,
+):
+    @pl.when(pl.program_id(0) == 0)
+    def _():
+        gu_ref[...] = jnp.zeros_like(gu_ref)
+        gd_ref[...] = jnp.zeros_like(gd_ref)
+
+    mid = mid_ref[...]
+    g = g_ref[...].astype(F32)
+    gain = gain_ref[...]
+    grad, gle_ref[...] = mix_grad(
+        g, mid, (c0_ref[...], c1_ref[...]), lg_ref[...], rt_ref[...], gl_ref[...], gain, cv_ref,
+        wt_ref[...], res_ref[...],
+    )
+    place = iota((RB, SLOTS), 1)
+    hit = (tcol_ref[:, 0:1] == place) | (tcol_ref[:, 1:2] == place)
+    grad = grad + mm(hit.astype(F32).astype(BF), back_ref[...])
+    grad_mid = g + rms_back(grad, mid, gain)
+    gm_ref[...] = grad_mid
+    out_grad = grad_mid.astype(BF)
+    grad_narrow = mm_nt(out_grad, u_ref[...]).astype(BF)
+    mixed = mixed_ref[...]
+    gu_ref[...] += 2.0 * mm_tn(nar_ref[...], out_grad)
+    gd_ref[...] += mm_tn(grad_narrow, mixed)
+    gx_ref[...] = (mm_nt(out_grad, w_ref[0]) + mm_nt(grad_narrow, d_ref[...])).astype(BF)
+
+
+def settle_grad(
+    tcol, back, mid, g, c0, c1, logits, routes, gl, gain, const_vec, router_t, residual_t,
+    mixed, narrow, w, down, up,
+):
     return call(
-        mix_grad_body,
+        settle_grad_body,
         (NB,),
         [
+            (tcol, (RB, 128), rows),
+            (back, None),
+            (mid, (RB, D), rows),
             (g, (RB, D), rows),
-            (mid, (RB, D), rows),
             (c0, (RB, D), rows),
             (c1, (RB, D), rows),
             (logits, (RB, 128), rows),
@@ -577,73 +875,22 @@
             (const_vec, None),
             (router_t, None),
             (residual_t, None),
-        ],
-        [
-            (out((T, D), BF), (RB, D), rows),
-            (out((T, D), BF), (RB, D), rows),
-            (out((T, D), F32), (RB, D), rows),
-            (out((T, 128), F32), (RB, 128), rows),
-        ],
-        name="mix_grad",
-        flops=2 * T * 128 * D * 6,
-        nbytes=16e6,
-    )
-
-
-def rms_back(grad, v, gain):
-    scale = rms_scale(v)
-    inner = grad * gain
-    return scale * inner - v * (scale**3 * jnp.mean(v * inner, axis=1, keepdims=True))
-
-
-def settle_grad_body(
-    tcol_ref, back_ref, gn_ref, mid_ref, g_ref, gain_ref, mixed_ref, nar_ref, w_ref, d_ref, u_ref,
-    gm_ref, gx_ref, gu_ref, gd_ref,
-):
-    @pl.when(pl.program_id(0) == 0)
-    def _():
-        gu_ref[...] = jnp.zeros_like(gu_ref)
-        gd_ref[...] = jnp.zeros_like(gd_ref)
-
-    place = iota((RB, SLOTS), 1)
-    hit = (tcol_ref[:, 0:1] == place) | (tcol_ref[:, 1:2] == place)
-    grad = gn_ref[...] + mm(hit.astype(F32).astype(BF), back_ref[...])
-    grad_mid = g_ref[...].astype(F32) + rms_back(grad, mid_ref[...], gain_ref[...])
-    gm_ref[...] = grad_mid
-    out_grad = grad_mid.astype(BF)
-    grad_narrow = mm_nt(out_grad, u_ref[...]).astype(BF)
-    mixed = mixed_ref[...]
-    gu_ref[...] += 2.0 * mm_tn(nar_ref[...], out_grad)
-    gd_ref[...] += mm_tn(grad_narrow, mixed)
-    gx_ref[...] = (mm_nt(out_grad, w_ref[...]) + mm_nt(grad_narrow, d_ref[...])).astype(BF)
-
-
-def settle_grad(tcol, back, gn, mid, g, gain, mixed, narrow, w, down, up):
-    return call(
-        settle_grad_body,
-        (NB,),
-        [
-            (tcol, (RB, 128), rows),
-            (back, None),
-            (gn, (RB, D), rows),
-            (mid, (RB, D), rows),
-            (g, (RB, D), rows),
-            (gain, None),
             (mixed, (RB, D), rows),
             (narrow, (RB, 128), rows),
-            (w, None),
+            (w, (1, D, D), lambda i: (3, 0, 0)),
             (down, None),
             (up, None),
         ],
         [
             (out((T, D), F32), (RB, D), rows),
             (out((T, D), BF), (RB, D), rows),
+            (out((T, 128), F32), (RB, 128), rows),
             (out((128, D), F32), None),
             (out((128, D), F32), None),
         ],
         name="settle_grad",
         flops=2 * T * SLOTS * D + 2 * T * D * D * 2,
-        nbytes=16e6,
+        nbytes=22e6,
     )
 
 
@@ -740,7 +987,7 @@
     for block, ref in enumerate((gq_ref, gk_ref, gv_ref)):
         cols = slice(block * D, (block + 1) * D)
         g = ref[...]
-        grad = grad + mm_nt(g, w_ref[:, cols])
+        grad = grad + mm_nt(g, w_ref[block])
         slim = slim + mm_nt(g, u_ref[:, cols])
         gu_ref[:, cols] += 2.0 * mm_tn(narrow, g)
     slim = slim.astype(BF)
@@ -757,7 +1004,7 @@
             (gq, (RB, D), rows),
             (gk, (RB, D), rows),
             (gv, (RB, D), rows),
-            (w, None),
+            (w, (3, D, D), lambda i: (0, 0, 0)),
             (down, None),
             (up, None),
             (normed, (RB, D), rows),
@@ -777,34 +1024,124 @@
     )
 
 
-def swap_pairs(axis):
-    return [(0, 1), (1, 0)]
-
-
-def gather_shared(w):
-    half = w.shape[1] // 2
-    core = lax.axis_index("c")
-    mine = lax.dynamic_slice_in_dim(w, core * half, half, axis=1)
-    mine = lax.all_gather(mine, ("z", "y"), axis=0, tiled=True)
-    other = lax.ppermute(mine, "c", swap_pairs("c"))
-    first = jnp.where(core == 0, mine, other)
-    second = jnp.where(core == 0, other, mine)
-    return jnp.concatenate([first, second], axis=1)
-
-
-def gather_expert(w):
+PIECE = 96
+
+
+def shared_body(p_ref, o_ref, local, zs, zr, ys, yr, xs, xr, cs, cr):
+    x, c, z, y = (lax.axis_index(name) for name in ("x", "c", "z", "y"))
+    mine, theirs = 2 * x + c, 2 * (1 - x) + c
+
+    def spot(quarter, column, j):
+        at = (2 * ((z + 4 - j) % 4) + column) * PIECE
+        return o_ref.at[quarter, pl.ds(pl.multiple_of(at, PIECE), PIECE), :]
+
+    others = [{"z": (z + d) % 4} for d in range(1, 4)]
+    others += [{"y": 1 - y}, {"x": 1 - x}, {"c": 1 - c}]
+    barrier = pltpu.get_barrier_semaphore()
+    for who in others:
+        pl.semaphore_signal(barrier, inc=1, device_id=who, device_id_type=pl.DeviceIdType.MESH)
+    pl.semaphore_wait(barrier, len(others))
+
+    started = []
+
+    def send(source, target, who, send_sem, recv_sem):
+        copy = pltpu.make_async_remote_copy(
+            src_ref=source,
+            dst_ref=target,
+            send_sem=send_sem,
+            recv_sem=recv_sem,
+            device_id=who,
+            device_id_type=pl.DeviceIdType.MESH,
+        )
+        copy.start()
+        started.append(copy)
+        return copy
+
+    core_copies = []
+
+    def to_core(source, target):
+        n = len(core_copies)
+        core_copies.append(send(source, target, others[5], cs.at[n], cr.at[n]))
+
+    own = pltpu.make_async_copy(p_ref, spot(mine, y, 0), local.at[0])
+    own.start()
+    z_copies = [
+        send(p_ref, spot(mine, y, 0), others[d], zs.at[d], zr.at[d]) for d in range(3)
+    ]
+    y_copies = [None] * 6
+    x_copies = [None] * 6
+
+    def along_y(n, source, target):
+        y_copies[n] = send(source, target, others[3], ys.at[n], yr.at[n])
+
+    def along_x(n, source, target):
+        x_copies[n] = send(source, target, others[4], xs.at[n], xr.at[n])
+
+    along_y(0, p_ref, spot(mine, y, 0))
+    along_x(0, p_ref, spot(mine, y, 0))
+    to_core(p_ref, spot(mine, y, 0))
+    for j in range(1, 4):
+        z_copies[j - 1].wait_recv()
+        piece = spot(mine, y, j)
+        along_y(j, piece, piece)
+        along_x(j, piece, piece)
+        to_core(piece, piece)
+    for j in range(4):
+        y_copies[j].wait_recv()
+        piece = spot(mine, 1 - y, j)
+        if j < 2:
+            along_x(4 + j, piece, piece)
+        to_core(piece, piece)
+        x_copies[j].wait_recv()
+        piece = spot(theirs, y, j)
+        if j >= 2:
+            along_y(2 + j, piece, piece)
+        to_core(piece, piece)
+    for j in range(4):
+        (x_copies[4 + j] if j < 2 else y_copies[2 + j]).wait_recv()
+        piece = spot(theirs, 1 - y, j)
+        to_core(piece, piece)
+    for copy in core_copies:
+        copy.wait_recv()
+    own.wait()
+    for copy in started:
+        copy.wait_send()
+
+
+def gather_shared(qkv, output):
+    rows_here = qkv.shape[0]
+    parts = jnp.concatenate([qkv.reshape(rows_here, 3, D).transpose(1, 0, 2), output[None]])
+    sizes = tuple(lax.axis_size(name) for name in ("x", "c", "z", "y"))
+    if sizes != (2, 2, 4, 2):
+        whole = lax.all_gather(parts, ("z", "y"), axis=1, tiled=True)
+        return whole
+    quarter = 2 * lax.axis_index("x") + lax.axis_index("c")
+    piece = lax.dynamic_index_in_dim(parts, quarter, axis=0, keepdims=False)
+    return comm_call(
+        shared_body,
+        [piece],
+        [jax.ShapeDtypeStruct((4, D, D), BF)],
+        [DMA((1,)), DMA((3,)), DMA((3,)), DMA((6,)), DMA((6,)), DMA((6,)), DMA((6,)), DMA((16,)), DMA((16,))],
+        "gather_shared",
+        0,
+        0,
+        5e7,
+    )[0]
+
+
+def gather_expert(w, split):
     count = w.shape[0]
     if count == 2:
         y = lax.axis_index("y")
         mine = lax.dynamic_index_in_dim(w, y, axis=0, keepdims=False)
         other = lax.ppermute(
-            lax.dynamic_index_in_dim(w, 1 - y, axis=0, keepdims=False), "y", swap_pairs("y")
+            lax.dynamic_index_in_dim(w, 1 - y, axis=0, keepdims=False), "y", [(0, 1), (1, 0)]
         )
+        if split:
+            return [lax.all_gather(part, "z", axis=0) for part in (mine, other)]
         w = jnp.where(y == 0, jnp.stack([mine, other]), jnp.stack([other, mine]))
-    elif count > 2:
-        w = lax.all_to_all(w, "y", 0, 0, tiled=True)
     w = lax.all_gather(w, "z", axis=0, tiled=True)
-    return w.reshape(-1, w.shape[-1])
+    return [w.reshape(-1, w.shape[-1])]
 
 
 def exchange(v):
@@ -834,15 +1171,13 @@
     w_down,
     out_grad,
 ):
-    qkv_full = []
-    out_full = []
+    each = w_gate_up.shape[1]
     gate_up_full = []
     down_full = []
     for layer in range(LAYERS):
-        qkv_full.append(gather_shared(query_key_value_weight[layer]))
-        out_full.append(gather_shared(output_weight[layer]))
-        gate_up_full.append(gather_expert(w_gate_up[layer]))
-        down_full.append(gather_expert(w_down[layer]))
+        gate_up_full.append(gather_expert(w_gate_up[layer], layer == 0))
+        down_full.append(gather_expert(w_down[layer], False)[0])
+    shared = [gather_shared(query_key_value_weight[0], output_weight[0])]
 
     which = adapter_of[0]
     down_sel = lax.dynamic_index_in_dim(adapter_down, which, axis=2, keepdims=False)
@@ -858,11 +1193,13 @@
     up_out = jnp.pad(up_t[:, 3], ((0, 0), (0, 112), (0, 0)))
     rcat = jnp.concatenate([router, const_proj[:, 0], const_proj[:, 1]], axis=2)
     rcat = jnp.pad(rcat, ((0, 0), (0, 0), (0, 112)))
-    rcat_t = rcat.transpose(0, 2, 1)
-    residual = pad_to(router_residual, (128, 128))
-    residual_t = residual.T
-
-    qf, kf, cos, sin, tcol, trow = prep(parents, segments.reshape(T, 1), routes)
+    rcat_t = rcat[:, :, :16].transpose(0, 2, 1)
+    residual = pad_to(router_residual, (16, 128))
+    residual_t = pad_to(router_residual.T, (16, 128))
+
+    qf, kf, cos, sin, tcol, trow, router_s, router_ts, residual_s, residual_ts = prep(
+        parents, segments.reshape(T, 1), routes, rcat, rcat_t, residual, residual_t
+    )
 
     stream = tokens
     earlier = jnp.zeros((T, 128), F32)
@@ -871,18 +1208,29 @@
         gain0 = norm_gain[layer, 0:1]
         gain1 = norm_gain[layer, 1:2]
         normed, narrow, qkv = project(
-            stream, gain0, qkv_full[layer], down_in[layer], up_in[layer], cos, sin
+            stream, gain0, shared[layer], down_in[layer], up_in[layer], cos, sin
         )
         mixed, aug = attend(qkv, qf, kf)
         mid, sent, logits, narrow_out = settle(
-            stream, mixed, out_full[layer], down_out[layer], up_out[layer], gain1, rcat[layer],
-            earlier, residual,
+            stream, mixed, shared[layer], down_out[layer], up_out[layer], gain1, router_s[layer],
+            earlier, residual_s,
         )
-        received = exchange(dispatch(trow, sent)).reshape(SLOTS, D)
-        produced, gate, up = expert_forward(received, gate_up_full[layer], down_full[layer])
-        returned = exchange(produced.reshape(NFFN, CAP, D)).reshape(SLOTS, D)
-        following, c0, c1 = combine(tcol, returned, mid, logits, routes, gain1, const_vec[layer])
-        saved.append((stream, normed, narrow, qkv, mixed, aug, mid, logits, narrow_out, gate, up, c0, c1))
+        received = exchange(dispatch(trow, sent))
+        if layer == 0:
+            later = lax.optimization_barrier(
+                (query_key_value_weight[1], output_weight[1], logits)
+            )
+            shared.append(gather_shared(later[0], later[1]))
+            returned, gate, up = expert_forward(received, gate_up_full[0], down_full[0], each)
+        else:
+            slot_grads = exchange(dispatch_grad(trow, out_grad, logits, routes))
+            returned, back = expert_both(
+                received, slot_grads, gate_up_full[1][0], down_full[1], each
+            )
+        following, c0, c1 = combine(
+            tcol, returned.reshape(SLOTS, D), mid, logits, routes, gain1, const_vec[layer]
+        )
+        saved.append((stream, normed, narrow, qkv, mixed, aug, mid, logits, narrow_out, c0, c1))
         stream = following
         earlier = logits
 
@@ -890,23 +1238,22 @@
     grad_logits = jnp.zeros((T, 128), F32)
     tree_grads = [None] * LAYERS
     for layer in reversed(range(LAYERS)):
-        x_in, normed, narrow, qkv, mixed, aug, mid, logits, narrow_out, gate, up, c0, c1 = saved[layer]
+        x_in, normed, narrow, qkv, mixed, aug, mid, logits, narrow_out, c0, c1 = saved[layer]
         gain0 = norm_gain[layer, 0:1]
         gain1 = norm_gain[layer, 1:2]
-        a, b, grad_normed, grad_earlier = mix_grad(
-            grad, mid, c0, c1, logits, routes, grad_logits, gain1, const_vec[layer], rcat_t[layer],
-            residual_t,
-        )
-        slot_grads = exchange(dispatch_grad(trow, a, b)).reshape(SLOTS, D)
-        grad_rows = expert_backward(slot_grads, gate, up, gate_up_full[layer], down_full[layer])
-        back = exchange(grad_rows.reshape(NFFN, CAP, D)).reshape(SLOTS, D)
-        grad_mid, grad_mixed, gu_out, gd_out = settle_grad(
-            tcol, back, grad_normed, mid, grad, gain1, mixed, narrow_out, out_full[layer],
+        if layer == 0:
+            back = expert_backward(
+                dispatch_grad(trow, grad, logits, routes), gate, up, gate_up_full[0], down_full[0],
+                each,
+            )
+        grad_mid, grad_mixed, grad_earlier, gu_out, gd_out = settle_grad(
+            tcol, back.reshape(SLOTS, D), mid, grad, c0, c1, logits, routes, grad_logits, gain1,
+            const_vec[layer], router_ts[layer], residual_ts, mixed, narrow_out, shared[layer],
             down_out[layer], up_out[layer],
         )
         gq, gk, gv = attend_grad(qkv, aug, kf, grad_mixed, mixed, cos, sin)
         grad, gu_in, gd_in = project_grad(
-            gq, gk, gv, qkv_full[layer], down_in[layer], up_in[layer], normed, narrow, x_in, gain0,
+            gq, gk, gv, shared[layer], down_in[layer], up_in[layer], normed, narrow, x_in, gain0,
             grad_mid,
         )
         grad_logits = grad_earlier

time: 961 us -> 753 us (0.78)
  blocking collectives: 205 us -> 22.1 us
  Pallas kernels: 392 us -> 545 us
  waiting for transfers between devices: 207 us -> 84.4 us
  starting transfers between devices: 53.2 us -> 23.4 us
    pallas_call x0 -> x5, Pallas kernels: none -> 250 us  [comm_call(): pl.pallas_call(body, in_specs=[pl.BlockSpec(memory_space=pl.ANY)] * len(i...]
    all_gather x4 -> x3, waiting for transfers between devices: 118 us -> 13.8 us  [gather_expert(): w = lax.all_gather(w, 'z', axis=0, tiled=True)]
    all_to_all x3 -> x0, blocking collectives: 99.6 us -> none  [exchange(): lax.all_to_all(v, ('x', 'c', 'y'), split_axis=0, concat_axis=0, tiled=True)]
    pallas_call x25 -> x19, Pallas kernels: 392 us -> 294 us  [call(): pl.pallas_call(body, grid=grid, in_specs=[spec(e) for e in ins], out_spec...]
    all_gather x2 -> x0, blocking collectives: 83.1 us -> none  [gather_shared(): mine = lax.all_gather(mine, ('z', 'y'), axis=0, tiled=True)]
    ppermute x4 -> x0, starting transfers between devices: 16.8 us -> none  [gather_shared(): other = lax.ppermute(mine, 'c', swap_pairs('c'))]
    another operation x32, local copies, waits for them, and re-layouts: 15.3 us -> 1.73 us  [per_device(): tree_grads[layer] = jnp.stack([jnp.stack(downs), jnp.stack(ups)])]
    all_to_all x5 -> x3, starting transfers between devices: 24.1 us -> 12.5 us  [exchange(): lax.all_to_all(v, ('x', 'c', 'y'), split_axis=0, concat_axis=0, tiled=True)]
  transfers between devices with their start and end apart: 20 -> 13, of which waited for: 8 -> 5; matrix products, arithmetic and copies ran while one was open for 6% -> 5% of each run, Pallas kernels for 15% -> 33%
where the time goes in v2:
time: 753 us; the launch traced here: 746 us
  Pallas kernels  545 us (72%)
  waiting for transfers between devices  84.4 us (11%)
  local copies, waits for them, and re-layouts  41.6 us (6%)
  starting transfers between devices  23.4 us (3%)
  blocking collectives  22.1 us (3%)
  between operations  15.3 us (2%)
  other arithmetic  14.1 us (2%)
    pallas_call x19, Pallas kernels, call(): pl.pallas_call(body, grid=grid, in_specs=[spec(e) for e in ins], out_spec...  294 us
    pallas_call x5, Pallas kernels, comm_call(): pl.pallas_call(body, in_specs=[pl.BlockSpec(memory_space=pl.ANY)] * len(i...  250 us
    all_to_all x3, waiting for transfers between devices, exchange(): lax.all_to_all(v, ('x', 'c', 'y'), split_axis=0, concat_axis=0, tiled=True)  45.2 us
    ppermute x4, waiting for transfers between devices, gather_expert(): lax.ppermute(lax.dynamic_index_in_dim(w, 1 - y, axis=0, keepdims=False),...  25.3 us
  transfers between devices with their start and end apart: 13, of which 5 were waited for; matrix products, arithmetic and copies ran while one was open for 5% of the time, Pallas kernels for 33%

profile of v2, /device:TPU:9, one launch (start us, length us, event | category | flops | bytes accessed | tf_op | source)
XLA Modules:
  0.0 745.8 jit_solution(42128061583453357)
XLA Ops:
  24.6 16.6 %collective-permute-done.2 = bf16[96,4096]{1,0:T(8,128)(2,1)S(1)} collective-permute-done((bf16[96,4096]{1,0:T(8,128)(2,1)}, bf16[96,4096]{1,0:T(8,128)(2,1)S(1)}, u32[]{:S(2)}, u32[]{:S(2)}) %collective-permute-start.2) | collective-permute-done | bytes 786464 | tf_op jit(solution)/shard_map/ppermute | solution.py:1137
  62.8 39.2 %gather_shared.2.w_ref = bf16[4,768,768]{2,1,0:T(8,128)(2,1)} custom-call(bf16[96,768]{1,0:T(8,128)(2,1)} %bitcast.130), custom_call_target="tpu_custom_call" | custom-call | bytes 50000000 | tf_op jit(solution)/shard_map/gather_shared/pallas_call | solution.py:561
  113.6 11.1 %project.2 = (bf16[1024,768]{1,0:T(8,128)(2,1)}, bf16[1024,128]{1,0:T(8,128)(2,1)}, bf16[1024,2304]{1,0:T(8,128)(2,1)}) custom-call(bf16[1024,768]{1,0:T(8,128)(2,1)} %x_ref.5, f32[1,768]{1,0:T(1,128)} %get-tuple-element.226.g_ref.gain_ref, bf16[4,768,768]{2,1,0:T(8,128)(2,1)} %gather_shared.2.w_ref, bf16[768,128]{1,0:T(8,128)(2,1)} %get-tuple-element.205.d_ref, ...), custom_call_target="tpu_custom_call" | custom-call | flops 3623878656 | bytes 12000000 | tf_op jit(solution)/shard_map/project/pallas_call | solution.py:71
  124.6 21.3 %attend.2 = (bf16[1024,768]{1,0:T(8,128)(2,1)}, bf16[6,1024,128]{2,1,0:T(8,128)(2,1)}) custom-call(bf16[1024,2304]{1,0:T(8,128)(2,1)} %get-tuple-element.106.q_ref.k_ref.v_ref, bf16[1024,2304]{1,0:T(8,128)(2,1)} %get-tuple-element.106.q_ref.k_ref.v_ref, bf16[1024,2304]{1,0:T(8,128)(2,1)} %get-tuple-element.106.q_ref.k_ref.v_ref, ...), custom_call_target="tpu_custom_call" | custom-call | flops 6442450944 | bytes 8000000 | tf_op jit(solution)/shard_map/attend/pallas_call | solution.py:71
  173.0 47.4 %gather_shared.3.w_ref = bf16[4,768,768]{2,1,0:T(8,128)(2,1)} custom-call(bf16[96,768]{1,0:T(8,128)(2,1)} %bitcast.131), custom_call_target="tpu_custom_call" | custom-call | bytes 50000000 | tf_op jit(solution)/shard_map/gather_shared/pallas_call | solution.py:561
  222.4 37.7 %expert_forward.1 = (bf16[8,192,768]{2,1,0:T(8,128)(2,1)}, bf16[4,384,2048]{2,1,0:T(8,128)(2,1)}, bf16[4,384,2048]{2,1,0:T(8,128)(2,1)}) custom-call(bf16[4,96,4096]{2,1,0:T(8,128)(2,1)} %bitcast.139, bf16[4,96,4096]{2,1,0:T(8,128)(2,1)} %bitcast.143, bf16[2048,768]{1,0:T(8,128)(2,1)} %bitcast.141, bf16[8,192,768]{2,1,0:T(8,128)(2,1)} %copy-done), custom_call_target="tpu_custom_call" | custom-call | flops 14495514624 | bytes 26000000 | tf_op jit(solution)/shard_map/expert_forward/pallas_call | solution.py:561
  260.1 10.1 %combine.2 = (f32[1024,768]{1,0:T(8,128)}, bf16[1024,768]{1,0:T(8,128)(2,1)}, bf16[1024,768]{1,0:T(8,128)(2,1)}) custom-call(s32[1024,128]{1,0:T(8,128)} %get-tuple-element.102.tcol_ref, bf16[1536,768]{1,0:T(8,128)(2,1)} %bitcast.147, f32[1024,768]{1,0:T(8,128)} %get-tuple-element.114.mid_ref, f32[1024,128]{1,0:T(8,128)} %get-tuple-element.115.lg_ref.earlier_ref, ...), custom_call_target="tpu_custom_call" | custom-call | flops 4831838208 | bytes 12000000 | tf_op jit(solution)/shard_map/combine/pallas_call | solution.py:71
  270.2 11.1 %project.3 = (bf16[1024,768]{1,0:T(8,128)(2,1)}, bf16[1024,128]{1,0:T(8,128)(2,1)}, bf16[1024,2304]{1,0:T(8,128)(2,1)}) custom-call(f32[1024,768]{1,0:T(8,128)} %get-tuple-element.116.x_ref, f32[1,768]{1,0:T(1,128)} %get-tuple-element.227.g_ref.gain_ref, bf16[4,768,768]{2,1,0:T(8,128)(2,1)} %gather_shared.3.w_ref, ...), custom_call_target="tpu_custom_call" | custom-call | flops 3623878656 | bytes 12000000 | tf_op jit(solution)/shard_map/project/pallas_call | solution.py:71
  281.4 21.8 %attend.3 = (bf16[1024,768]{1,0:T(8,128)(2,1)}, bf16[6,1024,128]{2,1,0:T(8,128)(2,1)}) custom-call(bf16[1024,2304]{1,0:T(8,128)(2,1)} %get-tuple-element.119.q_ref.k_ref.v_ref, bf16[1024,2304]{1,0:T(8,128)(2,1)} %get-tuple-element.119.q_ref.k_ref.v_ref, bf16[1024,2304]{1,0:T(8,128)(2,1)} %get-tuple-element.119.q_ref.k_ref.v_ref, ...), custom_call_target="tpu_custom_call" | custom-call | flops 6442450944 | bytes 8000000 | tf_op jit(solution)/shard_map/attend/pallas_call | solution.py:71
  322.7 10.3 %dispatch_grad.2 = bf16[8,192,768]{2,1,0:T(8,128)(2,1)} custom-call(s32[8,1024]{1,0:T(8,128)} %get-tuple-element.103.trow_ref, bf16[1024,768]{1,0:T(8,128)(2,1)} %g_ref.3, f32[1024,128]{1,0:T(8,128)} %get-tuple-element.122.lg_ref, s32[1024,2]{1,0:T(8,128)} %copy.119.rt_ref), custom_call_target="tpu_custom_call" | custom-call | flops 4831838208 | bytes 6000000 | tf_op jit(solution)/shard_map/dispatch_grad/pallas_call | solution.py:71
  333.1 17.9 %all-to-all-done.1.refs_2_ = bf16[8,192,768]{2,1,0:T(8,128)(2,1)S(1)} async-done(((bf16[8,192,768]{2,1,0:T(8,128)(2,1)}), bf16[8,192,768]{2,1,0:T(8,128)(2,1)S(1)}, u32[]{:S(2)}, u32[]{:S(2)}) %all-to-all-start.1) | async-done | bytes 2359328 | tf_op jit(solution)/shard_map/all_to_all | solution.py:1148
  358.0 27.4 %all-to-all-done.2.refs_3_ = bf16[8,192,768]{2,1,0:T(8,128)(2,1)} async-done(((bf16[8,192,768]{2,1,0:T(8,128)(2,1)}), bf16[8,192,768]{2,1,0:T(8,128)(2,1)}, u32[]{:S(2)}, u32[]{:S(2)}) %all-to-all-start.2) | async-done | bytes 2359328 | tf_op jit(solution)/shard_map/all_to_all | solution.py:1148
  385.4 13.7 %all-gather.8.cloned.1.call-done = bf16[8,96,4096]{2,1,0:T(8,128)(2,1)} async-done(((bf16[2,96,4096]{2,1,0:T(8,128)(2,1)}), bf16[8,96,4096]{2,1,0:T(8,128)(2,1)}) %all-gather.8.cloned.1.call-update) | async-done | bytes 6291472 | tf_op jit(solution)/shard_map/all_gather | solution.py:1143
  399.1 69.5 %expert_both.1 = (bf16[8,192,768]{2,1,0:T(8,128)(2,1)}, bf16[8,192,768]{2,1,0:T(8,128)(2,1)}) custom-call(bf16[768,4096]{1,0:T(8,128)(2,1)} %bitcast.138, bf16[2048,768]{1,0:T(8,128)(2,1)} %bitcast.145, bf16[8,192,768]{2,1,0:T(8,128)(2,1)} %copy-done.1, bf16[8,192,768]{2,1,0:T(8,128)(2,1)} %all-to-all-done.2.refs_3_), custom_call_target="tpu_custom_call" | custom-call | flops 28991029248 | bytes 26000000 | tf_op jit(solution)/shard_map/expert_both/pallas_call | solution.py:561
  478.8 25.7 %settle_grad.2 = (f32[1024,768]{1,0:T(8,128)}, bf16[1024,768]{1,0:T(8,128)(2,1)}, f32[1024,128]{1,0:T(8,128)}, f32[128,768]{1,0:T(8,128)}, f32[128,768]{1,0:T(8,128)}) custom-call(s32[1024,128]{1,0:T(8,128)} %get-tuple-element.102.tcol_ref, bf16[1536,768]{1,0:T(8,128)(2,1)} %bitcast.126, f32[1024,768]{1,0:T(8,128)} %get-tuple-element.124.mid_ref, ...), custom_call_target="tpu_custom_call" | custom-call | flops 4831838208 | bytes 22000000 | tf_op jit(solution)/shard_map/settle_grad/pallas_call | solution.py:71
  504.6 35.8 %attend_grad.2 = (bf16[1024,768]{1,0:T(8,128)(2,1)}, bf16[1024,768]{1,0:T(8,128)(2,1)}, bf16[1024,768]{1,0:T(8,128)(2,1)}) custom-call(bf16[1024,2304]{1,0:T(8,128)(2,1)} %get-tuple-element.119.q_ref.k_ref.v_ref, bf16[1024,2304]{1,0:T(8,128)(2,1)} %get-tuple-element.119.q_ref.k_ref.v_ref, bf16[1024,2304]{1,0:T(8,128)(2,1)} %get-tuple-element.119.q_ref.k_ref.v_ref, ...), custom_call_target="tpu_custom_call" | custom-call | flops 16106127360 | bytes 14000000 | tf_op jit(solution)/shard_map/attend_grad/pallas_call | solution.py:71
  540.3 13.5 %project_grad.2 = (f32[1024,768]{1,0:T(8,128)}, f32[128,2304]{1,0:T(8,128)}, f32[128,768]{1,0:T(8,128)}) custom-call(bf16[1024,768]{1,0:T(8,128)(2,1)} %get-tuple-element.135.gq_ref, bf16[1024,768]{1,0:T(8,128)(2,1)} %get-tuple-element.136.gk_ref, bf16[1024,768]{1,0:T(8,128)(2,1)} %get-tuple-element.137.gv_ref, bf16[4,768,768]{2,1,0:T(8,128)(2,1)} %gather_shared.3.w_ref, ...), custom_call_target="tpu_custom_call" | custom-call | flops 4711042048 | bytes 22000000 | tf_op jit(solution)/shard_map/project_grad/pallas_call | solution.py:71
  557.6 11.0 %dispatch_grad.3.refs_3_ = bf16[8,192,768]{2,1,0:T(8,128)(2,1)} custom-call(s32[8,1024]{1,0:T(8,128)} %get-tuple-element.103.trow_ref, f32[1024,768]{1,0:T(8,128)} %get-tuple-element.141.g_ref, f32[1024,128]{1,0:T(8,128)} %get-tuple-element.115.lg_ref.earlier_ref, s32[1024,2]{1,0:T(8,128)} %copy.119.rt_ref), custom_call_target="tpu_custom_call" | custom-call | flops 4831838208 | bytes 6000000 | tf_op jit(solution)/shard_map/dispatch_grad/pallas_call | solution.py:71
  568.6 56.5 %expert_backward.1 = bf16[8,192,768]{2,1,0:T(8,128)(2,1)} custom-call(bf16[4,96,4096]{2,1,0:T(8,128)(2,1)} %bitcast.140, bf16[4,96,4096]{2,1,0:T(8,128)(2,1)} %bitcast.144, bf16[2048,768]{1,0:T(8,128)(2,1)} %bitcast.142, bf16[8,192,768]{2,1,0:T(8,128)(2,1)} %dispatch_grad.3.refs_3_, bf16[4,384,2048]{2,1,0:T(8,128)(2,1)} %get-tuple-element.142.refs_4_, ...), custom_call_target="tpu_custom_call" | custom-call | flops 14495514624 | bytes 26000000 | tf_op jit(solution)/shard_map/expert_backward/pallas_call | solution.py:561
  625.1 25.6 %settle_grad.3 = (f32[1024,768]{1,0:T(8,128)}, bf16[1024,768]{1,0:T(8,128)(2,1)}, f32[1024,128]{1,0:T(8,128)}, f32[128,768]{1,0:T(8,128)}, f32[128,768]{1,0:T(8,128)}) custom-call(s32[1024,128]{1,0:T(8,128)} %get-tuple-element.102.tcol_ref, bf16[1536,768]{1,0:T(8,128)(2,1)} %bitcast.125, f32[1024,768]{1,0:T(8,128)} %get-tuple-element.114.mid_ref, ...), custom_call_target="tpu_custom_call" | custom-call | flops 4831838208 | bytes 22000000 | tf_op jit(solution)/shard_map/settle_grad/pallas_call | solution.py:71
  652.5 36.0 %attend_grad.3 = (bf16[1024,768]{1,0:T(8,128)(2,1)}, bf16[1024,768]{1,0:T(8,128)(2,1)}, bf16[1024,768]{1,0:T(8,128)(2,1)}) custom-call(bf16[1024,2304]{1,0:T(8,128)(2,1)} %get-tuple-element.106.q_ref.k_ref.v_ref, bf16[1024,2304]{1,0:T(8,128)(2,1)} %get-tuple-element.106.q_ref.k_ref.v_ref, bf16[1024,2304]{1,0:T(8,128)(2,1)} %get-tuple-element.106.q_ref.k_ref.v_ref, ...), custom_call_target="tpu_custom_call" | custom-call | flops 16106127360 | bytes 14000000 | tf_op jit(solution)/shard_map/attend_grad/pallas_call | solution.py:71
  688.5 13.3 %project_grad.3 = (f32[1024,768]{1,0:T(8,128)}, f32[128,2304]{1,0:T(8,128)}, f32[128,768]{1,0:T(8,128)}) custom-call(bf16[1024,768]{1,0:T(8,128)(2,1)} %get-tuple-element.149.gq_ref, bf16[1024,768]{1,0:T(8,128)(2,1)} %get-tuple-element.150.gk_ref, bf16[1024,768]{1,0:T(8,128)(2,1)} %get-tuple-element.151.gv_ref, bf16[4,768,768]{2,1,0:T(8,128)(2,1)} %gather_shared.2.w_ref, ...), custom_call_target="tpu_custom_call" | custom-call | flops 4711042048 | bytes 22000000 | tf_op jit(solution)/shard_map/project_grad/pallas_call | solution.py:71
  713.9 10.4 %all-reduce.7 = s32[8]{0:T(128)S(1)} all-reduce(s32[8]{0:T(128)S(1)} %dynamic-update-slice.9), channel_id=1, replica_groups=mesh['x'=2,'c'=2,'z'=4,'y'=2] {'z','y'}, use_global_device_ids=true, to_apply=%add.7 | all-reduce | flops 8 | bytes 64
  725.5 11.7 %all_to_all.25 = bf16[4,2,24576]{2,1,0:T(2,128)(2,1)S(1)} all-to-all(bf16[4,2,24576]{2,1,0:T(2,128)(2,1)S(1)} %reshape.249), channel_id=1, replica_groups=mesh['x'=2,'c'=2,'z'=4,'y'=2] {'x','c'}, dimensions={0} | all-to-all | bytes 786432 | tf_op jit(solution)/shard_map/all_to_all | solution.py:1276
  (176 shorter events, 136.0 us)
Async XLA Ops:
  7.2 213.8 %all-gather.14.cloned.1.call-start = ((), (), s32[]{:S(2)}) async-start(), calls=%async_computation.8 | async-start | bytes 3932160 | tf_op jit(solution)/shard_map/all_gather | solution.py:1141
  10.6 210.4 %all-gather.12.cloned.1.call-start = ((), (), s32[]{:S(2)}) async-start(), calls=%async_computation.7 | async-start | bytes 3932160 | tf_op jit(solution)/shard_map/all_gather | solution.py:1143
  12.2 10.0 %collective-permute-start.3 = (bf16[256,768]{1,0:T(8,128)(2,1)S(1)}, bf16[256,768]{1,0:T(8,128)(2,1)S(1)}, u32[]{:S(2)}, u32[]{:S(2)}) collective-permute-start(bf16[256,768]{1,0:T(8,128)(2,1)S(1)} %get-tuple-element.189), channel_id=1, source_target_pairs={{0,1},{1,0},{2,3},{3,2},{4,5},{5,4},{6,7},{7,6},{8,9},{9,8},{10,11... | collective-permute-start | bytes 1179656 | tf_op jit(solution)/shard_map/ppermute | solution.py:1137
  23.3 197.8 %all-gather.16.cloned.1.call-start = ((), (), s32[]{:S(2)}) async-start(), calls=%async_computation.9 | async-start | bytes 3932160 | tf_op jit(solution)/shard_map/all_gather | solution.py:1141
  23.3 17.9 %collective-permute-start.2 = (bf16[96,4096]{1,0:T(8,128)(2,1)}, bf16[96,4096]{1,0:T(8,128)(2,1)S(1)}, u32[]{:S(2)}, u32[]{:S(2)}) collective-permute-start(bf16[96,4096]{1,0:T(8,128)(2,1)} %get-tuple-element.180), channel_id=1, source_target_pairs={{0,1},{1,0},{2,3},{3,2},{4,5},{5,4},{6,7},{7,6},{8,9},{9,8},{10,11... | collective-permute-start | bytes 2359304 | tf_op jit(solution)/shard_map/ppermute | solution.py:1137
  42.1 315.9 %all-gather.10.cloned.1.call-start = ((), (), s32[]{:S(2)}) async-start(), calls=%async_computation.6 | async-start | bytes 3932160 | tf_op jit(solution)/shard_map/all_gather | solution.py:1143
  43.0 9.0 %collective-permute-start.1 = (bf16[256,768]{1,0:T(8,128)(2,1)}, bf16[256,768]{1,0:T(8,128)(2,1)}, u32[]{:S(2)}, u32[]{:S(2)}) collective-permute-start(bf16[256,768]{1,0:T(8,128)(2,1)} %get-tuple-element.191), channel_id=1, source_target_pairs={{0,1},{1,0},{2,3},{3,2},{4,5},{5,4},{6,7},{7,6},{8,9},{9,8},{10,11... | collective-permute-start | bytes 1179656 | tf_op jit(solution)/shard_map/ppermute | solution.py:1137
  45.2 110.1 %collective-permute-start = (bf16[96,4096]{1,0:T(8,128)(2,1)}, bf16[96,4096]{1,0:T(8,128)(2,1)}, u32[]{:S(2)}, u32[]{:S(2)}) collective-permute-start(bf16[96,4096]{1,0:T(8,128)(2,1)} %get-tuple-element.183), channel_id=1, source_target_pairs={{0,1},{1,0},{2,3},{3,2},{4,5},{5,4},{6,7},{7,6},{8,9},{9,8},{10,11... | collective-permute-start | bytes 2359304 | tf_op jit(solution)/shard_map/ppermute | solution.py:1137
  48.2 3.7 copy-start.13
  50.2 4.1 copy-start.12
  50.2 5.4 copy-start.16
  52.0 4.7 copy-start.17
  54.2 345.0 %all-gather.8.cloned.1.call-start = ((), (), s32[]{:S(2)}) async-start(), calls=%async_computation.5 | async-start | bytes 7864320 | tf_op jit(solution)/shard_map/all_gather | solution.py:1143
  54.3 4.6 copy-start.8
  62.8 39.2 %copy-start.6 = (bf16[2,4,1,768,16]{3,4,2,1,0:T(8,128)(2,1)S(1)}, bf16[2,4,1,768,16]{3,4,2,1,0:T(8,128)(2,1)}, u32[]{:S(2)}) copy-start(bf16[2,4,1,768,16]{3,4,2,1,0:T(8,128)(2,1)} %get-tuple-element.228) | copy-start | bytes 589828
  165.3 3.8 copy-start.7
  165.3 4.7 copy-start.2
  165.3 55.7 %all-to-all-start = ((bf16[8,192,768]{2,1,0:T(8,128)(2,1)}), bf16[8,192,768]{2,1,0:T(8,128)(2,1)S(1)}, u32[]{:S(2)}, u32[]{:S(2)}) async-start(bf16[8,192,768]{2,1,0:T(8,128)(2,1)} %dispatch.2), calls=%async_computation | async-start | bytes 4718592 | tf_op jit(solution)/shard_map/all_to_all | solution.py:1148
  173.0 47.4 %copy-start.15 = (f32[2,2,768]{2,1,0:T(2,128)S(1)}, f32[2,2,768]{2,1,0:T(2,128)}, u32[]{:S(2)}) copy-start(f32[2,2,768]{2,1,0:T(2,128)} %param.36) | copy-start | bytes 36868
  318.8 32.1 %all-to-all-start.1 = ((bf16[8,192,768]{2,1,0:T(8,128)(2,1)}), bf16[8,192,768]{2,1,0:T(8,128)(2,1)S(1)}, u32[]{:S(2)}, u32[]{:S(2)}) async-start(bf16[8,192,768]{2,1,0:T(8,128)(2,1)} %dispatch.3), calls=%async_computation.1 | async-start | bytes 4718592 | tf_op jit(solution)/shard_map/all_to_all | solution.py:1148
  333.1 24.2 %copy-start.9 = (bf16[2,128,768]{2,1,0:T(8,128)(2,1)S(1)}, bf16[2,128,768]{2,1,0:T(8,128)(2,1)}, u32[]{:S(2)}) copy-start(bf16[2,128,768]{2,1,0:T(8,128)(2,1)} %get-tuple-element.131) | copy-start | bytes 1179652
  352.4 33.0 %all-to-all-start.2 = ((bf16[8,192,768]{2,1,0:T(8,128)(2,1)}), bf16[8,192,768]{2,1,0:T(8,128)(2,1)}, u32[]{:S(2)}, u32[]{:S(2)}) async-start(bf16[8,192,768]{2,1,0:T(8,128)(2,1)} %dispatch_grad.2), calls=%async_computation.2 | async-start | bytes 4718592 | tf_op jit(solution)/shard_map/all_to_all | solution.py:1148
  704.5 8.0 %copy-start.18 = (u32[32]{0:T(128)S(1)}, u32[32]{0:T(128)}, u32[]{:S(2)}) copy-start(u32[32]{0:T(128)} %constant.186) | copy-start | bytes 388
  705.9 18.4 %all-to-all-start.3 = ((bf16[8,2,2,4,16,96]{5,4,3,2,1,0:T(8,128)(2,1)}), bf16[8,2,2,4,16,96]{5,4,3,2,1,0:T(8,128)(2,1)S(1)}, u32[]{:S(2)}, u32[]{:S(2)}) async-start(bf16[8,2,2,4,16,96]{5,4,3,2,1,0:T(8,128)(2,1)} %maximum_bitcast_fusion), calls=%async_computation.3 | async-start | bytes 1048576 | tf_op jit(solution)/shard_map/all_to_all | solution.py:1268
  (8 other events, 17.6 us)
Sparse Core Ops, SparseCore 0:
  10.7 63.3 all-gather.13
  75.7 68.5 all-gather.11
  145.9 73.4 all-gather.15
  220.8 63.1 all-gather.9
  285.5 113.6 all-gather.7

commit v3 on v2

--- a/solution.py
+++ b/solution.py
@@ -419,25 +419,29 @@
     return bit + change - 2 * bit * change
 
 
-def owner_at(p, h, each):
-    x, c, y = (lax.axis_index(name) for name in ("x", "c", "y"))
+PLANE, WIDE_SLICE = 0, 1
+OWNERS = (("x", "c", "y"), ("x", "c"))
+
+
+def owner_at(p, h, kind):
+    x = lax.axis_index("x")
     far, near = 1 - p // 2, 1 - p % 2
-    c = flip(c, h)
-    if each == 2:
-        x, y = flip(x, far), flip(y, near)
-    else:
+    if kind == WIDE_SLICE:
         x = 2 * flip(x // 2, far) + flip(x % 2, near)
-    return {"x": x, "c": c, "y": y}, (x * 2 + c) * each + y
+        c = flip(lax.axis_index("c"), h)
+        return {"x": x, "c": c}, x * 2 + c
+    x, c, y = flip(x, far), flip(lax.axis_index("c"), h), flip(lax.axis_index("y"), near)
+    return {"x": x, "c": c, "y": y}, (x * 2 + c) * 2 + y
 
 
 PLACES = [(p, h) for p in range(NP) for h in range(2)]
 
 
-def greet(each):
+def greet(kind):
     barrier = pltpu.get_barrier_semaphore()
     for p, h in PLACES[:-2] + PLACES[-1:]:
         pl.semaphore_signal(
-            barrier, inc=1, device_id=owner_at(p, h, each)[0], device_id_type=pl.DeviceIdType.MESH
+            barrier, inc=1, device_id=owner_at(p, h, kind)[0], device_id_type=pl.DeviceIdType.MESH
         )
     pl.semaphore_wait(barrier, NFFN - 1)
 
@@ -468,18 +472,18 @@
     return copies
 
 
-def fetch_blocks(source, rv, sems, each):
+def fetch_blocks(source, rv, sems, kind):
     copies = []
     for n, (p, h) in enumerate(PLACES):
-        number = owner_at(p, h, each)[1]
+        number = owner_at(p, h, kind)[1]
         copies.append(pltpu.make_async_copy(source.at[number], block_of(rv, p, h), sems.at[n]))
     for copy in copies:
         copy.start()
     return copies
 
 
-def give_back(pv, p, target, send, recv, each):
-    me = owner_at(NP - 1, 0, each)[1]
+def give_back(pv, p, target, send, recv, kind):
+    me = owner_at(NP - 1, 0, kind)[1]
     copies = []
     for h in range(2):
         n = 2 * p + h
@@ -491,7 +495,7 @@
                 dst_ref=target.at[me],
                 send_sem=send.at[n],
                 recv_sem=recv.at[n],
-                device_id=owner_at(p, h, each)[0],
+                device_id=owner_at(p, h, kind)[0],
                 device_id_type=pl.DeviceIdType.MESH,
             )
         copy.start()
@@ -523,14 +527,14 @@
     )
 
 
-def expert_body(split, each, *refs):
+def expert_body(split, kind, *refs):
     count = 2 if split else 1
     gate_ups = refs[:count]
     down_ref, rec_ref, ret_ref, gate_ref, up_ref = refs[count : count + 5]
     w1, w2, rv, pv, gv, uv, acc, wsem, rsem, gsem, usem, send, recv = refs[count + 5 :]
     weights = fetch_weights(split, gate_ups, down_ref, w1, w2, wsem)
-    blocks = fetch_blocks(rec_ref, rv, rsem, each)
-    greet(each)
+    blocks = fetch_blocks(rec_ref, rv, rsem, kind)
+    greet(kind)
     for copy in weights + blocks:
         copy.wait()
     stores = []
@@ -548,7 +552,7 @@
 
         lax.fori_loop(0, FF // FC, step, 0)
         pv[p] = acc[...].astype(BF)
-        moves += give_back(pv, p, ret_ref, send, recv, each)
+        moves += give_back(pv, p, ret_ref, send, recv, kind)
         for values, ref, sems in ((gv, gate_ref, gsem), (uv, up_ref, usem)):
             copy = pltpu.make_async_copy(values.at[p], ref.at[p], sems.at[p])
             copy.start()
@@ -557,11 +561,19 @@
         copy.wait()
 
 
-def comm_call(body, ins, outs, scratch, name, number, flops, nbytes):
+def comm_call(body, ins, outs, scratch, name, number, flops, nbytes, near=(), near_outs=()):
+    def specs(far, close):
+        return [pl.BlockSpec(memory_space=pl.ANY)] * len(far) + [
+            pl.BlockSpec(memory_space=pltpu.VMEM)
+        ] * len(close)
+
+    ins, outs, ins_specs, outs_specs = (
+        [*ins, *near], [*outs, *near_outs], specs(ins, near), specs(outs, near_outs)
+    )
     return pl.pallas_call(
         body,
-        in_specs=[pl.BlockSpec(memory_space=pl.ANY)] * len(ins),
-        out_specs=[pl.BlockSpec(memory_space=pl.ANY)] * len(outs),
+        in_specs=ins_specs,
+        out_specs=outs_specs,
         out_shape=outs,
         scratch_shapes=scratch,
         compiler_params=pltpu.CompilerParams(
@@ -583,11 +595,11 @@
 KEPT = jax.ShapeDtypeStruct((NP, PR, FF), BF)
 
 
-def expert_forward(received, gate_ups, down, each):
+def expert_forward(received, gate_ups, down, kind):
     split = len(gate_ups) == 2
 
     def body(*refs):
-        expert_body(split, each, *refs)
+        expert_body(split, kind, *refs)
 
     return comm_call(
         body,
@@ -602,122 +614,217 @@
     )
 
 
-def expert_both_body(each, gate_up_ref, down_ref, rec_ref, sg_ref, ret_ref, gret_ref, *scratch):
-    w1, w2, rv, sv, pv, qv, acc, gacc, wsem, rsem, ssem, send, recv, gsend, grecv = scratch
+def expert_both_body(
+    kind, gate_up_ref, down_ref, rec_ref, sg_ref, mid_ref, g_ref, gret_ref, out_ref, gn_ref,
+    gle_ref, tcol_ref, lg_ref, rt_ref, gain_ref, cv_ref, wt_ref, res_ref, *scratch,
+):
+    (
+        w1, w2, rv, sv, pv, qv, gv, uv, back, mid, g, acc,
+        wsem, rsem, ssem, msem, send, recv, gsend, grecv,
+    ) = scratch
     weights = fetch_weights(False, [gate_up_ref], down_ref, w1, w2, wsem)
-    blocks = fetch_blocks(rec_ref, rv, rsem, each) + fetch_blocks(sg_ref, sv, ssem, each)
-    greet(each)
+    blocks = fetch_blocks(rec_ref, rv, rsem, kind) + fetch_blocks(sg_ref, sv, ssem, kind)
+    extra = [
+        pltpu.make_async_copy(mid_ref, mid, msem.at[0]),
+        pltpu.make_async_copy(g_ref, g, msem.at[1]),
+    ]
+    for copy in extra:
+        copy.start()
+    greet(kind)
     for copy in weights + blocks:
         copy.wait()
     moves = []
     for p in range(NP):
         r = rv[p]
-        g = sv[p]
         acc[...] = jnp.zeros_like(acc)
-        gacc[...] = jnp.zeros_like(gacc)
 
         def step(f, carry):
             gate, up, part = forward_chunk(r, w1, w2, f)
+            gv[p, :, pl.ds(chunk_at(f), FC)] = gate.astype(BF)
+            uv[p, :, pl.ds(chunk_at(f), FC)] = up.astype(BF)
             acc[...] += part
-            gacc[...] += backward_chunk(g, gate, up, w1, w2, f)
             return carry
 
         lax.fori_loop(0, FF // FC, step, 0)
         pv[p] = acc[...].astype(BF)
-        qv[p] = gacc[...].astype(BF)
-        moves += give_back(pv, p, ret_ref, send, recv, each)
-        moves += give_back(qv, p, gret_ref, gsend, grecv, each)
-    for copy in moves:
+        moves += give_back(pv, p, back, send, recv, kind)
+    later = []
+    for p in range(NP):
+        grads = sv[p]
+        acc[...] = jnp.zeros_like(acc)
+
+        def step(f, carry):
+            at = pl.ds(chunk_at(f), FC)
+            gate = gv[p, :, at].astype(F32)
+            up = uv[p, :, at].astype(F32)
+            acc[...] += backward_chunk(grads, gate, up, w1, w2, f)
+            return carry
+
+        lax.fori_loop(0, FF // FC, step, 0)
+        qv[p] = acc[...].astype(BF)
+        later += give_back(qv, p, gret_ref, gsend, grecv, kind)
+    for copy in moves + extra:
         copy.wait()
 
-
-def expert_both(received, slot_grads, gate_up, down, each):
+    def finish(i, carry):
+        at = pl.ds(pl.multiple_of(i * RB, RB), RB)
+        logits, routes, middle = lg_ref[at, :], rt_ref[at, :], mid[at, :]
+        following, chosen = combine_rows(
+            tcol_ref[at, :], back, middle, logits, routes, gain_ref[...], cv_ref
+        )
+        out_ref[at, :] = following
+        gn_ref[at, :], gle_ref[at, :] = mix_grad(
+            g[at, :].astype(F32), middle, chosen, logits, routes, 0.0, gain_ref[...], cv_ref,
+            wt_ref[...], res_ref[...],
+        )
+        return carry
+
+    lax.fori_loop(0, NB, finish, 0)
+    for copy in later:
+        copy.wait()
+
+
+def expert_both(
+    received, slot_grads, gate_up, down, mid, g, tcol, logits, routes, gain, const_vec, router_t,
+    residual_t, kind,
+):
     def body(*refs):
-        expert_both_body(each, *refs)
+        far, near, outs, scratch = refs[:6], refs[6:13], refs[13:17], refs[17:]
+        expert_both_body(kind, *far, *outs, *near, *scratch)
 
     return comm_call(
         body,
-        [gate_up, down, received, slot_grads],
-        [BLOCKS, BLOCKS],
-        WEIGHTS + [ROWS, ROWS, ROWS, ROWS, SUM, SUM]
-        + [DMA((9,)), DMA((8,)), DMA((8,)), DMA((8,)), DMA((8,)), DMA((8,)), DMA((8,))],
+        [gate_up, down, received, slot_grads, mid, g],
+        [BLOCKS],
+        WEIGHTS
+        + [ROWS, ROWS, ROWS, ROWS, WIDE, WIDE, pltpu.VMEM((NFFN, CAP, D), BF)]
+        + [pltpu.VMEM((T, D), F32), pltpu.VMEM((T, D), g.dtype), SUM]
+        + [DMA((9,)), DMA((8,)), DMA((8,)), DMA((2,))]
+        + [DMA((8,)), DMA((8,)), DMA((8,)), DMA((8,))],
         "expert_both",
         2,
         2 * SLOTS * D * FF * 6,
         26e6,
-    )
-
-
-def expert_back_body(split, each, *refs):
+        [tcol, logits, routes, gain, const_vec, router_t, residual_t],
+        [out((T, D), F32), out((T, D), F32), out((T, 128), F32)],
+    )
+
+
+def expert_back_body(split, kind, *refs):
     count = 2 if split else 1
     gate_ups = refs[:count]
-    down_ref, sg_ref, gate_ref, up_ref, ret_ref = refs[count : count + 5]
-    w1, w2, rv, pv, gv, uv, acc, wsem, gsem, usem, dsend, drecv, send, recv = refs[count + 5 :]
+    down_ref, gate_ref, up_ref, g_ref, mid_ref, c0_ref, c1_ref = refs[count : count + 7]
+    trow_ref, lg_ref, rt_ref, gl_ref, gain_ref, cv_ref, wt_ref = refs[count + 7 : count + 14]
+    ret_ref, gn_ref = refs[count + 14 : count + 16]
+    (
+        w1, w2, sgv, rv, pv, gv, uv, first, second, g, mid, c0, c1, acc,
+        wsem, gsem, usem, msem, dsend, drecv, send, recv,
+    ) = refs[count + 16 :]
+    extra = [
+        pltpu.make_async_copy(ref, values, msem.at[n])
+        for n, (ref, values) in enumerate(
+            ((g_ref, g), (mid_ref, mid), (c0_ref, c0), (c1_ref, c1))
+        )
+    ]
+    for copy in extra:
+        copy.start()
     weights = fetch_weights(split, gate_ups, down_ref, w1, w2, wsem)
     for values, ref, sems in ((gv, gate_ref, gsem), (uv, up_ref, usem)):
         for p in range(NP):
             copy = pltpu.make_async_copy(ref.at[p], values.at[p], sems.at[p])
             copy.start()
             weights.append(copy)
-    greet(each)
+    extra[0].wait()
+
+    def gated(i, carry):
+        at = pl.ds(pl.multiple_of(i * RB, RB), RB)
+        gates = mix_terms(lg_ref[at, :], rt_ref[at, :])[0]
+        first[at, :] = (gates[0] * g[at, :]).astype(BF)
+        second[at, :] = (gates[1] * g[at, :]).astype(BF)
+        return carry
+
+    lax.fori_loop(0, NB, gated, 0)
+    greet(kind)
     arrivals = {}
+    for p, h in [(1, 0), (2, 0), (1, 1), (2, 1), (0, 0), (0, 1), (3, 1), (3, 0)]:
+        where, number = owner_at(p, h, kind)
+        place = number * CAP + iota((CAP, T), 0)
+        hit0 = (trow_ref[0:1, :] == place).astype(F32).astype(BF)
+        hit1 = (trow_ref[1:2, :] == place).astype(F32).astype(BF)
+        values = (mm(hit0, first[...]) + mm(hit1, second[...])).astype(BF)
+        n = 2 * p + h
+        if (p, h) == (NP - 1, 0):
+            rv[p, h * CAP : (h + 1) * CAP, :] = values
+            continue
+        sgv[p, h * CAP : (h + 1) * CAP, :] = values
+        copy = pltpu.make_async_remote_copy(
+            src_ref=block_of(sgv, p, h),
+            dst_ref=block_of(rv, p, h),
+            send_sem=dsend.at[n],
+            recv_sem=drecv.at[n],
+            device_id=where,
+            device_id_type=pl.DeviceIdType.MESH,
+        )
+        copy.start()
+        arrivals[p, h] = copy
+    for copy in weights + extra[1:]:
+        copy.wait()
+    moves = []
+
     for p in (3, 1, 2, 0):
         for h in range(2):
-            where, number = owner_at(p, h, each)
-            n = 2 * p + h
-            if (p, h) == (NP - 1, 0):
-                copy = pltpu.make_async_copy(sg_ref.at[number], block_of(rv, p, h), dsend.at[n])
-            else:
-                copy = pltpu.make_async_remote_copy(
-                    src_ref=sg_ref.at[number],
-                    dst_ref=block_of(rv, p, h),
-                    send_sem=dsend.at[n],
-                    recv_sem=drecv.at[n],
-                    device_id=where,
-                    device_id_type=pl.DeviceIdType.MESH,
-                )
-            copy.start()
-            arrivals[p, h] = copy
-    for copy in weights:
-        copy.wait()
-    moves = []
-    for p in (3, 1, 2, 0):
-        for h in range(2):
-            arrivals[p, h].wait()
-        g = rv[p]
+            if (p, h) in arrivals:
+                arrivals[p, h].wait()
+        grads = rv[p]
         acc[...] = jnp.zeros_like(acc)
 
         def step(f, carry):
             at = pl.ds(chunk_at(f), FC)
             gate = gv[p, :, at].astype(F32)
             up = uv[p, :, at].astype(F32)
-            acc[...] += backward_chunk(g, gate, up, w1, w2, f)
+            acc[...] += backward_chunk(grads, gate, up, w1, w2, f)
             return carry
 
         lax.fori_loop(0, FF // FC, step, 0)
         pv[p] = acc[...].astype(BF)
-        moves += give_back(pv, p, ret_ref, send, recv, each)
+        moves += give_back(pv, p, ret_ref, send, recv, kind)
+
+    def tidy(i, carry):
+        at = pl.ds(pl.multiple_of(i * RB, RB), RB)
+        gn_ref[at, :] = mix_grad(
+            g[at, :], mid[at, :], (c0[at, :], c1[at, :]), lg_ref[at, :], rt_ref[at, :],
+            gl_ref[at, :], gain_ref[...], cv_ref, wt_ref[...], None,
+        )[0]
+        return carry
+
+    lax.fori_loop(0, NB, tidy, 0)
     for copy in moves:
         copy.wait()
 
 
-def expert_backward(slot_grads, gate, up, gate_ups, down, each):
+def expert_backward(
+    gate, up, gate_ups, down, g, mid, c0, c1, trow, logits, routes, gl, gain, const_vec, router_t, kind
+):
     split = len(gate_ups) == 2
 
     def body(*refs):
-        expert_back_body(split, each, *refs)
-
+        expert_back_body(split, kind, *refs)
+
+    half, full = pltpu.VMEM((T, D), BF), pltpu.VMEM((T, D), F32)
     return comm_call(
         body,
-        [*gate_ups, down, slot_grads, gate, up],
+        [*gate_ups, down, gate, up, g, mid, c0, c1],
         [BLOCKS],
-        WEIGHTS + [ROWS, ROWS, WIDE, WIDE, SUM]
-        + [DMA((9,)), DMA((NP,)), DMA((NP,)), DMA((8,)), DMA((8,)), DMA((8,)), DMA((8,))],
+        WEIGHTS
+        + [ROWS, ROWS, ROWS, WIDE, WIDE, half, half, full, full, half, half, SUM]
+        + [DMA((9,)), DMA((NP,)), DMA((NP,)), DMA((4,)), DMA((8,)), DMA((8,)), DMA((8,)), DMA((8,))],
         "expert_backward",
         3,
         2 * SLOTS * D * FF * 3,
         26e6,
-    )[0]
+        [trow, logits, routes, gl, gain, const_vec, router_t],
+        [out((T, D), F32)],
+    )
 
 
 def mix_terms(logits, routes):
@@ -745,23 +852,28 @@
     return lax.rsqrt(jnp.mean(v * v, axis=1, keepdims=True) + EPSILON)
 
 
-def combine_body(tcol_ref, ret_ref, mid_ref, lg_ref, rt_ref, g_ref, cv_ref, x_ref, c0_ref, c1_ref):
+def combine_rows(tcol, back_ref, mid, logits, routes, gain, cv_ref):
     place = iota((RB, SLOTS), 1)
-    back = ret_ref[...]
+    back = back_ref[...].reshape(SLOTS, D)
     chosen = []
-    for k, c_ref in enumerate((c0_ref, c1_ref)):
-        hit = (tcol_ref[:, k : k + 1] == place).astype(F32).astype(BF)
-        value = mm(hit, back)
-        c_ref[...] = value.astype(BF)
-        chosen.append(value)
-    mid = mid_ref[...]
-    normed = mid * rms_scale(mid) * g_ref[...]
-    gates, weights, shares = mix_terms(lg_ref[...], rt_ref[...])
+    for k in range(2):
+        hit = (tcol[:, k : k + 1] == place).astype(F32).astype(BF)
+        chosen.append(mm(hit, back))
+    normed = mid * rms_scale(mid) * gain
+    gates, weights, shares = mix_terms(logits, routes)
     same = weights[0] + weights[1] * shares[0][0] + weights[2] * shares[1][0]
     moe = gates[0] * chosen[0] + gates[1] * chosen[1] + same * normed
     moe = moe + (weights[1] * shares[0][1]) * cv_ref[0:1, :]
     moe = moe + (weights[2] * shares[1][1]) * cv_ref[1:2, :]
-    x_ref[...] = mid + moe
+    return mid + moe, chosen
+
+
+def combine_body(tcol_ref, ret_ref, mid_ref, lg_ref, rt_ref, g_ref, cv_ref, x_ref, c0_ref, c1_ref):
+    x_ref[...], chosen = combine_rows(
+        tcol_ref[...], ret_ref, mid_ref[...], lg_ref[...], rt_ref[...], g_ref[...], cv_ref
+    )
+    c0_ref[...] = chosen[0].astype(BF)
+    c1_ref[...] = chosen[1].astype(BF)
 
 
 def combine(tcol, returned, mid, logits, routes, gain, const_vec):
@@ -815,7 +927,8 @@
         grad = grad + jnp.where(lane == 12 + 2 * c, tilt, 0.0)
         grad = grad - jnp.where(lane == 13 + 2 * c, tilt, 0.0)
     keep = weights[0] + weights[1] * shares[0][0] + weights[2] * shares[1][0]
-    return mm(spread_lanes(grad), wt) + keep * g, mm(spread_lanes(only), res)
+    residual = None if res is None else mm(spread_lanes(only), res)
+    return mm(spread_lanes(grad), wt) + keep * g, residual
 
 
 def rms_back(grad, v, gain):
@@ -824,86 +937,11 @@
     return scale * inner - v * (scale**3 * jnp.mean(v * inner, axis=1, keepdims=True))
 
 
-def settle_grad_body(
-    tcol_ref, back_ref, mid_ref, g_ref, c0_ref, c1_ref, lg_ref, rt_ref, gl_ref, gain_ref, cv_ref,
-    wt_ref, res_ref, mixed_ref, nar_ref, w_ref, d_ref, u_ref,
-    gm_ref, gx_ref, gle_ref, gu_ref, gd_ref,
-):
-    @pl.when(pl.program_id(0) == 0)
-    def _():
-        gu_ref[...] = jnp.zeros_like(gu_ref)
-        gd_ref[...] = jnp.zeros_like(gd_ref)
-
-    mid = mid_ref[...]
-    g = g_ref[...].astype(F32)
-    gain = gain_ref[...]
-    grad, gle_ref[...] = mix_grad(
-        g, mid, (c0_ref[...], c1_ref[...]), lg_ref[...], rt_ref[...], gl_ref[...], gain, cv_ref,
-        wt_ref[...], res_ref[...],
-    )
-    place = iota((RB, SLOTS), 1)
-    hit = (tcol_ref[:, 0:1] == place) | (tcol_ref[:, 1:2] == place)
-    grad = grad + mm(hit.astype(F32).astype(BF), back_ref[...])
-    grad_mid = g + rms_back(grad, mid, gain)
-    gm_ref[...] = grad_mid
-    out_grad = grad_mid.astype(BF)
-    grad_narrow = mm_nt(out_grad, u_ref[...]).astype(BF)
-    mixed = mixed_ref[...]
-    gu_ref[...] += 2.0 * mm_tn(nar_ref[...], out_grad)
-    gd_ref[...] += mm_tn(grad_narrow, mixed)
-    gx_ref[...] = (mm_nt(out_grad, w_ref[0]) + mm_nt(grad_narrow, d_ref[...])).astype(BF)
-
-
-def settle_grad(
-    tcol, back, mid, g, c0, c1, logits, routes, gl, gain, const_vec, router_t, residual_t,
-    mixed, narrow, w, down, up,
-):
-    return call(
-        settle_grad_body,
-        (NB,),
-        [
-            (tcol, (RB, 128), rows),
-            (back, None),
-            (mid, (RB, D), rows),
-            (g, (RB, D), rows),
-            (c0, (RB, D), rows),
-            (c1, (RB, D), rows),
-            (logits, (RB, 128), rows),
-            (routes, (RB, 2), rows),
-            (gl, (RB, 128), rows),
-            (gain, None),
-            (const_vec, None),
-            (router_t, None),
-            (residual_t, None),
-            (mixed, (RB, D), rows),
-            (narrow, (RB, 128), rows),
-            (w, (1, D, D), lambda i: (3, 0, 0)),
-            (down, None),
-            (up, None),
-        ],
-        [
-            (out((T, D), F32), (RB, D), rows),
-            (out((T, D), BF), (RB, D), rows),
-            (out((T, 128), F32), (RB, 128), rows),
-            (out((128, D), F32), None),
-            (out((128, D), F32), None),
-        ],
-        name="settle_grad",
-        flops=2 * T * SLOTS * D + 2 * T * D * D * 2,
-        nbytes=22e6,
-    )
-
-
-def attend_grad_body(
-    q_ref, k_ref, v_ref, aug_ref, kf_ref, g_ref, mixed_ref, cos_ref, sin_ref,
-    gq_ref, gk_ref, gv_ref, dqt,
-):
+def attend_back(q, k, v, aug, kf, g, mixed, dqt):
     lane = iota((T, 128), 1)
     low = lane < 64
     lane6 = lane & 63
-    q, k, v, kf, g = q_ref[...], k_ref[...], v_ref[...], kf_ref[...], g_ref[...]
-    aug = aug_ref[0]
-    product = g.astype(F32) * mixed_ref[...].astype(F32)
+    product = g.astype(F32) * mixed.astype(F32)
     d0 = jnp.sum(jnp.where(low, product, 0.0), axis=1, keepdims=True)
     d1 = jnp.sum(jnp.where(low, 0.0, product), axis=1, keepdims=True)
     a, b, c = three(-jnp.where(low, d1, d0))
@@ -916,126 +954,173 @@
     gs = (jnp.where(low, g, ga), jnp.where(low, ga, g))
     kt = k.T
     tri = iota((RB, RB), 0) <= iota((RB, RB), 1)
-    dqt[...] = jnp.zeros_like(dqt)
     low = low[:RB]
+    dks = []
+    dvs = []
     for i in range(NB):
         here = slice(i * RB, (i + 1) * RB)
-        dks = []
-        dvs = []
+        dk = [None, None]
+        dv = [None, None]
         for h in range(2):
-            dk = None
-            for j in range(i, NB):
-                there = slice(j * RB, (j + 1) * RB)
+            half = slice(h * 64, (h + 1) * 64)
+            for start, stop in ((i * RB, (i + 1) * RB), ((i + 1) * RB, T)):
+                if start == stop:
+                    continue
+                there = slice(start, stop)
                 p = jnp.exp2(mm_nt(ks[h][here], qs[h][there]) * LOG_SCALE)
-                if i == j:
+                if stop == (i + 1) * RB:
                     p = jnp.where(tri, p, 0.0)
                 ds = (p * mm_nt(vs[h][here], gs[h][there])).astype(BF)
                 p = p.astype(BF)
                 dv_part = mm(p, g[there])
                 dk_part = mm(ds, q[there])
-                dk = dk_part if dk is None else dk + dk_part
-                dv = dv_part if j == i else dv + dv_part
-                half = slice(h * 64, (h + 1) * 64)
-                dqt[half, there] += mm(kt[half, here], ds)
-            dks.append(dk)
-            dvs.append(dv)
-        gv_ref[here, :] = jnp.where(low, dvs[0], dvs[1]).astype(BF)
-        dk = (jnp.where(low, dks[0], dks[1]) * (1.0 / math.sqrt(HD))).astype(BF).astype(F32)
-        gk_ref[here, :] = turn(dk, cos_ref[here, :], -sin_ref[here, :]).astype(BF)
-    dq = (dqt[...].T * (1.0 / math.sqrt(HD))).astype(BF).astype(F32)
-    gq_ref[...] = turn(dq, cos_ref[...], -sin_ref[...]).astype(BF)
-
-
-def attend_grad(qkv, aug, kf, g, mixed, cos, sin):
-    def col(j):
-        return (0, j)
-
-    return call(
-        attend_grad_body,
-        (PAIRS,),
-        [
-            (qkv, (T, 128), col),
-            (qkv, (T, 128), lambda j: (0, PAIRS + j)),
-            (qkv, (T, 128), lambda j: (0, 2 * PAIRS + j)),
-            (aug, (1, T, 128), lambda j: (j, 0, 0)),
-            (kf, None),
-            (g, (T, 128), col),
-            (mixed, (T, 128), col),
-            (cos, None),
-            (sin, None),
+                dk[h] = dk_part if dk[h] is None else dk[h] + dk_part
+                dv[h] = dv_part if dv[h] is None else dv[h] + dv_part
+                part = mm(kt[half, here], ds)
+                if i == 0:
+                    dqt[half, there] = part
+                else:
+                    dqt[half, there] += part
+        dvs.append(jnp.where(low, dv[0], dv[1]))
+        dks.append(jnp.where(low, dk[0], dk[1]))
+    return dqt[...].T, jnp.concatenate(dks), jnp.concatenate(dvs)
+
+
+def layer_back_body(
+    back_ref, gn_ref, mid_ref, g_ref, mixed_ref, w_ref, qkv_ref, aug_ref, n_ref, x_ref,
+    tcol_ref, gain1_ref, gain0_ref, nar_out_ref, nar_ref, d_out_ref, u_out_ref, d_ref, u_ref,
+    kf_ref, cos_ref, sin_ref,
+    gx_ref, gu_out_ref, gd_out_ref, gu_ref, gd_ref,
+    back, gn, mid, g, mixed, w, qkv, aug, n, x, gmix, gproj, dqt, sems, row_sems, out_sems,
+):
+    def block(i):
+        return slice(i * RB, (i + 1) * RB)
+
+    def start(source, target, sem):
+        copy = pltpu.make_async_copy(source, target, sem)
+        copy.start()
+        return copy
+
+    by_row = [(gn_ref, gn), (mid_ref, mid), (g_ref, g), (mixed_ref, mixed)]
+    first = [start(back_ref, back, sems.at[0]), start(w_ref.at[3], w.at[3], sems.at[1])]
+    strips = [
+        [start(a.at[block(i), :], b.at[block(i), :], row_sems.at[i, m]) for m, (a, b) in enumerate(by_row)]
+        for i in range(NB)
+    ]
+    second = [start(qkv_ref, qkv, sems.at[2]), start(aug_ref, aug, sems.at[3])]
+    third = [start(w_ref.at[k], w.at[k], sems.at[4 + k]) for k in range(3)]
+    third += [start(n_ref, n, sems.at[7]), start(x_ref, x, sems.at[8])]
+    for copy in first:
+        copy.wait()
+    place = iota((RB, SLOTS), 1)
+    gu = jnp.zeros((128, D), F32)
+    gd = jnp.zeros((128, D), F32)
+    for i in range(NB):
+        at = block(i)
+        for copy in strips[i]:
+            copy.wait()
+        hit = (tcol_ref[at, 0:1] == place) | (tcol_ref[at, 1:2] == place)
+        grad = gn[at, :] + mm(hit.astype(F32).astype(BF), back[...])
+        grad_mid = g[at, :].astype(F32) + rms_back(grad, mid[at, :], gain1_ref[...])
+        gn[at, :] = grad_mid
+        out_grad = grad_mid.astype(BF)
+        grad_narrow = mm_nt(out_grad, u_out_ref[...]).astype(BF)
+        gu = gu + 2.0 * mm_tn(nar_out_ref[at, :], out_grad)
+        gd = gd + mm_tn(grad_narrow, mixed[at, :])
+        gmix[at, :] = (mm_nt(out_grad, w[3]) + mm_nt(grad_narrow, d_out_ref[...])).astype(BF)
+    gu_out_ref[...] = gu
+    gd_out_ref[...] = gd
+    for copy in second:
+        copy.wait()
+
+    def pair(j, carry):
+        def cols(part):
+            return pl.ds(pl.multiple_of(part * D + j * 128, 128), 128)
+
+        dq, dk, dv = attend_back(
+            qkv[:, cols(0)], qkv[:, cols(1)], qkv[:, cols(2)], aug[j], kf_ref[...],
+            gmix[:, cols(0)], mixed[:, cols(0)], dqt,
+        )
+        for part, value in enumerate((dq, dk)):
+            value = (value * (1.0 / math.sqrt(HD))).astype(BF).astype(F32)
+            gproj[:, cols(part)] = turn(value, cos_ref[...], -sin_ref[...]).astype(BF)
+        gproj[:, cols(2)] = dv.astype(BF)
+        return carry
+
+    lax.fori_loop(0, PAIRS, pair, 0)
+    for copy in third:
+        copy.wait()
+    gu_ref[...] = jnp.zeros_like(gu_ref)
+    gd_ref[...] = jnp.zeros_like(gd_ref)
+    stores = []
+    for i in range(NB):
+        at = block(i)
+        grad = jnp.zeros((RB, D), F32)
+        slim = jnp.zeros((RB, 128), F32)
+        narrow = nar_ref[at, :]
+        for part in range(3):
+            cols = slice(part * D, (part + 1) * D)
+            piece = gproj[at, cols]
+            grad = grad + mm_nt(piece, w[part])
+            slim = slim + mm_nt(piece, u_ref[:, cols])
+            gu_ref[:, cols] += 2.0 * mm_tn(narrow, piece)
+        slim = slim.astype(BF)
+        gd_ref[...] += mm_tn(slim, n[at, :])
+        grad = grad + mm_nt(slim, d_ref[...])
+        mid[at, :] = gn[at, :] + rms_back(grad, x[at, :].astype(F32), gain0_ref[...])
+        stores.append(start(mid.at[at, :], gx_ref.at[at, :], out_sems.at[i]))
+    for copy in stores:
+        copy.wait()
+
+
+def layer_back(
+    back, gn, mid, g, mixed, w, qkv, aug, n, x, tcol, gain1, gain0, narrow_out, narrow, down_out,
+    up_out, down, up, kf, cos, sin,
+):
+    far = [back, gn, mid, g, mixed, w, qkv, aug, n, x]
+    near = [
+        tcol, gain1, gain0, narrow_out, narrow, down_out, up_out, down, up, kf, cos, sin,
+    ]
+    outs = [out((128, D), F32), out((128, D), F32), out((128, 3 * D), F32), out((128, D), F32)]
+    anywhere = pl.BlockSpec(memory_space=pl.ANY)
+    close = pl.BlockSpec(memory_space=pltpu.VMEM)
+    return pl.pallas_call(
+        layer_back_body,
+        in_specs=[anywhere] * len(far) + [close] * len(near),
+        out_specs=[anywhere] + [close] * len(outs),
+        out_shape=[out((T, D), F32)] + outs,
+        scratch_shapes=[pltpu.VMEM(v.shape, v.dtype) for v in far]
+        + [
+            pltpu.VMEM((T, D), BF),
+            pltpu.VMEM((T, 3 * D), BF),
+            pltpu.VMEM((128, T), F32),
+            DMA((9,)),
+            DMA((NB, 4)),
+            DMA((NB,)),
         ],
-        [(out((T, D), BF), (T, 128), col)] * 3,
-        [pltpu.VMEM((128, T), F32)],
-        name="attend_grad",
-        flops=12 * 10 * T * T * 128,
-        nbytes=14e6,
-    )
-
-
-def project_grad_body(
-    gq_ref, gk_ref, gv_ref, w_ref, d_ref, u_ref, n_ref, nar_ref, x_ref, gain_ref, gm_ref,
-    gx_ref, gu_ref, gd_ref,
-):
-    @pl.when(pl.program_id(0) == 0)
-    def _():
-        gu_ref[...] = jnp.zeros_like(gu_ref)
-        gd_ref[...] = jnp.zeros_like(gd_ref)
-
-    grad = jnp.zeros((RB, D), F32)
-    slim = jnp.zeros((RB, 128), F32)
-    narrow = nar_ref[...]
-    for block, ref in enumerate((gq_ref, gk_ref, gv_ref)):
-        cols = slice(block * D, (block + 1) * D)
-        g = ref[...]
-        grad = grad + mm_nt(g, w_ref[block])
-        slim = slim + mm_nt(g, u_ref[:, cols])
-        gu_ref[:, cols] += 2.0 * mm_tn(narrow, g)
-    slim = slim.astype(BF)
-    gd_ref[...] += mm_tn(slim, n_ref[...])
-    grad = grad + mm_nt(slim, d_ref[...])
-    gx_ref[...] = gm_ref[...] + rms_back(grad, x_ref[...].astype(F32), gain_ref[...])
-
-
-def project_grad(gq, gk, gv, w, down, up, normed, narrow, x, gain, gm):
-    return call(
-        project_grad_body,
-        (NB,),
-        [
-            (gq, (RB, D), rows),
-            (gk, (RB, D), rows),
-            (gv, (RB, D), rows),
-            (w, (3, D, D), lambda i: (0, 0, 0)),
-            (down, None),
-            (up, None),
-            (normed, (RB, D), rows),
-            (narrow, (RB, 128), rows),
-            (x, (RB, D), rows),
-            (gain, None),
-            (gm, (RB, D), rows),
-        ],
-        [
-            (out((T, D), F32), (RB, D), rows),
-            (out((128, 3 * D), F32), None),
-            (out((128, D), F32), None),
-        ],
-        name="project_grad",
-        flops=2 * T * D * 3 * D * 1.3,
-        nbytes=22e6,
-    )
-
-
+        compiler_params=pltpu.CompilerParams(vmem_limit_bytes=VMEM_BYTES),
+        cost_estimate=pl.CostEstimate(
+            flops=int(12 * 10 * T * T * 128 + 2 * T * D * 5 * D), bytes_accessed=int(4e7), transcendentals=0
+        ),
+        name="layer_back",
+    )(*far, *near)
+
+
+AXES = ("x", "c", "zh", "zl", "y")
+EXPERT, SHARD = AXES[:2], AXES[2:]
 PIECE = 96
 
 
 def shared_body(p_ref, o_ref, local, zs, zr, ys, yr, xs, xr, cs, cr):
-    x, c, z, y = (lax.axis_index(name) for name in ("x", "c", "z", "y"))
+    x, c, y = (lax.axis_index(name) for name in ("x", "c", "y"))
+    z = 2 * lax.axis_index("zh") + lax.axis_index("zl")
     mine, theirs = 2 * x + c, 2 * (1 - x) + c
 
     def spot(quarter, column, j):
         at = (2 * ((z + 4 - j) % 4) + column) * PIECE
         return o_ref.at[quarter, pl.ds(pl.multiple_of(at, PIECE), PIECE), :]
 
-    others = [{"z": (z + d) % 4} for d in range(1, 4)]
+    others = [{"zh": (z + d) % 4 // 2, "zl": (z + d) % 2} for d in range(1, 4)]
     others += [{"y": 1 - y}, {"x": 1 - x}, {"c": 1 - c}]
     barrier = pltpu.get_barrier_semaphore()
     for who in others:
@@ -1108,13 +1193,15 @@
         copy.wait_send()
 
 
+def usual():
+    return tuple(lax.axis_size(name) for name in AXES) == (2, 2, 2, 2, 2)
+
+
 def gather_shared(qkv, output):
     rows_here = qkv.shape[0]
     parts = jnp.concatenate([qkv.reshape(rows_here, 3, D).transpose(1, 0, 2), output[None]])
-    sizes = tuple(lax.axis_size(name) for name in ("x", "c", "z", "y"))
-    if sizes != (2, 2, 4, 2):
-        whole = lax.all_gather(parts, ("z", "y"), axis=1, tiled=True)
-        return whole
+    if not usual():
+        return lax.all_gather(parts, SHARD, axis=1, tiled=True)
     quarter = 2 * lax.axis_index("x") + lax.axis_index("c")
     piece = lax.dynamic_index_in_dim(parts, quarter, axis=0, keepdims=False)
     return comm_call(
@@ -1129,27 +1216,168 @@
     )[0]
 
 
-def gather_expert(w, split):
-    count = w.shape[0]
-    if count == 2:
-        y = lax.axis_index("y")
-        mine = lax.dynamic_index_in_dim(w, y, axis=0, keepdims=False)
-        other = lax.ppermute(
-            lax.dynamic_index_in_dim(w, 1 - y, axis=0, keepdims=False), "y", [(0, 1), (1, 0)]
+SPAN = 96
+UNIT = LAYERS * 2 * 4 * R
+
+
+def adapters_body(*refs):
+    id_ref, parts = refs[0], refs[1 : 1 + 4 * LAYERS]
+    o_ref = refs[1 + 4 * LAYERS]
+    sbuf, rbuf, tbuf, ubuf, asend, arecv, bsend, brecv = refs[2 + 4 * LAYERS :]
+    x, c, y = (lax.axis_index(name) for name in ("x", "c", "y"))
+    z = 2 * lax.axis_index("zh") + lax.axis_index("zl")
+    mates = []
+    for dz in range(4):
+        for dy in range(2):
+            mates.append(((z + dz) % 4, flip(y, dy)))
+    groups = [(flip(x, dx), flip(c, dc)) for dx in range(2) for dc in range(2)]
+    barrier = pltpu.get_barrier_semaphore()
+    peers = [{"zh": a // 2, "zl": a % 2, "y": b} for a, b in mates[1:]]
+    peers += [{"x": a, "c": b} for a, b in groups[1:]]
+    for who in peers:
+        pl.semaphore_signal(barrier, inc=1, device_id=who, device_id_type=pl.DeviceIdType.MESH)
+    row = 0
+    for layer in range(LAYERS):
+        gd_in, gd_out, gu_in, gu_out = parts[4 * layer : 4 * layer + 4]
+        pieces = [gd_in[p * R : (p + 1) * R, :] for p in range(3)] + [gd_out[:R, :]]
+        pieces += [gu_in[p * R : (p + 1) * R, p * D : (p + 1) * D] for p in range(3)] + [gu_out[:R, :]]
+        for piece in pieces:
+            for s in range(8):
+                sbuf[s, row : row + R, :] = piece[:, s * SPAN : (s + 1) * SPAN].astype(BF)
+            row += R
+    sbuf[:, UNIT:, :] = jnp.broadcast_to(id_ref[0].astype(F32).astype(BF), (8, R, SPAN))
+    pl.semaphore_wait(barrier, len(peers))
+    me = 2 * z + y
+    copies = []
+    for n, (a, b) in enumerate(mates):
+        if n == 0:
+            rbuf[0] = sbuf[me]
+            continue
+        copy = pltpu.make_async_remote_copy(
+            src_ref=sbuf.at[2 * a + b],
+            dst_ref=rbuf.at[(4 - n // 2) % 4 * 2 + n % 2],
+            send_sem=asend.at[n],
+            recv_sem=arecv.at[(4 - n // 2) % 4 * 2 + n % 2],
+            device_id={"zh": a // 2, "zl": a % 2, "y": b},
+            device_id_type=pl.DeviceIdType.MESH,
         )
-        if split:
-            return [lax.all_gather(part, "z", axis=0) for part in (mine, other)]
-        w = jnp.where(y == 0, jnp.stack([mine, other]), jnp.stack([other, mine]))
-    w = lax.all_gather(w, "z", axis=0, tiled=True)
-    return [w.reshape(-1, w.shape[-1])]
-
-
-def exchange(v):
-    return lax.all_to_all(v, ("x", "c", "y"), split_axis=0, concat_axis=0, tiled=True)
+        copy.start()
+        copies.append(copy)
+    for copy in copies:
+        copy.wait()
+    masks = []
+    for n in range(8):
+        own = rbuf[n, UNIT : UNIT + R, :][0:1, 0:1].astype(F32)
+        masks.append([(own == k).astype(F32) for k in range(NA)])
+
+    def add(i, carry):
+        at = pl.ds(pl.multiple_of(i * 32, 32), 32)
+        sums = [jnp.zeros((32, SPAN), F32) for _ in range(NA)]
+        for n in range(8):
+            values = rbuf[n, at, :].astype(F32)
+            for k in range(NA):
+                sums[k] = sums[k] + values * masks[n][k]
+        for k in range(NA):
+            tbuf[k, at, :] = sums[k].astype(BF)
+        return carry
+
+    lax.fori_loop(0, UNIT // 32, add, 0)
+    copies = []
+    ubuf[0] = tbuf[pl.ds(2 * (2 * x + c), 2)]
+    for n, (a, b) in enumerate(groups):
+        if n == 0:
+            continue
+        copy = pltpu.make_async_remote_copy(
+            src_ref=tbuf.at[pl.ds(2 * (2 * a + b), 2)],
+            dst_ref=ubuf.at[n],
+            send_sem=bsend.at[n],
+            recv_sem=brecv.at[n],
+            device_id={"x": a, "c": b},
+            device_id_type=pl.DeviceIdType.MESH,
+        )
+        copy.start()
+        copies.append(copy)
+    for copy in copies:
+        copy.wait()
+    total = ubuf[0].astype(F32)
+    for n in range(1, 4):
+        total = total + ubuf[n].astype(F32)
+    o_ref[...] = total
+
+
+def adapters(own, parts):
+    specs = [pl.BlockSpec(memory_space=pltpu.SMEM)]
+    specs += [pl.BlockSpec(memory_space=pltpu.VMEM)] * len(parts)
+    return pl.pallas_call(
+        adapters_body,
+        in_specs=specs,
+        out_specs=pl.BlockSpec(memory_space=pltpu.VMEM),
+        out_shape=jax.ShapeDtypeStruct((2, UNIT, SPAN), F32),
+        scratch_shapes=[
+            pltpu.VMEM((8, UNIT + R, SPAN), BF),
+            pltpu.VMEM((8, UNIT + R, SPAN), BF),
+            pltpu.VMEM((NA, UNIT, SPAN), BF),
+            pltpu.VMEM((4, 2, UNIT, SPAN), BF),
+            DMA((8,)),
+            DMA((8,)),
+            DMA((4,)),
+            DMA((4,)),
+        ],
+        compiler_params=pltpu.CompilerParams(
+            vmem_limit_bytes=VMEM_BYTES, collective_id=4, has_side_effects=True
+        ),
+        name="adapters",
+    )(own, *parts)
+
+
+def both_rows(mine, other):
+    y = lax.axis_index("y")
+    return jnp.where(y == 0, jnp.stack([mine, other]), jnp.stack([other, mine]))
+
+
+def own_and_other(w):
+    y = lax.axis_index("y")
+    return [lax.dynamic_index_in_dim(w, e, axis=0, keepdims=False) for e in (y, 1 - y)]
+
+
+def across_y(v):
+    return lax.ppermute(v, "y", [(0, 1), (1, 0)])
+
+
+def move_expert(w):
+    mine, other = own_and_other(w)
+    return both_rows(mine, across_y(other))
+
+
+def gathered(w, axes):
+    return lax.all_gather(w, axes, axis=0, tiled=True).reshape(-1, w.shape[-1])
+
+
+def exchange(v, kind):
+    return lax.all_to_all(v, OWNERS[kind], split_axis=0, concat_axis=0, tiled=True)
 
 
 def pad_to(v, shape):
     return jnp.pad(v, [(0, n - m) for m, n in zip(v.shape, shape)])
+
+
+def adapters_plain(owners, parts):
+    layers = []
+    for gd_in, gd_out, gu_in, gu_out in parts:
+        downs = [gd_in[p * R : (p + 1) * R] for p in range(3)] + [gd_out[:R]]
+        ups = [gu_in[p * R : (p + 1) * R, p * D : (p + 1) * D] for p in range(3)] + [gu_out[:R]]
+        layers.append(jnp.concatenate(downs + ups))
+    compact = jnp.concatenate(layers).astype(BF)
+    ranks = lax.axis_size(SHARD)
+    pieces = compact.reshape(UNIT, ranks, D // ranks).transpose(1, 0, 2)
+    pieces = lax.all_to_all(pieces, SHARD, split_axis=0, concat_axis=0, tiled=True)
+    pick = (owners[None, :] == jnp.arange(NA, dtype=jnp.int32)[:, None]).astype(F32)
+    summed = jnp.dot(pick, pieces.reshape(ranks, -1).astype(F32), precision=HIGHEST).astype(BF)
+    groups = lax.axis_size(EXPERT)
+    summed = lax.all_to_all(
+        summed.reshape(groups, NA // groups, -1), EXPERT, split_axis=0, concat_axis=0, tiled=True
+    )
+    return jnp.sum(summed.astype(F32), axis=0)
 
 
 def per_device(
@@ -1171,13 +1399,21 @@
     w_down,
     out_grad,
 ):
-    each = w_gate_up.shape[1]
-    gate_up_full = []
-    down_full = []
-    for layer in range(LAYERS):
-        gate_up_full.append(gather_expert(w_gate_up[layer], layer == 0))
-        down_full.append(gather_expert(w_down[layer], False)[0])
-    shared = [gather_shared(query_key_value_weight[0], output_weight[0])]
+    fast = w_gate_up.shape[1] == 2
+    kind = PLANE if fast else WIDE_SLICE
+    barrier = lax.optimization_barrier
+    if fast:
+        mine, other = own_and_other(w_gate_up[0])
+        parts = [lax.all_gather(mine, ("zh", "zl"), axis=0)]
+        shared = [gather_shared(query_key_value_weight[0], output_weight[0])]
+        other, down_first, shared[0] = barrier((other, w_down[0], shared[0]))
+        parts.append(lax.all_gather(across_y(other), ("zh", "zl"), axis=0))
+        gate_up_full = [parts]
+        down_full = [gathered(move_expert(down_first), ("zh", "zl"))]
+    else:
+        shared = [gather_shared(query_key_value_weight[0], output_weight[0])]
+        gate_up_full = [[gathered(w_gate_up[layer, 0], SHARD)] for layer in range(LAYERS)]
+        down_full = [gathered(w_down[layer, 0], SHARD) for layer in range(LAYERS)]
 
     which = adapter_of[0]
     down_sel = lax.dynamic_index_in_dim(adapter_down, which, axis=2, keepdims=False)
@@ -1215,69 +1451,56 @@
             stream, mixed, shared[layer], down_out[layer], up_out[layer], gain1, router_s[layer],
             earlier, residual_s,
         )
-        received = exchange(dispatch(trow, sent))
+        received = exchange(dispatch(trow, sent), kind)
         if layer == 0:
+            if fast:
+                later = barrier((w_gate_up[1], w_down[1], logits))
+                gate_up_full.append([gathered(move_expert(later[0]), ("zh", "zl"))])
+                down_full.append(gathered(move_expert(later[1]), ("zh", "zl")))
             later = lax.optimization_barrier(
                 (query_key_value_weight[1], output_weight[1], logits)
             )
             shared.append(gather_shared(later[0], later[1]))
-            returned, gate, up = expert_forward(received, gate_up_full[0], down_full[0], each)
+            returned, gate, up = expert_forward(received, gate_up_full[0], down_full[0], kind)
         else:
-            slot_grads = exchange(dispatch_grad(trow, out_grad, logits, routes))
-            returned, back = expert_both(
-                received, slot_grads, gate_up_full[1][0], down_full[1], each
+            slot_grads = exchange(dispatch_grad(trow, out_grad, logits, routes), kind)
+            back, following, grad_normed, grad_logits = expert_both(
+                received, slot_grads, gate_up_full[1][0], down_full[1], mid, out_grad, tcol, logits,
+                routes, gain1, const_vec[1], router_ts[1], residual_ts, kind,
             )
-        following, c0, c1 = combine(
-            tcol, returned.reshape(SLOTS, D), mid, logits, routes, gain1, const_vec[layer]
-        )
+            c0 = c1 = None
+        if layer == 0:
+            following, c0, c1 = combine(
+                tcol, returned.reshape(SLOTS, D), mid, logits, routes, gain1, const_vec[0]
+            )
         saved.append((stream, normed, narrow, qkv, mixed, aug, mid, logits, narrow_out, c0, c1))
         stream = following
         earlier = logits
 
     grad = out_grad
-    grad_logits = jnp.zeros((T, 128), F32)
-    tree_grads = [None] * LAYERS
+    parts = [None] * LAYERS
     for layer in reversed(range(LAYERS)):
         x_in, normed, narrow, qkv, mixed, aug, mid, logits, narrow_out, c0, c1 = saved[layer]
         gain0 = norm_gain[layer, 0:1]
         gain1 = norm_gain[layer, 1:2]
         if layer == 0:
-            back = expert_backward(
-                dispatch_grad(trow, grad, logits, routes), gate, up, gate_up_full[0], down_full[0],
-                each,
+            back, grad_normed = expert_backward(
+                gate, up, gate_up_full[0], down_full[0], grad, mid, c0, c1, trow, logits, routes,
+                grad_logits, gain1, const_vec[0], router_ts[0], kind,
             )
-        grad_mid, grad_mixed, grad_earlier, gu_out, gd_out = settle_grad(
-            tcol, back.reshape(SLOTS, D), mid, grad, c0, c1, logits, routes, grad_logits, gain1,
-            const_vec[layer], router_ts[layer], residual_ts, mixed, narrow_out, shared[layer],
-            down_out[layer], up_out[layer],
+        grad, gu_out, gd_out, gu_in, gd_in = layer_back(
+            back.reshape(SLOTS, D), grad_normed, mid, grad, mixed, shared[layer], qkv, aug, normed,
+            x_in, tcol, gain1, gain0, narrow_out, narrow, down_out[layer], up_out[layer],
+            down_in[layer], up_in[layer], kf, cos, sin,
         )
-        gq, gk, gv = attend_grad(qkv, aug, kf, grad_mixed, mixed, cos, sin)
-        grad, gu_in, gd_in = project_grad(
-            gq, gk, gv, shared[layer], down_in[layer], up_in[layer], normed, narrow, x_in, gain0,
-            grad_mid,
-        )
-        grad_logits = grad_earlier
-        downs = [gd_in[p * R : (p + 1) * R] for p in range(3)] + [gd_out[:R]]
-        ups = [gu_in[p * R : (p + 1) * R, p * D : (p + 1) * D] for p in range(3)] + [gu_out[:R]]
-        tree_grads[layer] = jnp.stack([jnp.stack(downs), jnp.stack(ups)])
-
-    compact = jnp.stack(tree_grads).astype(BF)
-    ranks = lax.axis_size("z") * lax.axis_size("y")
-    span = D // ranks
-    pieces = compact.reshape(LAYERS, 2, 4, R, ranks, span).transpose(4, 0, 1, 2, 3, 5)
-    pieces = lax.all_to_all(pieces, ("z", "y"), split_axis=0, concat_axis=0, tiled=True)
-    owners = lax.all_gather(adapter_of, ("z", "y"), axis=0, tiled=True)
-    pick = (owners[None, :] == jnp.arange(NA, dtype=jnp.int32)[:, None]).astype(F32)
-    summed = jnp.dot(
-        pick, pieces.reshape(ranks, -1).astype(F32), precision=HIGHEST
-    ).astype(BF)
-    groups = lax.axis_size("x") * lax.axis_size("c")
-    each = NA // groups
-    summed = lax.all_to_all(
-        summed.reshape(groups, each, -1), ("x", "c"), split_axis=0, concat_axis=0, tiled=True
-    )
-    final = jnp.sum(summed.astype(F32), axis=0).reshape(each, LAYERS, 2, 4, R, span)
-    final = final.transpose(2, 1, 3, 0, 5, 4)
+        parts[layer] = (gd_in, gd_out, gu_in, gu_out)
+
+    if usual():
+        final = adapters(adapter_of, [v for layer in parts for v in layer])
+    else:
+        final = adapters_plain(lax.all_gather(adapter_of, SHARD, axis=0, tiled=True), parts)
+    share = final.shape[0]
+    final = final.reshape(share, LAYERS, 2, 4, R, -1).transpose(2, 1, 3, 0, 5, 4)
     return (stream, grad, final[0], final[1])
 
 
@@ -1285,10 +1508,9 @@
     owners, shards = mesh.shape["expert"], mesh.shape["shard"]
     each = NFFN // owners
     fine = jax.sharding.Mesh(
-        mesh.devices.reshape(owners // 2, 2, shards // each, each), ("x", "c", "z", "y")
-    )
-    expert, shard = ("x", "c"), ("z", "y")
-    both = expert + shard
+        mesh.devices.reshape(owners // 2, 2, shards // each**2, each, each), AXES
+    )
+    expert, shard, both = EXPERT, SHARD, AXES
     in_specs = (
         P(both, None),
         P(both, None),

time: 753 us -> 702 us (0.932)
  blocking collectives: 22.1 us -> 0 us
  Pallas kernels: 545 us -> 528 us
  waiting for transfers between devices: 84.4 us -> 95.3 us
  local copies, waits for them, and re-layouts: 41.6 us -> 33.9 us
    pallas_call x19 -> x11, Pallas kernels: 294 us -> 123 us  [call(): pl.pallas_call(body, grid=grid, in_specs=[spec(e) for e in ins], out_spec...]
    pallas_call x5 -> x8, Pallas kernels: 250 us -> 405 us  [the longest x5 271 us: comm_call(): pl.pallas_call(body, in_specs=ins_specs, out_specs=outs_specs, out_shape=...]
    ppermute x4, waiting for transfers between devices: 25.3 us -> 49.9 us  [across_y(): return lax.ppermute(v, 'y', [(0, 1), (1, 0)])]
    all_gather x5, waiting for transfers between devices: 13.8 us -> 0.03 us  [the longest x1 0.02 us: per_device(): parts.append(lax.all_gather(across_y(other), ('zh', 'zl'), axis=0))]
    all_to_all x1 -> x0, blocking collectives: 11.7 us -> none  [per_device(): lax.all_to_all(summed.reshape(groups, each, -1), ('x', 'c'), split_axis=0...]
    unnamed x1 -> x0, blocking collectives: 10.4 us -> none
    all_to_all x4 -> x3, starting transfers between devices: 19.2 us -> 17.5 us  [exchange(): lax.all_to_all(v, OWNERS[kind], split_axis=0, concat_axis=0, tiled=True)]
    all_to_all x4 -> x3, waiting for transfers between devices: 45.2 us -> 45.2 us  [exchange(): lax.all_to_all(v, OWNERS[kind], split_axis=0, concat_axis=0, tiled=True)]
  transfers between devices with their start and end apart: 13 -> 12, of which waited for: 5 -> 6; matrix products, arithmetic and copies ran while one was open for 5% -> 5% of each run, Pallas kernels for 33% -> 37%
where the time goes in v3:
time: 702 us; the launch traced here: 698 us
  Pallas kernels  528 us (75%)
  waiting for transfers between devices  95.3 us (14%)
  local copies, waits for them, and re-layouts  33.9 us (5%)
  starting transfers between devices  19.1 us (3%)
  between operations  15.1 us (2%)
    pallas_call x5, Pallas kernels, comm_call(): pl.pallas_call(body, in_specs=ins_specs, out_specs=outs_specs, out_shape=...  271 us
    pallas_call x11, Pallas kernels, call(): pl.pallas_call(body, grid=grid, in_specs=[spec(e) for e in ins], out_spec...  123 us
    pallas_call x2, Pallas kernels, layer_back(): pl.pallas_call(layer_back_body, in_specs=[anywhere] * len(far) + [close]...  106 us
    ppermute x4, waiting for transfers between devices, across_y(): return lax.ppermute(v, 'y', [(0, 1), (1, 0)])  49.9 us
    all_to_all x3, waiting for transfers between devices, exchange(): lax.all_to_all(v, OWNERS[kind], split_axis=0, concat_axis=0, tiled=True)  45.2 us
    pallas_call x1, Pallas kernels, adapters(): pl.pallas_call(adapters_body, in_specs=specs, out_specs=pl.BlockSpec(memo...  27.9 us
    all_to_all x3, starting transfers between devices, exchange(): lax.all_to_all(v, OWNERS[kind], split_axis=0, concat_axis=0, tiled=True)  17.5 us
  transfers between devices with their start and end apart: 12, of which 6 were waited for; matrix products, arithmetic and copies ran while one was open for 5% of the time, Pallas kernels for 37%

profile of v3, /device:TPU:9, one launch (start us, length us, event | category | flops | bytes accessed | tf_op | source)
XLA Modules:
  0.0 698.0 jit_solution(17150163119995873310)
XLA Ops:
  15.6 46.5 %gather_shared.2.w_ref = bf16[4,768,768]{2,1,0:T(8,128)(2,1)} custom-call(bf16[96,768]{1,0:T(8,128)(2,1)} %bitcast.126), custom_call_target="tpu_custom_call" | custom-call | bytes 50000000 | tf_op jit(solution)/shard_map/gather_shared/pallas_call | solution.py:573
  63.2 10.8 %collective-permute-done.3 = bf16[256,768]{1,0:T(8,128)(2,1)S(1)} collective-permute-done((bf16[256,768]{1,0:T(8,128)(2,1)S(1)}, bf16[256,768]{1,0:T(8,128)(2,1)S(1)}, u32[]{:S(2)}, u32[]{:S(2)}) %collective-permute-start.3) | collective-permute-done | bytes 393248 | tf_op jit(solution)/shard_map/ppermute | solution.py:1344
  79.7 14.1 %collective-permute-done.2 = bf16[96,4096]{1,0:T(8,128)(2,1)} collective-permute-done((bf16[96,4096]{1,0:T(8,128)(2,1)}, bf16[96,4096]{1,0:T(8,128)(2,1)}, u32[]{:S(2)}, u32[]{:S(2)}) %collective-permute-start.2) | collective-permute-done | bytes 786464 | tf_op jit(solution)/shard_map/ppermute | solution.py:1344
  116.5 11.1 %project.2 = (bf16[1024,768]{1,0:T(8,128)(2,1)}, bf16[1024,128]{1,0:T(8,128)(2,1)}, bf16[1024,2304]{1,0:T(8,128)(2,1)}) custom-call(bf16[1024,768]{1,0:T(8,128)(2,1)} %x_ref.5, f32[1,768]{1,0:T(1,128)} %get-tuple-element.192.g_ref.gain0_ref, bf16[4,768,768]{2,1,0:T(8,128)(2,1)} %gather_shared.2.w_ref, bf16[768,128]{1,0:T(8,128)(2,1)} %get-tuple-element.177.d_ref, ...), custom_call_target="tpu_custom_call" | custom-call | flops 3623878656 | bytes 12000000 | tf_op jit(solution)/shard_map/project/pallas_call | solution.py:71
  127.6 21.3 %attend.2 = (bf16[1024,768]{1,0:T(8,128)(2,1)}, bf16[6,1024,128]{2,1,0:T(8,128)(2,1)}) custom-call(bf16[1024,2304]{1,0:T(8,128)(2,1)} %get-tuple-element.100.q_ref.k_ref.v_ref.qkv_ref, bf16[1024,2304]{1,0:T(8,128)(2,1)} %get-tuple-element.100.q_ref.k_ref.v_ref.qkv_ref, bf16[1024,2304]{1,0:T(8,128)(2,1)} %get-tuple-element.100.q_ref.k_ref.v_ref.qkv_ref, ...), custom_call_target="tpu_custom_call" | custom-call | flops 6442450944 | bytes 8000000 | tf_op jit(solution)/shard_map/attend/pallas_call | solution.py:71
  149.8 8.6 %settle.2 = (f32[1024,768]{1,0:T(8,128)}, bf16[1024,768]{1,0:T(8,128)(2,1)}, f32[1024,128]{1,0:T(8,128)}, bf16[1024,128]{1,0:T(8,128)(2,1)}) custom-call(bf16[1024,768]{1,0:T(8,128)(2,1)} %x_ref.5, bf16[1024,768]{1,0:T(8,128)(2,1)} %get-tuple-element.103.mixed_ref, bf16[4,768,768]{2,1,0:T(8,128)(2,1)} %gather_shared.2.w_ref, ...), custom_call_target="tpu_custom_call" | custom-call | flops 2415919104 | bytes 10000000 | tf_op jit(solution)/shard_map/settle/pallas_call | solution.py:71
  158.8 8.8 %collective-permute-done.1 = bf16[256,768]{1,0:T(8,128)(2,1)S(1)} collective-permute-done((bf16[256,768]{1,0:T(8,128)(2,1)S(1)}, bf16[256,768]{1,0:T(8,128)(2,1)S(1)}, u32[]{:S(2)}, u32[]{:S(2)}) %collective-permute-start.1) | collective-permute-done | bytes 393248 | tf_op jit(solution)/shard_map/ppermute | solution.py:1344
  169.5 16.2 %collective-permute-done = bf16[96,4096]{1,0:T(8,128)(2,1)S(1)} collective-permute-done((bf16[96,4096]{1,0:T(8,128)(2,1)S(1)}, bf16[96,4096]{1,0:T(8,128)(2,1)S(1)}, u32[]{:S(2)}, u32[]{:S(2)}) %collective-permute-start) | collective-permute-done | bytes 786464 | tf_op jit(solution)/shard_map/ppermute | solution.py:1344
  194.0 7.8 %all-to-all-start = ((bf16[8,192,768]{2,1,0:T(8,128)(2,1)}), bf16[8,192,768]{2,1,0:T(8,128)(2,1)}, u32[]{:S(2)}, u32[]{:S(2)}) async-start(bf16[8,192,768]{2,1,0:T(8,128)(2,1)} %dispatch.2), calls=%async_computation | async-start | bytes 4718592 | tf_op jit(solution)/shard_map/all_to_all | solution.py:1357
  204.0 47.7 %gather_shared.3.w_ref = bf16[4,768,768]{2,1,0:T(8,128)(2,1)} custom-call(bf16[96,768]{1,0:T(8,128)(2,1)} %bitcast.127), custom_call_target="tpu_custom_call" | custom-call | bytes 50000000 | tf_op jit(solution)/shard_map/gather_shared/pallas_call | solution.py:573
  252.4 37.7 %expert_forward.1 = (bf16[8,192,768]{2,1,0:T(8,128)(2,1)}, bf16[4,384,2048]{2,1,0:T(8,128)(2,1)}, bf16[4,384,2048]{2,1,0:T(8,128)(2,1)}) custom-call(bf16[4,96,4096]{2,1,0:T(8,128)(2,1)} %bitcast.136, bf16[4,96,4096]{2,1,0:T(8,128)(2,1)} %bitcast.140, bf16[2048,768]{1,0:T(8,128)(2,1)} %bitcast.138, bf16[8,192,768]{2,1,0:T(8,128)(2,1)} %all-to-all-done.refs_3_), custom_call_target="tpu_custom_call" | custom-call | flops 14495514624 | bytes 26000000 | tf_op jit(solution)/shard_map/expert_forward/pallas_call | solution.py:573
  290.1 10.2 %combine.1 = (f32[1024,768]{1,0:T(8,128)}, bf16[1024,768]{1,0:T(8,128)(2,1)}, bf16[1024,768]{1,0:T(8,128)(2,1)}) custom-call(s32[1024,128]{1,0:T(8,128)} %get-tuple-element.110.tcol_ref.refs_6_, bf16[1536,768]{1,0:T(8,128)(2,1)} %bitcast.145, f32[1024,768]{1,0:T(8,128)} %get-tuple-element.115.mid_ref.refs_6_, ...), custom_call_target="tpu_custom_call" | custom-call | flops 4831838208 | bytes 12000000 | tf_op jit(solution)/shard_map/combine/pallas_call | solution.py:71
  300.3 11.1 %project.3 = (bf16[1024,768]{1,0:T(8,128)(2,1)}, bf16[1024,128]{1,0:T(8,128)(2,1)}, bf16[1024,2304]{1,0:T(8,128)(2,1)}) custom-call(f32[1024,768]{1,0:T(8,128)} %get-tuple-element.116.x_ref, f32[1,768]{1,0:T(1,128)} %get-tuple-element.193.g_ref.gain0_ref, bf16[4,768,768]{2,1,0:T(8,128)(2,1)} %gather_shared.3.w_ref, ...), custom_call_target="tpu_custom_call" | custom-call | flops 3623878656 | bytes 12000000 | tf_op jit(solution)/shard_map/project/pallas_call | solution.py:71
  311.4 21.7 %attend.3 = (bf16[1024,768]{1,0:T(8,128)(2,1)}, bf16[6,1024,128]{2,1,0:T(8,128)(2,1)}) custom-call(bf16[1024,2304]{1,0:T(8,128)(2,1)} %get-tuple-element.119.q_ref.k_ref.v_ref.qkv_ref, bf16[1024,2304]{1,0:T(8,128)(2,1)} %get-tuple-element.119.q_ref.k_ref.v_ref.qkv_ref, bf16[1024,2304]{1,0:T(8,128)(2,1)} %get-tuple-element.119.q_ref.k_ref.v_ref.qkv_ref, ...), custom_call_target="tpu_custom_call" | custom-call | flops 6442450944 | bytes 8000000 | tf_op jit(solution)/shard_map/attend/pallas_call | solution.py:71
  333.1 8.7 %settle.3 = (f32[1024,768]{1,0:T(8,128)}, bf16[1024,768]{1,0:T(8,128)(2,1)}, f32[1024,128]{1,0:T(8,128)}, bf16[1024,128]{1,0:T(8,128)(2,1)}) custom-call(f32[1024,768]{1,0:T(8,128)} %get-tuple-element.116.x_ref, bf16[1024,768]{1,0:T(8,128)(2,1)} %get-tuple-element.120.mixed_ref, bf16[4,768,768]{2,1,0:T(8,128)(2,1)} %gather_shared.3.w_ref, ...), custom_call_target="tpu_custom_call" | custom-call | flops 2415919104 | bytes 10000000 | tf_op jit(solution)/shard_map/settle/pallas_call | solution.py:71
  341.8 6.9 dispatch.3
  353.3 10.3 %dispatch_grad.1 = bf16[8,192,768]{2,1,0:T(8,128)(2,1)} custom-call(s32[8,1024]{1,0:T(8,128)} %get-tuple-element.109.trow_ref.refs_9_, bf16[1024,768]{1,0:T(8,128)(2,1)} %g_ref.3, f32[1024,128]{1,0:T(8,128)} %get-tuple-element.122.lg_ref.refs_7_, s32[1024,2]{1,0:T(8,128)} %copy.85.rt_ref.refs_8_.refs_11_), custom_call_target="tpu_custom_call" | custom-call | flops 4831838208 | bytes 6000000 | tf_op jit(solution)/shard_map/dispatch_grad/pallas_call | solution.py:71
  363.7 17.9 %all-to-all-done.1.refs_2_ = bf16[8,192,768]{2,1,0:T(8,128)(2,1)} async-done(((bf16[8,192,768]{2,1,0:T(8,128)(2,1)}), bf16[8,192,768]{2,1,0:T(8,128)(2,1)}, u32[]{:S(2)}, u32[]{:S(2)}) %all-to-all-start.1) | async-done | bytes 2359328 | tf_op jit(solution)/shard_map/all_to_all | solution.py:1357
  387.3 27.4 %all-to-all-done.2.refs_3_ = bf16[8,192,768]{2,1,0:T(8,128)(2,1)} async-done(((bf16[8,192,768]{2,1,0:T(8,128)(2,1)}), bf16[8,192,768]{2,1,0:T(8,128)(2,1)}, u32[]{:S(2)}, u32[]{:S(2)}) %all-to-all-start.2) | async-done | bytes 2359328 | tf_op jit(solution)/shard_map/all_to_all | solution.py:1357
  414.7 68.6 %expert_both.1 = (bf16[8,192,768]{2,1,0:T(8,128)(2,1)}, f32[1024,768]{1,0:T(8,128)}, f32[1024,768]{1,0:T(8,128)}, f32[1024,128]{1,0:T(8,128)}) custom-call(bf16[768,4096]{1,0:T(8,128)(2,1)} %bitcast.135, bf16[2048,768]{1,0:T(8,128)(2,1)} %bitcast.142, bf16[8,192,768]{2,1,0:T(8,128)(2,1)} %all-to-all-done.1.refs_2_, ...), custom_call_target="tpu_custom_call" | custom-call | flops 28991029248 | bytes 26000000 | tf_op jit(solution)/shard_map/expert_both/pallas_call | solution.py:573
  483.3 53.0 %layer_back.2 = (f32[1024,768]{1,0:T(8,128)}, f32[128,768]{1,0:T(8,128)}, f32[128,768]{1,0:T(8,128)}, f32[128,2304]{1,0:T(8,128)}, f32[128,768]{1,0:T(8,128)}) custom-call(bf16[1536,768]{1,0:T(8,128)(2,1)} %bitcast.144, f32[1024,768]{1,0:T(8,128)} %get-tuple-element.130.gn_ref, f32[1024,768]{1,0:T(8,128)} %get-tuple-element.123.refs_4_.mid_ref, ...), custom_call_target="tpu_custom_call" | custom-call | flops 22145925120 | bytes 40000000 | tf_op jit(solution)/shard_map/layer_back/pallas_call | solution.py:1087
  536.3 70.4 %expert_backward.1 = (bf16[8,192,768]{2,1,0:T(8,128)(2,1)}, f32[1024,768]{1,0:T(8,128)}) custom-call(bf16[4,96,4096]{2,1,0:T(8,128)(2,1)} %bitcast.137, bf16[4,96,4096]{2,1,0:T(8,128)(2,1)} %bitcast.141, bf16[2048,768]{1,0:T(8,128)(2,1)} %bitcast.139, bf16[4,384,2048]{2,1,0:T(8,128)(2,1)} %get-tuple-element.127.refs_3_, ...), custom_call_target="tpu_custom_call" | custom-call | flops 14495514624 | bytes 26000000 | tf_op jit(solution)/shard_map/expert_backward/pallas_call | solution.py:573
  606.8 53.2 %layer_back.3 = (f32[1024,768]{1,0:T(8,128)}, f32[128,768]{1,0:T(8,128)}, f32[128,768]{1,0:T(8,128)}, f32[128,2304]{1,0:T(8,128)}, f32[128,768]{1,0:T(8,128)}) custom-call(bf16[1536,768]{1,0:T(8,128)(2,1)} %bitcast.143, f32[1024,768]{1,0:T(8,128)} %get-tuple-element.140.gn_ref, f32[1024,768]{1,0:T(8,128)} %get-tuple-element.115.mid_ref.refs_6_, ...), custom_call_target="tpu_custom_call" | custom-call | flops 22145925120 | bytes 40000000 | tf_op jit(solution)/shard_map/layer_back/pallas_call | solution.py:1087
  660.0 27.9 %adapters.1 = f32[2,256,96]{2,1,0:T(8,128)} custom-call(s32[1]{0:T(128)} %copy.112.refs_0_, f32[128,768]{1,0:T(8,128)} %get-tuple-element.146.refs_1_, f32[128,768]{1,0:T(8,128)} %get-tuple-element.147.refs_2_, f32[128,2304]{1,0:T(8,128)} %get-tuple-element.148.refs_3_, f32[128,768]{1,0:T(8,128)} %get-tuple-element.149.refs_4_, ...), custom_call_target="tpu_custom_call" | custom-call | tf_op jit(solution)/shard_map/adapters/pallas_call | solution.py:1311
  (108 shorter events, 65.0 us)
Async XLA Ops:
  7.2 245.2 %all-gather.14.cloned.1.call-start = ((), (), s32[]{:S(2)}) async-start(), calls=%async_computation.6 | async-start | bytes 3932160 | tf_op jit(solution)/shard_map/all_gather | solution.py:1407
  10.7 241.7 %all-gather.12.cloned.1.call-start = ((), (), s32[]{:S(2)}) async-start(), calls=%async_computation.5 | async-start | bytes 3932160 | tf_op jit(solution)/shard_map/all_gather | solution.py:1353
  15.6 46.5 %copy-start.3 = (bf16[2,2,256,768]{3,2,1,0:T(8,128)(2,1)S(1)}, bf16[2,2,256,768]{3,2,1,0:T(8,128)(2,1)}, u32[]{:S(2)}) copy-start(bf16[2,2,256,768]{3,2,1,0:T(8,128)(2,1)} %param.38) | copy-start | bytes 4718596
  63.2 10.8 %collective-permute-start.3 = (bf16[256,768]{1,0:T(8,128)(2,1)S(1)}, bf16[256,768]{1,0:T(8,128)(2,1)S(1)}, u32[]{:S(2)}, u32[]{:S(2)}) collective-permute-start(bf16[256,768]{1,0:T(8,128)(2,1)S(1)} %get-tuple-element.167), channel_id=1, source_target_pairs={{0,1},{1,0},{2,3},{3,2},{4,5},{5,4},{6,7},{7,6},{8,9},{9,8},{10,11... | collective-permute-start | bytes 1179656 | tf_op jit(solution)/shard_map/ppermute | solution.py:1344
  75.1 177.4 %all-gather.16.cloned.1.call-start = ((), (), s32[]{:S(2)}) async-start(), calls=%async_computation.7 | async-start | bytes 3932160 | tf_op jit(solution)/shard_map/all_gather | solution.py:1410
  75.1 18.7 %collective-permute-start.2 = (bf16[96,4096]{1,0:T(8,128)(2,1)}, bf16[96,4096]{1,0:T(8,128)(2,1)}, u32[]{:S(2)}, u32[]{:S(2)}) collective-permute-start(bf16[96,4096]{1,0:T(8,128)(2,1)} %get-tuple-element.111), channel_id=1, source_target_pairs={{0,1},{1,0},{2,3},{3,2},{4,5},{5,4},{6,7},{7,6},{8,9},{9,8},{10,11... | collective-permute-start | bytes 2359304 | tf_op jit(solution)/shard_map/ppermute | solution.py:1344
  78.5 15.5 %copy-start.11 = (f32[2,2,768,2]{2,3,1,0:T(2,128)S(1)}, f32[2,2,768,2]{2,3,1,0:T(2,128)}, u32[]{:S(2)}) copy-start(f32[2,2,768,2]{2,3,1,0:T(2,128)} %param.35) | copy-start | bytes 73732
  78.6 15.5 %copy-start.10 = (f32[12,12]{1,0:T(8,128)S(1)}, f32[12,12]{1,0:T(8,128)}, u32[]{:S(2)}) copy-start(f32[12,12]{1,0:T(8,128)} %param.34) | copy-start | bytes 1732
  78.6 16.8 %copy-start.9 = (f32[2,768,12]{1,0,2:T(2,128)S(1)}, f32[2,768,12]{1,0,2:T(2,128)}, u32[]{:S(2)}) copy-start(f32[2,768,12]{1,0,2:T(2,128)} %param.33) | copy-start | bytes 221188
  78.6 16.8 %copy-start.14 = (s32[1024,2]{0,1:T(2,128)S(1)}, s32[1024,2]{0,1:T(2,128)}, u32[]{:S(2)}) copy-start(s32[1024,2]{0,1:T(2,128)} %param.27) | copy-start | bytes 24580
  78.6 17.9 %copy-start.15 = (s32[1,1024]{1,0:T(1,128)S(1)}, s32[1,1024]{1,0:T(1,128)}, u32[]{:S(2)}) copy-start(s32[1,1024]{1,0:T(1,128)} %param.24) | copy-start | bytes 12292
  93.8 293.5 %all-gather.10.cloned.1.call-start = ((), (), s32[]{:S(2)}) async-start(), calls=%async_computation.4 | async-start | bytes 3932160 | tf_op jit(solution)/shard_map/all_gather | solution.py:1353
  149.8 8.6 %copy-start.1 = (bf16[2,256,768]{2,1,0:T(8,128)(2,1)S(1)}, bf16[2,256,768]{2,1,0:T(8,128)(2,1)}, u32[]{:S(2)}) copy-start(bf16[2,256,768]{2,1,0:T(8,128)(2,1)} %get-tuple-element.108) | copy-start | bytes 2359300
  158.5 9.2 %collective-permute-start.1 = (bf16[256,768]{1,0:T(8,128)(2,1)S(1)}, bf16[256,768]{1,0:T(8,128)(2,1)S(1)}, u32[]{:S(2)}, u32[]{:S(2)}) collective-permute-start(bf16[256,768]{1,0:T(8,128)(2,1)S(1)} %get-tuple-element.169), channel_id=1, source_target_pairs={{0,1},{1,0},{2,3},{3,2},{4,5},{5,4},{6,7},{7,6},{8,9},{9,8},{10,11... | collective-permute-start | bytes 1179656 | tf_op jit(solution)/shard_map/ppermute | solution.py:1344
  168.7 246.0 %all-gather.8.cloned.1.call-start = ((), (), s32[]{:S(2)}) async-start(), calls=%async_computation.3 | async-start | bytes 7864320 | tf_op jit(solution)/shard_map/all_gather | solution.py:1353
  169.0 16.7 %collective-permute-start = (bf16[96,4096]{1,0:T(8,128)(2,1)S(1)}, bf16[96,4096]{1,0:T(8,128)(2,1)S(1)}, u32[]{:S(2)}, u32[]{:S(2)}) collective-permute-start(bf16[96,4096]{1,0:T(8,128)(2,1)S(1)} %get-tuple-element.159), channel_id=1, source_target_pairs={{0,1},{1,0},{2,3},{3,2},{4,5},{5,4},{6,7},{7,6},{8,9},{9,8},{10,11... | collective-permute-start | bytes 2359304 | tf_op jit(solution)/shard_map/ppermute | solution.py:1344
  194.0 7.8 %copy-start.4 = (bf16[96,768]{1,0:T(8,128)(2,1)S(1)}, bf16[96,768]{1,0:T(8,128)(2,1)}, u32[]{:S(2)}) copy-start(bf16[96,768]{1,0:T(8,128)(2,1)} %get-tuple-element.118) | copy-start | bytes 442372
  194.0 8.0 %copy-start.2 = (bf16[96,2304]{1,0:T(8,128)(2,1)S(1)}, bf16[96,2304]{1,0:T(8,128)(2,1)}, u32[]{:S(2)}) copy-start(bf16[96,2304]{1,0:T(8,128)(2,1)} %get-tuple-element.117) | copy-start | bytes 1327108
  194.0 58.3 %all-to-all-start = ((bf16[8,192,768]{2,1,0:T(8,128)(2,1)}), bf16[8,192,768]{2,1,0:T(8,128)(2,1)}, u32[]{:S(2)}, u32[]{:S(2)}) async-start(bf16[8,192,768]{2,1,0:T(8,128)(2,1)} %dispatch.2), calls=%async_computation | async-start | bytes 4718592 | tf_op jit(solution)/shard_map/all_to_all | solution.py:1357
  204.0 47.7 %copy-start.13 = (f32[2,2,768]{2,1,0:T(2,128)S(1)}, f32[2,2,768]{2,1,0:T(2,128)}, u32[]{:S(2)}) copy-start(f32[2,2,768]{2,1,0:T(2,128)} %param.36) | copy-start | bytes 36868
  348.7 32.9 %all-to-all-start.1 = ((bf16[8,192,768]{2,1,0:T(8,128)(2,1)}), bf16[8,192,768]{2,1,0:T(8,128)(2,1)}, u32[]{:S(2)}, u32[]{:S(2)}) async-start(bf16[8,192,768]{2,1,0:T(8,128)(2,1)} %dispatch.3), calls=%async_computation.1 | async-start | bytes 4718592 | tf_op jit(solution)/shard_map/all_to_all | solution.py:1357
  363.7 22.9 %copy-start.6 = (bf16[2,128,768]{2,1,0:T(8,128)(2,1)S(1)}, bf16[2,128,768]{2,1,0:T(8,128)(2,1)}, u32[]{:S(2)}) copy-start(bf16[2,128,768]{2,1,0:T(8,128)(2,1)} %get-tuple-element.124) | copy-start | bytes 1179652
  381.6 33.1 %all-to-all-start.2 = ((bf16[8,192,768]{2,1,0:T(8,128)(2,1)}), bf16[8,192,768]{2,1,0:T(8,128)(2,1)}, u32[]{:S(2)}, u32[]{:S(2)}) async-start(bf16[8,192,768]{2,1,0:T(8,128)(2,1)} %dispatch_grad.1), calls=%async_computation.2 | async-start | bytes 4718592 | tf_op jit(solution)/shard_map/all_to_all | solution.py:1357
  660.0 29.6 %copy-start = (f32[1024,768]{1,0:T(8,128)S(1)}, f32[1024,768]{1,0:T(8,128)}, u32[]{:S(2)}) copy-start(f32[1024,768]{1,0:T(8,128)} %get-tuple-element.200) | copy-start | bytes 9437188
  (4 other events, 12.5 us)
Sparse Core Ops, SparseCore 0:
  10.8 71.3 all-gather.13
  83.8 63.0 all-gather.11
  148.4 65.2 all-gather.15
  215.1 67.5 all-gather.9
  284.1 113.6 all-gather.7

commit v4 on v3

--- a/solution.py
+++ b/solution.py
@@ -1,3 +1,4 @@
+import functools
 import math
 
 import jax
@@ -30,7 +31,7 @@
 F32 = jnp.float32
 BF = jnp.bfloat16
 HIGHEST = lax.Precision.HIGHEST
-VMEM_BYTES = 56 * 1024 * 1024
+VMEM_BYTES = 60 * 1024 * 1024
 
 
 def mm(a, b):
@@ -415,6 +416,14 @@
 NP = NFFN // 2
 
 
+def split_refs(refs, *counts):
+    parts = []
+    for count in counts:
+        parts.append(refs[:count])
+        refs = refs[count:]
+    return *parts, refs
+
+
 def flip(bit, change):
     return bit + change - 2 * bit * change
 
@@ -425,12 +434,12 @@
 
 def owner_at(p, h, kind):
     x = lax.axis_index("x")
-    far, near = 1 - p // 2, 1 - p % 2
+    far, near, core = ((1, 1, h), (1 - h, h, 0), (1 - h, h, 1), (0, 0, h))[p]
     if kind == WIDE_SLICE:
         x = 2 * flip(x // 2, far) + flip(x % 2, near)
-        c = flip(lax.axis_index("c"), h)
+        c = flip(lax.axis_index("c"), core)
         return {"x": x, "c": c}, x * 2 + c
-    x, c, y = flip(x, far), flip(lax.axis_index("c"), h), flip(lax.axis_index("y"), near)
+    x, c, y = flip(x, far), flip(lax.axis_index("c"), core), flip(lax.axis_index("y"), near)
     return {"x": x, "c": c, "y": y}, (x * 2 + c) * 2 + y
 
 
@@ -561,24 +570,45 @@
         copy.wait()
 
 
+def own_copies(body, ins, near, outs, near_outs, scratch):
+    counts = len(ins), len(near), len(outs), len(near_outs), len(scratch)
+
+    def run(*refs):
+        far, near_far, targets, near_targets, inner, close = split_refs(refs, *counts)
+        close, near_close, sems = split_refs(close, len(near), len(near_outs))
+        loads = [
+            pltpu.make_async_copy(source, target, sems[0].at[n])
+            for n, (source, target) in enumerate(zip(near_far, close))
+        ]
+        for copy in loads:
+            copy.start()
+
+        def ready():
+            for copy in loads:
+                copy.wait()
+
+        def done(n):
+            copy = pltpu.make_async_copy(near_close[n], near_targets[n], sems[1].at[n])
+            copy.start()
+            return copy
+
+        body(far, close, targets, near_close, inner, ready, done)
+
+    extra = [pltpu.VMEM(v.shape, v.dtype) for v in (*near, *near_outs)]
+    extra += [DMA((max(1, len(near)),)), DMA((max(1, len(near_outs)),))]
+    return run, [*ins, *near], [*outs, *near_outs], [*scratch, *extra]
+
+
 def comm_call(body, ins, outs, scratch, name, number, flops, nbytes, near=(), near_outs=()):
-    def specs(far, close):
-        return [pl.BlockSpec(memory_space=pl.ANY)] * len(far) + [
-            pl.BlockSpec(memory_space=pltpu.VMEM)
-        ] * len(close)
-
-    ins, outs, ins_specs, outs_specs = (
-        [*ins, *near], [*outs, *near_outs], specs(ins, near), specs(outs, near_outs)
-    )
+    run, ins, outs, scratch = own_copies(body, ins, near, outs, near_outs, scratch)
+    far = {} if number is None else dict(collective_id=number, has_side_effects=True)
     return pl.pallas_call(
-        body,
-        in_specs=ins_specs,
-        out_specs=outs_specs,
+        run,
+        in_specs=[pl.BlockSpec(memory_space=pl.ANY)] * len(ins),
+        out_specs=[pl.BlockSpec(memory_space=pl.ANY)] * len(outs),
         out_shape=outs,
         scratch_shapes=scratch,
-        compiler_params=pltpu.CompilerParams(
-            vmem_limit_bytes=VMEM_BYTES, collective_id=number, has_side_effects=True
-        ),
+        compiler_params=pltpu.CompilerParams(vmem_limit_bytes=VMEM_BYTES, **far),
         cost_estimate=pl.CostEstimate(
             flops=int(flops), bytes_accessed=int(nbytes), transcendentals=0
         ),
@@ -598,8 +628,8 @@
 def expert_forward(received, gate_ups, down, kind):
     split = len(gate_ups) == 2
 
-    def body(*refs):
-        expert_body(split, kind, *refs)
+    def body(far, near, outs, near_outs, scratch, ready, done):
+        expert_body(split, kind, *far, *outs, *scratch)
 
     return comm_call(
         body,
@@ -614,25 +644,25 @@
     )
 
 
-def expert_both_body(
-    kind, gate_up_ref, down_ref, rec_ref, sg_ref, mid_ref, g_ref, gret_ref, out_ref, gn_ref,
-    gle_ref, tcol_ref, lg_ref, rt_ref, gain_ref, cv_ref, wt_ref, res_ref, *scratch,
-):
+def expert_both_body(kind, far, near, out_near, scratch, ready, done):
+    gate_up_ref, down_ref, rec_ref, sg_ref, mid_ref, g_ref, mixed_ref, shared_ref = far
+    tcol_ref, lg_ref, rt_ref, gain_ref, cv_ref, wt_ref, res_ref, nar_ref, d_ref, u_ref = near
+    out_ref, gm_ref, gle_ref, mix_ref, gu_ref, gd_ref = out_near
     (
-        w1, w2, rv, sv, pv, qv, gv, uv, back, mid, g, acc,
+        w1, w2, rv, sv, pv, gv, uv, back, gback, mid, g, mixed, w3, acc,
         wsem, rsem, ssem, msem, send, recv, gsend, grecv,
     ) = scratch
     weights = fetch_weights(False, [gate_up_ref], down_ref, w1, w2, wsem)
-    blocks = fetch_blocks(rec_ref, rv, rsem, kind) + fetch_blocks(sg_ref, sv, ssem, kind)
-    extra = [
-        pltpu.make_async_copy(mid_ref, mid, msem.at[0]),
-        pltpu.make_async_copy(g_ref, g, msem.at[1]),
-    ]
-    for copy in extra:
-        copy.start()
+    blocks = fetch_blocks(rec_ref, rv, rsem, kind)
     greet(kind)
     for copy in weights + blocks:
         copy.wait()
+    extra = fetch_blocks(sg_ref, sv, ssem, kind)
+    for n, (source, target) in enumerate(
+        ((mid_ref, mid), (g_ref, g), (mixed_ref, mixed), (shared_ref.at[3], w3))
+    ):
+        extra.append(pltpu.make_async_copy(source, target, msem.at[n]))
+        extra[-1].start()
     moves = []
     for p in range(NP):
         r = rv[p]
@@ -648,6 +678,8 @@
         lax.fori_loop(0, FF // FC, step, 0)
         pv[p] = acc[...].astype(BF)
         moves += give_back(pv, p, back, send, recv, kind)
+    for copy in extra:
+        copy.wait()
     later = []
     for p in range(NP):
         grads = sv[p]
@@ -661,10 +693,11 @@
             return carry
 
         lax.fori_loop(0, FF // FC, step, 0)
-        qv[p] = acc[...].astype(BF)
-        later += give_back(qv, p, gret_ref, gsend, grecv, kind)
-    for copy in moves + extra:
+        rv[p] = acc[...].astype(BF)
+        later += give_back(rv, p, gback, gsend, grecv, kind)
+    for copy in moves:
         copy.wait()
+    ready()
 
     def finish(i, carry):
         at = pl.ds(pl.multiple_of(i * RB, RB), RB)
@@ -673,68 +706,84 @@
             tcol_ref[at, :], back, middle, logits, routes, gain_ref[...], cv_ref
         )
         out_ref[at, :] = following
-        gn_ref[at, :], gle_ref[at, :] = mix_grad(
+        gm_ref[at, :], gle_ref[at, :] = mix_grad(
             g[at, :].astype(F32), middle, chosen, logits, routes, 0.0, gain_ref[...], cv_ref,
             wt_ref[...], res_ref[...],
         )
         return carry
 
     lax.fori_loop(0, NB, finish, 0)
+    stores = [done(0), done(2)]
+    gu_ref[...] = jnp.zeros_like(gu_ref)
+    gd_ref[...] = jnp.zeros_like(gd_ref)
     for copy in later:
         copy.wait()
 
+    def settle_one(i, carry):
+        at = pl.ds(pl.multiple_of(i * RB, RB), RB)
+        refs = (tcol_ref, mid, g, mixed, gain_ref, nar_ref, w3, d_ref, u_ref, gu_ref, gd_ref)
+        settle_back(refs, at, gm_ref, mix_ref, gback)
+        return carry
+
+    lax.fori_loop(0, NB, settle_one, 0)
+    for copy in stores + [done(n) for n in (1, 3, 4, 5)]:
+        copy.wait()
+
 
 def expert_both(
-    received, slot_grads, gate_up, down, mid, g, tcol, logits, routes, gain, const_vec, router_t,
-    residual_t, kind,
+    received, slot_grads, gate_up, down, mid, g, mixed, weights, tcol, logits, routes, gain,
+    const_vec, router_t, residual_t, narrow, down_out, up_out, kind,
 ):
-    def body(*refs):
-        far, near, outs, scratch = refs[:6], refs[6:13], refs[13:17], refs[17:]
-        expert_both_body(kind, *far, *outs, *near, *scratch)
-
+    def body(far, near, outs, near_outs, scratch, ready, done):
+        expert_both_body(kind, far, near, near_outs, scratch, ready, done)
+
+    half = pltpu.VMEM((T, D), BF)
+    landing = pltpu.VMEM((NFFN, CAP, D), BF)
     return comm_call(
         body,
-        [gate_up, down, received, slot_grads, mid, g],
-        [BLOCKS],
+        [gate_up, down, received, slot_grads, mid, g, mixed, weights],
+        [],
         WEIGHTS
-        + [ROWS, ROWS, ROWS, ROWS, WIDE, WIDE, pltpu.VMEM((NFFN, CAP, D), BF)]
-        + [pltpu.VMEM((T, D), F32), pltpu.VMEM((T, D), g.dtype), SUM]
-        + [DMA((9,)), DMA((8,)), DMA((8,)), DMA((2,))]
+        + [ROWS, ROWS, ROWS, WIDE, WIDE, landing, landing]
+        + [pltpu.VMEM((T, D), F32), pltpu.VMEM((T, D), g.dtype), half, pltpu.VMEM((D, D), BF), SUM]
+        + [DMA((9,)), DMA((8,)), DMA((8,)), DMA((4,))]
         + [DMA((8,)), DMA((8,)), DMA((8,)), DMA((8,))],
         "expert_both",
         2,
         2 * SLOTS * D * FF * 6,
         26e6,
-        [tcol, logits, routes, gain, const_vec, router_t, residual_t],
-        [out((T, D), F32), out((T, D), F32), out((T, 128), F32)],
-    )
-
-
-def expert_back_body(split, kind, *refs):
+        [tcol, logits, routes, gain, const_vec, router_t, residual_t, narrow, down_out, up_out],
+        [out((T, D), F32), out((T, D), F32), out((T, 128), F32), out((T, D), BF)]
+        + [out((128, D), F32), out((128, D), F32)],
+    )
+
+
+def expert_back_body(split, kind, far, near, out_near, outs, scratch, ready, done):
     count = 2 if split else 1
-    gate_ups = refs[:count]
-    down_ref, gate_ref, up_ref, g_ref, mid_ref, c0_ref, c1_ref = refs[count : count + 7]
-    trow_ref, lg_ref, rt_ref, gl_ref, gain_ref, cv_ref, wt_ref = refs[count + 7 : count + 14]
-    ret_ref, gn_ref = refs[count + 14 : count + 16]
+    gate_ups, (down_ref, gate_ref, up_ref, g_ref, mid_ref, c0_ref, c1_ref, mixed_ref, shared_ref) = (
+        far[:count], far[count:]
+    )
     (
-        w1, w2, sgv, rv, pv, gv, uv, first, second, g, mid, c0, c1, acc,
-        wsem, gsem, usem, msem, dsend, drecv, send, recv,
-    ) = refs[count + 16 :]
+        trow_ref, tcol_ref, lg_ref, rt_ref, gl_ref, gain_ref, cv_ref, wt_ref, nar_ref, d_ref, u_ref
+    ) = near
+    gm_ref, gu_ref, gd_ref = out_near
+    mix_out = outs[0]
+    (
+        w1, w2, sgv, rv, pv, gv, uv, back, first, second, g, mid, c0, c1, mixed, w3, acc,
+        wsem, gsem, usem, msem, dsend, drecv, send, recv, osem,
+    ) = scratch
     extra = [
         pltpu.make_async_copy(ref, values, msem.at[n])
         for n, (ref, values) in enumerate(
-            ((g_ref, g), (mid_ref, mid), (c0_ref, c0), (c1_ref, c1))
+            (
+                (g_ref, g), (mid_ref, mid), (c0_ref, c0), (c1_ref, c1), (mixed_ref, mixed),
+                (shared_ref.at[3], w3),
+            )
         )
     ]
-    for copy in extra:
-        copy.start()
-    weights = fetch_weights(split, gate_ups, down_ref, w1, w2, wsem)
-    for values, ref, sems in ((gv, gate_ref, gsem), (uv, up_ref, usem)):
-        for p in range(NP):
-            copy = pltpu.make_async_copy(ref.at[p], values.at[p], sems.at[p])
-            copy.start()
-            weights.append(copy)
+    extra[0].start()
     extra[0].wait()
+    ready()
 
     def gated(i, carry):
         at = pl.ds(pl.multiple_of(i * RB, RB), RB)
@@ -744,9 +793,17 @@
         return carry
 
     lax.fori_loop(0, NB, gated, 0)
+    weights = fetch_weights(split, gate_ups, down_ref, w1, w2, wsem)
+    for p in (3, 0, 1, 2):
+        for values, ref, sems in ((gv, gate_ref, gsem), (uv, up_ref, usem)):
+            copy = pltpu.make_async_copy(ref.at[p], values.at[p], sems.at[p])
+            copy.start()
+            weights.append(copy)
+    for copy in extra[1:]:
+        copy.start()
     greet(kind)
     arrivals = {}
-    for p, h in [(1, 0), (2, 0), (1, 1), (2, 1), (0, 0), (0, 1), (3, 1), (3, 0)]:
+    for p, h in PLACES[:-2] + [(3, 1), (3, 0)]:
         where, number = owner_at(p, h, kind)
         place = number * CAP + iota((CAP, T), 0)
         hit0 = (trow_ref[0:1, :] == place).astype(F32).astype(BF)
@@ -771,7 +828,7 @@
         copy.wait()
     moves = []
 
-    for p in (3, 1, 2, 0):
+    for p in (3, 0, 1, 2):
         for h in range(2):
             if (p, h) in arrivals:
                 arrivals[p, h].wait()
@@ -787,44 +844,64 @@
 
         lax.fori_loop(0, FF // FC, step, 0)
         pv[p] = acc[...].astype(BF)
-        moves += give_back(pv, p, ret_ref, send, recv, kind)
+        moves += give_back(pv, p, back, send, recv, kind)
 
     def tidy(i, carry):
         at = pl.ds(pl.multiple_of(i * RB, RB), RB)
-        gn_ref[at, :] = mix_grad(
+        gm_ref[at, :] = mix_grad(
             g[at, :], mid[at, :], (c0[at, :], c1[at, :]), lg_ref[at, :], rt_ref[at, :],
             gl_ref[at, :], gain_ref[...], cv_ref, wt_ref[...], None,
         )[0]
         return carry
 
     lax.fori_loop(0, NB, tidy, 0)
+    gu_ref[...] = jnp.zeros_like(gu_ref)
+    gd_ref[...] = jnp.zeros_like(gd_ref)
     for copy in moves:
         copy.wait()
 
+    def settle_one(i, carry):
+        at = pl.ds(pl.multiple_of(i * RB, RB), RB)
+        refs = (tcol_ref, mid, g, mixed, gain_ref, nar_ref, w3, d_ref, u_ref, gu_ref, gd_ref)
+        settle_back(refs, at, gm_ref, first, back)
+        return carry
+
+    lax.fori_loop(0, NB, settle_one, 0)
+    last = pltpu.make_async_copy(first, mix_out, osem.at[0])
+    last.start()
+    for copy in [last] + [done(n) for n in range(3)]:
+        copy.wait()
+
 
 def expert_backward(
-    gate, up, gate_ups, down, g, mid, c0, c1, trow, logits, routes, gl, gain, const_vec, router_t, kind
+    gate, up, gate_ups, down, g, mid, c0, c1, mixed, weights, trow, tcol, logits, routes, gl, gain,
+    const_vec, router_t, narrow, down_out, up_out, kind,
 ):
     split = len(gate_ups) == 2
 
-    def body(*refs):
-        expert_back_body(split, kind, *refs)
+    def body(far, near, outs, near_outs, scratch, ready, done):
+        expert_back_body(split, kind, far, near, near_outs, outs, scratch, ready, done)
 
     half, full = pltpu.VMEM((T, D), BF), pltpu.VMEM((T, D), F32)
-    return comm_call(
+    mix, gm, gu, gd = comm_call(
         body,
-        [*gate_ups, down, gate, up, g, mid, c0, c1],
-        [BLOCKS],
+        [*gate_ups, down, gate, up, g, mid, c0, c1, mixed, weights],
+        [out((T, D), BF)],
         WEIGHTS
-        + [ROWS, ROWS, ROWS, WIDE, WIDE, half, half, full, full, half, half, SUM]
-        + [DMA((9,)), DMA((NP,)), DMA((NP,)), DMA((4,)), DMA((8,)), DMA((8,)), DMA((8,)), DMA((8,))],
+        + [ROWS, ROWS, ROWS, WIDE, WIDE, pltpu.VMEM((NFFN, CAP, D), BF)]
+        + [half, half, full, full, half, half, half, pltpu.VMEM((D, D), BF), SUM]
+        + [DMA((9,)), DMA((NP,)), DMA((NP,)), DMA((6,))]
+        + [DMA((8,)), DMA((8,)), DMA((8,)), DMA((8,)), DMA((1,))],
         "expert_backward",
         3,
         2 * SLOTS * D * FF * 3,
         26e6,
-        [trow, logits, routes, gl, gain, const_vec, router_t],
-        [out((T, D), F32)],
-    )
+        [
+            trow, tcol, logits, routes, gl, gain, const_vec, router_t, narrow, down_out, up_out,
+        ],
+        [out((T, D), F32), out((128, D), F32), out((128, D), F32)],
+    )
+    return gm, mix, gu, gd
 
 
 def mix_terms(logits, routes):
@@ -929,6 +1006,21 @@
     keep = weights[0] + weights[1] * shares[0][0] + weights[2] * shares[1][0]
     residual = None if res is None else mm(spread_lanes(only), res)
     return mm(spread_lanes(grad), wt) + keep * g, residual
+
+
+def settle_back(refs, at, gm_ref, mix_ref, back_ref):
+    tcol_ref, mid_ref, g_ref, mixed_ref, gain_ref, nar_ref, w_ref, d_ref, u_ref, gu_ref, gd_ref = refs
+    place = iota((RB, SLOTS), 1)
+    tcol = tcol_ref[at, :]
+    hit = (tcol[:, 0:1] == place) | (tcol[:, 1:2] == place)
+    grad = gm_ref[at, :] + mm(hit.astype(F32).astype(BF), back_ref[...].reshape(SLOTS, D))
+    grad = g_ref[at, :].astype(F32) + rms_back(grad, mid_ref[at, :], gain_ref[...])
+    gm_ref[at, :] = grad
+    grad = grad.astype(BF)
+    slim = mm_nt(grad, u_ref[...]).astype(BF)
+    gu_ref[...] += 2.0 * mm_tn(nar_ref[at, :], grad)
+    gd_ref[...] += mm_tn(slim, mixed_ref[at, :])
+    mix_ref[at, :] = (mm_nt(grad, w_ref[...]) + mm_nt(slim, d_ref[...])).astype(BF)
 
 
 def rms_back(grad, v, gain):
@@ -986,65 +1078,57 @@
     return dqt[...].T, jnp.concatenate(dks), jnp.concatenate(dvs)
 
 
-def layer_back_body(
-    back_ref, gn_ref, mid_ref, g_ref, mixed_ref, w_ref, qkv_ref, aug_ref, n_ref, x_ref,
-    tcol_ref, gain1_ref, gain0_ref, nar_out_ref, nar_ref, d_out_ref, u_out_ref, d_ref, u_ref,
-    kf_ref, cos_ref, sin_ref,
-    gx_ref, gu_out_ref, gd_out_ref, gu_ref, gd_ref,
-    back, gn, mid, g, mixed, w, qkv, aug, n, x, gmix, gproj, dqt, sems, row_sems, out_sems,
-):
-    def block(i):
-        return slice(i * RB, (i + 1) * RB)
+def layer_back_body(far, near, out_near, gx_ref, scratch, ready, done):
+    gm_ref, mix_ref, mixed_ref, w_ref, qkv_ref, aug_ref, n_ref, x_ref = far
+    gain_ref, nar_ref, d_ref, u_ref, kf_ref, cos_ref, sin_ref = near
+    gu_ref, gd_ref = out_near
+    gm, mix, mixed, w, qkv, aug, n, x, gproj, dqt, sems, pair_sems, out_sems = scratch
 
     def start(source, target, sem):
         copy = pltpu.make_async_copy(source, target, sem)
         copy.start()
         return copy
 
-    by_row = [(gn_ref, gn), (mid_ref, mid), (g_ref, g), (mixed_ref, mixed)]
-    first = [start(back_ref, back, sems.at[0]), start(w_ref.at[3], w.at[3], sems.at[1])]
-    strips = [
-        [start(a.at[block(i), :], b.at[block(i), :], row_sems.at[i, m]) for m, (a, b) in enumerate(by_row)]
-        for i in range(NB)
+    def cols(part, j):
+        return pl.ds(pl.multiple_of(part * D + j * 128, 128), 128)
+
+    def of_pair(j):
+        copies = [
+            pltpu.make_async_copy(
+                qkv_ref.at[:, cols(part, j)], qkv.at[:, cols(part, j)], pair_sems.at[j, part]
+            )
+            for part in range(3)
+        ]
+        for k, (source, target) in enumerate(((mix_ref, mix), (mixed_ref, mixed))):
+            copies.append(
+                pltpu.make_async_copy(
+                    source.at[:, cols(0, j)], target.at[:, cols(0, j)], pair_sems.at[j, 3 + k]
+                )
+            )
+        copies.append(pltpu.make_async_copy(aug_ref.at[j], aug.at[j], pair_sems.at[j, 5]))
+        return copies
+
+    for j in range(PAIRS):
+        for copy in of_pair(j):
+            copy.start()
+    third = [start(w_ref.at[k], w.at[k], sems.at[k]) for k in range(3)]
+    third += [
+        start(source, target, sems.at[3 + k])
+        for k, (source, target) in enumerate(((n_ref, n), (x_ref, x), (gm_ref, gm)))
     ]
-    second = [start(qkv_ref, qkv, sems.at[2]), start(aug_ref, aug, sems.at[3])]
-    third = [start(w_ref.at[k], w.at[k], sems.at[4 + k]) for k in range(3)]
-    third += [start(n_ref, n, sems.at[7]), start(x_ref, x, sems.at[8])]
-    for copy in first:
-        copy.wait()
-    place = iota((RB, SLOTS), 1)
-    gu = jnp.zeros((128, D), F32)
-    gd = jnp.zeros((128, D), F32)
-    for i in range(NB):
-        at = block(i)
-        for copy in strips[i]:
+    ready()
+
+    def pair(j, carry):
+        for copy in of_pair(j):
             copy.wait()
-        hit = (tcol_ref[at, 0:1] == place) | (tcol_ref[at, 1:2] == place)
-        grad = gn[at, :] + mm(hit.astype(F32).astype(BF), back[...])
-        grad_mid = g[at, :].astype(F32) + rms_back(grad, mid[at, :], gain1_ref[...])
-        gn[at, :] = grad_mid
-        out_grad = grad_mid.astype(BF)
-        grad_narrow = mm_nt(out_grad, u_out_ref[...]).astype(BF)
-        gu = gu + 2.0 * mm_tn(nar_out_ref[at, :], out_grad)
-        gd = gd + mm_tn(grad_narrow, mixed[at, :])
-        gmix[at, :] = (mm_nt(out_grad, w[3]) + mm_nt(grad_narrow, d_out_ref[...])).astype(BF)
-    gu_out_ref[...] = gu
-    gd_out_ref[...] = gd
-    for copy in second:
-        copy.wait()
-
-    def pair(j, carry):
-        def cols(part):
-            return pl.ds(pl.multiple_of(part * D + j * 128, 128), 128)
-
         dq, dk, dv = attend_back(
-            qkv[:, cols(0)], qkv[:, cols(1)], qkv[:, cols(2)], aug[j], kf_ref[...],
-            gmix[:, cols(0)], mixed[:, cols(0)], dqt,
+            qkv[:, cols(0, j)], qkv[:, cols(1, j)], qkv[:, cols(2, j)], aug[j], kf_ref[...],
+            mix[:, cols(0, j)], mixed[:, cols(0, j)], dqt,
         )
         for part, value in enumerate((dq, dk)):
             value = (value * (1.0 / math.sqrt(HD))).astype(BF).astype(F32)
-            gproj[:, cols(part)] = turn(value, cos_ref[...], -sin_ref[...]).astype(BF)
-        gproj[:, cols(2)] = dv.astype(BF)
+            gproj[:, cols(part, j)] = turn(value, cos_ref[...], -sin_ref[...]).astype(BF)
+        gproj[:, cols(2, j)] = dv.astype(BF)
         return carry
 
     lax.fori_loop(0, PAIRS, pair, 0)
@@ -1054,56 +1138,46 @@
     gd_ref[...] = jnp.zeros_like(gd_ref)
     stores = []
     for i in range(NB):
-        at = block(i)
+        at = slice(i * RB, (i + 1) * RB)
         grad = jnp.zeros((RB, D), F32)
         slim = jnp.zeros((RB, 128), F32)
         narrow = nar_ref[at, :]
         for part in range(3):
-            cols = slice(part * D, (part + 1) * D)
-            piece = gproj[at, cols]
+            columns = slice(part * D, (part + 1) * D)
+            piece = gproj[at, columns]
             grad = grad + mm_nt(piece, w[part])
-            slim = slim + mm_nt(piece, u_ref[:, cols])
-            gu_ref[:, cols] += 2.0 * mm_tn(narrow, piece)
+            slim = slim + mm_nt(piece, u_ref[:, columns])
+            gu_ref[:, columns] += 2.0 * mm_tn(narrow, piece)
         slim = slim.astype(BF)
         gd_ref[...] += mm_tn(slim, n[at, :])
         grad = grad + mm_nt(slim, d_ref[...])
-        mid[at, :] = gn[at, :] + rms_back(grad, x[at, :].astype(F32), gain0_ref[...])
-        stores.append(start(mid.at[at, :], gx_ref.at[at, :], out_sems.at[i]))
-    for copy in stores:
+        gm[at, :] = gm[at, :] + rms_back(grad, x[at, :].astype(F32), gain_ref[...])
+        stores.append(start(gm.at[at, :], gx_ref.at[at, :], out_sems.at[i]))
+    for copy in stores + [done(0), done(1)]:
         copy.wait()
 
 
-def layer_back(
-    back, gn, mid, g, mixed, w, qkv, aug, n, x, tcol, gain1, gain0, narrow_out, narrow, down_out,
-    up_out, down, up, kf, cos, sin,
-):
-    far = [back, gn, mid, g, mixed, w, qkv, aug, n, x]
-    near = [
-        tcol, gain1, gain0, narrow_out, narrow, down_out, up_out, down, up, kf, cos, sin,
-    ]
-    outs = [out((128, D), F32), out((128, D), F32), out((128, 3 * D), F32), out((128, D), F32)]
-    anywhere = pl.BlockSpec(memory_space=pl.ANY)
-    close = pl.BlockSpec(memory_space=pltpu.VMEM)
-    return pl.pallas_call(
-        layer_back_body,
-        in_specs=[anywhere] * len(far) + [close] * len(near),
-        out_specs=[anywhere] + [close] * len(outs),
-        out_shape=[out((T, D), F32)] + outs,
-        scratch_shapes=[pltpu.VMEM(v.shape, v.dtype) for v in far]
-        + [
-            pltpu.VMEM((T, D), BF),
-            pltpu.VMEM((T, 3 * D), BF),
-            pltpu.VMEM((128, T), F32),
-            DMA((9,)),
-            DMA((NB, 4)),
-            DMA((NB,)),
-        ],
-        compiler_params=pltpu.CompilerParams(vmem_limit_bytes=VMEM_BYTES),
-        cost_estimate=pl.CostEstimate(
-            flops=int(12 * 10 * T * T * 128 + 2 * T * D * 5 * D), bytes_accessed=int(4e7), transcendentals=0
-        ),
-        name="layer_back",
-    )(*far, *near)
+def layer_back(gm, mix, mixed, w, qkv, aug, n, x, gain0, narrow, down, up, kf, cos, sin):
+    far = [gm, mix, mixed, w, qkv, aug, n, x]
+
+    def body(far, near, outs, near_outs, scratch, ready, done):
+        layer_back_body(far, near, near_outs, outs[0], scratch, ready, done)
+
+    shapes = [out((3, D, D), BF) if v is w else v for v in far]
+    return comm_call(
+        body,
+        far,
+        [out((T, D), F32)],
+        [pltpu.VMEM(v.shape, v.dtype) for v in shapes]
+        + [pltpu.VMEM((T, 3 * D), BF), pltpu.VMEM((128, T), F32)]
+        + [DMA((6,)), DMA((PAIRS, 6)), DMA((NB,))],
+        "layer_back",
+        None,
+        12 * 10 * T * T * 128 + 2 * T * D * 3 * D,
+        4e7,
+        [gain0, narrow, down, up, kf, cos, sin],
+        [out((128, 3 * D), F32), out((128, D), F32)],
+    )
 
 
 AXES = ("x", "c", "zh", "zl", "y")
@@ -1111,7 +1185,9 @@
 PIECE = 96
 
 
-def shared_body(p_ref, o_ref, local, zs, zr, ys, yr, xs, xr, cs, cr):
+def shared_body(count, *refs):
+    (p_ref,), away, (o_ref,), came, sems = split_refs(refs, 1, count, 1, count)
+    local, zs, zr, ys, yr, xs, xr, cs, cr, ws, wr = sems
     x, c, y = (lax.axis_index(name) for name in ("x", "c", "y"))
     z = 2 * lax.axis_index("zh") + lax.axis_index("zl")
     mine, theirs = 2 * x + c, 2 * (1 - x) + c
@@ -1165,6 +1241,10 @@
     along_y(0, p_ref, spot(mine, y, 0))
     along_x(0, p_ref, spot(mine, y, 0))
     to_core(p_ref, spot(mine, y, 0))
+    swaps = [
+        send(source, target, others[3], ws.at[n], wr.at[n])
+        for n, (source, target) in enumerate(zip(away, came))
+    ]
     for j in range(1, 4):
         z_copies[j - 1].wait_recv()
         piece = spot(mine, y, j)
@@ -1186,7 +1266,7 @@
         (x_copies[4 + j] if j < 2 else y_copies[2 + j]).wait_recv()
         piece = spot(theirs, 1 - y, j)
         to_core(piece, piece)
-    for copy in core_copies:
+    for copy in core_copies + swaps:
         copy.wait_recv()
     own.wait()
     for copy in started:
@@ -1197,23 +1277,25 @@
     return tuple(lax.axis_size(name) for name in AXES) == (2, 2, 2, 2, 2)
 
 
-def gather_shared(qkv, output):
+def gather_shared(qkv, output, away=()):
     rows_here = qkv.shape[0]
     parts = jnp.concatenate([qkv.reshape(rows_here, 3, D).transpose(1, 0, 2), output[None]])
     if not usual():
-        return lax.all_gather(parts, SHARD, axis=1, tiled=True)
+        return [lax.all_gather(parts, SHARD, axis=1, tiled=True)]
     quarter = 2 * lax.axis_index("x") + lax.axis_index("c")
     piece = lax.dynamic_index_in_dim(parts, quarter, axis=0, keepdims=False)
     return comm_call(
-        shared_body,
-        [piece],
-        [jax.ShapeDtypeStruct((4, D, D), BF)],
-        [DMA((1,)), DMA((3,)), DMA((3,)), DMA((6,)), DMA((6,)), DMA((6,)), DMA((6,)), DMA((16,)), DMA((16,))],
+        lambda far, near, outs, near_outs, scratch, ready, done: shared_body(
+            len(away), *far, *outs, *scratch
+        ),
+        [piece, *away],
+        [jax.ShapeDtypeStruct(v.shape, v.dtype) for v in (out((4, D, D), BF), *away)],
+        [DMA((n,)) for n in (1, 3, 3, 6, 6, 6, 6, 16, 16, 2, 2)],
         "gather_shared",
-        0,
+        5 if away else 0,
         0,
         5e7,
-    )[0]
+    )
 
 
 SPAN = 96
@@ -1236,25 +1318,25 @@
     peers += [{"x": a, "c": b} for a, b in groups[1:]]
     for who in peers:
         pl.semaphore_signal(barrier, inc=1, device_id=who, device_id_type=pl.DeviceIdType.MESH)
-    row = 0
     for layer in range(LAYERS):
         gd_in, gd_out, gu_in, gu_out = parts[4 * layer : 4 * layer + 4]
         pieces = [gd_in[p * R : (p + 1) * R, :] for p in range(3)] + [gd_out[:R, :]]
         pieces += [gu_in[p * R : (p + 1) * R, p * D : (p + 1) * D] for p in range(3)] + [gu_out[:R, :]]
-        for piece in pieces:
-            for s in range(8):
-                sbuf[s, row : row + R, :] = piece[:, s * SPAN : (s + 1) * SPAN].astype(BF)
-            row += R
-    sbuf[:, UNIT:, :] = jnp.broadcast_to(id_ref[0].astype(F32).astype(BF), (8, R, SPAN))
+        sbuf[:, layer * 128 : (layer + 1) * 128] = jnp.concatenate(pieces).T.astype(BF)
+    sbuf[:, UNIT:] = jnp.broadcast_to(id_ref[0].astype(F32).astype(BF), (D, 128))
+
+    def share(k):
+        return sbuf.at[pl.ds(pl.multiple_of(k * SPAN, SPAN), SPAN), :]
+
     pl.semaphore_wait(barrier, len(peers))
     me = 2 * z + y
     copies = []
     for n, (a, b) in enumerate(mates):
         if n == 0:
-            rbuf[0] = sbuf[me]
+            rbuf[0] = share(me)[...]
             continue
         copy = pltpu.make_async_remote_copy(
-            src_ref=sbuf.at[2 * a + b],
+            src_ref=share(2 * a + b),
             dst_ref=rbuf.at[(4 - n // 2) % 4 * 2 + n % 2],
             send_sem=asend.at[n],
             recv_sem=arecv.at[(4 - n // 2) % 4 * 2 + n % 2],
@@ -1267,21 +1349,21 @@
         copy.wait()
     masks = []
     for n in range(8):
-        own = rbuf[n, UNIT : UNIT + R, :][0:1, 0:1].astype(F32)
+        own = rbuf[n, 0:16, UNIT:][0:1, 0:1].astype(F32)
         masks.append([(own == k).astype(F32) for k in range(NA)])
 
     def add(i, carry):
-        at = pl.ds(pl.multiple_of(i * 32, 32), 32)
-        sums = [jnp.zeros((32, SPAN), F32) for _ in range(NA)]
+        at = pl.ds(pl.multiple_of(i * 16, 16), 16)
+        sums = [jnp.zeros((16, UNIT), F32) for _ in range(NA)]
         for n in range(8):
-            values = rbuf[n, at, :].astype(F32)
+            values = rbuf[n, at, :UNIT].astype(F32)
             for k in range(NA):
                 sums[k] = sums[k] + values * masks[n][k]
         for k in range(NA):
             tbuf[k, at, :] = sums[k].astype(BF)
         return carry
 
-    lax.fori_loop(0, UNIT // 32, add, 0)
+    lax.fori_loop(0, SPAN // 16, add, 0)
     copies = []
     ubuf[0] = tbuf[pl.ds(2 * (2 * x + c), 2)]
     for n, (a, b) in enumerate(groups):
@@ -1312,12 +1394,12 @@
         adapters_body,
         in_specs=specs,
         out_specs=pl.BlockSpec(memory_space=pltpu.VMEM),
-        out_shape=jax.ShapeDtypeStruct((2, UNIT, SPAN), F32),
+        out_shape=jax.ShapeDtypeStruct((2, SPAN, UNIT), F32),
         scratch_shapes=[
-            pltpu.VMEM((8, UNIT + R, SPAN), BF),
-            pltpu.VMEM((8, UNIT + R, SPAN), BF),
-            pltpu.VMEM((NA, UNIT, SPAN), BF),
-            pltpu.VMEM((4, 2, UNIT, SPAN), BF),
+            pltpu.VMEM((D, UNIT + 128), BF),
+            pltpu.VMEM((8, SPAN, UNIT + 128), BF),
+            pltpu.VMEM((NA, SPAN, UNIT), BF),
+            pltpu.VMEM((4, 2, SPAN, UNIT), BF),
             DMA((8,)),
             DMA((8,)),
             DMA((4,)),
@@ -1344,7 +1426,7 @@
     return lax.ppermute(v, "y", [(0, 1), (1, 0)])
 
 
-def move_expert(w):
+def swapped(w):
     mine, other = own_and_other(w)
     return both_rows(mine, across_y(other))
 
@@ -1377,7 +1459,8 @@
     summed = lax.all_to_all(
         summed.reshape(groups, NA // groups, -1), EXPERT, split_axis=0, concat_axis=0, tiled=True
     )
-    return jnp.sum(summed.astype(F32), axis=0)
+    summed = jnp.sum(summed.astype(F32), axis=0)
+    return summed.reshape(summed.shape[0], UNIT, -1).transpose(0, 2, 1)
 
 
 def per_device(
@@ -1405,13 +1488,16 @@
     if fast:
         mine, other = own_and_other(w_gate_up[0])
         parts = [lax.all_gather(mine, ("zh", "zl"), axis=0)]
-        shared = [gather_shared(query_key_value_weight[0], output_weight[0])]
-        other, down_first, shared[0] = barrier((other, w_down[0], shared[0]))
-        parts.append(lax.all_gather(across_y(other), ("zh", "zl"), axis=0))
+        down_mine, down_other = own_and_other(w_down[0])
+        first, other, down_other = gather_shared(
+            query_key_value_weight[0], output_weight[0], (other, down_other)
+        )
+        shared = [first]
+        parts.append(lax.all_gather(other, ("zh", "zl"), axis=0))
         gate_up_full = [parts]
-        down_full = [gathered(move_expert(down_first), ("zh", "zl"))]
+        down_full = [gathered(both_rows(down_mine, down_other), ("zh", "zl"))]
     else:
-        shared = [gather_shared(query_key_value_weight[0], output_weight[0])]
+        shared = gather_shared(query_key_value_weight[0], output_weight[0])
         gate_up_full = [[gathered(w_gate_up[layer, 0], SHARD)] for layer in range(LAYERS)]
         down_full = [gathered(w_down[layer, 0], SHARD) for layer in range(LAYERS)]
 
@@ -1451,22 +1537,24 @@
             stream, mixed, shared[layer], down_out[layer], up_out[layer], gain1, router_s[layer],
             earlier, residual_s,
         )
-        received = exchange(dispatch(trow, sent), kind)
+        buffer = dispatch(trow, sent)
+        received = exchange(buffer, kind)
         if layer == 0:
             if fast:
                 later = barrier((w_gate_up[1], w_down[1], logits))
-                gate_up_full.append([gathered(move_expert(later[0]), ("zh", "zl"))])
-                down_full.append(gathered(move_expert(later[1]), ("zh", "zl")))
+                gate_up_full.append([gathered(swapped(later[0]), ("zh", "zl"))])
+                down_full.append(gathered(swapped(later[1]), ("zh", "zl")))
             later = lax.optimization_barrier(
                 (query_key_value_weight[1], output_weight[1], logits)
             )
-            shared.append(gather_shared(later[0], later[1]))
+            shared += gather_shared(later[0], later[1])
             returned, gate, up = expert_forward(received, gate_up_full[0], down_full[0], kind)
         else:
             slot_grads = exchange(dispatch_grad(trow, out_grad, logits, routes), kind)
-            back, following, grad_normed, grad_logits = expert_both(
-                received, slot_grads, gate_up_full[1][0], down_full[1], mid, out_grad, tcol, logits,
-                routes, gain1, const_vec[1], router_ts[1], residual_ts, kind,
+            following, grad_mid, grad_logits, grad_mixed, gu_out, gd_out = expert_both(
+                received, slot_grads, gate_up_full[1][0], down_full[1], mid, out_grad, mixed,
+                shared[1], tcol, logits, routes, gain1, const_vec[1], router_ts[1], residual_ts,
+                narrow_out, down_out[1], up_out[1], kind,
             )
             c0 = c1 = None
         if layer == 0:
@@ -1484,13 +1572,13 @@
         gain0 = norm_gain[layer, 0:1]
         gain1 = norm_gain[layer, 1:2]
         if layer == 0:
-            back, grad_normed = expert_backward(
-                gate, up, gate_up_full[0], down_full[0], grad, mid, c0, c1, trow, logits, routes,
-                grad_logits, gain1, const_vec[0], router_ts[0], kind,
+            grad_mid, grad_mixed, gu_out, gd_out = expert_backward(
+                gate, up, gate_up_full[0], down_full[0], grad, mid, c0, c1, mixed, shared[0], trow,
+                tcol, logits, routes, grad_logits, gain1, const_vec[0], router_ts[0], narrow_out,
+                down_out[0], up_out[0], kind,
             )
-        grad, gu_out, gd_out, gu_in, gd_in = layer_back(
-            back.reshape(SLOTS, D), grad_normed, mid, grad, mixed, shared[layer], qkv, aug, normed,
-            x_in, tcol, gain1, gain0, narrow_out, narrow, down_out[layer], up_out[layer],
+        grad, gu_in, gd_in = layer_back(
+            grad_mid, grad_mixed, mixed, shared[layer], qkv, aug, normed, x_in, gain0, narrow,
             down_in[layer], up_in[layer], kf, cos, sin,
         )
         parts[layer] = (gd_in, gd_out, gu_in, gu_out)
@@ -1499,8 +1587,7 @@
         final = adapters(adapter_of, [v for layer in parts for v in layer])
     else:
         final = adapters_plain(lax.all_gather(adapter_of, SHARD, axis=0, tiled=True), parts)
-    share = final.shape[0]
-    final = final.reshape(share, LAYERS, 2, 4, R, -1).transpose(2, 1, 3, 0, 5, 4)
+    final = final.reshape(*final.shape[:2], LAYERS, 2, 4, R).transpose(3, 2, 4, 0, 1, 5)
     return (stream, grad, final[0], final[1])
 
 

time: 702 us -> 682 us (0.972)
  waiting for transfers between devices: 95.3 us -> 77.1 us
    ppermute x4 -> x2, waiting for transfers between devices: 49.9 us -> 28.5 us  [across_y(): return lax.ppermute(v, 'y', [(0, 1), (1, 0)])]
  transfers between devices with their start and end apart: 12 -> 10, of which waited for: 6 -> 5; matrix products, arithmetic and copies ran while one was open for 5% -> 5% of each run, Pallas kernels for 37% -> 39%
where the time goes in v4:
time: 682 us; the launch traced here: 678 us
  Pallas kernels  522 us (77%)
  waiting for transfers between devices  77.1 us (11%)
  local copies, waits for them, and re-layouts  38.5 us (6%)
  starting transfers between devices  16.9 us (2%)
  between operations  15.1 us (2%)
  other arithmetic  7.82 us (1%)
    pallas_call x7, Pallas kernels, comm_call(): pl.pallas_call(run, in_specs=[pl.BlockSpec(memory_space=pl.ANY)] * len(in...  371 us
    pallas_call x11, Pallas kernels, call(): pl.pallas_call(body, grid=grid, in_specs=[spec(e) for e in ins], out_spec...  123 us
    all_to_all x3, waiting for transfers between devices, exchange(): lax.all_to_all(v, OWNERS[kind], split_axis=0, concat_axis=0, tiled=True)  45.2 us
    ppermute x2, waiting for transfers between devices, across_y(): return lax.ppermute(v, 'y', [(0, 1), (1, 0)])  28.5 us
    pallas_call x1, Pallas kernels, adapters(): pl.pallas_call(adapters_body, in_specs=specs, out_specs=pl.BlockSpec(memo...  27.6 us
    all_to_all x3, starting transfers between devices, exchange(): lax.all_to_all(v, OWNERS[kind], split_axis=0, concat_axis=0, tiled=True)  15.6 us
  transfers between devices with their start and end apart: 10, of which 5 were waited for; matrix products, arithmetic and copies ran while one was open for 5% of the time, Pallas kernels for 39%

profile of v4, /device:TPU:9, one launch (start us, length us, event | category | flops | bytes accessed | tf_op | source)
XLA Modules:
  0.0 677.8 jit_solution(16672715699438264785)
XLA Ops:
  17.4 51.7 %gather_shared.2 = (bf16[4,768,768]{2,1,0:T(8,128)(2,1)}, bf16[96,4096]{1,0:T(8,128)(2,1)}, bf16[256,768]{1,0:T(8,128)(2,1)}) custom-call(bf16[96,768]{1,0:T(8,128)(2,1)} %bitcast.124, bf16[96,4096]{1,0:T(8,128)(2,1)} %get-tuple-element.169.refs_1_, bf16[256,768]{1,0:T(8,128)(2,1)} %get-tuple-element.179.refs_2_), custom_call_target="tpu_custom_call" | custom-call | bytes 50000000 | tf_op jit(solution)/shard_map/gather_shared/pallas_call | solution.py:605
  88.8 6.3 prep.1
  100.2 11.0 %project.2 = (bf16[1024,768]{1,0:T(8,128)(2,1)}, bf16[1024,128]{1,0:T(8,128)(2,1)}, bf16[1024,2304]{1,0:T(8,128)(2,1)}) custom-call(bf16[1024,768]{1,0:T(8,128)(2,1)} %refs_7_.1, f32[1,768]{1,0:T(1,128)} %get-tuple-element.204.g_ref.refs_8_, bf16[4,768,768]{2,1,0:T(8,128)(2,1)} %get-tuple-element.97.w_ref.refs_10_.refs_3_, ...), custom_call_target="tpu_custom_call" | custom-call | flops 3623878656 | bytes 12000000 | tf_op jit(solution)/shard_map/project/pallas_call | solution.py:72
  111.2 21.4 %attend.2 = (bf16[1024,768]{1,0:T(8,128)(2,1)}, bf16[6,1024,128]{2,1,0:T(8,128)(2,1)}) custom-call(bf16[1024,2304]{1,0:T(8,128)(2,1)} %get-tuple-element.100.q_ref.k_ref.v_ref.refs_4_, bf16[1024,2304]{1,0:T(8,128)(2,1)} %get-tuple-element.100.q_ref.k_ref.v_ref.refs_4_, bf16[1024,2304]{1,0:T(8,128)(2,1)} %get-tuple-element.100.q_ref.k_ref.v_ref.refs_4_, ...), custom_call_target="tpu_custom_call" | custom-call | flops 6442450944 | bytes 8000000 | tf_op jit(solution)/shard_map/attend/pallas_call | solution.py:72
  133.5 8.6 %settle.2 = (f32[1024,768]{1,0:T(8,128)}, bf16[1024,768]{1,0:T(8,128)(2,1)}, f32[1024,128]{1,0:T(8,128)}, bf16[1024,128]{1,0:T(8,128)(2,1)}) custom-call(bf16[1024,768]{1,0:T(8,128)(2,1)} %refs_7_.1, bf16[1024,768]{1,0:T(8,128)(2,1)} %get-tuple-element.103.mixed_ref.refs_9_.refs_2_, bf16[4,768,768]{2,1,0:T(8,128)(2,1)} %get-tuple-element.97.w_ref.refs_10_.refs_3_, ...), custom_call_target="tpu_custom_call" | custom-call | flops 2415919104 | bytes 10000000 | tf_op jit(solution)/shard_map/settle/pallas_call | solution.py:72
  142.4 10.4 %collective-permute-done.1 = bf16[256,768]{1,0:T(8,128)(2,1)S(1)} collective-permute-done((bf16[256,768]{1,0:T(8,128)(2,1)S(1)}, bf16[256,768]{1,0:T(8,128)(2,1)S(1)}, u32[]{:S(2)}, u32[]{:S(2)}) %collective-permute-start.1) | collective-permute-done | bytes 393248 | tf_op jit(solution)/shard_map/ppermute | solution.py:1426
  154.6 18.0 %collective-permute-done = bf16[96,4096]{1,0:T(8,128)(2,1)S(1)} collective-permute-done((bf16[96,4096]{1,0:T(8,128)(2,1)S(1)}, bf16[96,4096]{1,0:T(8,128)(2,1)S(1)}, u32[]{:S(2)}, u32[]{:S(2)}) %collective-permute-start) | collective-permute-done | bytes 786464 | tf_op jit(solution)/shard_map/ppermute | solution.py:1426
  174.1 6.9 %dispatch.2 = bf16[8,192,768]{2,1,0:T(8,128)(2,1)} custom-call(s32[8,1024]{1,0:T(8,128)} %get-tuple-element.109.trow_ref.refs_11_, bf16[1024,768]{1,0:T(8,128)(2,1)} %get-tuple-element.113.s_ref), custom_call_target="tpu_custom_call" | custom-call | flops 2415919104 | bytes 4000000 | tf_op jit(solution)/shard_map/dispatch/pallas_call | solution.py:72
  181.1 6.0 all-to-all-start
  189.3 48.3 %gather_shared.3.w_ref.refs_7_.refs_3_ = bf16[4,768,768]{2,1,0:T(8,128)(2,1)} custom-call(bf16[96,768]{1,0:T(8,128)(2,1)} %bitcast.122), custom_call_target="tpu_custom_call" | custom-call | bytes 50000000 | tf_op jit(solution)/shard_map/gather_shared/pallas_call | solution.py:605
  238.3 37.7 %expert_forward.1 = (bf16[8,192,768]{2,1,0:T(8,128)(2,1)}, bf16[4,384,2048]{2,1,0:T(8,128)(2,1)}, bf16[4,384,2048]{2,1,0:T(8,128)(2,1)}) custom-call(bf16[4,96,4096]{2,1,0:T(8,128)(2,1)} %bitcast.132, bf16[4,96,4096]{2,1,0:T(8,128)(2,1)} %bitcast.136, bf16[2048,768]{1,0:T(8,128)(2,1)} %bitcast.134, bf16[8,192,768]{2,1,0:T(8,128)(2,1)} %all-to-all-done.refs_3_), custom_call_target="tpu_custom_call" | custom-call | flops 14495514624 | bytes 26000000 | tf_op jit(solution)/shard_map/expert_forward/pallas_call | solution.py:605
  275.9 10.1 %combine.1 = (f32[1024,768]{1,0:T(8,128)}, bf16[1024,768]{1,0:T(8,128)(2,1)}, bf16[1024,768]{1,0:T(8,128)(2,1)}) custom-call(s32[1024,128]{1,0:T(8,128)} %get-tuple-element.110.tcol_ref.refs_8_.refs_12_, bf16[1536,768]{1,0:T(8,128)(2,1)} %bitcast.139, f32[1024,768]{1,0:T(8,128)} %get-tuple-element.115.mid_ref.refs_6_, ...), custom_call_target="tpu_custom_call" | custom-call | flops 4831838208 | bytes 12000000 | tf_op jit(solution)/shard_map/combine/pallas_call | solution.py:72
  286.0 11.1 %project.3 = (bf16[1024,768]{1,0:T(8,128)(2,1)}, bf16[1024,128]{1,0:T(8,128)(2,1)}, bf16[1024,2304]{1,0:T(8,128)(2,1)}) custom-call(f32[1024,768]{1,0:T(8,128)} %get-tuple-element.116.x_ref.refs_7_, f32[1,768]{1,0:T(1,128)} %get-tuple-element.205.g_ref.refs_8_, bf16[4,768,768]{2,1,0:T(8,128)(2,1)} %gather_shared.3.w_ref.refs_7_.refs_3_, ...), custom_call_target="tpu_custom_call" | custom-call | flops 3623878656 | bytes 12000000 | tf_op jit(solution)/shard_map/project/pallas_call | solution.py:72
  297.2 22.0 %attend.3 = (bf16[1024,768]{1,0:T(8,128)(2,1)}, bf16[6,1024,128]{2,1,0:T(8,128)(2,1)}) custom-call(bf16[1024,2304]{1,0:T(8,128)(2,1)} %get-tuple-element.119.q_ref.k_ref.v_ref.refs_4_, bf16[1024,2304]{1,0:T(8,128)(2,1)} %get-tuple-element.119.q_ref.k_ref.v_ref.refs_4_, bf16[1024,2304]{1,0:T(8,128)(2,1)} %get-tuple-element.119.q_ref.k_ref.v_ref.refs_4_, ...), custom_call_target="tpu_custom_call" | custom-call | flops 6442450944 | bytes 8000000 | tf_op jit(solution)/shard_map/attend/pallas_call | solution.py:72
  319.1 8.7 %settle.3 = (f32[1024,768]{1,0:T(8,128)}, bf16[1024,768]{1,0:T(8,128)(2,1)}, f32[1024,128]{1,0:T(8,128)}, bf16[1024,128]{1,0:T(8,128)(2,1)}) custom-call(f32[1024,768]{1,0:T(8,128)} %get-tuple-element.116.x_ref.refs_7_, bf16[1024,768]{1,0:T(8,128)(2,1)} %get-tuple-element.120.mixed_ref.refs_6_.refs_2_, ...), custom_call_target="tpu_custom_call" | custom-call | flops 2415919104 | bytes 10000000 | tf_op jit(solution)/shard_map/settle/pallas_call | solution.py:72
  327.8 6.9 %dispatch.3 = bf16[8,192,768]{2,1,0:T(8,128)(2,1)} custom-call(s32[8,1024]{1,0:T(8,128)} %get-tuple-element.109.trow_ref.refs_11_, bf16[1024,768]{1,0:T(8,128)(2,1)} %get-tuple-element.121.s_ref), custom_call_target="tpu_custom_call" | custom-call | flops 2415919104 | bytes 4000000 | tf_op jit(solution)/shard_map/dispatch/pallas_call | solution.py:72
  339.4 10.3 %dispatch_grad.1 = bf16[8,192,768]{2,1,0:T(8,128)(2,1)} custom-call(s32[8,1024]{1,0:T(8,128)} %get-tuple-element.109.trow_ref.refs_11_, bf16[1024,768]{1,0:T(8,128)(2,1)} %refs_5_.1, f32[1024,128]{1,0:T(8,128)} %get-tuple-element.122.lg_ref.refs_9_, s32[1024,2]{1,0:T(8,128)} %copy.89.rt_ref.refs_10_.refs_14_), custom_call_target="tpu_custom_call" | custom-call | flops 4831838208 | bytes 6000000 | tf_op jit(solution)/shard_map/dispatch_grad/pallas_call | solution.py:72
  349.7 17.9 %all-to-all-done.1.refs_2_ = bf16[8,192,768]{2,1,0:T(8,128)(2,1)} async-done(((bf16[8,192,768]{2,1,0:T(8,128)(2,1)}), bf16[8,192,768]{2,1,0:T(8,128)(2,1)}, u32[]{:S(2)}, u32[]{:S(2)}) %all-to-all-start.1) | async-done | bytes 2359328 | tf_op jit(solution)/shard_map/all_to_all | solution.py:1439
  373.4 27.4 %all-to-all-done.2.refs_3_ = bf16[8,192,768]{2,1,0:T(8,128)(2,1)} async-done(((bf16[8,192,768]{2,1,0:T(8,128)(2,1)}), bf16[8,192,768]{2,1,0:T(8,128)(2,1)}, u32[]{:S(2)}, u32[]{:S(2)}) %all-to-all-start.2) | async-done | bytes 2359328 | tf_op jit(solution)/shard_map/all_to_all | solution.py:1439
  403.4 74.5 %expert_both.1 = (f32[1024,768]{1,0:T(8,128)}, f32[1024,768]{1,0:T(8,128)}, f32[1024,128]{1,0:T(8,128)}, bf16[1024,768]{1,0:T(8,128)(2,1)}, f32[128,768]{1,0:T(8,128)}, /*index=5*/f32[128,768]{1,0:T(8,128)}) custom-call(bf16[768,4096]{1,0:T(8,128)(2,1)} %bitcast.131, bf16[2048,768]{1,0:T(8,128)(2,1)} %bitcast.138, ...), custom_call_target="tpu_custom_call" | custom-call | flops 28991029248 | bytes 26000000 | tf_op jit(solution)/shard_map/expert_both/pallas_call | solution.py:605
  477.9 44.6 %layer_back.2 = (f32[1024,768]{1,0:T(8,128)}, f32[128,2304]{1,0:T(8,128)}, f32[128,768]{1,0:T(8,128)}) custom-call(f32[1024,768]{1,0:T(8,128)} %get-tuple-element.130.refs_0_, bf16[1024,768]{1,0:T(8,128)(2,1)} %get-tuple-element.131.refs_1_, bf16[1024,768]{1,0:T(8,128)(2,1)} %get-tuple-element.120.mixed_ref.refs_6_.refs_2_, ...), custom_call_target="tpu_custom_call" | custom-call | flops 19730006016 | bytes 40000000 | tf_op jit(solution)/shard_map/layer_back/pallas_call | solution.py:605
  522.4 70.3 %expert_backward.1 = (bf16[1024,768]{1,0:T(8,128)(2,1)}, f32[1024,768]{1,0:T(8,128)}, f32[128,768]{1,0:T(8,128)}, f32[128,768]{1,0:T(8,128)}) custom-call(bf16[4,96,4096]{2,1,0:T(8,128)(2,1)} %bitcast.133, bf16[4,96,4096]{2,1,0:T(8,128)(2,1)} %bitcast.137, bf16[2048,768]{1,0:T(8,128)(2,1)} %bitcast.135, bf16[4,384,2048]{2,1,0:T(8,128)(2,1)} %get-tuple-element.128.refs_3_, ...), custom_call_target="tpu_custom_call" | custom-call | flops 14495514624 | bytes 26000000 | tf_op jit(solution)/shard_map/expert_backward/pallas_call | solution.py:605
  592.7 44.4 %layer_back.3 = (f32[1024,768]{1,0:T(8,128)}, f32[128,2304]{1,0:T(8,128)}, f32[128,768]{1,0:T(8,128)}) custom-call(f32[1024,768]{1,0:T(8,128)} %get-tuple-element.140.refs_0_, bf16[1024,768]{1,0:T(8,128)(2,1)} %get-tuple-element.141.refs_1_, bf16[1024,768]{1,0:T(8,128)(2,1)} %get-tuple-element.103.mixed_ref.refs_9_.refs_2_, ...), custom_call_target="tpu_custom_call" | custom-call | flops 19730006016 | bytes 40000000 | tf_op jit(solution)/shard_map/layer_back/pallas_call | solution.py:605
  637.2 27.6 %adapters.1 = f32[2,96,256]{2,1,0:T(8,128)} custom-call(s32[1]{0:T(128)} %copy.116.refs_0_, f32[128,768]{1,0:T(8,128)} %get-tuple-element.146.refs_1_, f32[128,768]{1,0:T(8,128)} %get-tuple-element.147.refs_2_, f32[128,2304]{1,0:T(8,128)} %get-tuple-element.148.refs_3_, f32[128,768]{1,0:T(8,128)} %get-tuple-element.149.refs_4_, ...), custom_call_target="tpu_custom_call" | custom-call | tf_op jit(solution)/shard_map/adapters/pallas_call | solution.py:1393
  (106 shorter events, 60.5 us)
Async XLA Ops:
  7.2 231.1 %all-gather.14.cloned.1.call-start = ((), (), s32[]{:S(2)}) async-start(), calls=%async_computation.6 | async-start | bytes 3932160 | tf_op jit(solution)/shard_map/all_gather | solution.py:1490
  9.4 1.4 copy-start.8
  10.7 227.6 %all-gather.12.cloned.1.call-start = ((), (), s32[]{:S(2)}) async-start(), calls=%async_computation.5 | async-start | bytes 3932160 | tf_op jit(solution)/shard_map/all_gather | solution.py:1435
  13.8 1.8 copy-start.3
  71.3 166.9 %all-gather.16.cloned.1.call-start = ((), (), s32[]{:S(2)}) async-start(), calls=%async_computation.7 | async-start | bytes 3932160 | tf_op jit(solution)/shard_map/all_gather | solution.py:1496
  72.1 301.3 %all-gather.10.cloned.1.call-start = ((), (), s32[]{:S(2)}) async-start(), calls=%async_computation.4 | async-start | bytes 3932160 | tf_op jit(solution)/shard_map/all_gather | solution.py:1435
  75.5 2.4 copy-start.9
  75.5 2.4 copy-start.14
  75.5 3.5 copy-start.15
  80.1 5.6 copy-start.5
  95.1 2.6 copy-start.12
  95.1 3.2 copy-start
  95.1 3.2 copy-start.7
  133.5 8.6 %copy-start.1 = (bf16[2,256,768]{2,1,0:T(8,128)(2,1)S(1)}, bf16[2,256,768]{2,1,0:T(8,128)(2,1)}, u32[]{:S(2)}) copy-start(bf16[2,256,768]{2,1,0:T(8,128)(2,1)} %get-tuple-element.108) | copy-start | bytes 2359300
  142.1 10.7 %collective-permute-start.1 = (bf16[256,768]{1,0:T(8,128)(2,1)S(1)}, bf16[256,768]{1,0:T(8,128)(2,1)S(1)}, u32[]{:S(2)}, u32[]{:S(2)}) collective-permute-start(bf16[256,768]{1,0:T(8,128)(2,1)S(1)} %get-tuple-element.181), channel_id=1, source_target_pairs={{0,1},{1,0},{2,3},{3,2},{4,5},{5,4},{6,7},{7,6},{8,9},{9,8},{10,11... | collective-permute-start | bytes 1179656 | tf_op jit(solution)/shard_map/ppermute | solution.py:1426
  153.9 249.5 %all-gather.8.cloned.1.call-start = ((), (), s32[]{:S(2)}) async-start(), calls=%async_computation.3 | async-start | bytes 7864320 | tf_op jit(solution)/shard_map/all_gather | solution.py:1435
  154.3 18.4 %collective-permute-start = (bf16[96,4096]{1,0:T(8,128)(2,1)S(1)}, bf16[96,4096]{1,0:T(8,128)(2,1)S(1)}, u32[]{:S(2)}, u32[]{:S(2)}) collective-permute-start(bf16[96,4096]{1,0:T(8,128)(2,1)S(1)} %get-tuple-element.171), channel_id=1, source_target_pairs={{0,1},{1,0},{2,3},{3,2},{4,5},{5,4},{6,7},{7,6},{8,9},{9,8},{10,11... | collective-permute-start | bytes 2359304 | tf_op jit(solution)/shard_map/ppermute | solution.py:1426
  181.1 6.0 copy-start.4
  181.1 6.3 copy-start.2
  181.1 57.1 %all-to-all-start = ((bf16[8,192,768]{2,1,0:T(8,128)(2,1)}), bf16[8,192,768]{2,1,0:T(8,128)(2,1)}, u32[]{:S(2)}, u32[]{:S(2)}) async-start(bf16[8,192,768]{2,1,0:T(8,128)(2,1)} %dispatch.2), calls=%async_computation | async-start | bytes 4718592 | tf_op jit(solution)/shard_map/all_to_all | solution.py:1439
  189.3 48.3 %copy-start.13 = (f32[2,2,768]{2,1,0:T(2,128)S(1)}, f32[2,2,768]{2,1,0:T(2,128)}, u32[]{:S(2)}) copy-start(f32[2,2,768]{2,1,0:T(2,128)} %param.36) | copy-start | bytes 36868
  334.8 32.8 %all-to-all-start.1 = ((bf16[8,192,768]{2,1,0:T(8,128)(2,1)}), bf16[8,192,768]{2,1,0:T(8,128)(2,1)}, u32[]{:S(2)}, u32[]{:S(2)}) async-start(bf16[8,192,768]{2,1,0:T(8,128)(2,1)} %dispatch.3), calls=%async_computation.1 | async-start | bytes 4718592 | tf_op jit(solution)/shard_map/all_to_all | solution.py:1439
  349.7 22.9 %copy-start.6 = (bf16[2,128,768]{2,1,0:T(8,128)(2,1)S(1)}, bf16[2,128,768]{2,1,0:T(8,128)(2,1)}, u32[]{:S(2)}) copy-start(bf16[2,128,768]{2,1,0:T(8,128)(2,1)} %get-tuple-element.124) | copy-start | bytes 1179652
  367.6 33.1 %all-to-all-start.2 = ((bf16[8,192,768]{2,1,0:T(8,128)(2,1)}), bf16[8,192,768]{2,1,0:T(8,128)(2,1)}, u32[]{:S(2)}, u32[]{:S(2)}) async-start(bf16[8,192,768]{2,1,0:T(8,128)(2,1)} %dispatch_grad.1), calls=%async_computation.2 | async-start | bytes 4718592 | tf_op jit(solution)/shard_map/all_to_all | solution.py:1439
  (2 other events, 2.3 us)
Sparse Core Ops, SparseCore 0:
  10.8 73.1 all-gather.13
  85.5 63.0 all-gather.11
  150.1 73.4 all-gather.15
  225.1 63.1 all-gather.9
  289.7 113.6 all-gather.7

commit v5 on v4

--- a/solution.py
+++ b/solution.py
@@ -644,40 +644,91 @@
     )
 
 
-def expert_both_body(kind, far, near, out_near, scratch, ready, done):
-    gate_up_ref, down_ref, rec_ref, sg_ref, mid_ref, g_ref, mixed_ref, shared_ref = far
-    tcol_ref, lg_ref, rt_ref, gain_ref, cv_ref, wt_ref, res_ref, nar_ref, d_ref, u_ref = near
-    out_ref, gm_ref, gle_ref, mix_ref, gu_ref, gd_ref = out_near
-    (
-        w1, w2, rv, sv, pv, gv, uv, back, gback, mid, g, mixed, w3, acc,
-        wsem, rsem, ssem, msem, send, recv, gsend, grecv,
-    ) = scratch
-    weights = fetch_weights(False, [gate_up_ref], down_ref, w1, w2, wsem)
-    blocks = fetch_blocks(rec_ref, rv, rsem, kind)
-    greet(kind)
-    for copy in weights + blocks:
+def expert_parts_body(kind, far, outs, scratch):
+    gate_up_ref, rec_ref = far
+    w1, rv, wsem, rsem, osem, *kept = scratch
+    load = pltpu.make_async_copy(gate_up_ref, w1, wsem.at[0])
+    load.start()
+    for copy in fetch_blocks(rec_ref, rv, rsem, kind) + [load]:
         copy.wait()
-    extra = fetch_blocks(sg_ref, sv, ssem, kind)
-    for n, (source, target) in enumerate(
-        ((mid_ref, mid), (g_ref, g), (mixed_ref, mixed), (shared_ref.at[3], w3))
-    ):
-        extra.append(pltpu.make_async_copy(source, target, msem.at[n]))
-        extra[-1].start()
-    moves = []
+    stores = []
     for p in range(NP):
         r = rv[p]
-        acc[...] = jnp.zeros_like(acc)
 
         def step(f, carry):
-            gate, up, part = forward_chunk(r, w1, w2, f)
-            gv[p, :, pl.ds(chunk_at(f), FC)] = gate.astype(BF)
-            uv[p, :, pl.ds(chunk_at(f), FC)] = up.astype(BF)
-            acc[...] += part
+            at = pl.ds(chunk_at(f), FC)
+            gate = mm(r, w1[:, at])
+            up = mm(r, w1[:, pl.ds(pl.multiple_of(FF + f * FC, FC), FC)])
+            s = sigmoid(gate)
+            silu = gate * s
+            kept[0][p, :, at] = (silu * up).astype(BF)
+            kept[1][p, :, at] = (up * s * (1.0 + gate * (1.0 - s))).astype(BF)
+            kept[2][p, :, at] = silu.astype(BF)
             return carry
 
         lax.fori_loop(0, FF // FC, step, 0)
-        pv[p] = acc[...].astype(BF)
+        for n in range(3):
+            stores.append(pltpu.make_async_copy(kept[n].at[p], outs[n].at[p], osem.at[p, n]))
+            stores[-1].start()
+    for copy in stores:
+        copy.wait()
+
+
+def expert_parts(received, gate_up, kind):
+    def body(far, near, outs, near_outs, scratch, ready, done):
+        expert_parts_body(kind, far, outs, scratch)
+
+    return comm_call(
+        body,
+        [gate_up, received],
+        [KEPT, KEPT, KEPT],
+        [WEIGHTS[0], ROWS, DMA((1,)), DMA((8,)), DMA((NP, 3)), WIDE, WIDE, WIDE],
+        "expert_parts",
+        None,
+        2 * SLOTS * D * FF * 2,
+        28e6,
+    )
+
+
+def expert_both_body(kind, far, near, mix_out, out_near, scratch, ready, done):
+    (
+        gate_up_ref, down_ref, active_ref, to_gate_ref, to_up_ref, sg_ref, mid_ref, g_ref,
+        mixed_ref, shared_ref,
+    ) = far
+    tcol_ref, lg_ref, rt_ref, gain_ref, cv_ref, wt_ref, res_ref, nar_ref, d_ref, u_ref = near
+    out_ref, gm_ref, gle_ref, gu_ref, gd_ref = out_near
+    (
+        w1, w2, qv, sv, pv, to_gate, to_up, av, back, gback, mid, g, mixed, w3, acc,
+        wsem, asem, ssem, msem, send, recv, gsend, grecv,
+    ) = scratch
+
+    def start(source, target, sem):
+        copy = pltpu.make_async_copy(source, target, sem)
+        copy.start()
+        return copy
+
+    load = start(down_ref, w2, wsem.at[0])
+    actives = [start(active_ref.at[p], av.at[p], asem.at[p]) for p in range(2)]
+    greet(kind)
+    load.wait()
+    moves = []
+    extra = []
+    for p in range(NP):
+        actives[p].wait()
+        pv[p] = mm(av[p % 2], w2[...]).astype(BF)
         moves += give_back(pv, p, back, send, recv, kind)
+        if p + 2 < NP:
+            actives.append(start(active_ref.at[p + 2], av.at[p % 2], asem.at[p + 2]))
+        if p == 0:
+            extra = fetch_blocks(sg_ref, sv, ssem, kind)
+            extra.append(start(gate_up_ref, w1, wsem.at[1]))
+            for n, (source, target) in enumerate(
+                (
+                    (to_gate_ref, to_gate), (to_up_ref, to_up), (mid_ref, mid), (g_ref, g),
+                    (mixed_ref, mixed), (shared_ref.at[3], w3),
+                )
+            ):
+                extra.append(start(source, target, msem.at[n]))
     for copy in extra:
         copy.wait()
     later = []
@@ -687,14 +738,17 @@
 
         def step(f, carry):
             at = pl.ds(chunk_at(f), FC)
-            gate = gv[p, :, at].astype(F32)
-            up = uv[p, :, at].astype(F32)
-            acc[...] += backward_chunk(grads, gate, up, w1, w2, f)
+            grad = mm_nt(grads, w2[at, :])
+            first = (grad * to_gate[p, :, at].astype(F32)).astype(BF)
+            second = (grad * to_up[p, :, at].astype(F32)).astype(BF)
+            acc[...] += mm_nt(first, w1[:, at]) + mm_nt(
+                second, w1[:, pl.ds(pl.multiple_of(FF + f * FC, FC), FC)]
+            )
             return carry
 
         lax.fori_loop(0, FF // FC, step, 0)
-        rv[p] = acc[...].astype(BF)
-        later += give_back(rv, p, gback, gsend, grecv, kind)
+        qv[p] = acc[...].astype(BF)
+        later += give_back(qv, p, gback, gsend, grecv, kind)
     for copy in moves:
         copy.wait()
     ready()
@@ -722,38 +776,39 @@
     def settle_one(i, carry):
         at = pl.ds(pl.multiple_of(i * RB, RB), RB)
         refs = (tcol_ref, mid, g, mixed, gain_ref, nar_ref, w3, d_ref, u_ref, gu_ref, gd_ref)
-        settle_back(refs, at, gm_ref, mix_ref, gback)
+        settle_back(refs, at, gm_ref, mixed, gback)
         return carry
 
     lax.fori_loop(0, NB, settle_one, 0)
-    for copy in stores + [done(n) for n in (1, 3, 4, 5)]:
+    stores.append(start(mixed, mix_out, msem.at[6]))
+    for copy in stores + [done(n) for n in (1, 3, 4)]:
         copy.wait()
 
 
 def expert_both(
-    received, slot_grads, gate_up, down, mid, g, mixed, weights, tcol, logits, routes, gain,
+    active, to_gate, to_up, slot_grads, gate_up, down, mid, g, mixed, weights, tcol, logits, routes, gain,
     const_vec, router_t, residual_t, narrow, down_out, up_out, kind,
 ):
     def body(far, near, outs, near_outs, scratch, ready, done):
-        expert_both_body(kind, far, near, near_outs, scratch, ready, done)
+        expert_both_body(kind, far, near, outs[0], near_outs, scratch, ready, done)
 
     half = pltpu.VMEM((T, D), BF)
     landing = pltpu.VMEM((NFFN, CAP, D), BF)
     return comm_call(
         body,
-        [gate_up, down, received, slot_grads, mid, g, mixed, weights],
-        [],
+        [gate_up, down, active, to_gate, to_up, slot_grads, mid, g, mixed, weights],
+        [out((T, D), BF)],
         WEIGHTS
-        + [ROWS, ROWS, ROWS, WIDE, WIDE, landing, landing]
+        + [ROWS, ROWS, ROWS, WIDE, WIDE, pltpu.VMEM((2, PR, FF), BF), landing, landing]
         + [pltpu.VMEM((T, D), F32), pltpu.VMEM((T, D), g.dtype), half, pltpu.VMEM((D, D), BF), SUM]
-        + [DMA((9,)), DMA((8,)), DMA((8,)), DMA((4,))]
+        + [DMA((2,)), DMA((NP,)), DMA((8,)), DMA((7,))]
         + [DMA((8,)), DMA((8,)), DMA((8,)), DMA((8,))],
         "expert_both",
         2,
-        2 * SLOTS * D * FF * 6,
-        26e6,
+        2 * SLOTS * D * FF * 4,
+        40e6,
         [tcol, logits, routes, gain, const_vec, router_t, residual_t, narrow, down_out, up_out],
-        [out((T, D), F32), out((T, D), F32), out((T, 128), F32), out((T, D), BF)]
+        [out((T, D), F32), out((T, D), F32), out((T, 128), F32)]
         + [out((128, D), F32), out((128, D), F32)],
     )
 
@@ -1542,8 +1597,9 @@
         if layer == 0:
             if fast:
                 later = barrier((w_gate_up[1], w_down[1], logits))
-                gate_up_full.append([gathered(swapped(later[0]), ("zh", "zl"))])
-                down_full.append(gathered(swapped(later[1]), ("zh", "zl")))
+                gate_up_next, down_next = barrier((swapped(later[0]), later[1]))
+                gate_up_full.append([gathered(gate_up_next, ("zh", "zl"))])
+                down_full.append(gathered(swapped(down_next), ("zh", "zl")))
             later = lax.optimization_barrier(
                 (query_key_value_weight[1], output_weight[1], logits)
             )
@@ -1551,8 +1607,8 @@
             returned, gate, up = expert_forward(received, gate_up_full[0], down_full[0], kind)
         else:
             slot_grads = exchange(dispatch_grad(trow, out_grad, logits, routes), kind)
-            following, grad_mid, grad_logits, grad_mixed, gu_out, gd_out = expert_both(
-                received, slot_grads, gate_up_full[1][0], down_full[1], mid, out_grad, mixed,
+            grad_mixed, following, grad_mid, grad_logits, gu_out, gd_out = expert_both(
+                *expert_parts(received, gate_up_full[1][0], kind), slot_grads, gate_up_full[1][0], down_full[1], mid, out_grad, mixed,
                 shared[1], tcol, logits, routes, gain1, const_vec[1], router_ts[1], residual_ts,
                 narrow_out, down_out[1], up_out[1], kind,
             )

time: 682 us -> 675 us (0.990)
  waiting for transfers between devices: 77.1 us -> 49.9 us
  Pallas kernels: 522 us -> 541 us
    all_to_all x3, waiting for transfers between devices: 45.2 us -> 17.9 us  [exchange(): lax.all_to_all(v, OWNERS[kind], split_axis=0, concat_axis=0, tiled=True)]
    pallas_call x7 -> x8, Pallas kernels: 371 us -> 390 us  [comm_call(): pl.pallas_call(run, in_specs=[pl.BlockSpec(memory_space=pl.ANY)] * len(in...]
    all_gather x3, waiting for transfers between devices: 2.64 us -> 12.4 us  [gathered(): return lax.all_gather(w, axes, axis=0, tiled=True).reshape(-1, w.shape[-1])]
    ppermute x2, waiting for transfers between devices: 28.5 us -> 18.8 us  [across_y(): return lax.ppermute(v, 'y', [(0, 1), (1, 0)])]
  transfers between devices with their start and end apart: 10 -> 10, of which waited for: 5 -> 3; matrix products, arithmetic and copies ran while one was open for 5% -> 6% of each run, Pallas kernels for 39% -> 42%
where the time goes in v5:
time: 675 us; the launch traced here: 671 us
  Pallas kernels  541 us (80%)
  waiting for transfers between devices  49.9 us (7%)
  local copies, waits for them, and re-layouts  41.5 us (6%)
  between operations  15.1 us (2%)
  starting transfers between devices  14.5 us (2%)
  other arithmetic  9.59 us (1%)
    pallas_call x8, Pallas kernels, comm_call(): pl.pallas_call(run, in_specs=[pl.BlockSpec(memory_space=pl.ANY)] * len(in...  390 us
    pallas_call x11, Pallas kernels, call(): pl.pallas_call(body, grid=grid, in_specs=[spec(e) for e in ins], out_spec...  123 us
    pallas_call x1, Pallas kernels, adapters(): pl.pallas_call(adapters_body, in_specs=specs, out_specs=pl.BlockSpec(memo...  27.1 us
    ppermute x2, waiting for transfers between devices, across_y(): return lax.ppermute(v, 'y', [(0, 1), (1, 0)])  18.8 us
    all_to_all x3, waiting for transfers between devices, exchange(): lax.all_to_all(v, OWNERS[kind], split_axis=0, concat_axis=0, tiled=True)  17.9 us
  transfers between devices with their start and end apart: 10, of which 3 were waited for; matrix products, arithmetic and copies ran while one was open for 6% of the time, Pallas kernels for 42%

profile of v5, /device:TPU:9, one launch (start us, length us, event | category | flops | bytes accessed | tf_op | source)
XLA Modules:
  0.0 671.2 jit_solution(6511446830154714616)
XLA Ops:
  17.3 51.7 %gather_shared.2 = (bf16[4,768,768]{2,1,0:T(8,128)(2,1)}, bf16[96,4096]{1,0:T(8,128)(2,1)}, bf16[256,768]{1,0:T(8,128)(2,1)}) custom-call(bf16[96,768]{1,0:T(8,128)(2,1)} %bitcast.124, bf16[96,4096]{1,0:T(8,128)(2,1)} %get-tuple-element.179.refs_1_, bf16[256,768]{1,0:T(8,128)(2,1)} %get-tuple-element.189.refs_2_), custom_call_target="tpu_custom_call" | custom-call | bytes 50000000 | tf_op jit(solution)/shard_map/gather_shared/pallas_call | solution.py:605
  87.1 6.3 prep.1
  98.0 11.1 %project.2 = (bf16[1024,768]{1,0:T(8,128)(2,1)}, bf16[1024,128]{1,0:T(8,128)(2,1)}, bf16[1024,2304]{1,0:T(8,128)(2,1)}) custom-call(bf16[1024,768]{1,0:T(8,128)(2,1)} %refs_7_.3, f32[1,768]{1,0:T(1,128)} %get-tuple-element.214.g_ref.refs_8_, bf16[4,768,768]{2,1,0:T(8,128)(2,1)} %get-tuple-element.102.w_ref.refs_10_.refs_3_, ...), custom_call_target="tpu_custom_call" | custom-call | flops 3623878656 | bytes 12000000 | tf_op jit(solution)/shard_map/project/pallas_call | solution.py:72
  109.0 21.4 %attend.2 = (bf16[1024,768]{1,0:T(8,128)(2,1)}, bf16[6,1024,128]{2,1,0:T(8,128)(2,1)}) custom-call(bf16[1024,2304]{1,0:T(8,128)(2,1)} %get-tuple-element.105.q_ref.k_ref.v_ref.refs_4_, bf16[1024,2304]{1,0:T(8,128)(2,1)} %get-tuple-element.105.q_ref.k_ref.v_ref.refs_4_, bf16[1024,2304]{1,0:T(8,128)(2,1)} %get-tuple-element.105.q_ref.k_ref.v_ref.refs_4_, ...), custom_call_target="tpu_custom_call" | custom-call | flops 6442450944 | bytes 8000000 | tf_op jit(solution)/shard_map/attend/pallas_call | solution.py:72
  131.2 8.7 %settle.2 = (f32[1024,768]{1,0:T(8,128)}, bf16[1024,768]{1,0:T(8,128)(2,1)}, f32[1024,128]{1,0:T(8,128)}, bf16[1024,128]{1,0:T(8,128)(2,1)}) custom-call(bf16[1024,768]{1,0:T(8,128)(2,1)} %refs_7_.3, bf16[1024,768]{1,0:T(8,128)(2,1)} %get-tuple-element.108.mixed_ref.refs_9_.refs_2_, bf16[4,768,768]{2,1,0:T(8,128)(2,1)} %get-tuple-element.102.w_ref.refs_10_.refs_3_, ...), custom_call_target="tpu_custom_call" | custom-call | flops 2415919104 | bytes 10000000 | tf_op jit(solution)/shard_map/settle/pallas_call | solution.py:72
  140.4 18.8 %collective-permute-done = bf16[96,4096]{1,0:T(8,128)(2,1)S(1)} collective-permute-done((bf16[96,4096]{1,0:T(8,128)(2,1)S(1)}, bf16[96,4096]{1,0:T(8,128)(2,1)S(1)}, u32[]{:S(2)}, u32[]{:S(2)}) %collective-permute-start) | collective-permute-done | bytes 786464 | tf_op jit(solution)/shard_map/ppermute | solution.py:1481
  160.8 7.0 %dispatch.2 = bf16[8,192,768]{2,1,0:T(8,128)(2,1)} custom-call(s32[8,1024]{1,0:T(8,128)} %get-tuple-element.116.trow_ref.refs_11_, bf16[1024,768]{1,0:T(8,128)(2,1)} %get-tuple-element.120.s_ref), custom_call_target="tpu_custom_call" | custom-call | flops 2415919104 | bytes 4000000 | tf_op jit(solution)/shard_map/dispatch/pallas_call | solution.py:72
  167.8 4.4 all-to-all-start
  179.7 50.4 %gather_shared.3.w_ref.refs_9_.refs_3_ = bf16[4,768,768]{2,1,0:T(8,128)(2,1)} custom-call(bf16[96,768]{1,0:T(8,128)(2,1)} %bitcast.122), custom_call_target="tpu_custom_call" | custom-call | bytes 50000000 | tf_op jit(solution)/shard_map/gather_shared/pallas_call | solution.py:605
  234.3 38.5 %expert_forward.1 = (bf16[8,192,768]{2,1,0:T(8,128)(2,1)}, bf16[4,384,2048]{2,1,0:T(8,128)(2,1)}, bf16[4,384,2048]{2,1,0:T(8,128)(2,1)}) custom-call(bf16[4,96,4096]{2,1,0:T(8,128)(2,1)} %bitcast.132, bf16[4,96,4096]{2,1,0:T(8,128)(2,1)} %bitcast.136, bf16[2048,768]{1,0:T(8,128)(2,1)} %bitcast.134, bf16[8,192,768]{2,1,0:T(8,128)(2,1)} %copy-done.3), custom_call_target="tpu_custom_call" | custom-call | flops 14495514624 | bytes 26000000 | tf_op jit(solution)/shard_map/expert_forward/pallas_call | solution.py:605
  272.8 10.2 %combine.1 = (f32[1024,768]{1,0:T(8,128)}, bf16[1024,768]{1,0:T(8,128)(2,1)}, bf16[1024,768]{1,0:T(8,128)(2,1)}) custom-call(s32[1024,128]{1,0:T(8,128)} %get-tuple-element.117.tcol_ref.refs_10_.refs_12_, bf16[1536,768]{1,0:T(8,128)(2,1)} %bitcast.139, f32[1024,768]{1,0:T(8,128)} %get-tuple-element.122.mid_ref.refs_6_, ...), custom_call_target="tpu_custom_call" | custom-call | flops 4831838208 | bytes 12000000 | tf_op jit(solution)/shard_map/combine/pallas_call | solution.py:72
  283.0 11.1 %project.3 = (bf16[1024,768]{1,0:T(8,128)(2,1)}, bf16[1024,128]{1,0:T(8,128)(2,1)}, bf16[1024,2304]{1,0:T(8,128)(2,1)}) custom-call(f32[1024,768]{1,0:T(8,128)} %get-tuple-element.123.x_ref.refs_7_, f32[1,768]{1,0:T(1,128)} %get-tuple-element.215.g_ref.refs_8_, bf16[4,768,768]{2,1,0:T(8,128)(2,1)} %gather_shared.3.w_ref.refs_9_.refs_3_, ...), custom_call_target="tpu_custom_call" | custom-call | flops 3623878656 | bytes 12000000 | tf_op jit(solution)/shard_map/project/pallas_call | solution.py:72
  294.1 21.7 %attend.3 = (bf16[1024,768]{1,0:T(8,128)(2,1)}, bf16[6,1024,128]{2,1,0:T(8,128)(2,1)}) custom-call(bf16[1024,2304]{1,0:T(8,128)(2,1)} %get-tuple-element.126.q_ref.k_ref.v_ref.refs_4_, bf16[1024,2304]{1,0:T(8,128)(2,1)} %get-tuple-element.126.q_ref.k_ref.v_ref.refs_4_, bf16[1024,2304]{1,0:T(8,128)(2,1)} %get-tuple-element.126.q_ref.k_ref.v_ref.refs_4_, ...), custom_call_target="tpu_custom_call" | custom-call | flops 6442450944 | bytes 8000000 | tf_op jit(solution)/shard_map/attend/pallas_call | solution.py:72
  315.8 8.7 %settle.3 = (f32[1024,768]{1,0:T(8,128)}, bf16[1024,768]{1,0:T(8,128)(2,1)}, f32[1024,128]{1,0:T(8,128)}, bf16[1024,128]{1,0:T(8,128)(2,1)}) custom-call(f32[1024,768]{1,0:T(8,128)} %get-tuple-element.123.x_ref.refs_7_, bf16[1024,768]{1,0:T(8,128)(2,1)} %get-tuple-element.127.mixed_ref.refs_8_.refs_2_, ...), custom_call_target="tpu_custom_call" | custom-call | flops 2415919104 | bytes 10000000 | tf_op jit(solution)/shard_map/settle/pallas_call | solution.py:72
  324.6 6.9 %dispatch.3 = bf16[8,192,768]{2,1,0:T(8,128)(2,1)} custom-call(s32[8,1024]{1,0:T(8,128)} %get-tuple-element.116.trow_ref.refs_11_, bf16[1024,768]{1,0:T(8,128)(2,1)} %get-tuple-element.128.s_ref), custom_call_target="tpu_custom_call" | custom-call | flops 2415919104 | bytes 4000000 | tf_op jit(solution)/shard_map/dispatch/pallas_call | solution.py:72
  335.4 10.3 %dispatch_grad.1 = bf16[8,192,768]{2,1,0:T(8,128)(2,1)} custom-call(s32[8,1024]{1,0:T(8,128)} %get-tuple-element.116.trow_ref.refs_11_, bf16[1024,768]{1,0:T(8,128)(2,1)} %refs_7_.2, f32[1024,128]{1,0:T(8,128)} %get-tuple-element.132.lg_ref.refs_11_, s32[1024,2]{1,0:T(8,128)} %copy.89.rt_ref.refs_12_.refs_14_), custom_call_target="tpu_custom_call" | custom-call | flops 4831838208 | bytes 6000000 | tf_op jit(solution)/shard_map/dispatch_grad/pallas_call | solution.py:72
  345.8 17.9 %all-to-all-done.1.refs_1_ = bf16[8,192,768]{2,1,0:T(8,128)(2,1)S(1)} async-done(((bf16[8,192,768]{2,1,0:T(8,128)(2,1)}), bf16[8,192,768]{2,1,0:T(8,128)(2,1)S(1)}, u32[]{:S(2)}, u32[]{:S(2)}) %all-to-all-start.1) | async-done | bytes 2359328 | tf_op jit(solution)/shard_map/all_to_all | solution.py:1494
  370.0 20.9 %expert_parts.1 = (bf16[4,384,2048]{2,1,0:T(8,128)(2,1)}, bf16[4,384,2048]{2,1,0:T(8,128)(2,1)}, bf16[4,384,2048]{2,1,0:T(8,128)(2,1)}) custom-call(bf16[768,4096]{1,0:T(8,128)(2,1)} %bitcast.130, bf16[8,192,768]{2,1,0:T(8,128)(2,1)} %copy-done.5), custom_call_target="tpu_custom_call" | custom-call | flops 9663676416 | bytes 28000000 | tf_op jit(solution)/shard_map/expert_parts/pallas_call | solution.py:605
  390.9 12.4 %all-gather.10.cloned.1.call-done = bf16[8,256,768]{2,1,0:T(8,128)(2,1)} async-done(((bf16[2,256,768]{2,1,0:T(8,128)(2,1)}), bf16[8,256,768]{2,1,0:T(8,128)(2,1)}) %all-gather.10.cloned.1.call-update) | async-done | bytes 3145744 | tf_op jit(solution)/shard_map/all_gather | solution.py:1490
  404.8 69.0 %expert_both.1 = (bf16[1024,768]{1,0:T(8,128)(2,1)}, f32[1024,768]{1,0:T(8,128)}, f32[1024,768]{1,0:T(8,128)}, f32[1024,128]{1,0:T(8,128)}, f32[128,768]{1,0:T(8,128)}, /*index=5*/f32[128,768]{1,0:T(8,128)}) custom-call(bf16[768,4096]{1,0:T(8,128)(2,1)} %bitcast.131, bf16[2048,768]{1,0:T(8,128)(2,1)} %bitcast.138, ...), custom_call_target="tpu_custom_call" | custom-call | flops 19327352832 | bytes 40000000 | tf_op jit(solution)/shard_map/expert_both/pallas_call | solution.py:605
  473.8 44.6 %layer_back.2 = (f32[1024,768]{1,0:T(8,128)}, f32[128,2304]{1,0:T(8,128)}, f32[128,768]{1,0:T(8,128)}) custom-call(f32[1024,768]{1,0:T(8,128)} %get-tuple-element.140.refs_0_, bf16[1024,768]{1,0:T(8,128)(2,1)} %get-tuple-element.141.refs_1_, bf16[1024,768]{1,0:T(8,128)(2,1)} %get-tuple-element.127.mixed_ref.refs_8_.refs_2_, ...), custom_call_target="tpu_custom_call" | custom-call | flops 19730006016 | bytes 40000000 | tf_op jit(solution)/shard_map/layer_back/pallas_call | solution.py:605
  518.4 70.3 %expert_backward.1 = (bf16[1024,768]{1,0:T(8,128)(2,1)}, f32[1024,768]{1,0:T(8,128)}, f32[128,768]{1,0:T(8,128)}, f32[128,768]{1,0:T(8,128)}) custom-call(bf16[4,96,4096]{2,1,0:T(8,128)(2,1)} %bitcast.133, bf16[4,96,4096]{2,1,0:T(8,128)(2,1)} %bitcast.137, bf16[2048,768]{1,0:T(8,128)(2,1)} %bitcast.135, bf16[4,384,2048]{2,1,0:T(8,128)(2,1)} %get-tuple-element.138.refs_3_, ...), custom_call_target="tpu_custom_call" | custom-call | flops 14495514624 | bytes 26000000 | tf_op jit(solution)/shard_map/expert_backward/pallas_call | solution.py:605
  588.7 44.4 %layer_back.3 = (f32[1024,768]{1,0:T(8,128)}, f32[128,2304]{1,0:T(8,128)}, f32[128,768]{1,0:T(8,128)}) custom-call(f32[1024,768]{1,0:T(8,128)} %get-tuple-element.150.refs_0_, bf16[1024,768]{1,0:T(8,128)(2,1)} %get-tuple-element.151.refs_1_, bf16[1024,768]{1,0:T(8,128)(2,1)} %get-tuple-element.108.mixed_ref.refs_9_.refs_2_, ...), custom_call_target="tpu_custom_call" | custom-call | flops 19730006016 | bytes 40000000 | tf_op jit(solution)/shard_map/layer_back/pallas_call | solution.py:605
  633.2 27.1 %adapters.1 = f32[2,96,256]{2,1,0:T(8,128)} custom-call(s32[1]{0:T(128)} %copy.116.refs_0_, f32[128,768]{1,0:T(8,128)} %get-tuple-element.156.refs_1_, f32[128,768]{1,0:T(8,128)} %get-tuple-element.157.refs_2_, f32[128,2304]{1,0:T(8,128)} %get-tuple-element.158.refs_3_, f32[128,768]{1,0:T(8,128)} %get-tuple-element.159.refs_4_, ...), custom_call_target="tpu_custom_call" | custom-call | tf_op jit(solution)/shard_map/adapters/pallas_call | solution.py:1448
  (117 shorter events, 62.0 us)
Async XLA Ops:
  7.2 225.7 %all-gather.14.cloned.1.call-start = ((), (), s32[]{:S(2)}) async-start(), calls=%async_computation.6 | async-start | bytes 3932160 | tf_op jit(solution)/shard_map/all_gather | solution.py:1545
  10.6 222.3 %all-gather.12.cloned.1.call-start = ((), (), s32[]{:S(2)}) async-start(), calls=%async_computation.5 | async-start | bytes 3932160 | tf_op jit(solution)/shard_map/all_gather | solution.py:1490
  71.2 161.7 %all-gather.16.cloned.1.call-start = ((), (), s32[]{:S(2)}) async-start(), calls=%async_computation.7 | async-start | bytes 3932160 | tf_op jit(solution)/shard_map/all_gather | solution.py:1551
  72.0 298.0 %all-gather.8.cloned.1.call-start = ((), (), s32[]{:S(2)}) async-start(), calls=%async_computation.3 | async-start | bytes 7864320 | tf_op jit(solution)/shard_map/all_gather | solution.py:1490
  74.7 1.9 copy-start.15
  74.7 3.2 copy-start.16
  74.8 3.2 copy-start.14
  75.5 4.5 copy-start.19
  75.5 5.6 copy-start.20
  81.1 3.8 copy-start
  85.0 2.1 copy-start.13
  87.1 7.2 %copy-start.17 = (f32[2,2,768]{2,1,0:T(2,128)S(1)}, f32[2,2,768]{2,1,0:T(2,128)}, u32[]{:S(2)}) copy-start(f32[2,2,768]{2,1,0:T(2,128)} %param.28) | copy-start | bytes 36868
  87.1 7.8 %copy-start.9 = (bf16[2,4,16,768]{3,2,0,1:T(8,128)(2,1)S(1)}, bf16[2,4,16,768]{3,2,0,1:T(8,128)(2,1)}, u32[]{:S(2)}) copy-start(bf16[2,4,16,768]{3,2,0,1:T(8,128)(2,1)} %copy-done.8) | copy-start | bytes 589828
  140.1 19.2 %collective-permute-start = (bf16[96,4096]{1,0:T(8,128)(2,1)S(1)}, bf16[96,4096]{1,0:T(8,128)(2,1)S(1)}, u32[]{:S(2)}, u32[]{:S(2)}) collective-permute-start(bf16[96,4096]{1,0:T(8,128)(2,1)S(1)} %get-tuple-element.181), channel_id=1, source_target_pairs={{0,1},{1,0},{2,3},{3,2},{4,5},{5,4},{6,7},{7,6},{8,9},{9,8},{10,11... | collective-permute-start | bytes 2359304 | tf_op jit(solution)/shard_map/ppermute | solution.py:1481
  167.8 4.4 copy-start.2
  167.8 65.0 %all-to-all-start = ((bf16[8,192,768]{2,1,0:T(8,128)(2,1)}), bf16[8,192,768]{2,1,0:T(8,128)(2,1)S(1)}, u32[]{:S(2)}, u32[]{:S(2)}) async-start(bf16[8,192,768]{2,1,0:T(8,128)(2,1)} %dispatch.2), calls=%async_computation | async-start | bytes 4718592 | tf_op jit(solution)/shard_map/all_to_all | solution.py:1494
  172.2 231.1 %all-gather.10.cloned.1.call-start = ((), (), s32[]{:S(2)}) async-start(), calls=%async_computation.4 | async-start | bytes 3932160 | tf_op jit(solution)/shard_map/all_gather | solution.py:1490
  172.2 2.2 copy-start.10
  173.0 57.7 %collective-permute-start.1 = (bf16[256,768]{1,0:T(8,128)(2,1)}, bf16[256,768]{1,0:T(8,128)(2,1)}, u32[]{:S(2)}, u32[]{:S(2)}) collective-permute-start(bf16[256,768]{1,0:T(8,128)(2,1)} %get-tuple-element.191), channel_id=1, source_target_pairs={{0,1},{1,0},{2,3},{3,2},{4,5},{5,4},{6,7},{7,6},{8,9},{9,8},{10,11... | collective-permute-start | bytes 1179656 | tf_op jit(solution)/shard_map/ppermute | solution.py:1481
  179.7 50.4 %copy-start.18 = (f32[2,2,768]{2,1,0:T(2,128)S(1)}, f32[2,2,768]{2,1,0:T(2,128)}, u32[]{:S(2)}) copy-start(f32[2,2,768]{2,1,0:T(2,128)} %param.36) | copy-start | bytes 36868
  331.5 32.1 %all-to-all-start.1 = ((bf16[8,192,768]{2,1,0:T(8,128)(2,1)}), bf16[8,192,768]{2,1,0:T(8,128)(2,1)S(1)}, u32[]{:S(2)}, u32[]{:S(2)}) async-start(bf16[8,192,768]{2,1,0:T(8,128)(2,1)} %dispatch.3), calls=%async_computation.1 | async-start | bytes 4718592 | tf_op jit(solution)/shard_map/all_to_all | solution.py:1494
  345.8 23.4 %copy-start.11 = (bf16[2,128,768]{2,1,0:T(8,128)(2,1)S(1)}, bf16[2,128,768]{2,1,0:T(8,128)(2,1)}, u32[]{:S(2)}) copy-start(bf16[2,128,768]{2,1,0:T(8,128)(2,1)} %get-tuple-element.134) | copy-start | bytes 1179652
  365.1 38.2 %all-to-all-start.2 = ((bf16[8,192,768]{2,1,0:T(8,128)(2,1)}), bf16[8,192,768]{2,1,0:T(8,128)(2,1)S(1)}, u32[]{:S(2)}, u32[]{:S(2)}) async-start(bf16[8,192,768]{2,1,0:T(8,128)(2,1)} %dispatch_grad.1), calls=%async_computation.2 | async-start | bytes 4718592 | tf_op jit(solution)/shard_map/all_to_all | solution.py:1494
  633.2 29.6 %copy-start.1 = (f32[1024,768]{1,0:T(8,128)S(1)}, f32[1024,768]{1,0:T(8,128)}, u32[]{:S(2)}) copy-start(f32[1024,768]{1,0:T(8,128)} %get-tuple-element.222) | copy-start | bytes 9437188
  (7 other events, 9.1 us)
Sparse Core Ops, SparseCore 0:
  10.7 73.1 all-gather.13
  85.5 63.0 all-gather.11
  150.1 73.4 all-gather.15
  225.0 114.6 all-gather.7
  341.1 62.0 all-gather.9

commit v6 on v5

--- a/solution.py
+++ b/solution.py
@@ -1360,7 +1360,7 @@
 def adapters_body(*refs):
     id_ref, parts = refs[0], refs[1 : 1 + 4 * LAYERS]
     o_ref = refs[1 + 4 * LAYERS]
-    sbuf, rbuf, tbuf, ubuf, asend, arecv, bsend, brecv = refs[2 + 4 * LAYERS :]
+    sbuf, rbuf, tbuf, ubuf, ibuf, jbuf, asend, arecv, bsend, brecv, isend, irecv = refs[2 + 4 * LAYERS :]
     x, c, y = (lax.axis_index(name) for name in ("x", "c", "y"))
     z = 2 * lax.axis_index("zh") + lax.axis_index("zl")
     mates = []
@@ -1378,7 +1378,7 @@
         pieces = [gd_in[p * R : (p + 1) * R, :] for p in range(3)] + [gd_out[:R, :]]
         pieces += [gu_in[p * R : (p + 1) * R, p * D : (p + 1) * D] for p in range(3)] + [gu_out[:R, :]]
         sbuf[:, layer * 128 : (layer + 1) * 128] = jnp.concatenate(pieces).T.astype(BF)
-    sbuf[:, UNIT:] = jnp.broadcast_to(id_ref[0].astype(F32).astype(BF), (D, 128))
+    ibuf[...] = jnp.broadcast_to(id_ref[0].astype(F32).astype(BF), (16, 128))
 
     def share(k):
         return sbuf.at[pl.ds(pl.multiple_of(k * SPAN, SPAN), SPAN), :]
@@ -1389,12 +1389,24 @@
     for n, (a, b) in enumerate(mates):
         if n == 0:
             rbuf[0] = share(me)[...]
+            jbuf[0] = ibuf[...]
             continue
+        at = (4 - n // 2) % 4 * 2 + n % 2
+        copy = pltpu.make_async_remote_copy(
+            src_ref=ibuf,
+            dst_ref=jbuf.at[at],
+            send_sem=isend.at[n],
+            recv_sem=irecv.at[at],
+            device_id={"zh": a // 2, "zl": a % 2, "y": b},
+            device_id_type=pl.DeviceIdType.MESH,
+        )
+        copy.start()
+        copies.append(copy)
         copy = pltpu.make_async_remote_copy(
             src_ref=share(2 * a + b),
-            dst_ref=rbuf.at[(4 - n // 2) % 4 * 2 + n % 2],
+            dst_ref=rbuf.at[at],
             send_sem=asend.at[n],
-            recv_sem=arecv.at[(4 - n // 2) % 4 * 2 + n % 2],
+            recv_sem=arecv.at[at],
             device_id={"zh": a // 2, "zl": a % 2, "y": b},
             device_id_type=pl.DeviceIdType.MESH,
         )
@@ -1404,14 +1416,14 @@
         copy.wait()
     masks = []
     for n in range(8):
-        own = rbuf[n, 0:16, UNIT:][0:1, 0:1].astype(F32)
+        own = jbuf[n][0:1, 0:1].astype(F32)
         masks.append([(own == k).astype(F32) for k in range(NA)])
 
     def add(i, carry):
         at = pl.ds(pl.multiple_of(i * 16, 16), 16)
         sums = [jnp.zeros((16, UNIT), F32) for _ in range(NA)]
         for n in range(8):
-            values = rbuf[n, at, :UNIT].astype(F32)
+            values = rbuf[n, at, :].astype(F32)
             for k in range(NA):
                 sums[k] = sums[k] + values * masks[n][k]
         for k in range(NA):
@@ -1451,14 +1463,18 @@
         out_specs=pl.BlockSpec(memory_space=pltpu.VMEM),
         out_shape=jax.ShapeDtypeStruct((2, SPAN, UNIT), F32),
         scratch_shapes=[
-            pltpu.VMEM((D, UNIT + 128), BF),
-            pltpu.VMEM((8, SPAN, UNIT + 128), BF),
+            pltpu.VMEM((D, UNIT), BF),
+            pltpu.VMEM((8, SPAN, UNIT), BF),
             pltpu.VMEM((NA, SPAN, UNIT), BF),
             pltpu.VMEM((4, 2, SPAN, UNIT), BF),
+            pltpu.VMEM((16, 128), BF),
+            pltpu.VMEM((8, 16, 128), BF),
             DMA((8,)),
             DMA((8,)),
             DMA((4,)),
             DMA((4,)),
+            DMA((8,)),
+            DMA((8,)),
         ],
         compiler_params=pltpu.CompilerParams(
             vmem_limit_bytes=VMEM_BYTES, collective_id=4, has_side_effects=True

time: 675 us -> 672 us (level)
  transfers between devices with their start and end apart: 10 -> 10, of which waited for: 3 -> 3; matrix products, arithmetic and copies ran while one was open for 6% -> 6% of each run, Pallas kernels for 42% -> 43%
where the time goes in v6:
time: 672 us; the launch traced here: 668 us
  Pallas kernels  537 us (80%)
  waiting for transfers between devices  49.9 us (7%)
  local copies, waits for them, and re-layouts  41.5 us (6%)
  between operations  15.1 us (2%)
  starting transfers between devices  14.5 us (2%)
  other arithmetic  9.59 us (1%)
    pallas_call x8, Pallas kernels, comm_call(): pl.pallas_call(run, in_specs=[pl.BlockSpec(memory_space=pl.ANY)] * len(in...  390 us
    pallas_call x11, Pallas kernels, call(): pl.pallas_call(body, grid=grid, in_specs=[spec(e) for e in ins], out_spec...  123 us
    pallas_call x1, Pallas kernels, adapters(): pl.pallas_call(adapters_body, in_specs=specs, out_specs=pl.BlockSpec(memo...  23.8 us
    ppermute x2, waiting for transfers between devices, across_y(): return lax.ppermute(v, 'y', [(0, 1), (1, 0)])  18.8 us
    all_to_all x3, waiting for transfers between devices, exchange(): lax.all_to_all(v, OWNERS[kind], split_axis=0, concat_axis=0, tiled=True)  17.9 us
  transfers between devices with their start and end apart: 10, of which 3 were waited for; matrix products, arithmetic and copies ran while one was open for 6% of the time, Pallas kernels for 43%

profile of v6, /device:TPU:9, one launch (start us, length us, event | category | flops | bytes accessed | tf_op | source)
XLA Modules:
  0.0 667.9 jit_solution(9224687949090188909)
XLA Ops:
  17.3 51.7 %gather_shared.2 = (bf16[4,768,768]{2,1,0:T(8,128)(2,1)}, bf16[96,4096]{1,0:T(8,128)(2,1)}, bf16[256,768]{1,0:T(8,128)(2,1)}) custom-call(bf16[96,768]{1,0:T(8,128)(2,1)} %bitcast.124, bf16[96,4096]{1,0:T(8,128)(2,1)} %get-tuple-element.179.refs_1_, bf16[256,768]{1,0:T(8,128)(2,1)} %get-tuple-element.189.refs_2_), custom_call_target="tpu_custom_call" | custom-call | bytes 50000000 | tf_op jit(solution)/shard_map/gather_shared/pallas_call | solution.py:605
  87.1 6.3 prep.1
  98.0 11.1 %project.2 = (bf16[1024,768]{1,0:T(8,128)(2,1)}, bf16[1024,128]{1,0:T(8,128)(2,1)}, bf16[1024,2304]{1,0:T(8,128)(2,1)}) custom-call(bf16[1024,768]{1,0:T(8,128)(2,1)} %refs_7_.3, f32[1,768]{1,0:T(1,128)} %get-tuple-element.214.g_ref.refs_8_, bf16[4,768,768]{2,1,0:T(8,128)(2,1)} %get-tuple-element.102.w_ref.refs_10_.refs_3_, ...), custom_call_target="tpu_custom_call" | custom-call | flops 3623878656 | bytes 12000000 | tf_op jit(solution)/shard_map/project/pallas_call | solution.py:72
  109.0 21.4 %attend.2 = (bf16[1024,768]{1,0:T(8,128)(2,1)}, bf16[6,1024,128]{2,1,0:T(8,128)(2,1)}) custom-call(bf16[1024,2304]{1,0:T(8,128)(2,1)} %get-tuple-element.105.q_ref.k_ref.v_ref.refs_4_, bf16[1024,2304]{1,0:T(8,128)(2,1)} %get-tuple-element.105.q_ref.k_ref.v_ref.refs_4_, bf16[1024,2304]{1,0:T(8,128)(2,1)} %get-tuple-element.105.q_ref.k_ref.v_ref.refs_4_, ...), custom_call_target="tpu_custom_call" | custom-call | flops 6442450944 | bytes 8000000 | tf_op jit(solution)/shard_map/attend/pallas_call | solution.py:72
  131.2 8.7 %settle.2 = (f32[1024,768]{1,0:T(8,128)}, bf16[1024,768]{1,0:T(8,128)(2,1)}, f32[1024,128]{1,0:T(8,128)}, bf16[1024,128]{1,0:T(8,128)(2,1)}) custom-call(bf16[1024,768]{1,0:T(8,128)(2,1)} %refs_7_.3, bf16[1024,768]{1,0:T(8,128)(2,1)} %get-tuple-element.108.mixed_ref.refs_9_.refs_2_, bf16[4,768,768]{2,1,0:T(8,128)(2,1)} %get-tuple-element.102.w_ref.refs_10_.refs_3_, ...), custom_call_target="tpu_custom_call" | custom-call | flops 2415919104 | bytes 10000000 | tf_op jit(solution)/shard_map/settle/pallas_call | solution.py:72
  140.4 18.8 %collective-permute-done = bf16[96,4096]{1,0:T(8,128)(2,1)S(1)} collective-permute-done((bf16[96,4096]{1,0:T(8,128)(2,1)S(1)}, bf16[96,4096]{1,0:T(8,128)(2,1)S(1)}, u32[]{:S(2)}, u32[]{:S(2)}) %collective-permute-start) | collective-permute-done | bytes 786464 | tf_op jit(solution)/shard_map/ppermute | solution.py:1497
  160.8 7.0 %dispatch.2 = bf16[8,192,768]{2,1,0:T(8,128)(2,1)} custom-call(s32[8,1024]{1,0:T(8,128)} %get-tuple-element.116.trow_ref.refs_11_, bf16[1024,768]{1,0:T(8,128)(2,1)} %get-tuple-element.120.s_ref), custom_call_target="tpu_custom_call" | custom-call | flops 2415919104 | bytes 4000000 | tf_op jit(solution)/shard_map/dispatch/pallas_call | solution.py:72
  167.8 4.4 all-to-all-start
  179.7 50.4 %gather_shared.3.w_ref.refs_9_.refs_3_ = bf16[4,768,768]{2,1,0:T(8,128)(2,1)} custom-call(bf16[96,768]{1,0:T(8,128)(2,1)} %bitcast.122), custom_call_target="tpu_custom_call" | custom-call | bytes 50000000 | tf_op jit(solution)/shard_map/gather_shared/pallas_call | solution.py:605
  234.3 38.5 %expert_forward.1 = (bf16[8,192,768]{2,1,0:T(8,128)(2,1)}, bf16[4,384,2048]{2,1,0:T(8,128)(2,1)}, bf16[4,384,2048]{2,1,0:T(8,128)(2,1)}) custom-call(bf16[4,96,4096]{2,1,0:T(8,128)(2,1)} %bitcast.132, bf16[4,96,4096]{2,1,0:T(8,128)(2,1)} %bitcast.136, bf16[2048,768]{1,0:T(8,128)(2,1)} %bitcast.134, bf16[8,192,768]{2,1,0:T(8,128)(2,1)} %copy-done.3), custom_call_target="tpu_custom_call" | custom-call | flops 14495514624 | bytes 26000000 | tf_op jit(solution)/shard_map/expert_forward/pallas_call | solution.py:605
  272.8 10.2 %combine.1 = (f32[1024,768]{1,0:T(8,128)}, bf16[1024,768]{1,0:T(8,128)(2,1)}, bf16[1024,768]{1,0:T(8,128)(2,1)}) custom-call(s32[1024,128]{1,0:T(8,128)} %get-tuple-element.117.tcol_ref.refs_10_.refs_12_, bf16[1536,768]{1,0:T(8,128)(2,1)} %bitcast.139, f32[1024,768]{1,0:T(8,128)} %get-tuple-element.122.mid_ref.refs_6_, ...), custom_call_target="tpu_custom_call" | custom-call | flops 4831838208 | bytes 12000000 | tf_op jit(solution)/shard_map/combine/pallas_call | solution.py:72
  283.0 11.1 %project.3 = (bf16[1024,768]{1,0:T(8,128)(2,1)}, bf16[1024,128]{1,0:T(8,128)(2,1)}, bf16[1024,2304]{1,0:T(8,128)(2,1)}) custom-call(f32[1024,768]{1,0:T(8,128)} %get-tuple-element.123.x_ref.refs_7_, f32[1,768]{1,0:T(1,128)} %get-tuple-element.215.g_ref.refs_8_, bf16[4,768,768]{2,1,0:T(8,128)(2,1)} %gather_shared.3.w_ref.refs_9_.refs_3_, ...), custom_call_target="tpu_custom_call" | custom-call | flops 3623878656 | bytes 12000000 | tf_op jit(solution)/shard_map/project/pallas_call | solution.py:72
  294.1 21.7 %attend.3 = (bf16[1024,768]{1,0:T(8,128)(2,1)}, bf16[6,1024,128]{2,1,0:T(8,128)(2,1)}) custom-call(bf16[1024,2304]{1,0:T(8,128)(2,1)} %get-tuple-element.126.q_ref.k_ref.v_ref.refs_4_, bf16[1024,2304]{1,0:T(8,128)(2,1)} %get-tuple-element.126.q_ref.k_ref.v_ref.refs_4_, bf16[1024,2304]{1,0:T(8,128)(2,1)} %get-tuple-element.126.q_ref.k_ref.v_ref.refs_4_, ...), custom_call_target="tpu_custom_call" | custom-call | flops 6442450944 | bytes 8000000 | tf_op jit(solution)/shard_map/attend/pallas_call | solution.py:72
  315.8 8.7 %settle.3 = (f32[1024,768]{1,0:T(8,128)}, bf16[1024,768]{1,0:T(8,128)(2,1)}, f32[1024,128]{1,0:T(8,128)}, bf16[1024,128]{1,0:T(8,128)(2,1)}) custom-call(f32[1024,768]{1,0:T(8,128)} %get-tuple-element.123.x_ref.refs_7_, bf16[1024,768]{1,0:T(8,128)(2,1)} %get-tuple-element.127.mixed_ref.refs_8_.refs_2_, ...), custom_call_target="tpu_custom_call" | custom-call | flops 2415919104 | bytes 10000000 | tf_op jit(solution)/shard_map/settle/pallas_call | solution.py:72
  324.6 6.9 %dispatch.3 = bf16[8,192,768]{2,1,0:T(8,128)(2,1)} custom-call(s32[8,1024]{1,0:T(8,128)} %get-tuple-element.116.trow_ref.refs_11_, bf16[1024,768]{1,0:T(8,128)(2,1)} %get-tuple-element.128.s_ref), custom_call_target="tpu_custom_call" | custom-call | flops 2415919104 | bytes 4000000 | tf_op jit(solution)/shard_map/dispatch/pallas_call | solution.py:72
  335.4 10.3 %dispatch_grad.1 = bf16[8,192,768]{2,1,0:T(8,128)(2,1)} custom-call(s32[8,1024]{1,0:T(8,128)} %get-tuple-element.116.trow_ref.refs_11_, bf16[1024,768]{1,0:T(8,128)(2,1)} %refs_7_.2, f32[1024,128]{1,0:T(8,128)} %get-tuple-element.132.lg_ref.refs_11_, s32[1024,2]{1,0:T(8,128)} %copy.89.rt_ref.refs_12_.refs_14_), custom_call_target="tpu_custom_call" | custom-call | flops 4831838208 | bytes 6000000 | tf_op jit(solution)/shard_map/dispatch_grad/pallas_call | solution.py:72
  345.8 17.9 %all-to-all-done.1.refs_1_ = bf16[8,192,768]{2,1,0:T(8,128)(2,1)S(1)} async-done(((bf16[8,192,768]{2,1,0:T(8,128)(2,1)}), bf16[8,192,768]{2,1,0:T(8,128)(2,1)S(1)}, u32[]{:S(2)}, u32[]{:S(2)}) %all-to-all-start.1) | async-done | bytes 2359328 | tf_op jit(solution)/shard_map/all_to_all | solution.py:1510
  370.0 20.9 %expert_parts.1 = (bf16[4,384,2048]{2,1,0:T(8,128)(2,1)}, bf16[4,384,2048]{2,1,0:T(8,128)(2,1)}, bf16[4,384,2048]{2,1,0:T(8,128)(2,1)}) custom-call(bf16[768,4096]{1,0:T(8,128)(2,1)} %bitcast.130, bf16[8,192,768]{2,1,0:T(8,128)(2,1)} %copy-done.5), custom_call_target="tpu_custom_call" | custom-call | flops 9663676416 | bytes 28000000 | tf_op jit(solution)/shard_map/expert_parts/pallas_call | solution.py:605
  390.9 12.4 %all-gather.10.cloned.1.call-done = bf16[8,256,768]{2,1,0:T(8,128)(2,1)} async-done(((bf16[2,256,768]{2,1,0:T(8,128)(2,1)}), bf16[8,256,768]{2,1,0:T(8,128)(2,1)}) %all-gather.10.cloned.1.call-update) | async-done | bytes 3145744 | tf_op jit(solution)/shard_map/all_gather | solution.py:1506
  404.8 69.0 %expert_both.1 = (bf16[1024,768]{1,0:T(8,128)(2,1)}, f32[1024,768]{1,0:T(8,128)}, f32[1024,768]{1,0:T(8,128)}, f32[1024,128]{1,0:T(8,128)}, f32[128,768]{1,0:T(8,128)}, /*index=5*/f32[128,768]{1,0:T(8,128)}) custom-call(bf16[768,4096]{1,0:T(8,128)(2,1)} %bitcast.131, bf16[2048,768]{1,0:T(8,128)(2,1)} %bitcast.138, ...), custom_call_target="tpu_custom_call" | custom-call | flops 19327352832 | bytes 40000000 | tf_op jit(solution)/shard_map/expert_both/pallas_call | solution.py:605
  473.8 44.6 %layer_back.2 = (f32[1024,768]{1,0:T(8,128)}, f32[128,2304]{1,0:T(8,128)}, f32[128,768]{1,0:T(8,128)}) custom-call(f32[1024,768]{1,0:T(8,128)} %get-tuple-element.140.refs_0_, bf16[1024,768]{1,0:T(8,128)(2,1)} %get-tuple-element.141.refs_1_, bf16[1024,768]{1,0:T(8,128)(2,1)} %get-tuple-element.127.mixed_ref.refs_8_.refs_2_, ...), custom_call_target="tpu_custom_call" | custom-call | flops 19730006016 | bytes 40000000 | tf_op jit(solution)/shard_map/layer_back/pallas_call | solution.py:605
  518.4 70.3 %expert_backward.1 = (bf16[1024,768]{1,0:T(8,128)(2,1)}, f32[1024,768]{1,0:T(8,128)}, f32[128,768]{1,0:T(8,128)}, f32[128,768]{1,0:T(8,128)}) custom-call(bf16[4,96,4096]{2,1,0:T(8,128)(2,1)} %bitcast.133, bf16[4,96,4096]{2,1,0:T(8,128)(2,1)} %bitcast.137, bf16[2048,768]{1,0:T(8,128)(2,1)} %bitcast.135, bf16[4,384,2048]{2,1,0:T(8,128)(2,1)} %get-tuple-element.138.refs_3_, ...), custom_call_target="tpu_custom_call" | custom-call | flops 14495514624 | bytes 26000000 | tf_op jit(solution)/shard_map/expert_backward/pallas_call | solution.py:605
  588.7 44.4 %layer_back.3 = (f32[1024,768]{1,0:T(8,128)}, f32[128,2304]{1,0:T(8,128)}, f32[128,768]{1,0:T(8,128)}) custom-call(f32[1024,768]{1,0:T(8,128)} %get-tuple-element.150.refs_0_, bf16[1024,768]{1,0:T(8,128)(2,1)} %get-tuple-element.151.refs_1_, bf16[1024,768]{1,0:T(8,128)(2,1)} %get-tuple-element.108.mixed_ref.refs_9_.refs_2_, ...), custom_call_target="tpu_custom_call" | custom-call | flops 19730006016 | bytes 40000000 | tf_op jit(solution)/shard_map/layer_back/pallas_call | solution.py:605
  633.2 23.8 %adapters.1 = f32[2,96,256]{2,1,0:T(8,128)} custom-call(s32[1]{0:T(128)} %copy.116.refs_0_, f32[128,768]{1,0:T(8,128)} %get-tuple-element.156.refs_1_, f32[128,768]{1,0:T(8,128)} %get-tuple-element.157.refs_2_, f32[128,2304]{1,0:T(8,128)} %get-tuple-element.158.refs_3_, f32[128,768]{1,0:T(8,128)} %get-tuple-element.159.refs_4_, ...), custom_call_target="tpu_custom_call" | custom-call | tf_op jit(solution)/shard_map/adapters/pallas_call | solution.py:1460
  (117 shorter events, 62.1 us)
Async XLA Ops:
  7.2 225.7 %all-gather.14.cloned.1.call-start = ((), (), s32[]{:S(2)}) async-start(), calls=%async_computation.6 | async-start | bytes 3932160 | tf_op jit(solution)/shard_map/all_gather | solution.py:1561
  10.6 222.3 %all-gather.12.cloned.1.call-start = ((), (), s32[]{:S(2)}) async-start(), calls=%async_computation.5 | async-start | bytes 3932160 | tf_op jit(solution)/shard_map/all_gather | solution.py:1506
  71.2 161.7 %all-gather.16.cloned.1.call-start = ((), (), s32[]{:S(2)}) async-start(), calls=%async_computation.7 | async-start | bytes 3932160 | tf_op jit(solution)/shard_map/all_gather | solution.py:1567
  72.0 298.0 %all-gather.8.cloned.1.call-start = ((), (), s32[]{:S(2)}) async-start(), calls=%async_computation.3 | async-start | bytes 7864320 | tf_op jit(solution)/shard_map/all_gather | solution.py:1506
  74.7 1.9 copy-start.15
  74.7 3.2 copy-start.16
  74.8 3.2 copy-start.14
  75.5 4.5 copy-start.19
  75.5 5.6 copy-start.20
  81.1 3.8 copy-start
  85.0 2.1 copy-start.13
  87.1 7.2 %copy-start.17 = (f32[2,2,768]{2,1,0:T(2,128)S(1)}, f32[2,2,768]{2,1,0:T(2,128)}, u32[]{:S(2)}) copy-start(f32[2,2,768]{2,1,0:T(2,128)} %param.28) | copy-start | bytes 36868
  87.1 7.8 %copy-start.9 = (bf16[2,4,16,768]{3,2,0,1:T(8,128)(2,1)S(1)}, bf16[2,4,16,768]{3,2,0,1:T(8,128)(2,1)}, u32[]{:S(2)}) copy-start(bf16[2,4,16,768]{3,2,0,1:T(8,128)(2,1)} %copy-done.8) | copy-start | bytes 589828
  140.1 19.2 %collective-permute-start = (bf16[96,4096]{1,0:T(8,128)(2,1)S(1)}, bf16[96,4096]{1,0:T(8,128)(2,1)S(1)}, u32[]{:S(2)}, u32[]{:S(2)}) collective-permute-start(bf16[96,4096]{1,0:T(8,128)(2,1)S(1)} %get-tuple-element.181), channel_id=1, source_target_pairs={{0,1},{1,0},{2,3},{3,2},{4,5},{5,4},{6,7},{7,6},{8,9},{9,8},{10,11... | collective-permute-start | bytes 2359304 | tf_op jit(solution)/shard_map/ppermute | solution.py:1497
  167.8 4.4 copy-start.2
  167.8 65.0 %all-to-all-start = ((bf16[8,192,768]{2,1,0:T(8,128)(2,1)}), bf16[8,192,768]{2,1,0:T(8,128)(2,1)S(1)}, u32[]{:S(2)}, u32[]{:S(2)}) async-start(bf16[8,192,768]{2,1,0:T(8,128)(2,1)} %dispatch.2), calls=%async_computation | async-start | bytes 4718592 | tf_op jit(solution)/shard_map/all_to_all | solution.py:1510
  172.2 231.1 %all-gather.10.cloned.1.call-start = ((), (), s32[]{:S(2)}) async-start(), calls=%async_computation.4 | async-start | bytes 3932160 | tf_op jit(solution)/shard_map/all_gather | solution.py:1506
  172.2 2.2 copy-start.10
  173.0 57.7 %collective-permute-start.1 = (bf16[256,768]{1,0:T(8,128)(2,1)}, bf16[256,768]{1,0:T(8,128)(2,1)}, u32[]{:S(2)}, u32[]{:S(2)}) collective-permute-start(bf16[256,768]{1,0:T(8,128)(2,1)} %get-tuple-element.191), channel_id=1, source_target_pairs={{0,1},{1,0},{2,3},{3,2},{4,5},{5,4},{6,7},{7,6},{8,9},{9,8},{10,11... | collective-permute-start | bytes 1179656 | tf_op jit(solution)/shard_map/ppermute | solution.py:1497
  179.7 50.4 %copy-start.18 = (f32[2,2,768]{2,1,0:T(2,128)S(1)}, f32[2,2,768]{2,1,0:T(2,128)}, u32[]{:S(2)}) copy-start(f32[2,2,768]{2,1,0:T(2,128)} %param.36) | copy-start | bytes 36868
  331.5 32.1 %all-to-all-start.1 = ((bf16[8,192,768]{2,1,0:T(8,128)(2,1)}), bf16[8,192,768]{2,1,0:T(8,128)(2,1)S(1)}, u32[]{:S(2)}, u32[]{:S(2)}) async-start(bf16[8,192,768]{2,1,0:T(8,128)(2,1)} %dispatch.3), calls=%async_computation.1 | async-start | bytes 4718592 | tf_op jit(solution)/shard_map/all_to_all | solution.py:1510
  345.8 23.4 %copy-start.11 = (bf16[2,128,768]{2,1,0:T(8,128)(2,1)S(1)}, bf16[2,128,768]{2,1,0:T(8,128)(2,1)}, u32[]{:S(2)}) copy-start(bf16[2,128,768]{2,1,0:T(8,128)(2,1)} %get-tuple-element.134) | copy-start | bytes 1179652
  365.1 38.2 %all-to-all-start.2 = ((bf16[8,192,768]{2,1,0:T(8,128)(2,1)}), bf16[8,192,768]{2,1,0:T(8,128)(2,1)S(1)}, u32[]{:S(2)}, u32[]{:S(2)}) async-start(bf16[8,192,768]{2,1,0:T(8,128)(2,1)} %dispatch_grad.1), calls=%async_computation.2 | async-start | bytes 4718592 | tf_op jit(solution)/shard_map/all_to_all | solution.py:1510
  633.2 26.2 %copy-start.1 = (f32[1024,768]{1,0:T(8,128)S(1)}, f32[1024,768]{1,0:T(8,128)}, u32[]{:S(2)}) copy-start(f32[1024,768]{1,0:T(8,128)} %get-tuple-element.222) | copy-start | bytes 9437188
  (7 other events, 9.1 us)
Sparse Core Ops, SparseCore 0:
  10.7 73.1 all-gather.13
  85.5 63.0 all-gather.11
  150.1 73.4 all-gather.15
  225.0 114.6 all-gather.7
  341.1 62.0 all-gather.9

commit v7 on v6

--- a/solution.py
+++ b/solution.py
@@ -770,13 +770,15 @@
     stores = [done(0), done(2)]
     gu_ref[...] = jnp.zeros_like(gu_ref)
     gd_ref[...] = jnp.zeros_like(gd_ref)
-    for copy in later:
-        copy.wait()
+    for p in range(NP):
+        for copy in later[2 * p : 2 * p + 2]:
+            copy.wait()
+        collect(p, kind, tcol_ref, gm_ref, gback)
 
     def settle_one(i, carry):
         at = pl.ds(pl.multiple_of(i * RB, RB), RB)
-        refs = (tcol_ref, mid, g, mixed, gain_ref, nar_ref, w3, d_ref, u_ref, gu_ref, gd_ref)
-        settle_back(refs, at, gm_ref, mixed, gback)
+        refs = (mid, g, mixed, gain_ref, nar_ref, w3, d_ref, u_ref, gu_ref, gd_ref)
+        settle_back(refs, at, gm_ref, mixed)
         return carry
 
     lax.fori_loop(0, NB, settle_one, 0)
@@ -912,13 +914,15 @@
     lax.fori_loop(0, NB, tidy, 0)
     gu_ref[...] = jnp.zeros_like(gu_ref)
     gd_ref[...] = jnp.zeros_like(gd_ref)
-    for copy in moves:
-        copy.wait()
+    for n, p in enumerate((3, 0, 1, 2)):
+        for copy in moves[2 * n : 2 * n + 2]:
+            copy.wait()
+        collect(p, kind, tcol_ref, gm_ref, back)
 
     def settle_one(i, carry):
         at = pl.ds(pl.multiple_of(i * RB, RB), RB)
-        refs = (tcol_ref, mid, g, mixed, gain_ref, nar_ref, w3, d_ref, u_ref, gu_ref, gd_ref)
-        settle_back(refs, at, gm_ref, first, back)
+        refs = (mid, g, mixed, gain_ref, nar_ref, w3, d_ref, u_ref, gu_ref, gd_ref)
+        settle_back(refs, at, gm_ref, first)
         return carry
 
     lax.fori_loop(0, NB, settle_one, 0)
@@ -1063,13 +1067,26 @@
     return mm(spread_lanes(grad), wt) + keep * g, residual
 
 
-def settle_back(refs, at, gm_ref, mix_ref, back_ref):
-    tcol_ref, mid_ref, g_ref, mixed_ref, gain_ref, nar_ref, w_ref, d_ref, u_ref, gu_ref, gd_ref = refs
-    place = iota((RB, SLOTS), 1)
-    tcol = tcol_ref[at, :]
-    hit = (tcol[:, 0:1] == place) | (tcol[:, 1:2] == place)
-    grad = gm_ref[at, :] + mm(hit.astype(F32).astype(BF), back_ref[...].reshape(SLOTS, D))
-    grad = g_ref[at, :].astype(F32) + rms_back(grad, mid_ref[at, :], gain_ref[...])
+def collect(p, kind, tcol_ref, gm_ref, back_ref):
+    numbers = [owner_at(p, h, kind)[1] for h in range(2)]
+
+    def one(i, carry):
+        at = pl.ds(pl.multiple_of(i * RB, RB), RB)
+        tcol = tcol_ref[at, :]
+        total = gm_ref[at, :]
+        for number in numbers:
+            place = number * CAP + iota((RB, CAP), 1)
+            hit = (tcol[:, 0:1] == place) | (tcol[:, 1:2] == place)
+            total = total + mm(hit.astype(F32).astype(BF), back_ref[number])
+        gm_ref[at, :] = total
+        return carry
+
+    lax.fori_loop(0, NB, one, 0)
+
+
+def settle_back(refs, at, gm_ref, mix_ref):
+    mid_ref, g_ref, mixed_ref, gain_ref, nar_ref, w_ref, d_ref, u_ref, gu_ref, gd_ref = refs
+    grad = g_ref[at, :].astype(F32) + rms_back(gm_ref[at, :], mid_ref[at, :], gain_ref[...])
     gm_ref[at, :] = grad
     grad = grad.astype(BF)
     slim = mm_nt(grad, u_ref[...]).astype(BF)

time: 672 us -> 670 us (level)
  no operation moved by 1% of the time
where the time goes in v7:
time: 670 us; the launch traced here: 667 us
  Pallas kernels  536 us (80%)
  waiting for transfers between devices  49.9 us (7%)
  local copies, waits for them, and re-layouts  41.5 us (6%)
  between operations  15.1 us (2%)
  starting transfers between devices  14.6 us (2%)
  other arithmetic  9.59 us (1%)
    pallas_call x8, Pallas kernels, comm_call(): pl.pallas_call(run, in_specs=[pl.BlockSpec(memory_space=pl.ANY)] * len(in...  389 us
    pallas_call x11, Pallas kernels, call(): pl.pallas_call(body, grid=grid, in_specs=[spec(e) for e in ins], out_spec...  123 us
    pallas_call x1, Pallas kernels, adapters(): pl.pallas_call(adapters_body, in_specs=specs, out_specs=pl.BlockSpec(memo...  23.8 us
    ppermute x2, waiting for transfers between devices, across_y(): return lax.ppermute(v, 'y', [(0, 1), (1, 0)])  18.8 us
    all_to_all x3, waiting for transfers between devices, exchange(): lax.all_to_all(v, OWNERS[kind], split_axis=0, concat_axis=0, tiled=True)  17.9 us
  transfers between devices with their start and end apart: 10, of which 3 were waited for; matrix products, arithmetic and copies ran while one was open for 6% of the time, Pallas kernels for 43%

profile of v7, /device:TPU:9, one launch (start us, length us, event | category | flops | bytes accessed | tf_op | source)
XLA Modules:
  0.0 666.6 jit_solution(8301741756496809244)
XLA Ops:
  17.3 51.7 %gather_shared.2 = (bf16[4,768,768]{2,1,0:T(8,128)(2,1)}, bf16[96,4096]{1,0:T(8,128)(2,1)}, bf16[256,768]{1,0:T(8,128)(2,1)}) custom-call(bf16[96,768]{1,0:T(8,128)(2,1)} %bitcast.124, bf16[96,4096]{1,0:T(8,128)(2,1)} %get-tuple-element.179.refs_1_, bf16[256,768]{1,0:T(8,128)(2,1)} %get-tuple-element.189.refs_2_), custom_call_target="tpu_custom_call" | custom-call | bytes 50000000 | tf_op jit(solution)/shard_map/gather_shared/pallas_call | solution.py:605
  87.1 6.3 prep.1
  98.0 11.1 %project.2 = (bf16[1024,768]{1,0:T(8,128)(2,1)}, bf16[1024,128]{1,0:T(8,128)(2,1)}, bf16[1024,2304]{1,0:T(8,128)(2,1)}) custom-call(bf16[1024,768]{1,0:T(8,128)(2,1)} %refs_7_.3, f32[1,768]{1,0:T(1,128)} %get-tuple-element.214.g_ref.refs_8_, bf16[4,768,768]{2,1,0:T(8,128)(2,1)} %get-tuple-element.102.w_ref.refs_10_.refs_3_, ...), custom_call_target="tpu_custom_call" | custom-call | flops 3623878656 | bytes 12000000 | tf_op jit(solution)/shard_map/project/pallas_call | solution.py:72
  109.0 21.3 %attend.2 = (bf16[1024,768]{1,0:T(8,128)(2,1)}, bf16[6,1024,128]{2,1,0:T(8,128)(2,1)}) custom-call(bf16[1024,2304]{1,0:T(8,128)(2,1)} %get-tuple-element.105.q_ref.k_ref.v_ref.refs_4_, bf16[1024,2304]{1,0:T(8,128)(2,1)} %get-tuple-element.105.q_ref.k_ref.v_ref.refs_4_, bf16[1024,2304]{1,0:T(8,128)(2,1)} %get-tuple-element.105.q_ref.k_ref.v_ref.refs_4_, ...), custom_call_target="tpu_custom_call" | custom-call | flops 6442450944 | bytes 8000000 | tf_op jit(solution)/shard_map/attend/pallas_call | solution.py:72
  131.2 8.7 %settle.2 = (f32[1024,768]{1,0:T(8,128)}, bf16[1024,768]{1,0:T(8,128)(2,1)}, f32[1024,128]{1,0:T(8,128)}, bf16[1024,128]{1,0:T(8,128)(2,1)}) custom-call(bf16[1024,768]{1,0:T(8,128)(2,1)} %refs_7_.3, bf16[1024,768]{1,0:T(8,128)(2,1)} %get-tuple-element.108.mixed_ref.refs_9_.refs_2_, bf16[4,768,768]{2,1,0:T(8,128)(2,1)} %get-tuple-element.102.w_ref.refs_10_.refs_3_, ...), custom_call_target="tpu_custom_call" | custom-call | flops 2415919104 | bytes 10000000 | tf_op jit(solution)/shard_map/settle/pallas_call | solution.py:72
  140.4 18.8 %collective-permute-done = bf16[96,4096]{1,0:T(8,128)(2,1)S(1)} collective-permute-done((bf16[96,4096]{1,0:T(8,128)(2,1)S(1)}, bf16[96,4096]{1,0:T(8,128)(2,1)S(1)}, u32[]{:S(2)}, u32[]{:S(2)}) %collective-permute-start) | collective-permute-done | bytes 786464 | tf_op jit(solution)/shard_map/ppermute | solution.py:1514
  160.8 7.0 %dispatch.2 = bf16[8,192,768]{2,1,0:T(8,128)(2,1)} custom-call(s32[8,1024]{1,0:T(8,128)} %get-tuple-element.116.trow_ref.refs_11_, bf16[1024,768]{1,0:T(8,128)(2,1)} %get-tuple-element.120.s_ref), custom_call_target="tpu_custom_call" | custom-call | flops 2415919104 | bytes 4000000 | tf_op jit(solution)/shard_map/dispatch/pallas_call | solution.py:72
  167.8 4.4 all-to-all-start
  179.6 50.4 %gather_shared.3.w_ref.refs_9_.refs_3_ = bf16[4,768,768]{2,1,0:T(8,128)(2,1)} custom-call(bf16[96,768]{1,0:T(8,128)(2,1)} %bitcast.122), custom_call_target="tpu_custom_call" | custom-call | bytes 50000000 | tf_op jit(solution)/shard_map/gather_shared/pallas_call | solution.py:605
  234.2 38.5 %expert_forward.1 = (bf16[8,192,768]{2,1,0:T(8,128)(2,1)}, bf16[4,384,2048]{2,1,0:T(8,128)(2,1)}, bf16[4,384,2048]{2,1,0:T(8,128)(2,1)}) custom-call(bf16[4,96,4096]{2,1,0:T(8,128)(2,1)} %bitcast.132, bf16[4,96,4096]{2,1,0:T(8,128)(2,1)} %bitcast.136, bf16[2048,768]{1,0:T(8,128)(2,1)} %bitcast.134, bf16[8,192,768]{2,1,0:T(8,128)(2,1)} %copy-done.3), custom_call_target="tpu_custom_call" | custom-call | flops 14495514624 | bytes 26000000 | tf_op jit(solution)/shard_map/expert_forward/pallas_call | solution.py:605
  272.8 10.2 %combine.1 = (f32[1024,768]{1,0:T(8,128)}, bf16[1024,768]{1,0:T(8,128)(2,1)}, bf16[1024,768]{1,0:T(8,128)(2,1)}) custom-call(s32[1024,128]{1,0:T(8,128)} %get-tuple-element.117.tcol_ref.refs_10_.refs_12_, bf16[1536,768]{1,0:T(8,128)(2,1)} %bitcast.139, f32[1024,768]{1,0:T(8,128)} %get-tuple-element.122.mid_ref.refs_6_, ...), custom_call_target="tpu_custom_call" | custom-call | flops 4831838208 | bytes 12000000 | tf_op jit(solution)/shard_map/combine/pallas_call | solution.py:72
  282.9 11.1 %project.3 = (bf16[1024,768]{1,0:T(8,128)(2,1)}, bf16[1024,128]{1,0:T(8,128)(2,1)}, bf16[1024,2304]{1,0:T(8,128)(2,1)}) custom-call(f32[1024,768]{1,0:T(8,128)} %get-tuple-element.123.x_ref.refs_7_, f32[1,768]{1,0:T(1,128)} %get-tuple-element.215.g_ref.refs_8_, bf16[4,768,768]{2,1,0:T(8,128)(2,1)} %gather_shared.3.w_ref.refs_9_.refs_3_, ...), custom_call_target="tpu_custom_call" | custom-call | flops 3623878656 | bytes 12000000 | tf_op jit(solution)/shard_map/project/pallas_call | solution.py:72
  294.1 21.7 %attend.3 = (bf16[1024,768]{1,0:T(8,128)(2,1)}, bf16[6,1024,128]{2,1,0:T(8,128)(2,1)}) custom-call(bf16[1024,2304]{1,0:T(8,128)(2,1)} %get-tuple-element.126.q_ref.k_ref.v_ref.refs_4_, bf16[1024,2304]{1,0:T(8,128)(2,1)} %get-tuple-element.126.q_ref.k_ref.v_ref.refs_4_, bf16[1024,2304]{1,0:T(8,128)(2,1)} %get-tuple-element.126.q_ref.k_ref.v_ref.refs_4_, ...), custom_call_target="tpu_custom_call" | custom-call | flops 6442450944 | bytes 8000000 | tf_op jit(solution)/shard_map/attend/pallas_call | solution.py:72
  315.8 8.7 %settle.3 = (f32[1024,768]{1,0:T(8,128)}, bf16[1024,768]{1,0:T(8,128)(2,1)}, f32[1024,128]{1,0:T(8,128)}, bf16[1024,128]{1,0:T(8,128)(2,1)}) custom-call(f32[1024,768]{1,0:T(8,128)} %get-tuple-element.123.x_ref.refs_7_, bf16[1024,768]{1,0:T(8,128)(2,1)} %get-tuple-element.127.mixed_ref.refs_8_.refs_2_, ...), custom_call_target="tpu_custom_call" | custom-call | flops 2415919104 | bytes 10000000 | tf_op jit(solution)/shard_map/settle/pallas_call | solution.py:72
  324.5 6.9 %dispatch.3 = bf16[8,192,768]{2,1,0:T(8,128)(2,1)} custom-call(s32[8,1024]{1,0:T(8,128)} %get-tuple-element.116.trow_ref.refs_11_, bf16[1024,768]{1,0:T(8,128)(2,1)} %get-tuple-element.128.s_ref), custom_call_target="tpu_custom_call" | custom-call | flops 2415919104 | bytes 4000000 | tf_op jit(solution)/shard_map/dispatch/pallas_call | solution.py:72
  335.4 10.3 %dispatch_grad.1 = bf16[8,192,768]{2,1,0:T(8,128)(2,1)} custom-call(s32[8,1024]{1,0:T(8,128)} %get-tuple-element.116.trow_ref.refs_11_, bf16[1024,768]{1,0:T(8,128)(2,1)} %refs_7_.2, f32[1024,128]{1,0:T(8,128)} %get-tuple-element.132.lg_ref.refs_11_, s32[1024,2]{1,0:T(8,128)} %copy.89.rt_ref.refs_12_.refs_14_), custom_call_target="tpu_custom_call" | custom-call | flops 4831838208 | bytes 6000000 | tf_op jit(solution)/shard_map/dispatch_grad/pallas_call | solution.py:72
  345.7 17.9 %all-to-all-done.1.refs_1_ = bf16[8,192,768]{2,1,0:T(8,128)(2,1)S(1)} async-done(((bf16[8,192,768]{2,1,0:T(8,128)(2,1)}), bf16[8,192,768]{2,1,0:T(8,128)(2,1)S(1)}, u32[]{:S(2)}, u32[]{:S(2)}) %all-to-all-start.1) | async-done | bytes 2359328 | tf_op jit(solution)/shard_map/all_to_all | solution.py:1527
  369.9 20.9 %expert_parts.1 = (bf16[4,384,2048]{2,1,0:T(8,128)(2,1)}, bf16[4,384,2048]{2,1,0:T(8,128)(2,1)}, bf16[4,384,2048]{2,1,0:T(8,128)(2,1)}) custom-call(bf16[768,4096]{1,0:T(8,128)(2,1)} %bitcast.130, bf16[8,192,768]{2,1,0:T(8,128)(2,1)} %copy-done.5), custom_call_target="tpu_custom_call" | custom-call | flops 9663676416 | bytes 28000000 | tf_op jit(solution)/shard_map/expert_parts/pallas_call | solution.py:605
  390.9 12.4 %all-gather.10.cloned.1.call-done = bf16[8,256,768]{2,1,0:T(8,128)(2,1)} async-done(((bf16[2,256,768]{2,1,0:T(8,128)(2,1)}), bf16[8,256,768]{2,1,0:T(8,128)(2,1)}) %all-gather.10.cloned.1.call-update) | async-done | bytes 3145744 | tf_op jit(solution)/shard_map/all_gather | solution.py:1523
  404.8 69.1 %expert_both.1 = (bf16[1024,768]{1,0:T(8,128)(2,1)}, f32[1024,768]{1,0:T(8,128)}, f32[1024,768]{1,0:T(8,128)}, f32[1024,128]{1,0:T(8,128)}, f32[128,768]{1,0:T(8,128)}, /*index=5*/f32[128,768]{1,0:T(8,128)}) custom-call(bf16[768,4096]{1,0:T(8,128)(2,1)} %bitcast.131, bf16[2048,768]{1,0:T(8,128)(2,1)} %bitcast.138, ...), custom_call_target="tpu_custom_call" | custom-call | flops 19327352832 | bytes 40000000 | tf_op jit(solution)/shard_map/expert_both/pallas_call | solution.py:605
  473.9 45.0 %layer_back.2 = (f32[1024,768]{1,0:T(8,128)}, f32[128,2304]{1,0:T(8,128)}, f32[128,768]{1,0:T(8,128)}) custom-call(f32[1024,768]{1,0:T(8,128)} %get-tuple-element.140.refs_0_, bf16[1024,768]{1,0:T(8,128)(2,1)} %get-tuple-element.141.refs_1_, bf16[1024,768]{1,0:T(8,128)(2,1)} %get-tuple-element.127.mixed_ref.refs_8_.refs_2_, ...), custom_call_target="tpu_custom_call" | custom-call | flops 19730006016 | bytes 40000000 | tf_op jit(solution)/shard_map/layer_back/pallas_call | solution.py:605
  518.9 68.6 %expert_backward.1 = (bf16[1024,768]{1,0:T(8,128)(2,1)}, f32[1024,768]{1,0:T(8,128)}, f32[128,768]{1,0:T(8,128)}, f32[128,768]{1,0:T(8,128)}) custom-call(bf16[4,96,4096]{2,1,0:T(8,128)(2,1)} %bitcast.133, bf16[4,96,4096]{2,1,0:T(8,128)(2,1)} %bitcast.137, bf16[2048,768]{1,0:T(8,128)(2,1)} %bitcast.135, bf16[4,384,2048]{2,1,0:T(8,128)(2,1)} %get-tuple-element.138.refs_3_, ...), custom_call_target="tpu_custom_call" | custom-call | flops 14495514624 | bytes 26000000 | tf_op jit(solution)/shard_map/expert_backward/pallas_call | solution.py:605
  587.5 44.5 %layer_back.3 = (f32[1024,768]{1,0:T(8,128)}, f32[128,2304]{1,0:T(8,128)}, f32[128,768]{1,0:T(8,128)}) custom-call(f32[1024,768]{1,0:T(8,128)} %get-tuple-element.150.refs_0_, bf16[1024,768]{1,0:T(8,128)(2,1)} %get-tuple-element.151.refs_1_, bf16[1024,768]{1,0:T(8,128)(2,1)} %get-tuple-element.108.mixed_ref.refs_9_.refs_2_, ...), custom_call_target="tpu_custom_call" | custom-call | flops 19730006016 | bytes 40000000 | tf_op jit(solution)/shard_map/layer_back/pallas_call | solution.py:605
  632.0 23.8 %adapters.1 = f32[2,96,256]{2,1,0:T(8,128)} custom-call(s32[1]{0:T(128)} %copy.116.refs_0_, f32[128,768]{1,0:T(8,128)} %get-tuple-element.156.refs_1_, f32[128,768]{1,0:T(8,128)} %get-tuple-element.157.refs_2_, f32[128,2304]{1,0:T(8,128)} %get-tuple-element.158.refs_3_, f32[128,768]{1,0:T(8,128)} %get-tuple-element.159.refs_4_, ...), custom_call_target="tpu_custom_call" | custom-call | tf_op jit(solution)/shard_map/adapters/pallas_call | solution.py:1477
  (117 shorter events, 62.1 us)
Async XLA Ops:
  7.2 225.7 %all-gather.14.cloned.1.call-start = ((), (), s32[]{:S(2)}) async-start(), calls=%async_computation.6 | async-start | bytes 3932160 | tf_op jit(solution)/shard_map/all_gather | solution.py:1578
  10.6 222.3 %all-gather.12.cloned.1.call-start = ((), (), s32[]{:S(2)}) async-start(), calls=%async_computation.5 | async-start | bytes 3932160 | tf_op jit(solution)/shard_map/all_gather | solution.py:1523
  71.2 161.7 %all-gather.16.cloned.1.call-start = ((), (), s32[]{:S(2)}) async-start(), calls=%async_computation.7 | async-start | bytes 3932160 | tf_op jit(solution)/shard_map/all_gather | solution.py:1584
  72.0 298.0 %all-gather.8.cloned.1.call-start = ((), (), s32[]{:S(2)}) async-start(), calls=%async_computation.3 | async-start | bytes 7864320 | tf_op jit(solution)/shard_map/all_gather | solution.py:1523
  74.7 1.9 copy-start.15
  74.7 3.2 copy-start.16
  74.8 3.2 copy-start.14
  75.5 4.5 copy-start.19
  75.5 5.6 copy-start.20
  81.1 3.8 copy-start
  85.0 2.1 copy-start.13
  87.1 7.2 %copy-start.17 = (f32[2,2,768]{2,1,0:T(2,128)S(1)}, f32[2,2,768]{2,1,0:T(2,128)}, u32[]{:S(2)}) copy-start(f32[2,2,768]{2,1,0:T(2,128)} %param.28) | copy-start | bytes 36868
  87.1 7.8 %copy-start.9 = (bf16[2,4,16,768]{3,2,0,1:T(8,128)(2,1)S(1)}, bf16[2,4,16,768]{3,2,0,1:T(8,128)(2,1)}, u32[]{:S(2)}) copy-start(bf16[2,4,16,768]{3,2,0,1:T(8,128)(2,1)} %copy-done.8) | copy-start | bytes 589828
  140.0 19.2 %collective-permute-start = (bf16[96,4096]{1,0:T(8,128)(2,1)S(1)}, bf16[96,4096]{1,0:T(8,128)(2,1)S(1)}, u32[]{:S(2)}, u32[]{:S(2)}) collective-permute-start(bf16[96,4096]{1,0:T(8,128)(2,1)S(1)} %get-tuple-element.181), channel_id=1, source_target_pairs={{0,1},{1,0},{2,3},{3,2},{4,5},{5,4},{6,7},{7,6},{8,9},{9,8},{10,11... | collective-permute-start | bytes 2359304 | tf_op jit(solution)/shard_map/ppermute | solution.py:1514
  167.8 4.4 copy-start.2
  167.8 65.0 %all-to-all-start = ((bf16[8,192,768]{2,1,0:T(8,128)(2,1)}), bf16[8,192,768]{2,1,0:T(8,128)(2,1)S(1)}, u32[]{:S(2)}, u32[]{:S(2)}) async-start(bf16[8,192,768]{2,1,0:T(8,128)(2,1)} %dispatch.2), calls=%async_computation | async-start | bytes 4718592 | tf_op jit(solution)/shard_map/all_to_all | solution.py:1527
  172.2 231.1 %all-gather.10.cloned.1.call-start = ((), (), s32[]{:S(2)}) async-start(), calls=%async_computation.4 | async-start | bytes 3932160 | tf_op jit(solution)/shard_map/all_gather | solution.py:1523
  172.2 2.2 copy-start.10
  173.0 57.7 %collective-permute-start.1 = (bf16[256,768]{1,0:T(8,128)(2,1)}, bf16[256,768]{1,0:T(8,128)(2,1)}, u32[]{:S(2)}, u32[]{:S(2)}) collective-permute-start(bf16[256,768]{1,0:T(8,128)(2,1)} %get-tuple-element.191), channel_id=1, source_target_pairs={{0,1},{1,0},{2,3},{3,2},{4,5},{5,4},{6,7},{7,6},{8,9},{9,8},{10,11... | collective-permute-start | bytes 1179656 | tf_op jit(solution)/shard_map/ppermute | solution.py:1514
  179.6 50.4 %copy-start.18 = (f32[2,2,768]{2,1,0:T(2,128)S(1)}, f32[2,2,768]{2,1,0:T(2,128)}, u32[]{:S(2)}) copy-start(f32[2,2,768]{2,1,0:T(2,128)} %param.36) | copy-start | bytes 36868
  331.5 32.1 %all-to-all-start.1 = ((bf16[8,192,768]{2,1,0:T(8,128)(2,1)}), bf16[8,192,768]{2,1,0:T(8,128)(2,1)S(1)}, u32[]{:S(2)}, u32[]{:S(2)}) async-start(bf16[8,192,768]{2,1,0:T(8,128)(2,1)} %dispatch.3), calls=%async_computation.1 | async-start | bytes 4718592 | tf_op jit(solution)/shard_map/all_to_all | solution.py:1527
  345.7 23.4 %copy-start.11 = (bf16[2,128,768]{2,1,0:T(8,128)(2,1)S(1)}, bf16[2,128,768]{2,1,0:T(8,128)(2,1)}, u32[]{:S(2)}) copy-start(bf16[2,128,768]{2,1,0:T(8,128)(2,1)} %get-tuple-element.134) | copy-start | bytes 1179652
  365.0 38.3 %all-to-all-start.2 = ((bf16[8,192,768]{2,1,0:T(8,128)(2,1)}), bf16[8,192,768]{2,1,0:T(8,128)(2,1)S(1)}, u32[]{:S(2)}, u32[]{:S(2)}) async-start(bf16[8,192,768]{2,1,0:T(8,128)(2,1)} %dispatch_grad.1), calls=%async_computation.2 | async-start | bytes 4718592 | tf_op jit(solution)/shard_map/all_to_all | solution.py:1527
  632.0 26.2 %copy-start.1 = (f32[1024,768]{1,0:T(8,128)S(1)}, f32[1024,768]{1,0:T(8,128)}, u32[]{:S(2)}) copy-start(f32[1024,768]{1,0:T(8,128)} %get-tuple-element.222) | copy-start | bytes 9437188
  (7 other events, 9.1 us)
Sparse Core Ops, SparseCore 0:
  10.7 73.1 all-gather.13
  85.5 63.0 all-gather.11
  150.1 73.4 all-gather.15
  225.0 114.6 all-gather.7
  341.1 62.0 all-gather.9

commit v8 on v7

--- a/solution.py
+++ b/solution.py
@@ -559,7 +559,7 @@
             acc[...] += part
             return carry
 
-        lax.fori_loop(0, FF // FC, step, 0)
+        lax.fori_loop(0, FF // FC, step, 0, unroll=2)
         pv[p] = acc[...].astype(BF)
         moves += give_back(pv, p, ret_ref, send, recv, kind)
         for values, ref, sems in ((gv, gate_ref, gsem), (uv, up_ref, usem)):
@@ -666,7 +666,7 @@
             kept[2][p, :, at] = silu.astype(BF)
             return carry
 
-        lax.fori_loop(0, FF // FC, step, 0)
+        lax.fori_loop(0, FF // FC, step, 0, unroll=2)
         for n in range(3):
             stores.append(pltpu.make_async_copy(kept[n].at[p], outs[n].at[p], osem.at[p, n]))
             stores[-1].start()
@@ -746,7 +746,7 @@
             )
             return carry
 
-        lax.fori_loop(0, FF // FC, step, 0)
+        lax.fori_loop(0, FF // FC, step, 0, unroll=2)
         qv[p] = acc[...].astype(BF)
         later += give_back(qv, p, gback, gsend, grecv, kind)
     for copy in moves:
@@ -899,7 +899,7 @@
             acc[...] += backward_chunk(grads, gate, up, w1, w2, f)
             return carry
 
-        lax.fori_loop(0, FF // FC, step, 0)
+        lax.fori_loop(0, FF // FC, step, 0, unroll=2)
         pv[p] = acc[...].astype(BF)
         moves += give_back(pv, p, back, send, recv, kind)
 

time: 670 us -> 670 us (level)
  transfers between devices with their start and end apart: 10 -> 10, of which waited for: 3 -> 3; matrix products, arithmetic and copies ran while one was open for 6% -> 6% of each run, Pallas kernels for 43% -> 42%
where the time goes in v8:
time: 670 us; the launch traced here: 666 us
  Pallas kernels  534 us (80%)
  waiting for transfers between devices  51.3 us (8%)
  local copies, waits for them, and re-layouts  41.5 us (6%)
  starting transfers between devices  15.1 us (2%)
  between operations  15.1 us (2%)
  other arithmetic  9.59 us (1%)
    pallas_call x8, Pallas kernels, comm_call(): pl.pallas_call(run, in_specs=[pl.BlockSpec(memory_space=pl.ANY)] * len(in...  387 us
    pallas_call x11, Pallas kernels, call(): pl.pallas_call(body, grid=grid, in_specs=[spec(e) for e in ins], out_spec...  123 us
    pallas_call x1, Pallas kernels, adapters(): pl.pallas_call(adapters_body, in_specs=specs, out_specs=pl.BlockSpec(memo...  23.7 us
    ppermute x2, waiting for transfers between devices, across_y(): return lax.ppermute(v, 'y', [(0, 1), (1, 0)])  18.9 us
    all_to_all x3, waiting for transfers between devices, exchange(): lax.all_to_all(v, OWNERS[kind], split_axis=0, concat_axis=0, tiled=True)  17.9 us
    all_gather x3, waiting for transfers between devices, gathered(): return lax.all_gather(w, axes, axis=0, tiled=True).reshape(-1, w.shape[-1])  13.7 us
  transfers between devices with their start and end apart: 10, of which 3 were waited for; matrix products, arithmetic and copies ran while one was open for 6% of the time, Pallas kernels for 42%

profile of v8, /device:TPU:9, one launch (start us, length us, event | category | flops | bytes accessed | tf_op | source)
XLA Modules:
  0.0 666.5 jit_solution(7456667090703620193)
XLA Ops:
  17.3 51.7 %gather_shared.2 = (bf16[4,768,768]{2,1,0:T(8,128)(2,1)}, bf16[96,4096]{1,0:T(8,128)(2,1)}, bf16[256,768]{1,0:T(8,128)(2,1)}) custom-call(bf16[96,768]{1,0:T(8,128)(2,1)} %bitcast.124, bf16[96,4096]{1,0:T(8,128)(2,1)} %get-tuple-element.179.refs_1_, bf16[256,768]{1,0:T(8,128)(2,1)} %get-tuple-element.189.refs_2_), custom_call_target="tpu_custom_call" | custom-call | bytes 50000000 | tf_op jit(solution)/shard_map/gather_shared/pallas_call | solution.py:605
  87.5 6.3 prep.1
  98.3 11.1 %project.2 = (bf16[1024,768]{1,0:T(8,128)(2,1)}, bf16[1024,128]{1,0:T(8,128)(2,1)}, bf16[1024,2304]{1,0:T(8,128)(2,1)}) custom-call(bf16[1024,768]{1,0:T(8,128)(2,1)} %refs_7_.3, f32[1,768]{1,0:T(1,128)} %get-tuple-element.214.g_ref.refs_8_, bf16[4,768,768]{2,1,0:T(8,128)(2,1)} %get-tuple-element.102.w_ref.refs_10_.refs_3_, ...), custom_call_target="tpu_custom_call" | custom-call | flops 3623878656 | bytes 12000000 | tf_op jit(solution)/shard_map/project/pallas_call | solution.py:72
  109.4 21.4 %attend.2 = (bf16[1024,768]{1,0:T(8,128)(2,1)}, bf16[6,1024,128]{2,1,0:T(8,128)(2,1)}) custom-call(bf16[1024,2304]{1,0:T(8,128)(2,1)} %get-tuple-element.105.q_ref.k_ref.v_ref.refs_4_, bf16[1024,2304]{1,0:T(8,128)(2,1)} %get-tuple-element.105.q_ref.k_ref.v_ref.refs_4_, bf16[1024,2304]{1,0:T(8,128)(2,1)} %get-tuple-element.105.q_ref.k_ref.v_ref.refs_4_, ...), custom_call_target="tpu_custom_call" | custom-call | flops 6442450944 | bytes 8000000 | tf_op jit(solution)/shard_map/attend/pallas_call | solution.py:72
  131.6 8.7 %settle.2 = (f32[1024,768]{1,0:T(8,128)}, bf16[1024,768]{1,0:T(8,128)(2,1)}, f32[1024,128]{1,0:T(8,128)}, bf16[1024,128]{1,0:T(8,128)(2,1)}) custom-call(bf16[1024,768]{1,0:T(8,128)(2,1)} %refs_7_.3, bf16[1024,768]{1,0:T(8,128)(2,1)} %get-tuple-element.108.mixed_ref.refs_9_.refs_2_, bf16[4,768,768]{2,1,0:T(8,128)(2,1)} %get-tuple-element.102.w_ref.refs_10_.refs_3_, ...), custom_call_target="tpu_custom_call" | custom-call | flops 2415919104 | bytes 10000000 | tf_op jit(solution)/shard_map/settle/pallas_call | solution.py:72
  140.7 18.9 %collective-permute-done = bf16[96,4096]{1,0:T(8,128)(2,1)S(1)} collective-permute-done((bf16[96,4096]{1,0:T(8,128)(2,1)S(1)}, bf16[96,4096]{1,0:T(8,128)(2,1)S(1)}, u32[]{:S(2)}, u32[]{:S(2)}) %collective-permute-start) | collective-permute-done | bytes 786464 | tf_op jit(solution)/shard_map/ppermute | solution.py:1514
  161.1 6.9 %dispatch.2 = bf16[8,192,768]{2,1,0:T(8,128)(2,1)} custom-call(s32[8,1024]{1,0:T(8,128)} %get-tuple-element.116.trow_ref.refs_11_, bf16[1024,768]{1,0:T(8,128)(2,1)} %get-tuple-element.120.s_ref), custom_call_target="tpu_custom_call" | custom-call | flops 2415919104 | bytes 4000000 | tf_op jit(solution)/shard_map/dispatch/pallas_call | solution.py:72
  168.1 4.5 all-to-all-start
  180.0 50.4 %gather_shared.3.w_ref.refs_9_.refs_3_ = bf16[4,768,768]{2,1,0:T(8,128)(2,1)} custom-call(bf16[96,768]{1,0:T(8,128)(2,1)} %bitcast.122), custom_call_target="tpu_custom_call" | custom-call | bytes 50000000 | tf_op jit(solution)/shard_map/gather_shared/pallas_call | solution.py:605
  234.6 38.4 %expert_forward.1 = (bf16[8,192,768]{2,1,0:T(8,128)(2,1)}, bf16[4,384,2048]{2,1,0:T(8,128)(2,1)}, bf16[4,384,2048]{2,1,0:T(8,128)(2,1)}) custom-call(bf16[4,96,4096]{2,1,0:T(8,128)(2,1)} %bitcast.132, bf16[4,96,4096]{2,1,0:T(8,128)(2,1)} %bitcast.136, bf16[2048,768]{1,0:T(8,128)(2,1)} %bitcast.134, bf16[8,192,768]{2,1,0:T(8,128)(2,1)} %copy-done.3), custom_call_target="tpu_custom_call" | custom-call | flops 14495514624 | bytes 26000000 | tf_op jit(solution)/shard_map/expert_forward/pallas_call | solution.py:605
  273.0 10.3 %combine.1 = (f32[1024,768]{1,0:T(8,128)}, bf16[1024,768]{1,0:T(8,128)(2,1)}, bf16[1024,768]{1,0:T(8,128)(2,1)}) custom-call(s32[1024,128]{1,0:T(8,128)} %get-tuple-element.117.tcol_ref.refs_10_.refs_12_, bf16[1536,768]{1,0:T(8,128)(2,1)} %bitcast.139, f32[1024,768]{1,0:T(8,128)} %get-tuple-element.122.mid_ref.refs_6_, ...), custom_call_target="tpu_custom_call" | custom-call | flops 4831838208 | bytes 12000000 | tf_op jit(solution)/shard_map/combine/pallas_call | solution.py:72
  283.3 11.1 %project.3 = (bf16[1024,768]{1,0:T(8,128)(2,1)}, bf16[1024,128]{1,0:T(8,128)(2,1)}, bf16[1024,2304]{1,0:T(8,128)(2,1)}) custom-call(f32[1024,768]{1,0:T(8,128)} %get-tuple-element.123.x_ref.refs_7_, f32[1,768]{1,0:T(1,128)} %get-tuple-element.215.g_ref.refs_8_, bf16[4,768,768]{2,1,0:T(8,128)(2,1)} %gather_shared.3.w_ref.refs_9_.refs_3_, ...), custom_call_target="tpu_custom_call" | custom-call | flops 3623878656 | bytes 12000000 | tf_op jit(solution)/shard_map/project/pallas_call | solution.py:72
  294.5 21.3 %attend.3 = (bf16[1024,768]{1,0:T(8,128)(2,1)}, bf16[6,1024,128]{2,1,0:T(8,128)(2,1)}) custom-call(bf16[1024,2304]{1,0:T(8,128)(2,1)} %get-tuple-element.126.q_ref.k_ref.v_ref.refs_4_, bf16[1024,2304]{1,0:T(8,128)(2,1)} %get-tuple-element.126.q_ref.k_ref.v_ref.refs_4_, bf16[1024,2304]{1,0:T(8,128)(2,1)} %get-tuple-element.126.q_ref.k_ref.v_ref.refs_4_, ...), custom_call_target="tpu_custom_call" | custom-call | flops 6442450944 | bytes 8000000 | tf_op jit(solution)/shard_map/attend/pallas_call | solution.py:72
  315.8 8.7 %settle.3 = (f32[1024,768]{1,0:T(8,128)}, bf16[1024,768]{1,0:T(8,128)(2,1)}, f32[1024,128]{1,0:T(8,128)}, bf16[1024,128]{1,0:T(8,128)(2,1)}) custom-call(f32[1024,768]{1,0:T(8,128)} %get-tuple-element.123.x_ref.refs_7_, bf16[1024,768]{1,0:T(8,128)(2,1)} %get-tuple-element.127.mixed_ref.refs_8_.refs_2_, ...), custom_call_target="tpu_custom_call" | custom-call | flops 2415919104 | bytes 10000000 | tf_op jit(solution)/shard_map/settle/pallas_call | solution.py:72
  324.5 6.9 %dispatch.3 = bf16[8,192,768]{2,1,0:T(8,128)(2,1)} custom-call(s32[8,1024]{1,0:T(8,128)} %get-tuple-element.116.trow_ref.refs_11_, bf16[1024,768]{1,0:T(8,128)(2,1)} %get-tuple-element.128.s_ref), custom_call_target="tpu_custom_call" | custom-call | flops 2415919104 | bytes 4000000 | tf_op jit(solution)/shard_map/dispatch/pallas_call | solution.py:72
  335.4 10.3 %dispatch_grad.1 = bf16[8,192,768]{2,1,0:T(8,128)(2,1)} custom-call(s32[8,1024]{1,0:T(8,128)} %get-tuple-element.116.trow_ref.refs_11_, bf16[1024,768]{1,0:T(8,128)(2,1)} %refs_7_.2, f32[1024,128]{1,0:T(8,128)} %get-tuple-element.132.lg_ref.refs_11_, s32[1024,2]{1,0:T(8,128)} %copy.89.rt_ref.refs_12_.refs_14_), custom_call_target="tpu_custom_call" | custom-call | flops 4831838208 | bytes 6000000 | tf_op jit(solution)/shard_map/dispatch_grad/pallas_call | solution.py:72
  345.7 17.9 %all-to-all-done.1.refs_1_ = bf16[8,192,768]{2,1,0:T(8,128)(2,1)S(1)} async-done(((bf16[8,192,768]{2,1,0:T(8,128)(2,1)}), bf16[8,192,768]{2,1,0:T(8,128)(2,1)S(1)}, u32[]{:S(2)}, u32[]{:S(2)}) %all-to-all-start.1) | async-done | bytes 2359328 | tf_op jit(solution)/shard_map/all_to_all | solution.py:1527
  370.2 19.4 %expert_parts.1 = (bf16[4,384,2048]{2,1,0:T(8,128)(2,1)}, bf16[4,384,2048]{2,1,0:T(8,128)(2,1)}, bf16[4,384,2048]{2,1,0:T(8,128)(2,1)}) custom-call(bf16[768,4096]{1,0:T(8,128)(2,1)} %bitcast.130, bf16[8,192,768]{2,1,0:T(8,128)(2,1)} %copy-done.5), custom_call_target="tpu_custom_call" | custom-call | flops 9663676416 | bytes 28000000 | tf_op jit(solution)/shard_map/expert_parts/pallas_call | solution.py:605
  389.6 13.7 %all-gather.10.cloned.1.call-done = bf16[8,256,768]{2,1,0:T(8,128)(2,1)} async-done(((bf16[2,256,768]{2,1,0:T(8,128)(2,1)}), bf16[8,256,768]{2,1,0:T(8,128)(2,1)}) %all-gather.10.cloned.1.call-update) | async-done | bytes 3145744 | tf_op jit(solution)/shard_map/all_gather | solution.py:1523
  404.8 69.3 %expert_both.1 = (bf16[1024,768]{1,0:T(8,128)(2,1)}, f32[1024,768]{1,0:T(8,128)}, f32[1024,768]{1,0:T(8,128)}, f32[1024,128]{1,0:T(8,128)}, f32[128,768]{1,0:T(8,128)}, /*index=5*/f32[128,768]{1,0:T(8,128)}) custom-call(bf16[768,4096]{1,0:T(8,128)(2,1)} %bitcast.131, bf16[2048,768]{1,0:T(8,128)(2,1)} %bitcast.138, ...), custom_call_target="tpu_custom_call" | custom-call | flops 19327352832 | bytes 40000000 | tf_op jit(solution)/shard_map/expert_both/pallas_call | solution.py:605
  474.1 44.6 %layer_back.2 = (f32[1024,768]{1,0:T(8,128)}, f32[128,2304]{1,0:T(8,128)}, f32[128,768]{1,0:T(8,128)}) custom-call(f32[1024,768]{1,0:T(8,128)} %get-tuple-element.140.refs_0_, bf16[1024,768]{1,0:T(8,128)(2,1)} %get-tuple-element.141.refs_1_, bf16[1024,768]{1,0:T(8,128)(2,1)} %get-tuple-element.127.mixed_ref.refs_8_.refs_2_, ...), custom_call_target="tpu_custom_call" | custom-call | flops 19730006016 | bytes 40000000 | tf_op jit(solution)/shard_map/layer_back/pallas_call | solution.py:605
  518.7 68.7 %expert_backward.1 = (bf16[1024,768]{1,0:T(8,128)(2,1)}, f32[1024,768]{1,0:T(8,128)}, f32[128,768]{1,0:T(8,128)}, f32[128,768]{1,0:T(8,128)}) custom-call(bf16[4,96,4096]{2,1,0:T(8,128)(2,1)} %bitcast.133, bf16[4,96,4096]{2,1,0:T(8,128)(2,1)} %bitcast.137, bf16[2048,768]{1,0:T(8,128)(2,1)} %bitcast.135, bf16[4,384,2048]{2,1,0:T(8,128)(2,1)} %get-tuple-element.138.refs_3_, ...), custom_call_target="tpu_custom_call" | custom-call | flops 14495514624 | bytes 26000000 | tf_op jit(solution)/shard_map/expert_backward/pallas_call | solution.py:605
  587.5 44.4 %layer_back.3 = (f32[1024,768]{1,0:T(8,128)}, f32[128,2304]{1,0:T(8,128)}, f32[128,768]{1,0:T(8,128)}) custom-call(f32[1024,768]{1,0:T(8,128)} %get-tuple-element.150.refs_0_, bf16[1024,768]{1,0:T(8,128)(2,1)} %get-tuple-element.151.refs_1_, bf16[1024,768]{1,0:T(8,128)(2,1)} %get-tuple-element.108.mixed_ref.refs_9_.refs_2_, ...), custom_call_target="tpu_custom_call" | custom-call | flops 19730006016 | bytes 40000000 | tf_op jit(solution)/shard_map/layer_back/pallas_call | solution.py:605
  631.9 23.7 %adapters.1 = f32[2,96,256]{2,1,0:T(8,128)} custom-call(s32[1]{0:T(128)} %copy.116.refs_0_, f32[128,768]{1,0:T(8,128)} %get-tuple-element.156.refs_1_, f32[128,768]{1,0:T(8,128)} %get-tuple-element.157.refs_2_, f32[128,2304]{1,0:T(8,128)} %get-tuple-element.158.refs_3_, f32[128,768]{1,0:T(8,128)} %get-tuple-element.159.refs_4_, ...), custom_call_target="tpu_custom_call" | custom-call | tf_op jit(solution)/shard_map/adapters/pallas_call | solution.py:1477
  (117 shorter events, 62.6 us)
Async XLA Ops:
  7.2 226.1 %all-gather.14.cloned.1.call-start = ((), (), s32[]{:S(2)}) async-start(), calls=%async_computation.6 | async-start | bytes 3932160 | tf_op jit(solution)/shard_map/all_gather | solution.py:1578
  10.6 222.7 %all-gather.12.cloned.1.call-start = ((), (), s32[]{:S(2)}) async-start(), calls=%async_computation.5 | async-start | bytes 3932160 | tf_op jit(solution)/shard_map/all_gather | solution.py:1523
  71.2 162.0 %all-gather.16.cloned.1.call-start = ((), (), s32[]{:S(2)}) async-start(), calls=%async_computation.7 | async-start | bytes 3932160 | tf_op jit(solution)/shard_map/all_gather | solution.py:1584
  72.0 298.2 %all-gather.8.cloned.1.call-start = ((), (), s32[]{:S(2)}) async-start(), calls=%async_computation.3 | async-start | bytes 7864320 | tf_op jit(solution)/shard_map/all_gather | solution.py:1523
  75.1 1.9 copy-start.15
  75.1 3.2 copy-start.16
  75.1 3.2 copy-start.14
  75.9 4.5 copy-start.19
  75.9 5.6 copy-start.20
  81.5 3.8 copy-start
  85.3 2.1 copy-start.13
  87.5 7.2 %copy-start.17 = (f32[2,2,768]{2,1,0:T(2,128)S(1)}, f32[2,2,768]{2,1,0:T(2,128)}, u32[]{:S(2)}) copy-start(f32[2,2,768]{2,1,0:T(2,128)} %param.28) | copy-start | bytes 36868
  87.5 7.8 %copy-start.9 = (bf16[2,4,16,768]{3,2,0,1:T(8,128)(2,1)S(1)}, bf16[2,4,16,768]{3,2,0,1:T(8,128)(2,1)}, u32[]{:S(2)}) copy-start(bf16[2,4,16,768]{3,2,0,1:T(8,128)(2,1)} %copy-done.8) | copy-start | bytes 589828
  140.4 19.2 %collective-permute-start = (bf16[96,4096]{1,0:T(8,128)(2,1)S(1)}, bf16[96,4096]{1,0:T(8,128)(2,1)S(1)}, u32[]{:S(2)}, u32[]{:S(2)}) collective-permute-start(bf16[96,4096]{1,0:T(8,128)(2,1)S(1)} %get-tuple-element.181), channel_id=1, source_target_pairs={{0,1},{1,0},{2,3},{3,2},{4,5},{5,4},{6,7},{7,6},{8,9},{9,8},{10,11... | collective-permute-start | bytes 2359304 | tf_op jit(solution)/shard_map/ppermute | solution.py:1514
  168.1 4.5 copy-start.2
  168.1 65.1 %all-to-all-start = ((bf16[8,192,768]{2,1,0:T(8,128)(2,1)}), bf16[8,192,768]{2,1,0:T(8,128)(2,1)S(1)}, u32[]{:S(2)}, u32[]{:S(2)}) async-start(bf16[8,192,768]{2,1,0:T(8,128)(2,1)} %dispatch.2), calls=%async_computation | async-start | bytes 4718592 | tf_op jit(solution)/shard_map/all_to_all | solution.py:1527
  172.6 230.7 %all-gather.10.cloned.1.call-start = ((), (), s32[]{:S(2)}) async-start(), calls=%async_computation.4 | async-start | bytes 3932160 | tf_op jit(solution)/shard_map/all_gather | solution.py:1523
  172.6 2.2 copy-start.10
  173.4 57.7 %collective-permute-start.1 = (bf16[256,768]{1,0:T(8,128)(2,1)}, bf16[256,768]{1,0:T(8,128)(2,1)}, u32[]{:S(2)}, u32[]{:S(2)}) collective-permute-start(bf16[256,768]{1,0:T(8,128)(2,1)} %get-tuple-element.191), channel_id=1, source_target_pairs={{0,1},{1,0},{2,3},{3,2},{4,5},{5,4},{6,7},{7,6},{8,9},{9,8},{10,11... | collective-permute-start | bytes 1179656 | tf_op jit(solution)/shard_map/ppermute | solution.py:1514
  180.0 50.4 %copy-start.18 = (f32[2,2,768]{2,1,0:T(2,128)S(1)}, f32[2,2,768]{2,1,0:T(2,128)}, u32[]{:S(2)}) copy-start(f32[2,2,768]{2,1,0:T(2,128)} %param.36) | copy-start | bytes 36868
  331.5 32.1 %all-to-all-start.1 = ((bf16[8,192,768]{2,1,0:T(8,128)(2,1)}), bf16[8,192,768]{2,1,0:T(8,128)(2,1)S(1)}, u32[]{:S(2)}, u32[]{:S(2)}) async-start(bf16[8,192,768]{2,1,0:T(8,128)(2,1)} %dispatch.3), calls=%async_computation.1 | async-start | bytes 4718592 | tf_op jit(solution)/shard_map/all_to_all | solution.py:1527
  345.7 23.7 %copy-start.11 = (bf16[2,128,768]{2,1,0:T(8,128)(2,1)S(1)}, bf16[2,128,768]{2,1,0:T(8,128)(2,1)}, u32[]{:S(2)}) copy-start(bf16[2,128,768]{2,1,0:T(8,128)(2,1)} %get-tuple-element.134) | copy-start | bytes 1179652
  365.0 38.2 %all-to-all-start.2 = ((bf16[8,192,768]{2,1,0:T(8,128)(2,1)}), bf16[8,192,768]{2,1,0:T(8,128)(2,1)S(1)}, u32[]{:S(2)}, u32[]{:S(2)}) async-start(bf16[8,192,768]{2,1,0:T(8,128)(2,1)} %dispatch_grad.1), calls=%async_computation.2 | async-start | bytes 4718592 | tf_op jit(solution)/shard_map/all_to_all | solution.py:1527
  631.9 26.2 %copy-start.1 = (f32[1024,768]{1,0:T(8,128)S(1)}, f32[1024,768]{1,0:T(8,128)}, u32[]{:S(2)}) copy-start(f32[1024,768]{1,0:T(8,128)} %get-tuple-element.222) | copy-start | bytes 9437188
  (7 other events, 9.1 us)
Sparse Core Ops, SparseCore 0:
  10.7 73.1 all-gather.13
  85.5 63.0 all-gather.11
  150.1 73.4 all-gather.15
  225.0 114.6 all-gather.7
  341.1 62.0 all-gather.9
